TPU v7x, 32 devices: a whole 2x2x4 slice. The times are simulated.
32 devices in a mesh: gx: 4 (over z), gy: 8 (over y, x, core).
Axes of the slice: x: 2, y: 2, z: 4, core: 2. Of those that a mesh axis runs over, the one named last changes fastest.
Arguments:
- thickness: float32 [2048, 1024], P('gy', 'gx'), may hold values from 0.5 to 2
- driving: float32 [2, 2048, 1024], P(None, 'gy', 'gx'), may hold values from -6 to 6
- observed: float32 [2, 2048, 1024], P(None, 'gy', 'gx'), may hold values from -2 to 2
- control: float32 [32, 4096], P('gy'), may hold values from 0.5 to 1.5
- ice_mask: int32 [8, 4], replicated, may hold values 0 or 1
- tile_block: int32 [8, 4, 1], replicated, may hold values from 0 to 31
Outputs:
- vel_u: float32 [2048, 1024], P('gy', 'gx')
- vel_v: float32 [2048, 1024], P('gy', 'gx')
- grad_control: float32 [32, 4096], P('gy')
Inputs may be any that keep to these rules, and one draw needn't show every extreme that they name: `tile_block`: every one of the 32 control blocks is named by at least one tile.
All inputs are finite; a program needn't handle non-finite values.
Results may differ from a plain program's by a relative error of at most 0.00015.
Values sent between devices are 32-bit elements; how exact they have to be, the bound alone decides.
No kernel may reach another device: no remote copies, remote signals or barrier semaphores. Data moves between devices by JAX's collectives and lax.ppermute only.
A program may use at most 64 MiB of HBM per device.

v0:
```python
import jax
import jax.numpy as jnp
from jax import lax
from jax.experimental import pallas as pl
from jax.experimental.pallas import tpu as pltpu
from jax.sharding import PartitionSpec as P

TILE = 256
PIC = 4
SW = 2
ADJ = 6
CT = 64
COARSE = 4096

LANES = 128
HALO = 16
OBS = 8
MARGIN = 8
TOP = MARGIN + HALO
ROWS = TILE + 2 * TOP
STEP = 16
PACK = COARSE // LANES
VMEM_LIMIT = 40 * 1024 * 1024

STRIP = ((0, HALO), (HALO, HALO), (2 * HALO, HALO), (3 * HALO, OBS), (3 * HALO + OBS, OBS))

visc_scale = 0.1
strain_floor = 0.05


def lanes_of(rows):
    return lax.broadcasted_iota(jnp.int32, (rows, LANES), 1)


def pack_kernel(thick, drive, obs, top, bottom, left, right, corners):
    fields = (thick, drive.at[0], drive.at[1], obs.at[0], obs.at[1])
    for field, (first, count) in zip(fields, STRIP):
        top[first : first + count, :] = field[0:count, :]
        bottom[first : first + count, :] = field[TILE - count : TILE, :]
    half = TILE // 2
    lane = lanes_of(half)
    for out, col, end in ((left, 0, False), (right, LANES, True)):
        packed = jnp.zeros((half, LANES), jnp.float32)
        for part in range(2):
            for field, (first, count) in zip(fields, STRIP):
                cells = field[part * half : (part + 1) * half, col : col + LANES]
                start = part * 64 + first
                source = LANES - count if end else 0
                moved = pltpu.roll(cells, (start - source) % LANES, 1)
                packed = jnp.where((lane >= start) & (lane < start + count), moved, packed)
        out[...] = packed
    lane = lanes_of(8)
    places = ((top, 0, 0), (top, LANES, LANES - HALO), (bottom, 0, 0), (bottom, LANES, LANES - HALO))
    for k, (strip, col, source) in enumerate(places):
        packed = jnp.zeros((8, LANES), jnp.float32)
        for g in range(8):
            cells = strip[8 * g : 8 * g + 8, col : col + LANES]
            moved = pltpu.roll(cells, (HALO * g - source) % LANES, 1)
            packed = jnp.where((lane >= HALO * g) & (lane < HALO * g + HALO), moved, packed)
        corners[k] = packed


def shift_east(tiles, lane):
    rolled = [pltpu.roll(t, LANES - 1, 1) for t in tiles]
    return [jnp.where(lane == LANES - 1, rolled[(c + 1) % 3], rolled[c]) for c in range(3)]


def shift_west(tiles, lane):
    rolled = [pltpu.roll(t, 1, 1) for t in tiles]
    return [jnp.where(lane == 0, rolled[(c + 2) % 3], rolled[c]) for c in range(3)]


def row_range(reach):
    wide = -(-reach // 8) * 8
    return TOP - wide, TILE + 2 * wide


def over_rows(reach, body):
    start, count = row_range(reach)

    def step(i, carry):
        body(pl.multiple_of(start + i * STEP, 8))
        return carry

    lax.fori_loop(0, count // STEP, step, 0)


def model_kernel(
    tile_block, ice_mask, gathered, thick, drive, obs, north, south, west, east, corner_nw, corner_ne, corner_sw, corner_se,
    vel_u, vel_v, sums,
    ext, fr, ice, visc, vel, coef, blocks, patch, small,
):
    tile_rows, tile_cols = ice_mask.shape
    owned = gathered.shape[1]
    row_tile = lax.axis_index("gy")
    col_tile = lax.axis_index("gx")

    fields = (thick, drive.at[0], drive.at[1], obs.at[0], obs.at[1])
    half = TILE // 2
    lane = lanes_of(half)
    lane8 = lanes_of(8)
    for f, (field, (first, count)) in enumerate(zip(fields, STRIP)):
        for c in range(2):
            cols = slice(c * LANES, (c + 1) * LANES)
            ext[f, c, TOP : TOP + TILE, :] = field[:, cols]
            ext[f, c, TOP - count : TOP, :] = north[first : first + count, cols]
            ext[f, c, TOP + TILE : TOP + TILE + count, :] = south[first : first + count, cols]
        for part in range(2):
            start = part * 64 + first
            from_east = pltpu.roll(east[...], (LANES - start) % LANES, 1)
            from_west = pltpu.roll(west[...], (2 * LANES - count - start) % LANES, 1)
            ext[f, 2, TOP + part * half : TOP + (part + 1) * half, :] = jnp.where(
                lane < count, from_east, jnp.where(lane >= LANES - count, from_west, 0.0)
            )
        for g in range(first // 8, (first + count) // 8):
            for at, lo, hi in (
                (TOP - count, corner_nw, corner_ne),
                (TOP + TILE, corner_sw, corner_se),
            ):
                from_east = pltpu.roll(hi[...], (LANES - HALO * g) % LANES, 1)
                from_west = pltpu.roll(lo[...], (2 * LANES - HALO - HALO * g) % LANES, 1)
                row = at + 8 * g - first
                ext[f, 2, row : row + 8, :] = jnp.where(
                    lane8 < HALO, from_east, jnp.where(lane8 >= LANES - HALO, from_west, 0.0)
                )

    masks = {}
    owner_row = lax.broadcasted_iota(jnp.int32, (owned, LANES), 0)
    for dr in (-1, 0, 1):
        for ds in (-1, 0, 1):
            row, col = row_tile + dr, col_tile + ds
            inside = (row >= 0) & (row < tile_rows) & (col >= 0) & (col < tile_cols)
            row = jnp.clip(row, 0, tile_rows - 1)
            col = jnp.clip(col, 0, tile_cols - 1)
            masks[dr, ds] = jnp.where(inside, ice_mask[row, col], 0).astype(jnp.float32)
            block = tile_block[row, col]
            holder = block // owned
            place = block - holder * owned
            spot = (dr + 1) * 3 + ds + 1
            for j in range(PACK) if dr == 0 else ((PACK - 2, PACK - 1) if dr < 0 else (0, 1)):
                held = gathered[holder, :, j * LANES : (j + 1) * LANES]
                blocks[spot, j : j + 1, :] = jnp.sum(jnp.where(owner_row == place, held, 0.0), axis=0, keepdims=True)
    for dr, first, count in ((-1, MARGIN, HALO), (0, TOP, TILE), (1, TOP + TILE, HALO)):
        rows_lane = lanes_of(count)
        for c in range(2):
            ice[c, first : first + count, :] = jnp.full((count, LANES), masks[dr, 0])
        ice[2, first : first + count, :] = jnp.where(
            rows_lane < HALO, masks[dr, 1], jnp.where(rows_lane >= LANES - HALO, masks[dr, -1], 0.0)
        )

    for dr, first, count, at in ((-1, PACK - 2, 2, 0), (0, 0, PACK, 4), (1, 0, 2, 68)):
        lo, mid, hi = (blocks[(dr + 1) * 3 + k, first : first + count, :] for k in range(3))
        wide = lanes_of(count)
        even = jnp.where(wide < 64, mid, jnp.where(wide < 96, pltpu.roll(hi, 64, 1), pltpu.roll(lo, 64, 1)))
        odd = jnp.where(wide < 64, pltpu.roll(mid, 64, 1), jnp.where(wide < 96, hi, lo))
        patch[pl.ds(at, count, stride=2), :] = jnp.exp(even)
        patch[pl.ds(at + 1, count, stride=2), :] = jnp.exp(odd)
    cells = patch[...]
    lane72 = lanes_of(72)
    for c in range(3):
        source = 32 * c + lane72 // 4
        if c == 2:
            source = jnp.where(lane72 < 64, source, source + 32)
        wide = jnp.take_along_axis(cells, source, axis=1)
        for j in range(4):
            fr[c, pl.ds(MARGIN + j, 72, stride=4), :] = wide

    lane = lanes_of(STEP)
    tiles = range(3)

    def load(ref, row, *lead):
        return [ref[(*lead, c, pl.ds(row, STEP), slice(None))] for c in tiles]

    def store(ref, row, values, *lead):
        for c in tiles:
            ref[(*lead, c, pl.ds(row, STEP), slice(None))] = values[c]

    def viscosity(reach, now):
        def body(row):
            thickness = load(ext, row, 0)
            if now is None:
                store(visc, row, [visc_scale * t * strain_floor ** (-1.0 / 3.0) for t in thickness])
                return
            u, v = load(vel, row, now, 0), load(vel, row, now, 1)
            u_n, v_n = load(vel, row - 1, now, 0), load(vel, row - 1, now, 1)
            u_s, v_s = load(vel, row + 1, now, 0), load(vel, row + 1, now, 1)
            u_e, u_w = shift_east(u, lane), shift_west(u, lane)
            v_e, v_w = shift_east(v, lane), shift_west(v, lane)
            result = []
            for c in tiles:
                ux, vx = u_e[c] - u_w[c], v_e[c] - v_w[c]
                uy, vy = u_s[c] - u_n[c], v_s[c] - v_n[c]
                shear = uy + vx
                strain = 0.25 * (ux * ux + vy * vy + ux * vy + 0.25 * (shear * shear)) + strain_floor
                result.append(visc_scale * thickness[c] * jnp.exp(jnp.log(strain) * (-1.0 / 3.0)))
            store(visc, row, result)

        over_rows(reach, body)

    def coefficients(row):
        m, m_n, m_s = load(visc, row), load(visc, row - 1), load(visc, row + 1)
        m_w = shift_west(m, lane)
        w = [0.5 * (m[c] + m_w[c]) for c in tiles]
        e = shift_east(w, lane)
        s = [0.5 * (m[c] + m_s[c]) for c in tiles]
        n = [0.5 * (m[c] + m_n[c]) for c in tiles]
        friction, mask = load(fr, row), load(ice, row)
        scale_u, scale_v = [], []
        for c in tiles:
            across, along = e[c] + w[c], s[c] + n[c]
            scale_u.append(mask[c] / (friction[c] + 4.0 * across + along))
            scale_v.append(mask[c] / (friction[c] + across + 4.0 * along))
        corners = []
        for shifted in (
            shift_west(m_s, lane), shift_west(m_n, lane), shift_east(m_s, lane), shift_east(m_n, lane),
        ):
            corners.append([0.5 * m[c] + 0.25 * shifted[c] for c in tiles])
            corners.append([0.25 * m[c] + 0.5 * shifted[c] for c in tiles])
        return [e, w, s, n, scale_u, scale_v] + corners

    def relaxed(row, now, k, forcing):
        e, w, s, n, scale_u, scale_v, sw_u, sw_v, nw_u, nw_v, se_u, se_v, ne_u, ne_v = k
        u, v = load(vel, row, now, 0), load(vel, row, now, 1)
        u_n, v_n = load(vel, row - 1, now, 0), load(vel, row - 1, now, 1)
        u_s, v_s = load(vel, row + 1, now, 0), load(vel, row + 1, now, 1)
        to_west_u, to_east_u, to_west_v, to_east_v = [], [], [], []
        for c in tiles:
            u4 = 4.0 * u[c]
            to_west_u.append(w[c] * u4 + (sw_u[c] * v_s[c] - nw_u[c] * v_n[c]))
            to_east_u.append(e[c] * u4 + (ne_u[c] * v_n[c] - se_u[c] * v_s[c]))
            to_west_v.append(w[c] * v[c] + (sw_v[c] * u_s[c] - nw_v[c] * u_n[c]))
            to_east_v.append(e[c] * v[c] + (ne_v[c] * u_n[c] - se_v[c] * u_s[c]))
        to_west_u, to_west_v = shift_east(to_west_u, lane), shift_east(to_west_v, lane)
        to_east_u, to_east_v = shift_west(to_east_u, lane), shift_west(to_east_v, lane)
        new_u, new_v = [], []
        for c in tiles:
            mid_u = s[c] * u_s[c] + n[c] * u_n[c]
            mid_v = 4.0 * (s[c] * v_s[c] + n[c] * v_n[c])
            new_u.append(scale_u[c] * (forcing[0][c] + mid_u + (to_west_u[c] + to_east_u[c])))
            new_v.append(scale_v[c] * (forcing[1][c] + mid_v + (to_west_v[c] + to_east_v[c])))
        return new_u, new_v

    def put(row, new, values):
        store(vel, row, values[0], new, 0)
        store(vel, row, values[1], new, 1)

    reach = HALO
    now = None
    for picard in range(PIC):
        if picard > 0:
            reach -= 1
        viscosity(reach, now)
        reach -= 1

        def first_sweep(row, now=now, new=0 if now is None else 1 - now):
            k = coefficients(row)
            for i, values in enumerate(k):
                store(coef, row, values, i)
            forcing = load(ext, row, 1), load(ext, row, 2)
            if now is None:
                put(row, new, [[k[4 + i][c] * forcing[i][c] for c in tiles] for i in range(2)])
            else:
                put(row, new, relaxed(row, now, k, forcing))

        over_rows(reach, first_sweep)
        now = 0 if now is None else 1 - now
        for sweep in range(1, SW):
            reach -= 1

            def next_sweep(row, now=now):
                k = [load(coef, row, i) for i in range(14)]
                put(row, 1 - now, relaxed(row, now, k, (load(ext, row, 1), load(ext, row, 2))))

            over_rows(reach, next_sweep)
            now = 1 - now

    final = now
    spare = (1 - now, 2)

    def first_adjoint(row):
        for i in range(2):
            u, seen, scale = load(vel, row, final, i), load(ext, row, 3 + i), load(coef, row, 4 + i)
            misfit = [u[c] - seen[c] for c in tiles]
            store(ext, row, misfit, 1 + i)
            store(vel, row, [scale[c] * misfit[c] for c in tiles], spare[0], i)

    over_rows(reach, first_adjoint)
    for i, out in enumerate((vel_u, vel_v)):
        for c in range(2):
            out[:, c * LANES : (c + 1) * LANES] = vel[final, i, c, TOP : TOP + TILE, :]
    for sweep in range(1, ADJ):
        reach -= 1

        def adjoint_sweep(row, now=spare[(sweep + 1) % 2], new=spare[sweep % 2]):
            k = [load(coef, row, i) for i in range(14)]
            put(row, new, relaxed(row, now, k, (load(ext, row, 1), load(ext, row, 2))))

        over_rows(reach, adjoint_sweep)
    last = spare[(ADJ - 1) % 2]

    def gradient(row):
        for c in range(2):
            at = (c, pl.ds(row, STEP), slice(None))
            dot = vel[(final, 0, *at)] * vel[(last, 0, *at)] + vel[(final, 1, *at)] * vel[(last, 1, *at)]
            visc[at] = -fr[at] * dot

    over_rows(0, gradient)
    down = [sum(visc[c, pl.ds(TOP + j, CT, stride=4), :] for j in range(4)) for c in range(2)]
    k = lax.broadcasted_iota(jnp.int32, (LANES, LANES), 0)
    l = lanes_of(LANES) % CT
    total = jnp.zeros((CT, LANES), jnp.float32)
    for c in range(2):
        total += jnp.dot(
            down[c],
            (k // 4 + 32 * c == l).astype(jnp.float32),
            precision=lax.Precision.HIGHEST,
            preferred_element_type=jnp.float32,
        )
    small[...] = total
    sums[...] = jnp.where(
        lanes_of(PACK) < CT, small[pl.ds(0, PACK, stride=2), :], small[pl.ds(1, PACK, stride=2), :]
    )


def collect_kernel(tile_block, gathered, out, total):
    owned = out.shape[0]
    first = lax.axis_index("gy") * owned
    tile_rows, tile_cols = tile_block.shape
    total[...] = jnp.zeros_like(total)

    def step(t, carry):
        col = t // tile_rows
        place = tile_block[t - col * tile_rows, col] - first

        @pl.when((place >= 0) & (place < owned))
        def _():
            total[place] += gathered[t]

        return carry

    lax.fori_loop(0, tile_rows * tile_cols, step, 0)
    for j in range(PACK):
        out[:, j * LANES : (j + 1) * LANES] = total[:, j, :]


def in_vmem(count):
    return [pl.BlockSpec(memory_space=pltpu.VMEM)] * count


def in_smem(count):
    return [pl.BlockSpec(memory_space=pltpu.SMEM)] * count


def per_device(thickness, driving, observed, control, ice_mask, tile_block):
    f32 = jnp.float32
    rows, cols = lax.axis_size("gy"), lax.axis_size("gx")
    tile_block = tile_block[:, :, 0]
    params = pltpu.CompilerParams(vmem_limit_bytes=VMEM_LIMIT)

    gathered = lax.all_gather(control, "gy", axis=0)
    top, bottom, left, right, corners = pl.pallas_call(
        pack_kernel,
        out_shape=(
            jax.ShapeDtypeStruct((64, TILE), f32),
            jax.ShapeDtypeStruct((64, TILE), f32),
            jax.ShapeDtypeStruct((TILE // 2, LANES), f32),
            jax.ShapeDtypeStruct((TILE // 2, LANES), f32),
            jax.ShapeDtypeStruct((4, 8, LANES), f32),
        ),
        in_specs=in_vmem(3),
        out_specs=in_vmem(5),
        compiler_params=params,
        name="pack",
    )(thickness, driving, observed)

    def moved(cells, dr, ds):
        pairs = []
        for r in range(rows):
            for s in range(cols):
                if 0 <= r + dr < rows and 0 <= s + ds < cols:
                    pairs.append((s * rows + r, (s + ds) * rows + r + dr))
        return lax.ppermute(cells, ("gx", "gy"), pairs)

    north, south = moved(bottom, 1, 0), moved(top, -1, 0)
    west, east = moved(right, 0, 1), moved(left, 0, -1)
    corner_se, corner_sw = moved(corners[0], -1, -1), moved(corners[1], -1, 1)
    corner_ne, corner_nw = moved(corners[2], 1, -1), moved(corners[3], 1, 1)

    vel_u, vel_v, sums = pl.pallas_call(
        model_kernel,
        out_shape=(
            jax.ShapeDtypeStruct((TILE, TILE), f32),
            jax.ShapeDtypeStruct((TILE, TILE), f32),
            jax.ShapeDtypeStruct((PACK, LANES), f32),
        ),
        in_specs=in_smem(2) + in_vmem(12),
        out_specs=in_vmem(3),
        scratch_shapes=[
            pltpu.VMEM((5, 3, ROWS, LANES), f32),
            pltpu.VMEM((3, ROWS, LANES), f32),
            pltpu.VMEM((3, ROWS, LANES), f32),
            pltpu.VMEM((3, ROWS, LANES), f32),
            pltpu.VMEM((3, 2, 3, ROWS, LANES), f32),
            pltpu.VMEM((14, 3, ROWS, LANES), f32),
            pltpu.VMEM((9, PACK, LANES), f32),
            pltpu.VMEM((72, LANES), f32),
            pltpu.VMEM((CT, LANES), f32),
        ],
        compiler_params=params,
        name="model",
    )(
        tile_block, ice_mask, gathered, thickness, driving, observed, north, south, west, east,
        corner_nw, corner_ne, corner_sw, corner_se,
    )

    tiles = lax.all_gather(sums, ("gx", "gy"), axis=0)
    gradient = pl.pallas_call(
        collect_kernel,
        out_shape=jax.ShapeDtypeStruct(control.shape, f32),
        in_specs=in_smem(1) + in_vmem(1),
        out_specs=pl.BlockSpec(memory_space=pltpu.VMEM),
        scratch_shapes=[pltpu.VMEM((control.shape[0], PACK, LANES), f32)],
        compiler_params=params,
        name="collect",
    )(tile_block, tiles)
    return vel_u, vel_v, gradient


def solution(mesh):
    return jax.shard_map(
        per_device,
        mesh=mesh,
        in_specs=(P("gy", "gx"), P(None, "gy", "gx"), P(None, "gy", "gx"), P("gy", None), P(), P()),
        out_specs=(P("gy", "gx"), P("gy", "gx"), P("gy", None)),
        check_vma=False,
    )
```

profile of v0, /device:TPU:0, one launch (start us, length us, event | category | flops | bytes accessed | tf_op | source)
XLA Modules:
  0.0 123.7 jit_solution(7829982083411438419)
XLA Ops:
  0.6 0.0 copy-start
  0.6 1.0 copy-done
  1.7 0.0 copy-start.2
  1.7 1.0 copy-done.2
  2.7 0.0 copy-start.4
  2.7 0.9 copy-done.4
  3.7 0.0 copy-start.6
  3.7 0.0 copy-start.3
  3.7 0.0 copy-start.5
  3.7 0.4 pack.1
  4.1 0.0 copy-start.1
  4.1 1.4 %collective-permute-start.7 = (f32[8,128]{1,0:T(8,128)S(1)}, f32[8,128]{1,0:T(8,128)S(1)}, u32[]{:S(2)}, u32[]{:S(2)}) collective-permute-start(f32[8,128]{1,0:T(8,128)S(1)} %get-tuple-element.19), channel_id=1, source_target_pairs={{9,0},{17,8},{25,16},{10,1},{18,9},{26,17},{11,2},{19,10},{27,18},... | collective-permute-start | bytes 12296 | tf_op jit(solution)/shard_map/ppermute | solution.py:382
  5.5 0.7 collective-permute-start.6
  6.2 0.7 collective-permute-start.5
  6.9 10.1 %collective-permute-start.4 = (f32[8,128]{1,0:T(8,128)S(1)}, f32[8,128]{1,0:T(8,128)S(1)}, u32[]{:S(2)}, u32[]{:S(2)}) collective-permute-start(f32[8,128]{1,0:T(8,128)S(1)} %get-tuple-element.22), channel_id=1, source_target_pairs={{0,9},{8,17},{16,25},{1,10},{9,18},{17,26},{2,11},{10,19},{18,27},... | collective-permute-start | bytes 12296 | tf_op jit(solution)/shard_map/ppermute | solution.py:382
  17.0 2.6 %collective-permute-start = (f32[64,256]{1,0:T(8,128)S(1)}, f32[64,256]{1,0:T(8,128)S(1)}, u32[]{:S(2)}, u32[]{:S(2)}) collective-permute-start(f32[64,256]{1,0:T(8,128)S(1)} %get-tuple-element.11), channel_id=1, source_target_pairs={{0,1},{8,9},{16,17},{24,25},{1,2},{9,10},{17,18},{25,26},{2,3},{10... | collective-permute-start | bytes 196616 | tf_op jit(solution)/shard_map/ppermute | solution.py:382
  19.6 0.0 collective-permute-done.7.corner_se
  19.6 1.3 %collective-permute-start.1 = (f32[64,256]{1,0:T(8,128)S(1)}, f32[64,256]{1,0:T(8,128)S(1)}, u32[]{:S(2)}, u32[]{:S(2)}) collective-permute-start(f32[64,256]{1,0:T(8,128)S(1)} %get-tuple-element.12), channel_id=1, source_target_pairs={{1,0},{9,8},{17,16},{25,24},{2,1},{10,9},{18,17},{26,25},{3,2},{11... | collective-permute-start | bytes 196616 | tf_op jit(solution)/shard_map/ppermute | solution.py:382
  20.9 0.0 collective-permute-done.6.corner_sw
  21.0 3.5 %collective-permute-start.2 = (f32[128,128]{1,0:T(8,128)S(1)}, f32[128,128]{1,0:T(8,128)S(1)}, u32[]{:S(2)}, u32[]{:S(2)}) collective-permute-start(f32[128,128]{1,0:T(8,128)S(1)} %get-tuple-element.13), channel_id=1, source_target_pairs={{0,8},{8,16},{16,24},{1,9},{9,17},{17,25},{2,10},{10,18},{18,26},{... | collective-permute-start | bytes 196616 | tf_op jit(solution)/shard_map/ppermute | solution.py:382
  24.5 0.0 collective-permute-done.5.corner_ne
  24.5 1.3 %collective-permute-start.3 = (f32[128,128]{1,0:T(8,128)S(1)}, f32[128,128]{1,0:T(8,128)S(1)}, u32[]{:S(2)}, u32[]{:S(2)}) collective-permute-start(f32[128,128]{1,0:T(8,128)S(1)} %get-tuple-element.14), channel_id=1, source_target_pairs={{8,0},{16,8},{24,16},{9,1},{17,9},{25,17},{10,2},{18,10},{26,18},{... | collective-permute-start | bytes 196616 | tf_op jit(solution)/shard_map/ppermute | solution.py:382
  25.8 0.0 copy-done.6
  25.8 0.0 copy-start.7
  25.8 13.1 %all-gather.2.gathered = f32[8,4,4096]{2,1,0:T(4,128)S(1)} all-gather(f32[1,4,4096]{2,1,0:T(4,128)S(1)} %bitcast.12), channel_id=2, replica_groups=mesh['gx'=4,'gy'=8] {'gy'}, dimensions={0}, use_global_device_ids=true | all-gather | bytes 589824 | tf_op jit(solution)/shard_map/all_gather | solution.py:360
  38.9 0.0 copy-done.7
  38.9 0.0 copy-start.8
  38.9 0.1 copy.12.tile_block
  39.0 0.6 copy-done.8
  39.6 0.1 copy.13.ice_mask
  39.7 0.0 collective-permute-done.4.corner_nw
  39.7 0.0 collective-permute-done.north
  39.7 0.0 collective-permute-done.1.south
  39.7 0.0 collective-permute-done.2.west
  39.7 0.0 collective-permute-done.3.east
  39.7 0.0 copy-done.3
  39.7 0.0 copy-done.5
  39.7 0.0 copy-done.1
  39.8 40.1 %model.1 = (f32[256,256]{1,0:T(8,128)}, f32[256,256]{1,0:T(8,128)}, f32[32,128]{1,0:T(8,128)S(1)}) custom-call(s32[8,4]{1,0:T(8,128)S(1)} %copy.12.tile_block, s32[8,4]{1,0:T(8,128)S(1)} %copy.13.ice_mask, f32[8,4,4096]{2,1,0:T(4,128)S(1)} %all-gather.2.gathered, f32[256,256]{1,0:T(8,128)S(1)} %copy-done.5, f32[2,256,256]{2,1,0:T(8,128)S(1)} %copy-done.1, ...), custom_call_target="tpu_custom_call" | custom-call | tf_op jit(solution)/shard_map/model/pallas_call | solution.py:389
  79.8 41.8 %all-gather.1 = f32[1024,128]{1,0:T(8,128)S(1)} all-gather(f32[32,128]{1,0:T(8,128)S(1)} %get-tuple-element.18), channel_id=3, replica_groups=mesh['gx'=4,'gy'=8] {'gx','gy'}, dimensions={0}, use_global_device_ids=true | all-gather | bytes 540672 | tf_op jit(solution)/shard_map/all_gather | solution.py:416
  121.7 2.0 %collect.1 = f32[4,4096]{1,0:T(4,128)} custom-call(s32[8,4]{1,0:T(8,128)S(1)} %copy.12.tile_block, f32[32,32,128]{2,1,0:T(8,128)S(1)} %bitcast.11), custom_call_target="tpu_custom_call" | custom-call | tf_op jit(solution)/shard_map/collect/pallas_call | solution.py:417
  (1 shorter events, 0.0 us)
Async XLA Ops:
  0.6 1.0 copy-start
  1.7 1.0 copy-start.2
  2.7 0.9 copy-start.4
  3.7 22.1 %copy-start.6 = (f32[4,4096]{1,0:T(4,128)S(1)}, f32[4,4096]{1,0:T(4,128)}, u32[]{:S(2)}) copy-start(f32[4,4096]{1,0:T(4,128)} %param.9) | copy-start | bytes 196612
  3.7 36.1 %copy-start.3 = (f32[2,256,256]{2,1,0:T(8,128)S(1)}, f32[2,256,256]{2,1,0:T(8,128)}, u32[]{:S(2)}) copy-start(f32[2,256,256]{2,1,0:T(8,128)} %obs.3) | copy-start | bytes 1572868
  3.7 36.1 %copy-start.5 = (f32[256,256]{1,0:T(8,128)S(1)}, f32[256,256]{1,0:T(8,128)}, u32[]{:S(2)}) copy-start(f32[256,256]{1,0:T(8,128)} %thick.3) | copy-start | bytes 786436
  4.1 35.7 %copy-start.1 = (f32[2,256,256]{2,1,0:T(8,128)S(1)}, f32[2,256,256]{2,1,0:T(8,128)}, u32[]{:S(2)}) copy-start(f32[2,256,256]{2,1,0:T(8,128)} %drive.3) | copy-start | bytes 1572868
  4.1 15.5 %collective-permute-start.7 = (f32[8,128]{1,0:T(8,128)S(1)}, f32[8,128]{1,0:T(8,128)S(1)}, u32[]{:S(2)}, u32[]{:S(2)}) collective-permute-start(f32[8,128]{1,0:T(8,128)S(1)} %get-tuple-element.19), channel_id=1, source_target_pairs={{9,0},{17,8},{25,16},{10,1},{18,9},{26,17},{11,2},{19,10},{27,18},... | collective-permute-start | bytes 12296 | tf_op jit(solution)/shard_map/ppermute | solution.py:382
  5.5 15.4 %collective-permute-start.6 = (f32[8,128]{1,0:T(8,128)S(1)}, f32[8,128]{1,0:T(8,128)S(1)}, u32[]{:S(2)}, u32[]{:S(2)}) collective-permute-start(f32[8,128]{1,0:T(8,128)S(1)} %get-tuple-element.20), channel_id=1, source_target_pairs={{1,8},{9,16},{17,24},{2,9},{10,17},{18,25},{3,10},{11,18},{19,26},... | collective-permute-start | bytes 12296 | tf_op jit(solution)/shard_map/ppermute | solution.py:382
  6.2 18.3 %collective-permute-start.5 = (f32[8,128]{1,0:T(8,128)S(1)}, f32[8,128]{1,0:T(8,128)S(1)}, u32[]{:S(2)}, u32[]{:S(2)}) collective-permute-start(f32[8,128]{1,0:T(8,128)S(1)} %get-tuple-element.21), channel_id=1, source_target_pairs={{8,1},{16,9},{24,17},{9,2},{17,10},{25,18},{10,3},{18,11},{26,19},... | collective-permute-start | bytes 12296 | tf_op jit(solution)/shard_map/ppermute | solution.py:382
  6.9 32.8 %collective-permute-start.4 = (f32[8,128]{1,0:T(8,128)S(1)}, f32[8,128]{1,0:T(8,128)S(1)}, u32[]{:S(2)}, u32[]{:S(2)}) collective-permute-start(f32[8,128]{1,0:T(8,128)S(1)} %get-tuple-element.22), channel_id=1, source_target_pairs={{0,9},{8,17},{16,25},{1,10},{9,18},{17,26},{2,11},{10,19},{18,27},... | collective-permute-start | bytes 12296 | tf_op jit(solution)/shard_map/ppermute | solution.py:382
  17.0 22.7 %collective-permute-start = (f32[64,256]{1,0:T(8,128)S(1)}, f32[64,256]{1,0:T(8,128)S(1)}, u32[]{:S(2)}, u32[]{:S(2)}) collective-permute-start(f32[64,256]{1,0:T(8,128)S(1)} %get-tuple-element.11), channel_id=1, source_target_pairs={{0,1},{8,9},{16,17},{24,25},{1,2},{9,10},{17,18},{25,26},{2,3},{10... | collective-permute-start | bytes 196616 | tf_op jit(solution)/shard_map/ppermute | solution.py:382
  19.6 20.1 %collective-permute-start.1 = (f32[64,256]{1,0:T(8,128)S(1)}, f32[64,256]{1,0:T(8,128)S(1)}, u32[]{:S(2)}, u32[]{:S(2)}) collective-permute-start(f32[64,256]{1,0:T(8,128)S(1)} %get-tuple-element.12), channel_id=1, source_target_pairs={{1,0},{9,8},{17,16},{25,24},{2,1},{10,9},{18,17},{26,25},{3,2},{11... | collective-permute-start | bytes 196616 | tf_op jit(solution)/shard_map/ppermute | solution.py:382
  21.0 18.8 %collective-permute-start.2 = (f32[128,128]{1,0:T(8,128)S(1)}, f32[128,128]{1,0:T(8,128)S(1)}, u32[]{:S(2)}, u32[]{:S(2)}) collective-permute-start(f32[128,128]{1,0:T(8,128)S(1)} %get-tuple-element.13), channel_id=1, source_target_pairs={{0,8},{8,16},{16,24},{1,9},{9,17},{17,25},{2,10},{10,18},{18,26},{... | collective-permute-start | bytes 196616 | tf_op jit(solution)/shard_map/ppermute | solution.py:382
  24.5 15.3 %collective-permute-start.3 = (f32[128,128]{1,0:T(8,128)S(1)}, f32[128,128]{1,0:T(8,128)S(1)}, u32[]{:S(2)}, u32[]{:S(2)}) collective-permute-start(f32[128,128]{1,0:T(8,128)S(1)} %get-tuple-element.14), channel_id=1, source_target_pairs={{8,0},{16,8},{24,16},{9,1},{17,9},{25,17},{10,2},{18,10},{26,18},{... | collective-permute-start | bytes 196616 | tf_op jit(solution)/shard_map/ppermute | solution.py:382
  25.8 13.2 %copy-start.7 = (s32[8,4,1]{0,2,1:T(1,128)S(1)}, s32[8,4,1]{0,2,1:T(1,128)}, u32[]{:S(2)}) copy-start(s32[8,4,1]{0,2,1:T(1,128)} %param.11) | copy-start | bytes 388
  38.9 0.7 copy-start.8
where the time goes:
time: 124 us
  blocking collectives  55 us (44%)
  Pallas kernels  42.5 us (34%)
  starting transfers between devices  21.6 us (17%)
  local copies, waits for them, and re-layouts  3.82 us (3%)
    all_gather x1, blocking collectives, per_device(): tiles = lax.all_gather(sums, ('gx', 'gy'), axis=0)  41.8 us
    pallas_call x1, Pallas kernels, per_device(): pl.pallas_call(model_kernel, out_shape=(jax.ShapeDtypeStruct((TILE, TILE)...  40.1 us
    ppermute x8, starting transfers between devices, moved(): return lax.ppermute(cells, ('gx', 'gy'), pairs)  21.6 us
    all_gather x1, blocking collectives, per_device(): gathered = lax.all_gather(control, 'gy', axis=0)  13.1 us
    unnamed x19, local copies, waits for them, and re-layouts  3.73 us
  transfers between devices with their start and end apart: 8, of which 0 were waited for; matrix products, arithmetic and copies ran while one was open for 0% of the time, Pallas kernels for 0%

commit v1 on v0

--- a/solution.py
+++ b/solution.py
@@ -18,12 +18,15 @@
 MARGIN = 8
 TOP = MARGIN + HALO
 ROWS = TILE + 2 * TOP
-STEP = 16
+STEP = 32
 PACK = COARSE // LANES
 VMEM_LIMIT = 40 * 1024 * 1024
 
 STRIP = ((0, HALO), (HALO, HALO), (2 * HALO, HALO), (3 * HALO, OBS), (3 * HALO + OBS, OBS))
 
+PATCH_ROWS = ((-1, PACK - 2, 2, 0), (0, 0, PACK, 4), (1, 0, 2, CT + 4))
+PATCH = CT + 8
+
 visc_scale = 0.1
 strain_floor = 0.05
 
@@ -32,32 +35,86 @@
     return lax.broadcasted_iota(jnp.int32, (rows, LANES), 1)
 
 
-def pack_kernel(thick, drive, obs, top, bottom, left, right, corners):
-    fields = (thick, drive.at[0], drive.at[1], obs.at[0], obs.at[1])
-    for field, (first, count) in zip(fields, STRIP):
-        top[first : first + count, :] = field[0:count, :]
-        bottom[first : first + count, :] = field[TILE - count : TILE, :]
+def patch_lanes(count, ds):
+    lane = lanes_of(count)
+    return (lane < CT) if ds == 0 else ((lane >= CT) & (lane < 96) if ds > 0 else lane >= 96)
+
+
+def pack_kernel(
+    tile_block, control, thick, drive, obs, top, bottom, left, right, patches,
+    held, owned_blocks, sems,
+):
+    copies = []
+    for f, field in enumerate((thick, drive.at[0], drive.at[1], obs.at[0], obs.at[1])):
+        copies.append(pltpu.make_async_copy(field, held.at[f], sems.at[f]))
+        copies[-1].start()
+
+    tile_rows, tile_cols = tile_block.shape
+    owned = control.shape[0]
+    mine = lax.axis_index("gy") * owned
+    col_tile = lax.axis_index("gx")
+    for j in range(PACK):
+        owned_blocks[:, j, :] = control[:, j * LANES : (j + 1) * LANES]
+    patches[...] = jnp.zeros_like(patches)
+
+    def fill(target, carry):
+        for dr, first, count, at in PATCH_ROWS:
+            for ds in (-1, 0, 1):
+                row = jnp.clip(target + dr, 0, tile_rows - 1)
+                col = jnp.clip(col_tile + ds, 0, tile_cols - 1)
+                place = tile_block[row, col] - mine
+
+                @pl.when((place >= 0) & (place < owned))
+                def _():
+                    cells = owned_blocks[place, first : first + count, :]
+                    turned = pltpu.roll(cells, CT, 1)
+                    even, odd = (cells, turned) if ds == 0 else (turned, cells)
+                    inside = patch_lanes(count, ds)
+                    rows = pl.ds(at, count, stride=2)
+                    patches[target, rows, :] += jnp.where(inside, even, 0.0)
+                    rows = pl.ds(at + 1, count, stride=2)
+                    patches[target, rows, :] += jnp.where(inside, odd, 0.0)
+
+        return carry
+
+    lax.fori_loop(0, tile_rows, fill, 0)
+
+    for copy in copies:
+        copy.wait()
+    for f, (first, count) in enumerate(STRIP):
+        for c in range(2):
+            cols = slice(c * LANES, (c + 1) * LANES)
+            top[c, first : first + count, :] = held[f, 0:count, cols]
+            bottom[c, first : first + count, :] = held[f, TILE - count : TILE, cols]
     half = TILE // 2
     lane = lanes_of(half)
     for out, col, end in ((left, 0, False), (right, LANES, True)):
         packed = jnp.zeros((half, LANES), jnp.float32)
         for part in range(2):
-            for field, (first, count) in zip(fields, STRIP):
-                cells = field[part * half : (part + 1) * half, col : col + LANES]
+            for f, (first, count) in enumerate(STRIP):
+                cells = held[f, part * half : (part + 1) * half, col : col + LANES]
                 start = part * 64 + first
                 source = LANES - count if end else 0
                 moved = pltpu.roll(cells, (start - source) % LANES, 1)
                 packed = jnp.where((lane >= start) & (lane < start + count), moved, packed)
         out[...] = packed
-    lane = lanes_of(8)
-    places = ((top, 0, 0), (top, LANES, LANES - HALO), (bottom, 0, 0), (bottom, LANES, LANES - HALO))
-    for k, (strip, col, source) in enumerate(places):
-        packed = jnp.zeros((8, LANES), jnp.float32)
-        for g in range(8):
-            cells = strip[8 * g : 8 * g + 8, col : col + LANES]
-            moved = pltpu.roll(cells, (HALO * g - source) % LANES, 1)
-            packed = jnp.where((lane >= HALO * g) & (lane < HALO * g + HALO), moved, packed)
-        corners[k] = packed
+
+
+def frame_cells(west, east, rows, start, count):
+    from_east = pltpu.roll(east[rows, :], (LANES - start) % LANES, 1)
+    from_west = pltpu.roll(west[rows, :], (2 * LANES - count - start) % LANES, 1)
+    lane = lanes_of(from_east.shape[0])
+    return jnp.where(lane < count, from_east, jnp.where(lane >= LANES - count, from_west, 0.0))
+
+
+def corner_kernel(top, bottom, west, east, top_wide, bottom_wide):
+    half = TILE // 2
+    for narrow, wide, part in ((top, top_wide, 0), (bottom, bottom_wide, 1)):
+        for c in range(2):
+            wide[c] = narrow[c]
+        for first, count in STRIP:
+            rows = slice(half - count, half) if part else slice(0, count)
+            wide[2, first : first + count, :] = frame_cells(west, east, rows, part * 64 + first, count)
 
 
 def shift_east(tiles, lane):
@@ -71,7 +128,7 @@
 
 
 def row_range(reach):
-    wide = -(-reach // 8) * 8
+    wide = HALO if reach > 0 else 0
     return TOP - wide, TILE + 2 * wide
 
 
@@ -86,84 +143,51 @@
 
 
 def model_kernel(
-    tile_block, ice_mask, gathered, thick, drive, obs, north, south, west, east, corner_nw, corner_ne, corner_sw, corner_se,
+    ice_mask, patches, thick, drive, obs, north, south, west, east,
     vel_u, vel_v, sums,
-    ext, fr, ice, visc, vel, coef, blocks, patch, small,
+    ext, fr, ice, visc, vel, coef, small,
 ):
     tile_rows, tile_cols = ice_mask.shape
-    owned = gathered.shape[1]
     row_tile = lax.axis_index("gy")
     col_tile = lax.axis_index("gx")
 
+    cells = jnp.exp(sum(patches[j] for j in range(tile_rows)))
+    lane = lanes_of(PATCH)
+    for c in range(3):
+        source = 32 * c + lane // 4
+        if c == 2:
+            source = jnp.where(lane < CT, source, source + 32)
+        wide = jnp.take_along_axis(cells, source, axis=1)
+        for j in range(4):
+            fr[c, pl.ds(MARGIN + j, PATCH, stride=4), :] = wide
+
     fields = (thick, drive.at[0], drive.at[1], obs.at[0], obs.at[1])
     half = TILE // 2
-    lane = lanes_of(half)
-    lane8 = lanes_of(8)
     for f, (field, (first, count)) in enumerate(zip(fields, STRIP)):
-        for c in range(2):
-            cols = slice(c * LANES, (c + 1) * LANES)
-            ext[f, c, TOP : TOP + TILE, :] = field[:, cols]
-            ext[f, c, TOP - count : TOP, :] = north[first : first + count, cols]
-            ext[f, c, TOP + TILE : TOP + TILE + count, :] = south[first : first + count, cols]
+        for c in range(3):
+            if c < 2:
+                ext[f, c, TOP : TOP + TILE, :] = field[:, c * LANES : (c + 1) * LANES]
+            ext[f, c, TOP - count : TOP, :] = north[c, first : first + count, :]
+            ext[f, c, TOP + TILE : TOP + TILE + count, :] = south[c, first : first + count, :]
         for part in range(2):
-            start = part * 64 + first
-            from_east = pltpu.roll(east[...], (LANES - start) % LANES, 1)
-            from_west = pltpu.roll(west[...], (2 * LANES - count - start) % LANES, 1)
-            ext[f, 2, TOP + part * half : TOP + (part + 1) * half, :] = jnp.where(
-                lane < count, from_east, jnp.where(lane >= LANES - count, from_west, 0.0)
+            ext[f, 2, TOP + part * half : TOP + (part + 1) * half, :] = frame_cells(
+                west, east, slice(None), part * 64 + first, count
             )
-        for g in range(first // 8, (first + count) // 8):
-            for at, lo, hi in (
-                (TOP - count, corner_nw, corner_ne),
-                (TOP + TILE, corner_sw, corner_se),
-            ):
-                from_east = pltpu.roll(hi[...], (LANES - HALO * g) % LANES, 1)
-                from_west = pltpu.roll(lo[...], (2 * LANES - HALO - HALO * g) % LANES, 1)
-                row = at + 8 * g - first
-                ext[f, 2, row : row + 8, :] = jnp.where(
-                    lane8 < HALO, from_east, jnp.where(lane8 >= LANES - HALO, from_west, 0.0)
-                )
-
-    masks = {}
-    owner_row = lax.broadcasted_iota(jnp.int32, (owned, LANES), 0)
-    for dr in (-1, 0, 1):
+
+    for dr, first, count in ((-1, MARGIN, HALO), (0, TOP, TILE), (1, TOP + TILE, HALO)):
+        masks = []
         for ds in (-1, 0, 1):
             row, col = row_tile + dr, col_tile + ds
             inside = (row >= 0) & (row < tile_rows) & (col >= 0) & (col < tile_cols)
             row = jnp.clip(row, 0, tile_rows - 1)
             col = jnp.clip(col, 0, tile_cols - 1)
-            masks[dr, ds] = jnp.where(inside, ice_mask[row, col], 0).astype(jnp.float32)
-            block = tile_block[row, col]
-            holder = block // owned
-            place = block - holder * owned
-            spot = (dr + 1) * 3 + ds + 1
-            for j in range(PACK) if dr == 0 else ((PACK - 2, PACK - 1) if dr < 0 else (0, 1)):
-                held = gathered[holder, :, j * LANES : (j + 1) * LANES]
-                blocks[spot, j : j + 1, :] = jnp.sum(jnp.where(owner_row == place, held, 0.0), axis=0, keepdims=True)
-    for dr, first, count in ((-1, MARGIN, HALO), (0, TOP, TILE), (1, TOP + TILE, HALO)):
-        rows_lane = lanes_of(count)
+            masks.append(jnp.where(inside, ice_mask[row, col], 0).astype(jnp.float32))
+        lane = lanes_of(count)
         for c in range(2):
-            ice[c, first : first + count, :] = jnp.full((count, LANES), masks[dr, 0])
+            ice[c, first : first + count, :] = jnp.full((count, LANES), masks[1])
         ice[2, first : first + count, :] = jnp.where(
-            rows_lane < HALO, masks[dr, 1], jnp.where(rows_lane >= LANES - HALO, masks[dr, -1], 0.0)
+            lane < HALO, masks[2], jnp.where(lane >= LANES - HALO, masks[0], 0.0)
         )
-
-    for dr, first, count, at in ((-1, PACK - 2, 2, 0), (0, 0, PACK, 4), (1, 0, 2, 68)):
-        lo, mid, hi = (blocks[(dr + 1) * 3 + k, first : first + count, :] for k in range(3))
-        wide = lanes_of(count)
-        even = jnp.where(wide < 64, mid, jnp.where(wide < 96, pltpu.roll(hi, 64, 1), pltpu.roll(lo, 64, 1)))
-        odd = jnp.where(wide < 64, pltpu.roll(mid, 64, 1), jnp.where(wide < 96, hi, lo))
-        patch[pl.ds(at, count, stride=2), :] = jnp.exp(even)
-        patch[pl.ds(at + 1, count, stride=2), :] = jnp.exp(odd)
-    cells = patch[...]
-    lane72 = lanes_of(72)
-    for c in range(3):
-        source = 32 * c + lane72 // 4
-        if c == 2:
-            source = jnp.where(lane72 < 64, source, source + 32)
-        wide = jnp.take_along_axis(cells, source, axis=1)
-        for j in range(4):
-            fr[c, pl.ds(MARGIN + j, 72, stride=4), :] = wide
 
     lane = lanes_of(STEP)
     tiles = range(3)
@@ -322,23 +346,26 @@
     )
 
 
-def collect_kernel(tile_block, gathered, out, total):
+def pick_kernel(tile_block, gathered, out):
     owned = out.shape[0]
     first = lax.axis_index("gy") * owned
-    tile_rows, tile_cols = tile_block.shape
-    total[...] = jnp.zeros_like(total)
-
-    def step(t, carry):
-        col = t // tile_rows
-        place = tile_block[t - col * tile_rows, col] - first
+    col_tile = lax.axis_index("gx")
+    out[...] = jnp.zeros_like(out)
+
+    def step(row, carry):
+        place = tile_block[row, col_tile] - first
 
         @pl.when((place >= 0) & (place < owned))
         def _():
-            total[place] += gathered[t]
+            out[place] += gathered[row]
 
         return carry
 
-    lax.fori_loop(0, tile_rows * tile_cols, step, 0)
+    lax.fori_loop(0, tile_block.shape[0], step, 0)
+
+
+def add_kernel(parts, out):
+    total = sum(parts[i] for i in range(parts.shape[0]))
     for j in range(PACK):
         out[:, j * LANES : (j + 1) * LANES] = total[:, j, :]
 
@@ -353,47 +380,50 @@
 
 def per_device(thickness, driving, observed, control, ice_mask, tile_block):
     f32 = jnp.float32
-    rows, cols = lax.axis_size("gy"), lax.axis_size("gx")
+    rows = lax.axis_size("gy")
     tile_block = tile_block[:, :, 0]
     params = pltpu.CompilerParams(vmem_limit_bytes=VMEM_LIMIT)
 
-    gathered = lax.all_gather(control, "gy", axis=0)
-    top, bottom, left, right, corners = pl.pallas_call(
+    def shape(*sizes):
+        return jax.ShapeDtypeStruct(sizes, f32)
+
+    top, bottom, left, right, patches = pl.pallas_call(
         pack_kernel,
         out_shape=(
-            jax.ShapeDtypeStruct((64, TILE), f32),
-            jax.ShapeDtypeStruct((64, TILE), f32),
-            jax.ShapeDtypeStruct((TILE // 2, LANES), f32),
-            jax.ShapeDtypeStruct((TILE // 2, LANES), f32),
-            jax.ShapeDtypeStruct((4, 8, LANES), f32),
+            shape(2, 64, LANES), shape(2, 64, LANES), shape(TILE // 2, LANES), shape(TILE // 2, LANES),
+            shape(rows, PATCH, LANES),
         ),
-        in_specs=in_vmem(3),
+        in_specs=in_smem(1) + in_vmem(1) + [pl.BlockSpec(memory_space=pltpu.HBM)] * 3,
         out_specs=in_vmem(5),
+        scratch_shapes=[
+            pltpu.VMEM((5, TILE, TILE), f32),
+            pltpu.VMEM((control.shape[0], PACK, LANES), f32),
+            pltpu.SemaphoreType.DMA((5,)),
+        ],
         compiler_params=params,
         name="pack",
-    )(thickness, driving, observed)
-
-    def moved(cells, dr, ds):
-        pairs = []
-        for r in range(rows):
-            for s in range(cols):
-                if 0 <= r + dr < rows and 0 <= s + ds < cols:
-                    pairs.append((s * rows + r, (s + ds) * rows + r + dr))
-        return lax.ppermute(cells, ("gx", "gy"), pairs)
-
-    north, south = moved(bottom, 1, 0), moved(top, -1, 0)
-    west, east = moved(right, 0, 1), moved(left, 0, -1)
-    corner_se, corner_sw = moved(corners[0], -1, -1), moved(corners[1], -1, 1)
-    corner_ne, corner_nw = moved(corners[2], 1, -1), moved(corners[3], 1, 1)
+    )(tile_block, control, thickness, driving, observed)
+
+    def moved(cells, axis, step):
+        count = lax.axis_size(axis)
+        return lax.ppermute(cells, axis, [(i, i + step) for i in range(count) if 0 <= i + step < count])
+
+    west, east = moved(right, "gx", 1), moved(left, "gx", -1)
+    patches = lax.all_to_all(patches, "gy", 0, 0, tiled=True)
+    top, bottom = pl.pallas_call(
+        corner_kernel,
+        out_shape=(shape(3, 64, LANES), shape(3, 64, LANES)),
+        in_specs=in_vmem(4),
+        out_specs=in_vmem(2),
+        compiler_params=params,
+        name="corners",
+    )(top, bottom, west, east)
+    north, south = moved(bottom, "gy", 1), moved(top, "gy", -1)
 
     vel_u, vel_v, sums = pl.pallas_call(
         model_kernel,
-        out_shape=(
-            jax.ShapeDtypeStruct((TILE, TILE), f32),
-            jax.ShapeDtypeStruct((TILE, TILE), f32),
-            jax.ShapeDtypeStruct((PACK, LANES), f32),
-        ),
-        in_specs=in_smem(2) + in_vmem(12),
+        out_shape=(shape(TILE, TILE), shape(TILE, TILE), shape(PACK, LANES)),
+        in_specs=in_smem(1) + in_vmem(8),
         out_specs=in_vmem(3),
         scratch_shapes=[
             pltpu.VMEM((5, 3, ROWS, LANES), f32),
@@ -402,27 +432,28 @@
             pltpu.VMEM((3, ROWS, LANES), f32),
             pltpu.VMEM((3, 2, 3, ROWS, LANES), f32),
             pltpu.VMEM((14, 3, ROWS, LANES), f32),
-            pltpu.VMEM((9, PACK, LANES), f32),
-            pltpu.VMEM((72, LANES), f32),
             pltpu.VMEM((CT, LANES), f32),
         ],
         compiler_params=params,
         name="model",
-    )(
-        tile_block, ice_mask, gathered, thickness, driving, observed, north, south, west, east,
-        corner_nw, corner_ne, corner_sw, corner_se,
-    )
-
-    tiles = lax.all_gather(sums, ("gx", "gy"), axis=0)
-    gradient = pl.pallas_call(
-        collect_kernel,
-        out_shape=jax.ShapeDtypeStruct(control.shape, f32),
+    )(ice_mask, patches, thickness, driving, observed, north, south, west, east)
+
+    owned = pl.pallas_call(
+        pick_kernel,
+        out_shape=shape(control.shape[0], PACK, LANES),
         in_specs=in_smem(1) + in_vmem(1),
         out_specs=pl.BlockSpec(memory_space=pltpu.VMEM),
-        scratch_shapes=[pltpu.VMEM((control.shape[0], PACK, LANES), f32)],
         compiler_params=params,
-        name="collect",
-    )(tile_block, tiles)
+        name="pick",
+    )(tile_block, lax.all_gather(sums, "gy", axis=0))
+    gradient = pl.pallas_call(
+        add_kernel,
+        out_shape=shape(*control.shape),
+        in_specs=in_vmem(1),
+        out_specs=pl.BlockSpec(memory_space=pltpu.VMEM),
+        compiler_params=params,
+        name="add",
+    )(lax.all_gather(owned, "gx", axis=0))
     return vel_u, vel_v, gradient
 
 

time: 124 us -> 83.6 us (0.67)
  blocking collectives: 55 us -> 25.8 us
  Pallas kernels: 42.5 us -> 30.1 us
  waiting for transfers between devices: 0.02 us -> 8.9 us
  starting transfers between devices: 21.6 us -> 12.8 us
    all_gather x2, blocking collectives: 54.9 us -> 25.8 us  [the longest x1 14.1 us: per_device(): lax.all_gather(owned, 'gx', axis=0)]
    ppermute x8 -> x4, starting transfers between devices: 21.6 us -> 7.16 us  [moved(): lax.ppermute(cells, axis, [(i, i + step) for i in range(count) if 0 <= i...]
    pallas_call x3 -> x5, Pallas kernels: 42.5 us -> 30.1 us  [the longest x1 25.7 us: per_device(): pl.pallas_call(model_kernel, out_shape=(shape(TILE, TILE), shape(TILE, TI...]
    ppermute x8 -> x4, waiting for transfers between devices: 0.02 us -> 8.9 us  [moved(): lax.ppermute(cells, axis, [(i, i + step) for i in range(count) if 0 <= i...]
    all_to_all x0 -> x1, starting transfers between devices: none -> 5.6 us  [per_device(): patches = lax.all_to_all(patches, 'gy', 0, 0, tiled=True)]
    unnamed x19 -> x17, local copies, waits for them, and re-layouts: 3.73 us -> 3.97 us
  transfers between devices with their start and end apart: 8 -> 5, of which waited for: 0 -> 3; matrix products, arithmetic and copies ran while one was open for 0% -> 0% of each run, Pallas kernels for 0% -> 0%
where the time goes in v1:
time: 83.6 us; the launch traced here: 83 us
  Pallas kernels  30.1 us (36%)
  blocking collectives  25.8 us (31%)
  starting transfers between devices  12.8 us (15%)
  waiting for transfers between devices  8.9 us (11%)
  local copies, waits for them, and re-layouts  4.73 us (6%)
    pallas_call x1, Pallas kernels, per_device(): pl.pallas_call(model_kernel, out_shape=(shape(TILE, TILE), shape(TILE, TI...  25.7 us
    all_gather x1, blocking collectives, per_device(): lax.all_gather(owned, 'gx', axis=0)  14.1 us
    all_gather x1, blocking collectives, per_device(): lax.all_gather(sums, 'gy', axis=0)  11.6 us
    ppermute x4, waiting for transfers between devices, moved(): lax.ppermute(cells, axis, [(i, i + step) for i in range(count) if 0 <= i...  8.9 us
    ppermute x4, starting transfers between devices, moved(): lax.ppermute(cells, axis, [(i, i + step) for i in range(count) if 0 <= i...  7.16 us
    all_to_all x1, starting transfers between devices, per_device(): patches = lax.all_to_all(patches, 'gy', 0, 0, tiled=True)  5.6 us
    unnamed x17, local copies, waits for them, and re-layouts  3.97 us
    pallas_call x1, Pallas kernels, per_device(): pl.pallas_call(pack_kernel, out_shape=(shape(2, 64, LANES), shape(2, 64,...  2.89 us
  transfers between devices with their start and end apart: 5, of which 3 were waited for; matrix products, arithmetic and copies ran while one was open for 0% of the time, Pallas kernels for 0%

profile of v1, /device:TPU:0, one launch (start us, length us, event | category | flops | bytes accessed | tf_op | source)
XLA Modules:
  0.0 83.0 jit_solution(9828376452855894126)
XLA Ops:
  0.6 0.8 copy.12.tile_block
  1.4 0.0 copy-start
  1.4 1.0 %copy-done = f32[2,256,256]{2,1,0:T(8,128)S(1)} copy-done((f32[2,256,256]{2,1,0:T(8,128)S(1)}, f32[2,256,256]{2,1,0:T(8,128)}, u32[]{:S(2)}) %copy-start) | copy-done | bytes 524312
  2.4 0.0 copy-start.2
  2.4 1.0 %copy-done.2 = f32[2,256,256]{2,1,0:T(8,128)S(1)} copy-done((f32[2,256,256]{2,1,0:T(8,128)S(1)}, f32[2,256,256]{2,1,0:T(8,128)}, u32[]{:S(2)}) %copy-start.2) | copy-done | bytes 524312
  3.5 0.0 copy-start.4
  3.5 0.9 %copy-done.4 = f32[256,256]{1,0:T(8,128)S(1)} copy-done((f32[256,256]{1,0:T(8,128)S(1)}, f32[256,256]{1,0:T(8,128)}, u32[]{:S(2)}) %copy-start.4) | copy-done | bytes 262168
  4.4 0.0 copy-start.6
  4.4 0.8 %copy-done.6 = f32[4,4096]{1,0:T(4,128)S(1)} copy-done((f32[4,4096]{1,0:T(4,128)S(1)}, f32[4,4096]{1,0:T(4,128)}, u32[]{:S(2)}) %copy-start.6) | copy-done | bytes 65560
  5.3 0.0 copy-start.3
  5.3 2.9 %pack.1 = (f32[2,64,128]{2,1,0:T(8,128)S(1)}, f32[2,64,128]{2,1,0:T(8,128)S(1)}, f32[128,128]{1,0:T(8,128)S(1)}, f32[128,128]{1,0:T(8,128)S(1)}, f32[8,72,128]{2,1,0:T(8,128)}) custom-call(s32[8,4]{1,0:T(8,128)S(1)} %copy.12.tile_block, f32[4,4096]{1,0:T(4,128)S(1)} %copy-done.6, f32[256,256]{1,0:T(8,128)S(1)} %copy-done.4, f32[2,256,256]{2,1,0:T(8,128)S(1)} %copy-done, ...), custom_call_target="tpu_custom_call" | custom-call | tf_op jit(solution)/shard_map/pack/pallas_call | solution.py:390
  8.2 0.0 copy-start.1
  8.2 5.6 %all-to-all-start = ((f32[8,72,128]{2,1,0:T(8,128)}), f32[8,72,128]{2,1,0:T(8,128)S(1)}, u32[]{:S(2)}, u32[]{:S(2)}) async-start(f32[8,72,128]{2,1,0:T(8,128)} %get-tuple-element.13), calls=%async_computation | async-start | bytes 589824 | tf_op jit(solution)/shard_map/all_to_all | solution.py:412
  13.8 0.0 copy-start.5
  13.8 3.3 %collective-permute-start = (f32[128,128]{1,0:T(8,128)S(1)}, f32[128,128]{1,0:T(8,128)S(1)}, u32[]{:S(2)}, u32[]{:S(2)}) collective-permute-start(f32[128,128]{1,0:T(8,128)S(1)} %get-tuple-element.16), channel_id=1, source_target_pairs={{0,8},{8,16},{16,24},{1,9},{9,17},{17,25},{2,10},{10,18},{18,26},{... | collective-permute-start | bytes 196616 | tf_op jit(solution)/shard_map/ppermute | solution.py:409
  17.1 1.3 %collective-permute-start.1 = (f32[128,128]{1,0:T(8,128)S(1)}, f32[128,128]{1,0:T(8,128)S(1)}, u32[]{:S(2)}, u32[]{:S(2)}) collective-permute-start(f32[128,128]{1,0:T(8,128)S(1)} %get-tuple-element.17), channel_id=1, source_target_pairs={{8,0},{16,8},{24,16},{9,1},{17,9},{25,17},{10,2},{18,10},{26,18},{... | collective-permute-start | bytes 196616 | tf_op jit(solution)/shard_map/ppermute | solution.py:409
  18.4 0.7 collective-permute-done.west
  19.1 4.2 %collective-permute-done.1.east = f32[128,128]{1,0:T(8,128)S(1)} collective-permute-done((f32[128,128]{1,0:T(8,128)S(1)}, f32[128,128]{1,0:T(8,128)S(1)}, u32[]{:S(2)}, u32[]{:S(2)}) %collective-permute-start.1) | collective-permute-done | bytes 65568 | tf_op jit(solution)/shard_map/ppermute | solution.py:409
  23.2 0.1 corners.1
  23.3 0.0 copy-start.7
  23.3 1.3 %collective-permute-start.2 = (f32[3,64,128]{2,1,0:T(8,128)S(1)}, f32[3,64,128]{2,1,0:T(8,128)S(1)}, u32[]{:S(2)}, u32[]{:S(2)}) collective-permute-start(f32[3,64,128]{2,1,0:T(8,128)S(1)} %get-tuple-element.18), channel_id=1, source_target_pairs={{0,1},{1,2},{2,3},{3,4},{4,5},{5,6},{6,7},{8,9},{9,10},{10,11},{11... | collective-permute-start | bytes 294920 | tf_op jit(solution)/shard_map/ppermute | solution.py:409
  24.6 1.3 %collective-permute-start.3 = (f32[3,64,128]{2,1,0:T(8,128)S(1)}, f32[3,64,128]{2,1,0:T(8,128)S(1)}, u32[]{:S(2)}, u32[]{:S(2)}) collective-permute-start(f32[3,64,128]{2,1,0:T(8,128)S(1)} %get-tuple-element.19), channel_id=1, source_target_pairs={{1,0},{2,1},{3,2},{4,3},{5,4},{6,5},{7,6},{9,8},{10,9},{11,10},{12... | collective-permute-start | bytes 294920 | tf_op jit(solution)/shard_map/ppermute | solution.py:409
  25.9 0.0 copy-done.7
  26.0 0.1 copy.13.ice_mask
  26.0 0.0 collective-permute-done.2.north
  26.0 4.0 %collective-permute-done.3.south = f32[3,64,128]{2,1,0:T(8,128)S(1)} collective-permute-done((f32[3,64,128]{2,1,0:T(8,128)S(1)}, f32[3,64,128]{2,1,0:T(8,128)S(1)}, u32[]{:S(2)}, u32[]{:S(2)}) %collective-permute-start.3) | collective-permute-done | bytes 98336 | tf_op jit(solution)/shard_map/ppermute | solution.py:409
  30.1 0.0 all-to-all-done.patches
  30.1 0.0 copy-done.3
  30.1 0.0 copy-done.1
  30.1 0.0 copy-done.5
  30.1 25.7 %model.1 = (f32[256,256]{1,0:T(8,128)}, f32[256,256]{1,0:T(8,128)}, f32[32,128]{1,0:T(8,128)S(1)}) custom-call(s32[8,4]{1,0:T(8,128)S(1)} %copy.13.ice_mask, f32[8,72,128]{2,1,0:T(8,128)S(1)} %all-to-all-done.patches, f32[256,256]{1,0:T(8,128)S(1)} %copy-done.5, f32[2,256,256]{2,1,0:T(8,128)S(1)} %copy-done.1, f32[2,256,256]{2,1,0:T(8,128)S(1)} %copy-done.3, ...), custom_call_target="tpu_custom_call" | custom-call | tf_op jit(solution)/shard_map/model/pallas_call | solution.py:423
  55.8 11.6 %all-gather = f32[256,128]{1,0:T(8,128)S(1)} all-gather(f32[32,128]{1,0:T(8,128)S(1)} %get-tuple-element.22), channel_id=2, replica_groups=mesh['gx'=4,'gy'=8] {'gy'}, dimensions={0}, use_global_device_ids=true | all-gather | bytes 147456 | tf_op jit(solution)/shard_map/all_gather | solution.py:448
  67.5 0.7 pick.1
  68.2 14.1 %all-gather.1 = f32[16,32,128]{2,1,0:T(8,128)S(1)} all-gather(f32[4,32,128]{2,1,0:T(8,128)S(1)} %pick.1), channel_id=3, replica_groups=mesh['gx'=4,'gy'=8] {'gx'}, dimensions={0}, use_global_device_ids=true | all-gather | bytes 327680 | tf_op jit(solution)/shard_map/all_gather | solution.py:456
  82.3 0.7 add.1
Async XLA Ops:
  1.4 1.0 %copy-start = (f32[2,256,256]{2,1,0:T(8,128)S(1)}, f32[2,256,256]{2,1,0:T(8,128)}, u32[]{:S(2)}) copy-start(f32[2,256,256]{2,1,0:T(8,128)} %drive.3) | copy-start | bytes 1572868
  2.4 1.0 %copy-start.2 = (f32[2,256,256]{2,1,0:T(8,128)S(1)}, f32[2,256,256]{2,1,0:T(8,128)}, u32[]{:S(2)}) copy-start(f32[2,256,256]{2,1,0:T(8,128)} %obs.3) | copy-start | bytes 1572868
  3.5 0.9 %copy-start.4 = (f32[256,256]{1,0:T(8,128)S(1)}, f32[256,256]{1,0:T(8,128)}, u32[]{:S(2)}) copy-start(f32[256,256]{1,0:T(8,128)} %thick.3) | copy-start | bytes 786436
  4.4 0.8 %copy-start.6 = (f32[4,4096]{1,0:T(4,128)S(1)}, f32[4,4096]{1,0:T(4,128)}, u32[]{:S(2)}) copy-start(f32[4,4096]{1,0:T(4,128)} %control.1) | copy-start | bytes 196612
  5.3 24.8 %copy-start.3 = (f32[2,256,256]{2,1,0:T(8,128)S(1)}, f32[2,256,256]{2,1,0:T(8,128)}, u32[]{:S(2)}) copy-start(f32[2,256,256]{2,1,0:T(8,128)} %obs.3) | copy-start | bytes 1572868
  8.2 21.9 %copy-start.1 = (f32[2,256,256]{2,1,0:T(8,128)S(1)}, f32[2,256,256]{2,1,0:T(8,128)}, u32[]{:S(2)}) copy-start(f32[2,256,256]{2,1,0:T(8,128)} %drive.3) | copy-start | bytes 1572868
  8.2 21.9 %all-to-all-start = ((f32[8,72,128]{2,1,0:T(8,128)}), f32[8,72,128]{2,1,0:T(8,128)S(1)}, u32[]{:S(2)}, u32[]{:S(2)}) async-start(f32[8,72,128]{2,1,0:T(8,128)} %get-tuple-element.13), calls=%async_computation | async-start | bytes 589824 | tf_op jit(solution)/shard_map/all_to_all | solution.py:412
  13.8 16.3 %copy-start.5 = (f32[256,256]{1,0:T(8,128)S(1)}, f32[256,256]{1,0:T(8,128)}, u32[]{:S(2)}) copy-start(f32[256,256]{1,0:T(8,128)} %thick.3) | copy-start | bytes 786436
  13.8 5.3 %collective-permute-start = (f32[128,128]{1,0:T(8,128)S(1)}, f32[128,128]{1,0:T(8,128)S(1)}, u32[]{:S(2)}, u32[]{:S(2)}) collective-permute-start(f32[128,128]{1,0:T(8,128)S(1)} %get-tuple-element.16), channel_id=1, source_target_pairs={{0,8},{8,16},{16,24},{1,9},{9,17},{17,25},{2,10},{10,18},{18,26},{... | collective-permute-start | bytes 196616 | tf_op jit(solution)/shard_map/ppermute | solution.py:409
  17.1 6.2 %collective-permute-start.1 = (f32[128,128]{1,0:T(8,128)S(1)}, f32[128,128]{1,0:T(8,128)S(1)}, u32[]{:S(2)}, u32[]{:S(2)}) collective-permute-start(f32[128,128]{1,0:T(8,128)S(1)} %get-tuple-element.17), channel_id=1, source_target_pairs={{8,0},{16,8},{24,16},{9,1},{17,9},{25,17},{10,2},{18,10},{26,18},{... | collective-permute-start | bytes 196616 | tf_op jit(solution)/shard_map/ppermute | solution.py:409
  23.3 2.6 %copy-start.7 = (s32[8,4]{0,1:T(4,128)S(1)}, s32[8,4]{0,1:T(4,128)}, u32[]{:S(2)}) copy-start(s32[8,4]{0,1:T(4,128)} %param.10) | copy-start | bytes 388
  23.3 2.7 %collective-permute-start.2 = (f32[3,64,128]{2,1,0:T(8,128)S(1)}, f32[3,64,128]{2,1,0:T(8,128)S(1)}, u32[]{:S(2)}, u32[]{:S(2)}) collective-permute-start(f32[3,64,128]{2,1,0:T(8,128)S(1)} %get-tuple-element.18), channel_id=1, source_target_pairs={{0,1},{1,2},{2,3},{3,4},{4,5},{5,6},{6,7},{8,9},{9,10},{10,11},{11... | collective-permute-start | bytes 294920 | tf_op jit(solution)/shard_map/ppermute | solution.py:409
  24.6 5.4 %collective-permute-start.3 = (f32[3,64,128]{2,1,0:T(8,128)S(1)}, f32[3,64,128]{2,1,0:T(8,128)S(1)}, u32[]{:S(2)}, u32[]{:S(2)}) collective-permute-start(f32[3,64,128]{2,1,0:T(8,128)S(1)} %get-tuple-element.19), channel_id=1, source_target_pairs={{1,0},{2,1},{3,2},{4,3},{5,4},{6,5},{7,6},{9,8},{10,9},{11,10},{12... | collective-permute-start | bytes 294920 | tf_op jit(solution)/shard_map/ppermute | solution.py:409

commit v2 on v1

--- a/solution.py
+++ b/solution.py
@@ -18,9 +18,9 @@
 MARGIN = 8
 TOP = MARGIN + HALO
 ROWS = TILE + 2 * TOP
-STEP = 32
 PACK = COARSE // LANES
 VMEM_LIMIT = 40 * 1024 * 1024
+PACK_VMEM_LIMIT = 62 * 1024 * 1024
 
 STRIP = ((0, HALO), (HALO, HALO), (2 * HALO, HALO), (3 * HALO, OBS), (3 * HALO + OBS, OBS))
 
@@ -49,7 +49,7 @@
         copies.append(pltpu.make_async_copy(field, held.at[f], sems.at[f]))
         copies[-1].start()
 
-    tile_rows, tile_cols = tile_block.shape
+    tile_cols, tile_rows = tile_block.shape
     owned = control.shape[0]
     mine = lax.axis_index("gy") * owned
     col_tile = lax.axis_index("gx")
@@ -62,7 +62,7 @@
             for ds in (-1, 0, 1):
                 row = jnp.clip(target + dr, 0, tile_rows - 1)
                 col = jnp.clip(col_tile + ds, 0, tile_cols - 1)
-                place = tile_block[row, col] - mine
+                place = tile_block[col, row] - mine
 
                 @pl.when((place >= 0) & (place < owned))
                 def _():
@@ -127,27 +127,22 @@
     return [jnp.where(lane == 0, rolled[(c + 2) % 3], rolled[c]) for c in range(3)]
 
 
-def row_range(reach):
-    wide = HALO if reach > 0 else 0
-    return TOP - wide, TILE + 2 * wide
-
-
-def over_rows(reach, body):
-    start, count = row_range(reach)
-
-    def step(i, carry):
-        body(pl.multiple_of(start + i * STEP, 8))
+def over_rows(framed, body):
+    start, count, step = (MARGIN, TILE + 2 * HALO, 48) if framed else (TOP, TILE, 64)
+
+    def block(i, carry):
+        body(pl.multiple_of(start + i * step, 8), step)
         return carry
 
-    lax.fori_loop(0, count // STEP, step, 0)
+    lax.fori_loop(0, count // step, block, 0)
 
 
 def model_kernel(
     ice_mask, patches, thick, drive, obs, north, south, west, east,
     vel_u, vel_v, sums,
-    ext, fr, ice, visc, vel, coef, small,
+    ext, fr, ice, visc, vel, coef, small, sems,
 ):
-    tile_rows, tile_cols = ice_mask.shape
+    tile_cols, tile_rows = ice_mask.shape
     row_tile = lax.axis_index("gy")
     col_tile = lax.axis_index("gx")
 
@@ -181,7 +176,7 @@
             inside = (row >= 0) & (row < tile_rows) & (col >= 0) & (col < tile_cols)
             row = jnp.clip(row, 0, tile_rows - 1)
             col = jnp.clip(col, 0, tile_cols - 1)
-            masks.append(jnp.where(inside, ice_mask[row, col], 0).astype(jnp.float32))
+            masks.append(jnp.where(inside, ice_mask[col, row], 0).astype(jnp.float32))
         lane = lanes_of(count)
         for c in range(2):
             ice[c, first : first + count, :] = jnp.full((count, LANES), masks[1])
@@ -189,46 +184,47 @@
             lane < HALO, masks[2], jnp.where(lane >= LANES - HALO, masks[0], 0.0)
         )
 
-    lane = lanes_of(STEP)
     tiles = range(3)
 
-    def load(ref, row, *lead):
-        return [ref[(*lead, c, pl.ds(row, STEP), slice(None))] for c in tiles]
-
-    def store(ref, row, values, *lead):
+    def load(ref, at, *lead):
+        return [ref[(*lead, c, at, slice(None))] for c in tiles]
+
+    def store(ref, at, values, *lead):
         for c in tiles:
-            ref[(*lead, c, pl.ds(row, STEP), slice(None))] = values[c]
-
-    def viscosity(reach, now):
-        def body(row):
-            thickness = load(ext, row, 0)
-            if now is None:
-                store(visc, row, [visc_scale * t * strain_floor ** (-1.0 / 3.0) for t in thickness])
-                return
-            u, v = load(vel, row, now, 0), load(vel, row, now, 1)
-            u_n, v_n = load(vel, row - 1, now, 0), load(vel, row - 1, now, 1)
-            u_s, v_s = load(vel, row + 1, now, 0), load(vel, row + 1, now, 1)
-            u_e, u_w = shift_east(u, lane), shift_west(u, lane)
-            v_e, v_w = shift_east(v, lane), shift_west(v, lane)
-            result = []
-            for c in tiles:
-                ux, vx = u_e[c] - u_w[c], v_e[c] - v_w[c]
-                uy, vy = u_s[c] - u_n[c], v_s[c] - v_n[c]
-                shear = uy + vx
-                strain = 0.25 * (ux * ux + vy * vy + ux * vy + 0.25 * (shear * shear)) + strain_floor
-                result.append(visc_scale * thickness[c] * jnp.exp(jnp.log(strain) * (-1.0 / 3.0)))
-            store(visc, row, result)
-
-        over_rows(reach, body)
-
-    def coefficients(row):
-        m, m_n, m_s = load(visc, row), load(visc, row - 1), load(visc, row + 1)
+            ref[(*lead, c, at, slice(None))] = values[c]
+
+    def load_around(row, step, now):
+        rows = [pl.ds(row, step), pl.ds(row - 1, step), pl.ds(row + 1, step)]
+        return [load(vel, at, now, i) for i in range(2) for at in rows]
+
+    def first_viscosity(row, step):
+        at = pl.ds(row, step)
+        store(visc, at, [visc_scale * strain_floor ** (-1.0 / 3.0) * t for t in load(ext, at, 0)])
+
+    def viscosity(row, step):
+        at, lane = pl.ds(row, step), lanes_of(step)
+        thickness = load(ext, at, 0)
+        u, u_n, u_s, v, v_n, v_s = load_around(row, step, 1)
+        u_e, u_w = shift_east(u, lane), shift_west(u, lane)
+        v_e, v_w = shift_east(v, lane), shift_west(v, lane)
+        result = []
+        for c in tiles:
+            ux, vx = u_e[c] - u_w[c], v_e[c] - v_w[c]
+            uy, vy = u_s[c] - u_n[c], v_s[c] - v_n[c]
+            shear = uy + vx
+            strain = 0.25 * (ux * ux + vy * vy + ux * vy + 0.25 * (shear * shear)) + strain_floor
+            result.append(visc_scale * thickness[c] * jnp.exp(jnp.log(strain) * (-1.0 / 3.0)))
+        store(visc, at, result)
+
+    def coefficients(row, step):
+        at, lane = pl.ds(row, step), lanes_of(step)
+        m, m_n, m_s = load(visc, at), load(visc, pl.ds(row - 1, step)), load(visc, pl.ds(row + 1, step))
         m_w = shift_west(m, lane)
         w = [0.5 * (m[c] + m_w[c]) for c in tiles]
         e = shift_east(w, lane)
         s = [0.5 * (m[c] + m_s[c]) for c in tiles]
         n = [0.5 * (m[c] + m_n[c]) for c in tiles]
-        friction, mask = load(fr, row), load(ice, row)
+        friction, mask = load(fr, at), load(ice, at)
         scale_u, scale_v = [], []
         for c in tiles:
             across, along = e[c] + w[c], s[c] + n[c]
@@ -240,13 +236,15 @@
         ):
             corners.append([0.5 * m[c] + 0.25 * shifted[c] for c in tiles])
             corners.append([0.25 * m[c] + 0.5 * shifted[c] for c in tiles])
-        return [e, w, s, n, scale_u, scale_v] + corners
-
-    def relaxed(row, now, k, forcing):
+        k = [e, w, s, n, scale_u, scale_v] + corners
+        for i, values in enumerate(k):
+            store(coef, at, values, i)
+        return k
+
+    def relax(row, step, k, now, new):
+        at, lane = pl.ds(row, step), lanes_of(step)
         e, w, s, n, scale_u, scale_v, sw_u, sw_v, nw_u, nw_v, se_u, se_v, ne_u, ne_v = k
-        u, v = load(vel, row, now, 0), load(vel, row, now, 1)
-        u_n, v_n = load(vel, row - 1, now, 0), load(vel, row - 1, now, 1)
-        u_s, v_s = load(vel, row + 1, now, 0), load(vel, row + 1, now, 1)
+        u, u_n, u_s, v, v_n, v_s = load_around(row, step, now)
         to_west_u, to_east_u, to_west_v, to_east_v = [], [], [], []
         for c in tiles:
             u4 = 4.0 * u[c]
@@ -256,79 +254,75 @@
             to_east_v.append(e[c] * v[c] + (ne_v[c] * u_n[c] - se_v[c] * u_s[c]))
         to_west_u, to_west_v = shift_east(to_west_u, lane), shift_east(to_west_v, lane)
         to_east_u, to_east_v = shift_west(to_east_u, lane), shift_west(to_east_v, lane)
+        right_u, right_v = load(ext, at, 1), load(ext, at, 2)
         new_u, new_v = [], []
         for c in tiles:
             mid_u = s[c] * u_s[c] + n[c] * u_n[c]
             mid_v = 4.0 * (s[c] * v_s[c] + n[c] * v_n[c])
-            new_u.append(scale_u[c] * (forcing[0][c] + mid_u + (to_west_u[c] + to_east_u[c])))
-            new_v.append(scale_v[c] * (forcing[1][c] + mid_v + (to_west_v[c] + to_east_v[c])))
-        return new_u, new_v
-
-    def put(row, new, values):
-        store(vel, row, values[0], new, 0)
-        store(vel, row, values[1], new, 1)
-
-    reach = HALO
-    now = None
-    for picard in range(PIC):
-        if picard > 0:
-            reach -= 1
-        viscosity(reach, now)
-        reach -= 1
-
-        def first_sweep(row, now=now, new=0 if now is None else 1 - now):
-            k = coefficients(row)
-            for i, values in enumerate(k):
-                store(coef, row, values, i)
-            forcing = load(ext, row, 1), load(ext, row, 2)
-            if now is None:
-                put(row, new, [[k[4 + i][c] * forcing[i][c] for c in tiles] for i in range(2)])
-            else:
-                put(row, new, relaxed(row, now, k, forcing))
-
-        over_rows(reach, first_sweep)
-        now = 0 if now is None else 1 - now
-        for sweep in range(1, SW):
-            reach -= 1
-
-            def next_sweep(row, now=now):
-                k = [load(coef, row, i) for i in range(14)]
-                put(row, 1 - now, relaxed(row, now, k, (load(ext, row, 1), load(ext, row, 2))))
-
-            over_rows(reach, next_sweep)
-            now = 1 - now
-
-    final = now
-    spare = (1 - now, 2)
-
-    def first_adjoint(row):
+            new_u.append(scale_u[c] * (right_u[c] + mid_u + (to_west_u[c] + to_east_u[c])))
+            new_v.append(scale_v[c] * (right_v[c] + mid_v + (to_west_v[c] + to_east_v[c])))
+        store(vel, at, new_u, new, 0)
+        store(vel, at, new_v, new, 1)
+
+    def sweep(framed, now, new):
+        def body(row, step):
+            at = pl.ds(row, step)
+            relax(row, step, [load(coef, at, i) for i in range(14)], now, new)
+
+        over_rows(framed, body)
+
+    def first_start(row, step):
+        k = coefficients(row, step)
+        at = pl.ds(row, step)
         for i in range(2):
-            u, seen, scale = load(vel, row, final, i), load(ext, row, 3 + i), load(coef, row, 4 + i)
-            misfit = [u[c] - seen[c] for c in tiles]
-            store(ext, row, misfit, 1 + i)
-            store(vel, row, [scale[c] * misfit[c] for c in tiles], spare[0], i)
-
-    over_rows(reach, first_adjoint)
+            right = load(ext, at, 1 + i)
+            store(vel, at, [k[4 + i][c] * right[c] for c in tiles], 0, i)
+
+    over_rows(True, first_viscosity)
+    over_rows(True, first_start)
+    sweep(True, 0, 1)
+
+    def iteration(i, carry):
+        over_rows(True, viscosity)
+        over_rows(True, lambda row, step: relax(row, step, coefficients(row, step), 1, 0))
+        sweep(True, 0, 1)
+        return carry
+
+    lax.fori_loop(1, PIC, iteration, 0)
+    copies = []
     for i, out in enumerate((vel_u, vel_v)):
         for c in range(2):
-            out[:, c * LANES : (c + 1) * LANES] = vel[final, i, c, TOP : TOP + TILE, :]
-    for sweep in range(1, ADJ):
-        reach -= 1
-
-        def adjoint_sweep(row, now=spare[(sweep + 1) % 2], new=spare[sweep % 2]):
-            k = [load(coef, row, i) for i in range(14)]
-            put(row, new, relaxed(row, now, k, (load(ext, row, 1), load(ext, row, 2))))
-
-        over_rows(reach, adjoint_sweep)
-    last = spare[(ADJ - 1) % 2]
-
-    def gradient(row):
+            copies.append(
+                pltpu.make_async_copy(
+                    vel.at[1, i, c, TOP : TOP + TILE, :], out.at[:, c * LANES : (c + 1) * LANES], sems.at[2 * i + c]
+                )
+            )
+            copies[-1].start()
+
+    def first_adjoint(row, step):
+        at = pl.ds(row, step)
+        for i in range(2):
+            u, seen, scale = load(vel, at, 1, i), load(ext, at, 3 + i), load(coef, at, 4 + i)
+            misfit = [u[c] - seen[c] for c in tiles]
+            store(ext, at, misfit, 1 + i)
+            store(vel, at, [scale[c] * misfit[c] for c in tiles], 2, i)
+
+    over_rows(True, first_adjoint)
+
+    def two_sweeps(i, carry):
+        sweep(True, 2, 0)
+        sweep(True, 0, 2)
+        return carry
+
+    lax.fori_loop(0, (ADJ - 2) // 2, two_sweeps, 0)
+    sweep(False, 2, 0)
+
+    def gradient(row, step):
         for c in range(2):
-            at = (c, pl.ds(row, STEP), slice(None))
-            dot = vel[(final, 0, *at)] * vel[(last, 0, *at)] + vel[(final, 1, *at)] * vel[(last, 1, *at)]
-            visc[at] = -fr[at] * dot
-
-    over_rows(0, gradient)
+            at = (c, pl.ds(row, step), slice(None))
+            visc[at] = -fr[at] * (vel[(1, 0, *at)] * vel[(0, 0, *at)] + vel[(1, 1, *at)] * vel[(0, 1, *at)])
+
+    over_rows(False, gradient)
     down = [sum(visc[c, pl.ds(TOP + j, CT, stride=4), :] for j in range(4)) for c in range(2)]
     k = lax.broadcasted_iota(jnp.int32, (LANES, LANES), 0)
     l = lanes_of(LANES) % CT
@@ -341,27 +335,33 @@
             preferred_element_type=jnp.float32,
         )
     small[...] = total
-    sums[...] = jnp.where(
+    packed = jnp.where(
         lanes_of(PACK) < CT, small[pl.ds(0, PACK, stride=2), :], small[pl.ds(1, PACK, stride=2), :]
     )
-
-
-def pick_kernel(tile_block, gathered, out):
-    owned = out.shape[0]
+    for j in range(sums.shape[0]):
+        sums[j] = packed
+    for copy in copies:
+        copy.wait()
+
+
+def pick_kernel(tile_block, gathered, out, total):
+    owned = total.shape[0]
     first = lax.axis_index("gy") * owned
     col_tile = lax.axis_index("gx")
-    out[...] = jnp.zeros_like(out)
+    total[...] = jnp.zeros_like(total)
 
     def step(row, carry):
-        place = tile_block[row, col_tile] - first
+        place = tile_block[col_tile, row] - first
 
         @pl.when((place >= 0) & (place < owned))
         def _():
-            out[place] += gathered[row]
+            total[place] += gathered[row]
 
         return carry
 
-    lax.fori_loop(0, tile_block.shape[0], step, 0)
+    lax.fori_loop(0, tile_block.shape[1], step, 0)
+    for j in range(out.shape[0]):
+        out[j] = total[...]
 
 
 def add_kernel(parts, out):
@@ -380,8 +380,8 @@
 
 def per_device(thickness, driving, observed, control, ice_mask, tile_block):
     f32 = jnp.float32
-    rows = lax.axis_size("gy")
-    tile_block = tile_block[:, :, 0]
+    rows, cols = lax.axis_size("gy"), lax.axis_size("gx")
+    tile_block, ice_mask = tile_block[:, :, 0].T, ice_mask.T
     params = pltpu.CompilerParams(vmem_limit_bytes=VMEM_LIMIT)
 
     def shape(*sizes):
@@ -400,7 +400,7 @@
             pltpu.VMEM((control.shape[0], PACK, LANES), f32),
             pltpu.SemaphoreType.DMA((5,)),
         ],
-        compiler_params=params,
+        compiler_params=pltpu.CompilerParams(vmem_limit_bytes=PACK_VMEM_LIMIT),
         name="pack",
     )(tile_block, control, thickness, driving, observed)
 
@@ -422,9 +422,9 @@
 
     vel_u, vel_v, sums = pl.pallas_call(
         model_kernel,
-        out_shape=(shape(TILE, TILE), shape(TILE, TILE), shape(PACK, LANES)),
+        out_shape=(shape(TILE, TILE), shape(TILE, TILE), shape(rows, PACK, LANES)),
         in_specs=in_smem(1) + in_vmem(8),
-        out_specs=in_vmem(3),
+        out_specs=[pl.BlockSpec(memory_space=pltpu.HBM)] * 2 + in_vmem(1),
         scratch_shapes=[
             pltpu.VMEM((5, 3, ROWS, LANES), f32),
             pltpu.VMEM((3, ROWS, LANES), f32),
@@ -433,19 +433,22 @@
             pltpu.VMEM((3, 2, 3, ROWS, LANES), f32),
             pltpu.VMEM((14, 3, ROWS, LANES), f32),
             pltpu.VMEM((CT, LANES), f32),
+            pltpu.SemaphoreType.DMA((4,)),
         ],
         compiler_params=params,
         name="model",
     )(ice_mask, patches, thickness, driving, observed, north, south, west, east)
 
-    owned = pl.pallas_call(
+    owned = (control.shape[0], PACK, LANES)
+    parts = pl.pallas_call(
         pick_kernel,
-        out_shape=shape(control.shape[0], PACK, LANES),
+        out_shape=shape(cols, *owned),
         in_specs=in_smem(1) + in_vmem(1),
         out_specs=pl.BlockSpec(memory_space=pltpu.VMEM),
+        scratch_shapes=[pltpu.VMEM(owned, f32)],
         compiler_params=params,
         name="pick",
-    )(tile_block, lax.all_gather(sums, "gy", axis=0))
+    )(tile_block, lax.all_to_all(sums, "gy", 0, 0, tiled=True))
     gradient = pl.pallas_call(
         add_kernel,
         out_shape=shape(*control.shape),
@@ -453,7 +456,7 @@
         out_specs=pl.BlockSpec(memory_space=pltpu.VMEM),
         compiler_params=params,
         name="add",
-    )(lax.all_gather(owned, "gx", axis=0))
+    )(lax.all_to_all(parts, "gx", 0, 0, tiled=True))
     return vel_u, vel_v, gradient
 
 

time: 83.6 us -> 75.5 us (0.903)
  local copies, waits for them, and re-layouts: 4.73 us -> 0.87 us
  Pallas kernels: 30.1 us -> 27.2 us
  blocking collectives: 25.8 us -> 24.2 us
    all_gather x2 -> x0, blocking collectives: 25.8 us -> none  [the longest x1 14.1 us: per_device(): lax.all_gather(owned, 'gx', axis=0)]
    all_to_all x0 -> x2, blocking collectives: none -> 24.2 us  [the longest x1 12.4 us: per_device(): lax.all_to_all(parts, 'gx', 0, 0, tiled=True)]
    pallas_call x1, Pallas kernels: 25.7 us -> 22.4 us  [per_device(): pl.pallas_call(model_kernel, out_shape=(shape(TILE, TILE), shape(TILE, TI...]
    unnamed x17 -> x14, local copies, waits for them, and re-layouts: 3.97 us -> 0.87 us
where the time goes in v2:
time: 75.5 us; the launch traced here: 75 us
  Pallas kernels  27.2 us (36%)
  blocking collectives  24.2 us (32%)
  starting transfers between devices  12.8 us (17%)
  waiting for transfers between devices  9.2 us (12%)
  local copies, waits for them, and re-layouts  0.87 us (1%)
  between operations  0.77 us (1%)
    pallas_call x1, Pallas kernels, per_device(): pl.pallas_call(model_kernel, out_shape=(shape(TILE, TILE), shape(TILE, TI...  22.4 us
    all_to_all x1, blocking collectives, per_device(): lax.all_to_all(parts, 'gx', 0, 0, tiled=True)  12.4 us
    all_to_all x1, blocking collectives, per_device(): lax.all_to_all(sums, 'gy', 0, 0, tiled=True)  11.8 us
    ppermute x4, waiting for transfers between devices, moved(): lax.ppermute(cells, axis, [(i, i + step) for i in range(count) if 0 <= i...  9.19 us
    ppermute x4, starting transfers between devices, moved(): lax.ppermute(cells, axis, [(i, i + step) for i in range(count) if 0 <= i...  7.45 us
    all_to_all x1, starting transfers between devices, per_device(): patches = lax.all_to_all(patches, 'gy', 0, 0, tiled=True)  5.36 us
    pallas_call x1, Pallas kernels, per_device(): pl.pallas_call(pack_kernel, out_shape=(shape(2, 64, LANES), shape(2, 64,...  3.31 us
  transfers between devices with their start and end apart: 5, of which 3 were waited for; matrix products, arithmetic and copies ran while one was open for 0% of the time, Pallas kernels for 0%

profile of v2, /device:TPU:0, one launch (start us, length us, event | category | flops | bytes accessed | tf_op | source)
XLA Modules:
  0.0 75.0 jit_solution(3759262388971386467)
XLA Ops:
  0.6 0.0 copy-start.1
  0.6 3.3 %pack.1 = (f32[2,64,128]{2,1,0:T(8,128)}, f32[2,64,128]{2,1,0:T(8,128)}, f32[128,128]{1,0:T(8,128)}, f32[128,128]{1,0:T(8,128)}, f32[8,72,128]{2,1,0:T(8,128)}) custom-call(s32[4,8]{1,0:T(4,128)} %bitcast.4, f32[4,4096]{1,0:T(4,128)} %control.1, f32[256,256]{1,0:T(8,128)} %thick.3, f32[2,256,256]{2,1,0:T(8,128)} %drive.3, f32[2,256,256]{2,1,0:T(8,128)} %obs.3), custom_call_target="tpu_custom_call" | custom-call | tf_op jit(solution)/shard_map/pack/pallas_call | solution.py:390
  4.0 0.0 copy-start
  4.0 0.0 copy-start.3
  4.0 5.4 %all-to-all-start = ((f32[8,72,128]{2,1,0:T(8,128)}), f32[8,72,128]{2,1,0:T(8,128)S(1)}, u32[]{:S(2)}, u32[]{:S(2)}) async-start(f32[8,72,128]{2,1,0:T(8,128)} %get-tuple-element.13), calls=%async_computation | async-start | bytes 589824 | tf_op jit(solution)/shard_map/all_to_all | solution.py:412
  9.3 0.0 copy-start.2
  9.3 3.6 %collective-permute-start = (f32[128,128]{1,0:T(8,128)}, f32[128,128]{1,0:T(8,128)S(1)}, u32[]{:S(2)}, u32[]{:S(2)}) collective-permute-start(f32[128,128]{1,0:T(8,128)} %get-tuple-element.16), channel_id=1, source_target_pairs={{0,8},{8,16},{16,24},{1,9},{9,17},{17,25},{2,10},{10,18},{18,26},{... | collective-permute-start | bytes 196616 | tf_op jit(solution)/shard_map/ppermute | solution.py:409
  12.9 1.3 %collective-permute-start.1 = (f32[128,128]{1,0:T(8,128)}, f32[128,128]{1,0:T(8,128)S(1)}, u32[]{:S(2)}, u32[]{:S(2)}) collective-permute-start(f32[128,128]{1,0:T(8,128)} %get-tuple-element.17), channel_id=1, source_target_pairs={{8,0},{16,8},{24,16},{9,1},{17,9},{25,17},{10,2},{18,10},{26,18},{... | collective-permute-start | bytes 196616 | tf_op jit(solution)/shard_map/ppermute | solution.py:409
  14.2 1.0 %collective-permute-done.west = f32[128,128]{1,0:T(8,128)S(1)} collective-permute-done((f32[128,128]{1,0:T(8,128)}, f32[128,128]{1,0:T(8,128)S(1)}, u32[]{:S(2)}, u32[]{:S(2)}) %collective-permute-start) | collective-permute-done | bytes 65568 | tf_op jit(solution)/shard_map/ppermute | solution.py:409
  15.2 4.1 %collective-permute-done.1.east = f32[128,128]{1,0:T(8,128)S(1)} collective-permute-done((f32[128,128]{1,0:T(8,128)}, f32[128,128]{1,0:T(8,128)S(1)}, u32[]{:S(2)}, u32[]{:S(2)}) %collective-permute-start.1) | collective-permute-done | bytes 65568 | tf_op jit(solution)/shard_map/ppermute | solution.py:409
  19.3 0.0 copy-done.3
  19.3 0.0 copy-start.4
  19.3 0.8 %copy-done.4 = f32[2,64,128]{2,1,0:T(8,128)S(1)} copy-done((f32[2,64,128]{2,1,0:T(8,128)S(1)}, f32[2,64,128]{2,1,0:T(8,128)}, u32[]{:S(2)}) %copy-start.4) | copy-done | bytes 65560
  20.1 0.1 corners.1
  20.2 0.0 copy-start.6
  20.2 1.3 %collective-permute-start.2 = (f32[3,64,128]{2,1,0:T(8,128)S(1)}, f32[3,64,128]{2,1,0:T(8,128)S(1)}, u32[]{:S(2)}, u32[]{:S(2)}) collective-permute-start(f32[3,64,128]{2,1,0:T(8,128)S(1)} %get-tuple-element.18), channel_id=1, source_target_pairs={{0,1},{1,2},{2,3},{3,4},{4,5},{5,6},{6,7},{8,9},{9,10},{10,11},{11... | collective-permute-start | bytes 294920 | tf_op jit(solution)/shard_map/ppermute | solution.py:409
  21.6 1.3 %collective-permute-start.3 = (f32[3,64,128]{2,1,0:T(8,128)S(1)}, f32[3,64,128]{2,1,0:T(8,128)S(1)}, u32[]{:S(2)}, u32[]{:S(2)}) collective-permute-start(f32[3,64,128]{2,1,0:T(8,128)S(1)} %get-tuple-element.19), channel_id=1, source_target_pairs={{1,0},{2,1},{3,2},{4,3},{5,4},{6,5},{7,6},{9,8},{10,9},{11,10},{12... | collective-permute-start | bytes 294920 | tf_op jit(solution)/shard_map/ppermute | solution.py:409
  22.9 0.0 collective-permute-done.2.north
  22.9 4.1 %collective-permute-done.3.south = f32[3,64,128]{2,1,0:T(8,128)S(1)} collective-permute-done((f32[3,64,128]{2,1,0:T(8,128)S(1)}, f32[3,64,128]{2,1,0:T(8,128)S(1)}, u32[]{:S(2)}, u32[]{:S(2)}) %collective-permute-start.3) | collective-permute-done | bytes 98336 | tf_op jit(solution)/shard_map/ppermute | solution.py:409
  27.0 0.0 all-to-all-done.patches
  27.0 0.0 copy-done.1
  27.0 0.0 copy-done
  27.0 0.0 copy-done.2
  27.0 0.0 copy-done.6
  27.0 22.4 %model.1 = (f32[256,256]{1,0:T(8,128)}, f32[256,256]{1,0:T(8,128)}, f32[8,32,128]{2,1,0:T(8,128)S(1)}) custom-call(s32[4,8]{1,0:T(4,128)S(1)} %bitcast.6, f32[8,72,128]{2,1,0:T(8,128)S(1)} %all-to-all-done.patches, f32[256,256]{1,0:T(8,128)S(1)} %copy-done.2, f32[2,256,256]{2,1,0:T(8,128)S(1)} %copy-done, f32[2,256,256]{2,1,0:T(8,128)S(1)} %copy-done.1, ...), custom_call_target="tpu_custom_call" | custom-call | tf_op jit(solution)/shard_map/model/pallas_call | solution.py:423
  49.4 0.0 copy-start.5
  49.4 11.8 %all_to_all.15.gathered = f32[8,32,128]{2,1,0:T(8,128)S(1)} all-to-all(f32[8,32,128]{2,1,0:T(8,128)S(1)} %get-tuple-element.22), channel_id=1, replica_groups=mesh['gx'=4,'gy'=8] {'gy'}, dimensions={0} | all-to-all | bytes 262144 | tf_op jit(solution)/shard_map/all_to_all | solution.py:451
  61.2 0.0 copy-done.5
  61.2 0.7 pick.1
  62.0 12.4 %all_to_all.16.parts = f32[4,4,32,128]{3,2,1,0:T(8,128)S(1)} all-to-all(f32[4,4,32,128]{3,2,1,0:T(8,128)S(1)} %pick.1), channel_id=1, replica_groups=mesh['gx'=4,'gy'=8] {'gx'}, dimensions={0} | all-to-all | bytes 524288 | tf_op jit(solution)/shard_map/all_to_all | solution.py:459
  74.4 0.7 add.1
Async XLA Ops:
  0.6 26.4 %copy-start.1 = (f32[2,256,256]{2,1,0:T(8,128)S(1)}, f32[2,256,256]{2,1,0:T(8,128)}, u32[]{:S(2)}) copy-start(f32[2,256,256]{2,1,0:T(8,128)} %obs.3) | copy-start | bytes 1572868
  4.0 23.0 %copy-start = (f32[2,256,256]{2,1,0:T(8,128)S(1)}, f32[2,256,256]{2,1,0:T(8,128)}, u32[]{:S(2)}) copy-start(f32[2,256,256]{2,1,0:T(8,128)} %drive.3) | copy-start | bytes 1572868
  4.0 15.3 %copy-start.3 = (f32[2,64,128]{2,1,0:T(8,128)S(1)}, f32[2,64,128]{2,1,0:T(8,128)}, u32[]{:S(2)}) copy-start(f32[2,64,128]{2,1,0:T(8,128)} %get-tuple-element.14.top) | copy-start | bytes 196612
  4.0 23.0 %all-to-all-start = ((f32[8,72,128]{2,1,0:T(8,128)}), f32[8,72,128]{2,1,0:T(8,128)S(1)}, u32[]{:S(2)}, u32[]{:S(2)}) async-start(f32[8,72,128]{2,1,0:T(8,128)} %get-tuple-element.13), calls=%async_computation | async-start | bytes 589824 | tf_op jit(solution)/shard_map/all_to_all | solution.py:412
  9.3 17.7 %copy-start.2 = (f32[256,256]{1,0:T(8,128)S(1)}, f32[256,256]{1,0:T(8,128)}, u32[]{:S(2)}) copy-start(f32[256,256]{1,0:T(8,128)} %thick.3) | copy-start | bytes 786436
  9.3 5.9 %collective-permute-start = (f32[128,128]{1,0:T(8,128)}, f32[128,128]{1,0:T(8,128)S(1)}, u32[]{:S(2)}, u32[]{:S(2)}) collective-permute-start(f32[128,128]{1,0:T(8,128)} %get-tuple-element.16), channel_id=1, source_target_pairs={{0,8},{8,16},{16,24},{1,9},{9,17},{17,25},{2,10},{10,18},{18,26},{... | collective-permute-start | bytes 196616 | tf_op jit(solution)/shard_map/ppermute | solution.py:409
  12.9 6.4 %collective-permute-start.1 = (f32[128,128]{1,0:T(8,128)}, f32[128,128]{1,0:T(8,128)S(1)}, u32[]{:S(2)}, u32[]{:S(2)}) collective-permute-start(f32[128,128]{1,0:T(8,128)} %get-tuple-element.17), channel_id=1, source_target_pairs={{8,0},{16,8},{24,16},{9,1},{17,9},{25,17},{10,2},{18,10},{26,18},{... | collective-permute-start | bytes 196616 | tf_op jit(solution)/shard_map/ppermute | solution.py:409
  19.3 0.8 %copy-start.4 = (f32[2,64,128]{2,1,0:T(8,128)S(1)}, f32[2,64,128]{2,1,0:T(8,128)}, u32[]{:S(2)}) copy-start(f32[2,64,128]{2,1,0:T(8,128)} %get-tuple-element.15.bottom) | copy-start | bytes 196612
  20.2 6.8 %copy-start.6 = (s32[8,4]{0,1:T(4,128)S(1)}, s32[8,4]{0,1:T(4,128)}, u32[]{:S(2)}) copy-start(s32[8,4]{0,1:T(4,128)} %param.10) | copy-start | bytes 388
  20.2 2.6 %collective-permute-start.2 = (f32[3,64,128]{2,1,0:T(8,128)S(1)}, f32[3,64,128]{2,1,0:T(8,128)S(1)}, u32[]{:S(2)}, u32[]{:S(2)}) collective-permute-start(f32[3,64,128]{2,1,0:T(8,128)S(1)} %get-tuple-element.18), channel_id=1, source_target_pairs={{0,1},{1,2},{2,3},{3,4},{4,5},{5,6},{6,7},{8,9},{9,10},{10,11},{11... | collective-permute-start | bytes 294920 | tf_op jit(solution)/shard_map/ppermute | solution.py:409
  21.6 5.4 %collective-permute-start.3 = (f32[3,64,128]{2,1,0:T(8,128)S(1)}, f32[3,64,128]{2,1,0:T(8,128)S(1)}, u32[]{:S(2)}, u32[]{:S(2)}) collective-permute-start(f32[3,64,128]{2,1,0:T(8,128)S(1)} %get-tuple-element.19), channel_id=1, source_target_pairs={{1,0},{2,1},{3,2},{4,3},{5,4},{6,5},{7,6},{9,8},{10,9},{11,10},{12... | collective-permute-start | bytes 294920 | tf_op jit(solution)/shard_map/ppermute | solution.py:409
  49.4 11.8 %copy-start.5 = (s32[8,4,1]{0,2,1:T(1,128)S(1)}, s32[8,4,1]{0,2,1:T(1,128)}, u32[]{:S(2)}) copy-start(s32[8,4,1]{0,2,1:T(1,128)} %param.11) | copy-start | bytes 388

commit v3 on v2

--- a/solution.py
+++ b/solution.py
@@ -40,15 +40,33 @@
     return (lane < CT) if ds == 0 else ((lane >= CT) & (lane < 96) if ds > 0 else lane >= 96)
 
 
-def pack_kernel(
-    tile_block, control, thick, drive, obs, top, bottom, left, right, patches,
-    held, owned_blocks, sems,
-):
+def is_even(axis):
+    return lax.axis_index(axis) % 2 == 0
+
+
+def columns_kernel(thick, drive, obs, first_pair, second_pair, held, sems):
     copies = []
     for f, field in enumerate((thick, drive.at[0], drive.at[1], obs.at[0], obs.at[1])):
         copies.append(pltpu.make_async_copy(field, held.at[f], sems.at[f]))
         copies[-1].start()
-
+    half = TILE // 2
+    lane = lanes_of(half)
+    left = jnp.zeros((half, LANES), jnp.float32)
+    right = jnp.zeros((half, LANES), jnp.float32)
+    for f, (first, count) in enumerate(STRIP):
+        copies[f].wait()
+        for part in range(2):
+            rows = slice(part * half, (part + 1) * half)
+            start = part * 64 + first
+            inside = (lane >= start) & (lane < start + count)
+            left = jnp.where(inside, pltpu.roll(held[f, rows, :LANES], start, 1), left)
+            right = jnp.where(inside, pltpu.roll(held[f, rows, LANES:], (start + count) % LANES, 1), right)
+    even = is_even("gx")
+    first_pair[...] = jnp.where(even, right, left)
+    second_pair[...] = jnp.where(even, left, right)
+
+
+def patches_kernel(tile_block, control, after, patches, owned_blocks):
     tile_cols, tile_rows = tile_block.shape
     owned = control.shape[0]
     mine = lax.axis_index("gy") * owned
@@ -79,42 +97,33 @@
 
     lax.fori_loop(0, tile_rows, fill, 0)
 
-    for copy in copies:
-        copy.wait()
-    for f, (first, count) in enumerate(STRIP):
-        for c in range(2):
-            cols = slice(c * LANES, (c + 1) * LANES)
-            top[c, first : first + count, :] = held[f, 0:count, cols]
-            bottom[c, first : first + count, :] = held[f, TILE - count : TILE, cols]
-    half = TILE // 2
-    lane = lanes_of(half)
-    for out, col, end in ((left, 0, False), (right, LANES, True)):
-        packed = jnp.zeros((half, LANES), jnp.float32)
-        for part in range(2):
-            for f, (first, count) in enumerate(STRIP):
-                cells = held[f, part * half : (part + 1) * half, col : col + LANES]
-                start = part * 64 + first
-                source = LANES - count if end else 0
-                moved = pltpu.roll(cells, (start - source) % LANES, 1)
-                packed = jnp.where((lane >= start) & (lane < start + count), moved, packed)
-        out[...] = packed
-
-
-def frame_cells(west, east, rows, start, count):
-    from_east = pltpu.roll(east[rows, :], (LANES - start) % LANES, 1)
-    from_west = pltpu.roll(west[rows, :], (2 * LANES - count - start) % LANES, 1)
+
+def sides(axis, first_pair, second_pair):
+    even = is_even(axis)
+    return jnp.where(even, second_pair, first_pair), jnp.where(even, first_pair, second_pair)
+
+
+def frame_cells(west, east, start, count):
+    from_east = pltpu.roll(east, (LANES - start) % LANES, 1)
+    from_west = pltpu.roll(west, (2 * LANES - count - start) % LANES, 1)
     lane = lanes_of(from_east.shape[0])
     return jnp.where(lane < count, from_east, jnp.where(lane >= LANES - count, from_west, 0.0))
 
 
-def corner_kernel(top, bottom, west, east, top_wide, bottom_wide):
+def rows_kernel(thick, drive, obs, first_col, second_col, first_pair, second_pair):
     half = TILE // 2
-    for narrow, wide, part in ((top, top_wide, 0), (bottom, bottom_wide, 1)):
-        for c in range(2):
-            wide[c] = narrow[c]
-        for first, count in STRIP:
-            rows = slice(half - count, half) if part else slice(0, count)
-            wide[2, first : first + count, :] = frame_cells(west, east, rows, part * 64 + first, count)
+    west, east = sides("gx", first_col[...], second_col[...])
+    even = is_even("gy")
+    for field, (first, count) in zip((thick, drive.at[0], drive.at[1], obs.at[0], obs.at[1]), STRIP):
+        for c in range(3):
+            if c < 2:
+                cols = slice(c * LANES, (c + 1) * LANES)
+                top, bottom = field[0:count, cols], field[TILE - count : TILE, cols]
+            else:
+                top = frame_cells(west[:count], east[:count], first, count)
+                bottom = frame_cells(west[half - count :], east[half - count :], 64 + first, count)
+            first_pair[c, first : first + count, :] = jnp.where(even, bottom, top)
+            second_pair[c, first : first + count, :] = jnp.where(even, top, bottom)
 
 
 def shift_east(tiles, lane):
@@ -138,7 +147,7 @@
 
 
 def model_kernel(
-    ice_mask, patches, thick, drive, obs, north, south, west, east,
+    ice_mask, patches, thick, drive, obs, first_row, second_row, first_col, second_col,
     vel_u, vel_v, sums,
     ext, fr, ice, visc, vel, coef, small, sems,
 ):
@@ -158,15 +167,18 @@
 
     fields = (thick, drive.at[0], drive.at[1], obs.at[0], obs.at[1])
     half = TILE // 2
+    west, east = sides("gx", first_col[...], second_col[...])
+    even = is_even("gy")
     for f, (field, (first, count)) in enumerate(zip(fields, STRIP)):
         for c in range(3):
             if c < 2:
                 ext[f, c, TOP : TOP + TILE, :] = field[:, c * LANES : (c + 1) * LANES]
-            ext[f, c, TOP - count : TOP, :] = north[c, first : first + count, :]
-            ext[f, c, TOP + TILE : TOP + TILE + count, :] = south[c, first : first + count, :]
+            one, two = first_row[c, first : first + count, :], second_row[c, first : first + count, :]
+            ext[f, c, TOP - count : TOP, :] = jnp.where(even, two, one)
+            ext[f, c, TOP + TILE : TOP + TILE + count, :] = jnp.where(even, one, two)
         for part in range(2):
             ext[f, 2, TOP + part * half : TOP + (part + 1) * half, :] = frame_cells(
-                west, east, slice(None), part * 64 + first, count
+                west, east, part * 64 + first, count
             )
 
     for dr, first, count in ((-1, MARGIN, HALO), (0, TOP, TILE), (1, TOP + TILE, HALO)):
@@ -338,8 +350,10 @@
     packed = jnp.where(
         lanes_of(PACK) < CT, small[pl.ds(0, PACK, stride=2), :], small[pl.ds(1, PACK, stride=2), :]
     )
-    for j in range(sums.shape[0]):
-        sums[j] = packed
+    part = PACK // sums.shape[0]
+    for i in range(sums.shape[0]):
+        for j in range(sums.shape[1]):
+            sums[i, j] = packed[i * part : (i + 1) * part]
     for copy in copies:
         copy.wait()
 
@@ -347,27 +361,30 @@
 def pick_kernel(tile_block, gathered, out, total):
     owned = total.shape[0]
     first = lax.axis_index("gy") * owned
-    col_tile = lax.axis_index("gx")
+    tile_cols, tile_rows = tile_block.shape
     total[...] = jnp.zeros_like(total)
 
-    def step(row, carry):
-        place = tile_block[col_tile, row] - first
+    def step(t, carry):
+        col = t // tile_rows
+        place = tile_block[col, t - col * tile_rows] - first
 
         @pl.when((place >= 0) & (place < owned))
         def _():
-            total[place] += gathered[row]
+            total[place] += gathered[t]
 
         return carry
 
-    lax.fori_loop(0, tile_block.shape[1], step, 0)
+    lax.fori_loop(0, tile_cols * tile_rows, step, 0)
     for j in range(out.shape[0]):
         out[j] = total[...]
 
 
-def add_kernel(parts, out):
-    total = sum(parts[i] for i in range(parts.shape[0]))
-    for j in range(PACK):
-        out[:, j * LANES : (j + 1) * LANES] = total[:, j, :]
+def join_kernel(parts, out):
+    share = parts.shape[2]
+    for i in range(parts.shape[0]):
+        for j in range(share):
+            at = (i * share + j) * LANES
+            out[:, at : at + LANES] = parts[i, :, j, :]
 
 
 def in_vmem(count):
@@ -387,42 +404,49 @@
     def shape(*sizes):
         return jax.ShapeDtypeStruct(sizes, f32)
 
-    top, bottom, left, right, patches = pl.pallas_call(
-        pack_kernel,
-        out_shape=(
-            shape(2, 64, LANES), shape(2, 64, LANES), shape(TILE // 2, LANES), shape(TILE // 2, LANES),
-            shape(rows, PATCH, LANES),
-        ),
-        in_specs=in_smem(1) + in_vmem(1) + [pl.BlockSpec(memory_space=pltpu.HBM)] * 3,
-        out_specs=in_vmem(5),
-        scratch_shapes=[
-            pltpu.VMEM((5, TILE, TILE), f32),
-            pltpu.VMEM((control.shape[0], PACK, LANES), f32),
-            pltpu.SemaphoreType.DMA((5,)),
-        ],
+    def swap(axis, cells_first, cells_second):
+        count = lax.axis_size(axis)
+        received = []
+        for cells, low in ((cells_second, 1), (cells_first, 0)):
+            pairs = [(i, i + 1) for i in range(low, count - 1, 2)]
+            received.append(lax.ppermute(cells, axis, pairs + [(j, i) for i, j in pairs]))
+        return received[1], received[0]
+
+    fields = thickness, driving, observed
+    columns = pl.pallas_call(
+        columns_kernel,
+        out_shape=[shape(TILE // 2, LANES)] * 2,
+        in_specs=[pl.BlockSpec(memory_space=pltpu.HBM)] * 3,
+        out_specs=in_vmem(2),
+        scratch_shapes=[pltpu.VMEM((5, TILE, TILE), f32), pltpu.SemaphoreType.DMA((5,))],
         compiler_params=pltpu.CompilerParams(vmem_limit_bytes=PACK_VMEM_LIMIT),
-        name="pack",
-    )(tile_block, control, thickness, driving, observed)
-
-    def moved(cells, axis, step):
-        count = lax.axis_size(axis)
-        return lax.ppermute(cells, axis, [(i, i + step) for i in range(count) if 0 <= i + step < count])
-
-    west, east = moved(right, "gx", 1), moved(left, "gx", -1)
+        name="columns",
+    )(*fields)
+    columns_in = swap("gx", *columns)
+    patches = pl.pallas_call(
+        patches_kernel,
+        out_shape=shape(rows, PATCH, LANES),
+        in_specs=in_smem(1) + in_vmem(1) + [pl.BlockSpec(memory_space=pl.ANY)],
+        out_specs=pl.BlockSpec(memory_space=pltpu.VMEM),
+        scratch_shapes=[pltpu.VMEM((control.shape[0], PACK, LANES), f32)],
+        compiler_params=params,
+        cost_estimate=pl.CostEstimate(flops=10**7, bytes_accessed=10**7, transcendentals=0),
+        name="patches",
+    )(tile_block, control, columns[0])
     patches = lax.all_to_all(patches, "gy", 0, 0, tiled=True)
-    top, bottom = pl.pallas_call(
-        corner_kernel,
-        out_shape=(shape(3, 64, LANES), shape(3, 64, LANES)),
-        in_specs=in_vmem(4),
+    strips = pl.pallas_call(
+        rows_kernel,
+        out_shape=[shape(3, 64, LANES)] * 2,
+        in_specs=in_vmem(5),
         out_specs=in_vmem(2),
         compiler_params=params,
-        name="corners",
-    )(top, bottom, west, east)
-    north, south = moved(bottom, "gy", 1), moved(top, "gy", -1)
+        name="rows",
+    )(*fields, *columns_in)
+    rows_in = swap("gy", *strips)
 
     vel_u, vel_v, sums = pl.pallas_call(
         model_kernel,
-        out_shape=(shape(TILE, TILE), shape(TILE, TILE), shape(rows, PACK, LANES)),
+        out_shape=(shape(TILE, TILE), shape(TILE, TILE), shape(cols, rows, PACK // cols, LANES)),
         in_specs=in_smem(1) + in_vmem(8),
         out_specs=[pl.BlockSpec(memory_space=pltpu.HBM)] * 2 + in_vmem(1),
         scratch_shapes=[
@@ -437,25 +461,26 @@
         ],
         compiler_params=params,
         name="model",
-    )(ice_mask, patches, thickness, driving, observed, north, south, west, east)
-
-    owned = (control.shape[0], PACK, LANES)
+    )(ice_mask, patches, *fields, *rows_in, *columns_in)
+
+    share = (control.shape[0], PACK // cols, LANES)
+    sums = lax.all_to_all(sums.reshape(cols * rows, *share[1:]), ("gx", "gy"), 0, 0, tiled=True)
     parts = pl.pallas_call(
         pick_kernel,
-        out_shape=shape(cols, *owned),
+        out_shape=shape(cols, *share),
         in_specs=in_smem(1) + in_vmem(1),
         out_specs=pl.BlockSpec(memory_space=pltpu.VMEM),
-        scratch_shapes=[pltpu.VMEM(owned, f32)],
+        scratch_shapes=[pltpu.VMEM(share, f32)],
         compiler_params=params,
         name="pick",
-    )(tile_block, lax.all_to_all(sums, "gy", 0, 0, tiled=True))
+    )(tile_block, sums)
     gradient = pl.pallas_call(
-        add_kernel,
+        join_kernel,
         out_shape=shape(*control.shape),
         in_specs=in_vmem(1),
         out_specs=pl.BlockSpec(memory_space=pltpu.VMEM),
         compiler_params=params,
-        name="add",
+        name="join",
     )(lax.all_to_all(parts, "gx", 0, 0, tiled=True))
     return vel_u, vel_v, gradient
 

time: 75.5 us -> 71.5 us (0.947)
  waiting for transfers between devices: 9.2 us -> 3.09 us
  Pallas kernels: 27.2 us -> 29.8 us
  starting transfers between devices: 12.8 us -> 10.8 us
  blocking collectives: 24.2 us -> 25.8 us
    ppermute x4, waiting for transfers between devices: 9.19 us -> 3.08 us  [swap(): lax.ppermute(cells, axis, pairs + [(j, i) for i, j in pairs])]
    all_to_all x1, blocking collectives: 11.8 us -> 17.7 us  [per_device(): lax.all_to_all(sums.reshape(cols * rows, *share[1:]), ('gx', 'gy'), 0, 0,...]
    all_to_all x1, blocking collectives: 12.4 us -> 8.15 us  [per_device(): lax.all_to_all(parts, 'gx', 0, 0, tiled=True)]
    pallas_call x4 -> x5, Pallas kernels: 4.8 us -> 7.44 us  [the longest x1 2.97 us: per_device(): pl.pallas_call(patches_kernel, out_shape=shape(rows, PATCH, LANES), in_sp...]
    ppermute x4, starting transfers between devices: 7.45 us -> 5.96 us  [swap(): lax.ppermute(cells, axis, pairs + [(j, i) for i, j in pairs])]
  transfers between devices with their start and end apart: 5 -> 5, of which waited for: 3 -> 2; matrix products, arithmetic and copies ran while one was open for 0% -> 0% of each run, Pallas kernels for 0% -> 0%
where the time goes in v3:
time: 71.5 us; the launch traced here: 71.2 us
  Pallas kernels  29.8 us (42%)
  blocking collectives  25.8 us (36%)
  starting transfers between devices  10.8 us (15%)
  waiting for transfers between devices  3.09 us (4%)
  local copies, waits for them, and re-layouts  0.92 us (1%)
  between operations  0.77 us (1%)
    pallas_call x1, Pallas kernels, per_device(): pl.pallas_call(model_kernel, out_shape=(shape(TILE, TILE), shape(TILE, TI...  22.4 us
    all_to_all x1, blocking collectives, per_device(): lax.all_to_all(sums.reshape(cols * rows, *share[1:]), ('gx', 'gy'), 0, 0,...  17.7 us
    all_to_all x1, blocking collectives, per_device(): lax.all_to_all(parts, 'gx', 0, 0, tiled=True)  8.15 us
    ppermute x4, starting transfers between devices, swap(): lax.ppermute(cells, axis, pairs + [(j, i) for i, j in pairs])  5.96 us
    all_to_all x1, starting transfers between devices, per_device(): patches = lax.all_to_all(patches, 'gy', 0, 0, tiled=True)  4.86 us
    ppermute x4, waiting for transfers between devices, swap(): lax.ppermute(cells, axis, pairs + [(j, i) for i, j in pairs])  3.08 us
    pallas_call x1, Pallas kernels, per_device(): pl.pallas_call(patches_kernel, out_shape=shape(rows, PATCH, LANES), in_sp...  2.97 us
    pallas_call x1, Pallas kernels, per_device(): pl.pallas_call(columns_kernel, out_shape=[shape(TILE // 2, LANES)] * 2, i...  2.35 us
  transfers between devices with their start and end apart: 5, of which 2 were waited for; matrix products, arithmetic and copies ran while one was open for 0% of the time, Pallas kernels for 0%

profile of v3, /device:TPU:0, one launch (start us, length us, event | category | flops | bytes accessed | tf_op | source)
XLA Modules:
  0.0 71.2 jit_solution(10202578759734704851)
XLA Ops:
  0.6 0.0 copy-start.3
  0.6 0.0 copy-start.6
  0.7 0.0 copy-start.1
  0.7 2.3 %columns.1 = (f32[128,128]{1,0:T(8,128)}, f32[128,128]{1,0:T(8,128)}) custom-call(f32[256,256]{1,0:T(8,128)} %thick.5, f32[2,256,256]{2,1,0:T(8,128)} %drive.5, f32[2,256,256]{2,1,0:T(8,128)} %obs.5), custom_call_target="tpu_custom_call" | custom-call | tf_op jit(solution)/shard_map/columns/pallas_call | solution.py:416
  3.0 0.0 copy-start
  3.0 0.0 copy-done.3
  3.0 0.0 copy-done.6
  3.0 0.0 copy-start.4
  3.1 0.9 %copy-done.4 = f32[128,128]{1,0:T(8,128)S(1)} copy-done((f32[128,128]{1,0:T(8,128)S(1)}, f32[128,128]{1,0:T(8,128)}, u32[]{:S(2)}) %copy-start.4) | copy-done | bytes 65560
  3.9 3.0 %patches.1 = f32[8,72,128]{2,1,0:T(8,128)} custom-call(s32[4,8]{1,0:T(4,128)S(1)} %bitcast.6, f32[4,4096]{1,0:T(4,128)S(1)} %copy-done.3, f32[128,128]{1,0:T(8,128)S(1)} %copy-done.4), custom_call_target="tpu_custom_call" | custom-call | flops 10000000 | bytes 10000000 | tf_op jit(solution)/shard_map/patches/pallas_call | solution.py:426
  6.9 0.0 copy-start.8
  6.9 0.0 copy-start.5
  6.9 0.0 copy-start.2
  6.9 4.9 %all-to-all-start = ((f32[8,72,128]{2,1,0:T(8,128)}), f32[8,72,128]{2,1,0:T(8,128)S(1)}, u32[]{:S(2)}, u32[]{:S(2)}) async-start(f32[8,72,128]{2,1,0:T(8,128)} %patches.1), calls=%async_computation | async-start | bytes 589824 | tf_op jit(solution)/shard_map/all_to_all | solution.py:436
  11.8 0.0 copy-done.8
  11.8 0.7 collective-permute-start.1
  12.5 0.0 copy-done.5
  12.5 4.6 %collective-permute-start = (f32[128,128]{1,0:T(8,128)S(1)}, f32[128,128]{1,0:T(8,128)S(1)}, u32[]{:S(2)}, u32[]{:S(2)}) collective-permute-start(f32[128,128]{1,0:T(8,128)S(1)} %copy-done.5), channel_id=1, source_target_pairs={{0,8},{16,24},{8,0},{24,16},{1,9},{17,25},{9,1},{25,17},{2,10},{18... | collective-permute-start | bytes 196616 | tf_op jit(solution)/shard_map/ppermute | solution.py:412
  17.0 0.0 collective-permute-done.1.second_col
  17.0 2.5 %collective-permute-done.first_col = f32[128,128]{1,0:T(8,128)S(1)} collective-permute-done((f32[128,128]{1,0:T(8,128)S(1)}, f32[128,128]{1,0:T(8,128)S(1)}, u32[]{:S(2)}, u32[]{:S(2)}) %collective-permute-start) | collective-permute-done | bytes 65568 | tf_op jit(solution)/shard_map/ppermute | solution.py:412
  19.5 0.0 copy-done.1
  19.5 0.0 copy-done
  19.5 0.0 copy-done.2
  19.5 0.1 rows.1
  19.6 0.0 copy-start.7
  19.6 0.1 collective-permute-start.2
  19.7 0.7 collective-permute-start.3
  20.4 0.6 collective-permute-done.2.first_row
  21.0 0.0 collective-permute-done.3.second_row
  21.0 0.0 all-to-all-done.patches
  21.0 0.0 copy-done.7
  21.0 22.4 %model.1 = (f32[256,256]{1,0:T(8,128)}, f32[256,256]{1,0:T(8,128)}, f32[4,8,8,128]{3,2,1,0:T(8,128)S(1)}) custom-call(s32[4,8]{1,0:T(4,128)S(1)} %bitcast.8, f32[8,72,128]{2,1,0:T(8,128)S(1)} %all-to-all-done.patches, f32[256,256]{1,0:T(8,128)S(1)} %copy-done.2, f32[2,256,256]{2,1,0:T(8,128)S(1)} %copy-done, f32[2,256,256]{2,1,0:T(8,128)S(1)} %copy-done.1, ...), custom_call_target="tpu_custom_call" | custom-call | tf_op jit(solution)/shard_map/model/pallas_call | solution.py:447
  43.4 17.7 %all_to_all.15.gathered = f32[32,8,128]{2,1,0:T(8,128)S(1)} all-to-all(f32[32,8,128]{2,1,0:T(8,128)S(1)} %bitcast.5), channel_id=1, replica_groups=mesh['gx'=4,'gy'=8] {'gx','gy'}, dimensions={0} | all-to-all | bytes 262144 | tf_op jit(solution)/shard_map/all_to_all | solution.py:467
  61.0 1.3 %pick.1 = f32[4,4,8,128]{3,2,1,0:T(8,128)S(1)} custom-call(s32[4,8]{1,0:T(4,128)S(1)} %bitcast.7, f32[32,8,128]{2,1,0:T(8,128)S(1)} %all_to_all.15.gathered), custom_call_target="tpu_custom_call" | custom-call | tf_op jit(solution)/shard_map/pick/pallas_call | solution.py:468
  62.4 8.1 %all_to_all.16.parts = f32[4,4,8,128]{3,2,1,0:T(8,128)S(1)} all-to-all(f32[4,4,8,128]{3,2,1,0:T(8,128)S(1)} %pick.1), channel_id=1, replica_groups=mesh['gx'=4,'gy'=8] {'gx'}, dimensions={0} | all-to-all | bytes 131072 | tf_op jit(solution)/shard_map/all_to_all | solution.py:484
  70.5 0.7 join.1
Async XLA Ops:
  0.6 2.4 %copy-start.3 = (f32[4,4096]{1,0:T(4,128)S(1)}, f32[4,4096]{1,0:T(4,128)}, u32[]{:S(2)}) copy-start(f32[4,4096]{1,0:T(4,128)} %control.1) | copy-start | bytes 196612
  0.6 2.4 %copy-start.6 = (s32[8,4,1]{0,2,1:T(1,128)S(1)}, s32[8,4,1]{0,2,1:T(1,128)}, u32[]{:S(2)}) copy-start(s32[8,4,1]{0,2,1:T(1,128)} %param.11) | copy-start | bytes 388
  0.7 18.9 %copy-start.1 = (f32[2,256,256]{2,1,0:T(8,128)S(1)}, f32[2,256,256]{2,1,0:T(8,128)}, u32[]{:S(2)}) copy-start(f32[2,256,256]{2,1,0:T(8,128)} %obs.5) | copy-start | bytes 1572868
  3.0 16.5 %copy-start = (f32[2,256,256]{2,1,0:T(8,128)S(1)}, f32[2,256,256]{2,1,0:T(8,128)}, u32[]{:S(2)}) copy-start(f32[2,256,256]{2,1,0:T(8,128)} %drive.5) | copy-start | bytes 1572868
  3.0 0.9 %copy-start.4 = (f32[128,128]{1,0:T(8,128)S(1)}, f32[128,128]{1,0:T(8,128)}, u32[]{:S(2)}) copy-start(f32[128,128]{1,0:T(8,128)} %get-tuple-element.10.after) | copy-start | bytes 196612
  6.9 4.9 %copy-start.8 = (f32[128,128]{1,0:T(8,128)S(1)}, f32[128,128]{1,0:T(8,128)}, u32[]{:S(2)}) copy-start(f32[128,128]{1,0:T(8,128)} %get-tuple-element.11) | copy-start | bytes 196612
  6.9 5.5 %copy-start.5 = (f32[128,128]{1,0:T(8,128)S(1)}, f32[128,128]{1,0:T(8,128)}, u32[]{:S(2)}) copy-start(f32[128,128]{1,0:T(8,128)} %get-tuple-element.10.after) | copy-start | bytes 196612
  6.9 12.6 %copy-start.2 = (f32[256,256]{1,0:T(8,128)S(1)}, f32[256,256]{1,0:T(8,128)}, u32[]{:S(2)}) copy-start(f32[256,256]{1,0:T(8,128)} %thick.5) | copy-start | bytes 786436
  6.9 14.1 %all-to-all-start = ((f32[8,72,128]{2,1,0:T(8,128)}), f32[8,72,128]{2,1,0:T(8,128)S(1)}, u32[]{:S(2)}, u32[]{:S(2)}) async-start(f32[8,72,128]{2,1,0:T(8,128)} %patches.1), calls=%async_computation | async-start | bytes 589824 | tf_op jit(solution)/shard_map/all_to_all | solution.py:436
  11.8 5.2 %collective-permute-start.1 = (f32[128,128]{1,0:T(8,128)S(1)}, f32[128,128]{1,0:T(8,128)S(1)}, u32[]{:S(2)}, u32[]{:S(2)}) collective-permute-start(f32[128,128]{1,0:T(8,128)S(1)} %copy-done.8), channel_id=1, source_target_pairs={{8,16},{16,8},{9,17},{17,9},{10,18},{18,10},{11,19},{19,11},{12,20... | collective-permute-start | bytes 196616 | tf_op jit(solution)/shard_map/ppermute | solution.py:412
  12.5 7.0 %collective-permute-start = (f32[128,128]{1,0:T(8,128)S(1)}, f32[128,128]{1,0:T(8,128)S(1)}, u32[]{:S(2)}, u32[]{:S(2)}) collective-permute-start(f32[128,128]{1,0:T(8,128)S(1)} %copy-done.5), channel_id=1, source_target_pairs={{0,8},{16,24},{8,0},{24,16},{1,9},{17,25},{9,1},{25,17},{2,10},{18... | collective-permute-start | bytes 196616 | tf_op jit(solution)/shard_map/ppermute | solution.py:412
  19.6 1.4 %copy-start.7 = (s32[8,4]{0,1:T(4,128)S(1)}, s32[8,4]{0,1:T(4,128)}, u32[]{:S(2)}) copy-start(s32[8,4]{0,1:T(4,128)} %param.10) | copy-start | bytes 388
  19.6 1.4 %collective-permute-start.2 = (f32[3,64,128]{2,1,0:T(8,128)S(1)}, f32[3,64,128]{2,1,0:T(8,128)S(1)}, u32[]{:S(2)}, u32[]{:S(2)}) collective-permute-start(f32[3,64,128]{2,1,0:T(8,128)S(1)} %get-tuple-element.12), channel_id=1, source_target_pairs={{0,1},{2,3},{4,5},{6,7},{1,0},{3,2},{5,4},{7,6},{8,9},{10,11},{12,... | collective-permute-start | bytes 294920 | tf_op jit(solution)/shard_map/ppermute | solution.py:412
  19.7 1.3 %collective-permute-start.3 = (f32[3,64,128]{2,1,0:T(8,128)S(1)}, f32[3,64,128]{2,1,0:T(8,128)S(1)}, u32[]{:S(2)}, u32[]{:S(2)}) collective-permute-start(f32[3,64,128]{2,1,0:T(8,128)S(1)} %get-tuple-element.13), channel_id=1, source_target_pairs={{1,2},{3,4},{5,6},{2,1},{4,3},{6,5},{9,10},{11,12},{13,14},{10,9},... | collective-permute-start | bytes 294920 | tf_op jit(solution)/shard_map/ppermute | solution.py:412

commit v4 on v3

v4 whole, which is shorter than its diff:
```python
import jax
import jax.numpy as jnp
from jax import lax
from jax.experimental import pallas as pl
from jax.experimental.pallas import tpu as pltpu
from jax.sharding import PartitionSpec as P

TILE = 256
PIC = 4
SW = 2
ADJ = 6
CT = 64
COARSE = 4096

LANES = 128
HALO = 16
OBS = 8
MARGIN = 8
TOP = MARGIN + HALO
ROWS = TILE + 2 * TOP
HALF = TILE // 2
SIDE = 2 * ROWS
BAND = LANES // 2
ALL_ROWS = SIDE + HALF + 2 * TOP
MAIN = (0, ROWS)
SIDES = (SIDE,)
GROUP = 8
BLOCKS = 4
PACK = COARSE // LANES
VMEM_LIMIT = 40 * 1024 * 1024
PACK_VMEM_LIMIT = 62 * 1024 * 1024

STRIP = ((0, HALO), (HALO, HALO), (2 * HALO, HALO), (3 * HALO, OBS), (3 * HALO + OBS, OBS))

PATCH_ROWS = ((-1, PACK - 2, 2, 0), (0, 0, PACK, 4), (1, 0, 2, CT + 4))
PATCH = CT + 8

visc_scale = 0.1
strain_floor = 0.05


def lanes_of(rows):
    return lax.broadcasted_iota(jnp.int32, (rows, LANES), 1)


def patch_lanes(count, ds):
    lane = lanes_of(count)
    return (lane < CT) if ds == 0 else ((lane >= CT) & (lane < 96) if ds > 0 else lane >= 96)


def is_even(axis):
    return lax.axis_index(axis) % 2 == 0


def columns_kernel(thick, drive, obs, first_pair, second_pair, held, sems):
    copies = []
    for f, field in enumerate((thick, drive.at[0], drive.at[1], obs.at[0], obs.at[1])):
        copies.append(pltpu.make_async_copy(field, held.at[f], sems.at[f]))
        copies[-1].start()
    lane = lanes_of(HALF)
    left = jnp.zeros((HALF, LANES), jnp.float32)
    right = jnp.zeros((HALF, LANES), jnp.float32)
    for f, (first, count) in enumerate(STRIP):
        copies[f].wait()
        for part in range(2):
            rows = slice(part * HALF, (part + 1) * HALF)
            start = part * BAND + first
            inside = (lane >= start) & (lane < start + count)
            left = jnp.where(inside, pltpu.roll(held[f, rows, :LANES], start, 1), left)
            right = jnp.where(inside, pltpu.roll(held[f, rows, LANES:], (start + count) % LANES, 1), right)
    even = is_even("gx")
    first_pair[...] = jnp.where(even, right, left)
    second_pair[...] = jnp.where(even, left, right)


def patches_kernel(tile_block, control, patches, owned_blocks):
    tile_cols, tile_rows = tile_block.shape
    owned = control.shape[0]
    mine = lax.axis_index("gy") * owned
    col_tile = lax.axis_index("gx")
    for j in range(PACK):
        owned_blocks[:, j, :] = control[:, j * LANES : (j + 1) * LANES]
    patches[...] = jnp.zeros_like(patches)

    def spread(row, carry):
        for ds in (-1, 0, 1):
            col = col_tile + ds
            place = tile_block[jnp.clip(col, 0, tile_cols - 1), row] - mine

            @pl.when((col >= 0) & (col < tile_cols) & (place >= 0) & (place < owned))
            def _():
                for dr, first, count, at in PATCH_ROWS:
                    target = row - dr

                    @pl.when((target >= 0) & (target < tile_rows))
                    def _():
                        cells = owned_blocks[place, first : first + count, :]
                        turned = pltpu.roll(cells, CT, 1)
                        inside = patch_lanes(count, ds)
                        for j, new in enumerate((cells, turned) if ds == 0 else (turned, cells)):
                            rows = pl.ds(at + j, count, stride=2)
                            patches[target, rows, :] = jnp.where(inside, new, patches[target, rows, :])

        return carry

    lax.fori_loop(0, tile_rows, spread, 0)


def sides(axis, first_pair, second_pair):
    even = is_even(axis)
    return jnp.where(even, second_pair, first_pair), jnp.where(even, first_pair, second_pair)


def choose_side(lane, high, east, west, low):
    place = lane % BAND
    return jnp.where(
        place < HALO, high, jnp.where(place < 2 * HALO, east, jnp.where(place < 3 * HALO, west, low))
    )


def turn(cells, source, target):
    shift = (target - source) % LANES
    return pltpu.roll(cells, shift, 1) if shift else cells


def rows_kernel(thick, drive, obs, first_col, second_col, first_pair, second_pair):
    west, east = sides("gx", first_col[...], second_col[...])
    even = is_even("gy")
    for field, (first, count) in zip((thick, drive.at[0], drive.at[1], obs.at[0], obs.at[1]), STRIP):
        strips = []
        for rows, packed_rows, source, target in (
            (slice(0, count), slice(0, count), first, BAND),
            (slice(TILE - count, TILE), slice(HALF - count, HALF), BAND + first, 0),
        ):
            low, high = field[rows, :LANES], field[rows, LANES:]
            sides_row = choose_side(
                lanes_of(count),
                turn(high, LANES - HALO, target),
                turn(east[packed_rows], source, target + HALO),
                turn(west[packed_rows], source, target + 3 * HALO - count),
                turn(low, 0, target + 3 * HALO),
            )
            strips.append((low, high, sides_row))
        for c in range(3):
            top, bottom = strips[0][c], strips[1][c]
            first_pair[c, first : first + count, :] = jnp.where(even, bottom, top)
            second_pair[c, first : first + count, :] = jnp.where(even, top, bottom)


def shift_east(tiles, lane):
    rolled = [pltpu.roll(t, LANES - 1, 1) for t in tiles]
    if len(tiles) == 1:
        return rolled
    return [jnp.where(lane == LANES - 1, rolled[1 - c], rolled[c]) for c in range(2)]


def shift_west(tiles, lane):
    rolled = [pltpu.roll(t, 1, 1) for t in tiles]
    if len(tiles) == 1:
        return rolled
    return [jnp.where(lane == 0, rolled[1 - c], rolled[c]) for c in range(2)]


def over_rows(framed, body):
    start = MARGIN if framed else TOP
    wide = 2 * HALO if framed else 0
    main, side = (TILE + wide) // BLOCKS, (HALF + wide) // BLOCKS

    def block(i, carry):
        row = pl.multiple_of(start + i * main, 8)
        side_row = pl.multiple_of(start + i * side, 8)
        for g in range(0, main, GROUP):
            body(MAIN, row + g)
            if g < side:
                body(SIDES, side_row + g)
        return carry

    lax.fori_loop(0, BLOCKS, block, 0)


def join_parts(ref, leads, whole):
    edge = HALO // 2

    def join(row, upper, lower, count):
        lane = lanes_of(count)
        for lead in leads:
            def at(tile_row):
                return (*lead, pl.ds(tile_row, count), slice(None))

            mixed = ref[at(SIDE + row)]
            if whole:
                place = lane % BAND
                upper_lane = lane < BAND
                from_high = jnp.where(
                    upper_lane,
                    turn(ref[at(ROWS + row)], LANES - HALO, 0),
                    turn(ref[at(ROWS + row + HALF)], LANES - HALO, BAND),
                )
                from_low = jnp.where(
                    upper_lane,
                    turn(ref[at(row)], edge, BAND - edge),
                    turn(ref[at(row + HALF)], edge, LANES - edge),
                )
                ref[at(SIDE + row)] = jnp.where(
                    place < edge, from_high, jnp.where(place >= BAND - edge, from_low, mixed)
                )
            for wanted, band, main_row in ((upper, 0, row), (lower, BAND, row + HALF)):
                if wanted:
                    low = turn(mixed, band + 3 * HALO, 0)
                    high = turn(mixed, band + edge, LANES - edge)
                    ref[at(main_row)] = jnp.where(lane < edge, low, ref[at(main_row)])
                    ref[at(ROWS + main_row)] = jnp.where(lane >= LANES - edge, high, ref[at(ROWS + main_row)])

    step = 32

    def middle(i, carry):
        join(pl.multiple_of(TOP + i * step, 8), True, True, step)
        return carry

    lax.fori_loop(0, HALF // step, middle, 0)
    if whole:
        join(MARGIN, True, False, HALO)
        join(TOP + HALF, False, True, HALO)


def model_kernel(
    ice_mask, patches, thick, drive, obs, first_row, second_row, first_col, second_col,
    vel_u, vel_v, sums,
    ext, fr, ice, visc, vel, coef, small, sems,
):
    tile_cols, tile_rows = ice_mask.shape
    row_tile = lax.axis_index("gy")
    col_tile = lax.axis_index("gx")

    cells = 0.5 * jnp.exp(sum(patches[j] for j in range(tile_rows)))
    lane = lanes_of(PATCH)
    for c in range(2):
        wide = jnp.take_along_axis(cells, 32 * c + lane // 4, axis=1)
        for j in range(4):
            fr[pl.ds(MAIN[c] + MARGIN + j, PATCH, stride=4), :] = wide
    lane = lanes_of(40)
    place = lane % BAND // 4
    source = jnp.where(place < 8, 60 + place, (116 + place) % LANES)
    wide = jnp.where(
        lane < BAND,
        jnp.take_along_axis(cells[:40], source, axis=1),
        jnp.take_along_axis(cells[PATCH - 40 :], source, axis=1),
    )
    for j in range(4):
        fr[pl.ds(SIDE + MARGIN + j, 40, stride=4), :] = wide

    west, east = sides("gx", first_col[...], second_col[...])
    even = is_even("gy")
    lane = lanes_of(HALF)
    upper = lane < BAND
    for f, (field, (first, count)) in enumerate(zip((thick, drive.at[0], drive.at[1], obs.at[0], obs.at[1]), STRIP)):
        scale = 0.5 if f in (1, 2) else 1.0
        frames = []
        for c in range(3):
            one, two = scale * first_row[c, first : first + count, :], scale * second_row[c, first : first + count, :]
            frames.append((jnp.where(even, two, one), jnp.where(even, one, two)))
        for c in range(2):
            ext[f, MAIN[c] + TOP : MAIN[c] + TOP + TILE, :] = scale * field[:, c * LANES : (c + 1) * LANES]
            ext[f, MAIN[c] + TOP - count : MAIN[c] + TOP, :] = frames[c][0]
            ext[f, MAIN[c] + TOP + TILE : MAIN[c] + TOP + TILE + count, :] = frames[c][1]
        halves = (slice(0, HALF), slice(HALF, TILE))
        high = [turn(field[halves[b], LANES:], LANES - HALO, BAND * b) for b in range(2)]
        low = [turn(field[halves[b], :LANES], 0, BAND * b + 3 * HALO) for b in range(2)]
        here = SIDE + TOP
        ext[f, here : here + HALF, :] = scale * choose_side(
            lane,
            jnp.where(upper, high[0], high[1]),
            turn(east, first, HALO),
            turn(west, first, 3 * HALO - count),
            jnp.where(upper, low[0], low[1]),
        )
        upper_few = lanes_of(count) < BAND
        above = turn(ext[f, here + HALF - count : here + HALF, :], 0, BAND)
        below = turn(ext[f, here : here + count, :], 0, BAND)
        ext[f, here - count : here, :] = jnp.where(upper_few, frames[2][0], above)
        ext[f, here + HALF : here + HALF + count, :] = jnp.where(upper_few, below, frames[2][1])

    side_ice = []
    for dr, first, count in ((-1, MARGIN, HALO), (0, TOP, TILE), (1, TOP + TILE, HALO)):
        masks = []
        for ds in (-1, 0, 1):
            row, col = row_tile + dr, col_tile + ds
            inside = (row >= 0) & (row < tile_rows) & (col >= 0) & (col < tile_cols)
            row = jnp.clip(row, 0, tile_rows - 1)
            col = jnp.clip(col, 0, tile_cols - 1)
            masks.append(jnp.where(inside, ice_mask[col, row], 0).astype(jnp.float32))
        for c in range(2):
            ice[MAIN[c] + first : MAIN[c] + first + count, :] = jnp.full((count, LANES), masks[1])
        side_ice.append(choose_side(lanes_of(HALO), masks[1], masks[2], masks[0], masks[1]))
    upper = lanes_of(HALO) < BAND
    for i in range(HALF // HALO):
        ice[SIDE + TOP + i * HALO : SIDE + TOP + (i + 1) * HALO, :] = side_ice[1]
    ice[SIDE + MARGIN : SIDE + TOP, :] = jnp.where(upper, side_ice[0], side_ice[1])
    ice[SIDE + TOP + HALF : SIDE + TOP + HALF + HALO, :] = jnp.where(upper, side_ice[1], side_ice[2])

    lane = lanes_of(GROUP)

    def load(ref, part, row, *lead):
        return [ref[(*lead, pl.ds(row + tile, GROUP), slice(None))] for tile in part]

    def store(ref, part, row, values, *lead):
        for tile, value in zip(part, values):
            ref[(*lead, pl.ds(row + tile, GROUP), slice(None))] = value

    def load_around(part, row, now):
        return [load(vel, part, r, now, i) for i in range(2) for r in (row, row - 1, row + 1)]

    def first_viscosity(part, row):
        store(visc, part, row, [0.25 * visc_scale * strain_floor ** (-1.0 / 3.0) * t for t in load(ext, part, row, 0)])

    def viscosity(part, row):
        thickness = load(ext, part, row, 0)
        u, u_n, u_s, v, v_n, v_s = load_around(part, row, 1)
        u_e, u_w = shift_east(u, lane), shift_west(u, lane)
        v_e, v_w = shift_east(v, lane), shift_west(v, lane)
        result = []
        for c in range(len(part)):
            ux, vx = u_e[c] - u_w[c], v_e[c] - v_w[c]
            uy, vy = u_s[c] - u_n[c], v_s[c] - v_n[c]
            shear = uy + vx
            strain = 0.25 * (ux * (ux + vy) + vy * vy) + (0.0625 * (shear * shear) + strain_floor)
            result.append((0.25 * visc_scale) * thickness[c] * jnp.exp(jnp.log(strain) * (-1.0 / 3.0)))
        store(visc, part, row, result)

    def inverse(x):
        near = pl.reciprocal(x, approx=True)
        return near * (2.0 - x * near)

    def coefficients(part, row):
        tiles = range(len(part))
        q, q_n, q_s = load(visc, part, row), load(visc, part, row - 1), load(visc, part, row + 1)
        q_w = shift_west(q, lane)
        w = [q[c] + q_w[c] for c in tiles]
        e = shift_east(w, lane)
        s = [q[c] + q_s[c] for c in tiles]
        n = [q[c] + q_n[c] for c in tiles]
        friction, mask = load(fr, part, row), load(ice, part, row)
        scale_u, scale_v = [], []
        for c in tiles:
            across, along = e[c] + w[c], s[c] + n[c]
            scale_u.append(mask[c] * inverse(friction[c] + along + 4.0 * across))
            scale_v.append(mask[c] * inverse(friction[c] + across + 4.0 * along))
        corners = []
        half = [0.5 * q[c] for c in tiles]
        for shifted in (
            shift_west(q_s, lane), shift_west(q_n, lane), shift_east(q_s, lane), shift_east(q_n, lane),
        ):
            corners.append([q[c] + 0.5 * shifted[c] for c in tiles])
            corners.append([half[c] + shifted[c] for c in tiles])
        k = [e, w, s, n, scale_u, scale_v] + corners
        for i, values in enumerate(k):
            store(coef, part, row, values, i)
        return k

    def relax(part, row, k, now, new):
        tiles = range(len(part))
        e, w, s, n, scale_u, scale_v, sw_u, sw_v, nw_u, nw_v, se_u, se_v, ne_u, ne_v = k
        u, u_n, u_s, v, v_n, v_s = load_around(part, row, now)
        to_west_u, to_east_u, to_west_v, to_east_v = [], [], [], []
        for c in tiles:
            u4 = 4.0 * u[c]
            to_west_u.append(w[c] * u4 + (sw_u[c] * v_s[c] - nw_u[c] * v_n[c]))
            to_east_u.append(e[c] * u4 + (ne_u[c] * v_n[c] - se_u[c] * v_s[c]))
            to_west_v.append(w[c] * v[c] + (sw_v[c] * u_s[c] - nw_v[c] * u_n[c]))
            to_east_v.append(e[c] * v[c] + (ne_v[c] * u_n[c] - se_v[c] * u_s[c]))
        to_west_u, to_west_v = shift_east(to_west_u, lane), shift_east(to_west_v, lane)
        to_east_u, to_east_v = shift_west(to_east_u, lane), shift_west(to_east_v, lane)
        right_u, right_v = load(ext, part, row, 1), load(ext, part, row, 2)
        new_u, new_v = [], []
        for c in tiles:
            mid_u = s[c] * u_s[c] + n[c] * u_n[c]
            mid_v = 4.0 * (s[c] * v_s[c] + n[c] * v_n[c])
            new_u.append(scale_u[c] * (right_u[c] + mid_u + (to_west_u[c] + to_east_u[c])))
            new_v.append(scale_v[c] * (right_v[c] + mid_v + (to_west_v[c] + to_east_v[c])))
        store(vel, part, row, new_u, new, 0)
        store(vel, part, row, new_v, new, 1)

    def sweep(framed, now, new):
        over_rows(framed, lambda part, row: relax(part, row, [load(coef, part, row, i) for i in range(14)], now, new))

    def first_start(part, row):
        k = coefficients(part, row)
        for i in range(2):
            right = load(ext, part, row, 1 + i)
            store(vel, part, row, [a * b for a, b in zip(k[4 + i], right)], 0, i)

    over_rows(True, first_viscosity)
    over_rows(True, first_start)
    sweep(True, 0, 1)

    def iteration(i, carry):
        @pl.when(i == PIC - 1)
        def _():
            join_parts(vel, ((1, 0), (1, 1)), True)

        over_rows(True, viscosity)
        over_rows(True, lambda part, row: relax(part, row, coefficients(part, row), 1, 0))
        sweep(True, 0, 1)
        return carry

    lax.fori_loop(1, PIC, iteration, 0)
    join_parts(vel, ((1, 0), (1, 1)), False)
    copies = []
    for i, out in enumerate((vel_u, vel_v)):
        for c in range(2):
            copies.append(
                pltpu.make_async_copy(
                    vel.at[1, i, MAIN[c] + TOP : MAIN[c] + TOP + TILE, :],
                    out.at[:, c * LANES : (c + 1) * LANES],
                    sems.at[2 * i + c],
                )
            )
            copies[-1].start()

    def first_adjoint(part, row):
        for i in range(2):
            u, seen, scale = load(vel, part, row, 1, i), load(ext, part, row, 3 + i), load(coef, part, row, 4 + i)
            misfit = [0.5 * (a - b) for a, b in zip(u, seen)]
            store(ext, part, row, misfit, 1 + i)
            store(vel, part, row, [a * b for a, b in zip(scale, misfit)], 2, i)

    over_rows(True, first_adjoint)

    def two_sweeps(i, carry):
        sweep(True, 2, 0)
        sweep(True, 0, 2)
        return carry

    lax.fori_loop(0, (ADJ - 2) // 2, two_sweeps, 0)
    sweep(False, 2, 0)

    def gradient(part, row):
        u, v, lu, lv = (load(vel, part, row, j, i) for j in (1, 0) for i in range(2))
        friction = load(fr, part, row)
        store(visc, part, row, [-2.0 * friction[c] * (u[c] * lu[c] + v[c] * lv[c]) for c in range(len(part))])

    over_rows(False, gradient)
    join_parts(visc, ((),), False)
    down = [sum(visc[pl.ds(MAIN[c] + TOP + j, CT, stride=4), :] for j in range(4)) for c in range(2)]
    k = lax.broadcasted_iota(jnp.int32, (LANES, LANES), 0)
    l = lanes_of(LANES) % CT
    total = jnp.zeros((CT, LANES), jnp.float32)
    for c in range(2):
        total += jnp.dot(
            down[c],
            (k // 4 + 32 * c == l).astype(jnp.float32),
            precision=lax.Precision.HIGHEST,
            preferred_element_type=jnp.float32,
        )
    small[...] = total
    packed = jnp.where(
        lanes_of(PACK) < CT, small[pl.ds(0, PACK, stride=2), :], small[pl.ds(1, PACK, stride=2), :]
    )
    part = PACK // sums.shape[0]
    for i in range(sums.shape[0]):
        for j in range(sums.shape[1]):
            sums[i, j] = packed[i * part : (i + 1) * part]
    for copy in copies:
        copy.wait()


def pick_kernel(tile_block, gathered, out):
    owned = out.shape[1]
    first = lax.axis_index("gy") * owned
    tile_cols, tile_rows = tile_block.shape
    total = [jnp.zeros(out.shape[2:], jnp.float32) for _ in range(owned)]
    for t in range(tile_cols * tile_rows):
        place = tile_block[t // tile_rows, t % tile_rows] - first
        cells = gathered[t]
        total = [total[b] + jnp.where(place == b, cells, 0.0) for b in range(owned)]
    for b in range(owned):
        for j in range(out.shape[0]):
            out[j, b] = total[b]


def join_kernel(parts, out):
    share = parts.shape[2]
    for i in range(parts.shape[0]):
        for j in range(share):
            at = (i * share + j) * LANES
            out[:, at : at + LANES] = parts[i, :, j, :]


def in_vmem(count):
    return [pl.BlockSpec(memory_space=pltpu.VMEM)] * count


def in_smem(count):
    return [pl.BlockSpec(memory_space=pltpu.SMEM)] * count


def per_device(thickness, driving, observed, control, ice_mask, tile_block):
    f32 = jnp.float32
    rows, cols = lax.axis_size("gy"), lax.axis_size("gx")
    tile_block, ice_mask = tile_block[:, :, 0].T, ice_mask.T
    params = pltpu.CompilerParams(vmem_limit_bytes=VMEM_LIMIT)

    def shape(*sizes):
        return jax.ShapeDtypeStruct(sizes, f32)

    def swap(axis, cells_first, cells_second):
        count = lax.axis_size(axis)
        received = []
        for cells, low in ((cells_second, 1), (cells_first, 0)):
            pairs = [(i, i + 1) for i in range(low, count - 1, 2)]
            received.append(lax.ppermute(cells, axis, pairs + [(j, i) for i, j in pairs]))
        return received[1], received[0]

    fields = thickness, driving, observed
    columns = pl.pallas_call(
        columns_kernel,
        out_shape=[shape(HALF, LANES)] * 2,
        in_specs=[pl.BlockSpec(memory_space=pltpu.HBM)] * 3,
        out_specs=in_vmem(2),
        scratch_shapes=[pltpu.VMEM((5, TILE, TILE), f32), pltpu.SemaphoreType.DMA((5,))],
        compiler_params=pltpu.CompilerParams(vmem_limit_bytes=PACK_VMEM_LIMIT),
        name="columns",
    )(*fields)
    columns_in = swap("gx", *columns)
    patches = pl.pallas_call(
        patches_kernel,
        out_shape=shape(rows, PATCH, LANES),
        in_specs=in_smem(1) + in_vmem(1),
        out_specs=pl.BlockSpec(memory_space=pltpu.VMEM),
        scratch_shapes=[pltpu.VMEM((control.shape[0], PACK, LANES), f32)],
        compiler_params=params,
        name="patches",
    )(tile_block, control)
    patches = lax.all_to_all(patches, "gy", 0, 0, tiled=True)
    strips = pl.pallas_call(
        rows_kernel,
        out_shape=[shape(3, 64, LANES)] * 2,
        in_specs=in_vmem(5),
        out_specs=in_vmem(2),
        compiler_params=params,
        name="rows",
    )(*fields, *columns_in)
    rows_in = swap("gy", *strips)

    vel_u, vel_v, sums = pl.pallas_call(
        model_kernel,
        out_shape=(shape(TILE, TILE), shape(TILE, TILE), shape(cols, rows, PACK // cols, LANES)),
        in_specs=in_smem(1) + in_vmem(8),
        out_specs=[pl.BlockSpec(memory_space=pltpu.HBM)] * 2 + in_vmem(1),
        scratch_shapes=[
            pltpu.VMEM((5, ALL_ROWS, LANES), f32),
            pltpu.VMEM((ALL_ROWS, LANES), f32),
            pltpu.VMEM((ALL_ROWS, LANES), f32),
            pltpu.VMEM((ALL_ROWS, LANES), f32),
            pltpu.VMEM((3, 2, ALL_ROWS, LANES), f32),
            pltpu.VMEM((14, ALL_ROWS, LANES), f32),
            pltpu.VMEM((CT, LANES), f32),
            pltpu.SemaphoreType.DMA((4,)),
        ],
        compiler_params=params,
        name="model",
    )(ice_mask, patches, *fields, *rows_in, *columns_in)

    share = (control.shape[0], PACK // cols, LANES)
    sums = lax.all_to_all(sums.reshape(cols * rows, *share[1:]), ("gx", "gy"), 0, 0, tiled=True)
    parts = pl.pallas_call(
        pick_kernel,
        out_shape=shape(cols, *share),
        in_specs=in_smem(1) + in_vmem(1),
        out_specs=pl.BlockSpec(memory_space=pltpu.VMEM),
        compiler_params=params,
        name="pick",
    )(tile_block, sums)
    gradient = pl.pallas_call(
        join_kernel,
        out_shape=shape(*control.shape),
        in_specs=in_vmem(1),
        out_specs=pl.BlockSpec(memory_space=pltpu.VMEM),
        compiler_params=params,
        name="join",
    )(lax.all_to_all(parts, "gx", 0, 0, tiled=True))
    return vel_u, vel_v, gradient


def solution(mesh):
    return jax.shard_map(
        per_device,
        mesh=mesh,
        in_specs=(P("gy", "gx"), P(None, "gy", "gx"), P(None, "gy", "gx"), P("gy", None), P(), P()),
        out_specs=(P("gy", "gx"), P("gy", "gx"), P("gy", None)),
        check_vma=False,
    )
```

time: 71.5 us -> 102 us (1.43)
  Pallas kernels: 29.8 us -> 58.6 us
  blocking collectives: 25.8 us -> 30.2 us
  starting transfers between devices: 10.8 us -> 8.2 us
    pallas_call x1, Pallas kernels: 22.4 us -> 52.7 us  [per_device(): pl.pallas_call(model_kernel, out_shape=(shape(TILE, TILE), shape(TILE, TI...]
    all_to_all x1, blocking collectives: 17.7 us -> 22 us  [per_device(): lax.all_to_all(sums.reshape(cols * rows, *share[1:]), ('gx', 'gy'), 0, 0,...]
    ppermute x4, starting transfers between devices: 5.96 us -> 3.28 us  [swap(): lax.ppermute(cells, axis, pairs + [(j, i) for i, j in pairs])]
  transfers between devices with their start and end apart: 5 -> 5, of which waited for: 2 -> 2; matrix products, arithmetic and copies ran while one was open for 0% -> 0% of each run, Pallas kernels for 0% -> 2%
where the time goes in v4:
time: 102 us
  Pallas kernels  58.6 us (57%)
  blocking collectives  30.2 us (30%)
  starting transfers between devices  8.2 us (8%)
  waiting for transfers between devices  2.92 us (3%)
  local copies, waits for them, and re-layouts  1.54 us (2%)
    pallas_call x1, Pallas kernels, per_device(): pl.pallas_call(model_kernel, out_shape=(shape(TILE, TILE), shape(TILE, TI...  52.7 us
    all_to_all x1, blocking collectives, per_device(): lax.all_to_all(sums.reshape(cols * rows, *share[1:]), ('gx', 'gy'), 0, 0,...  22 us
    all_to_all x1, blocking collectives, per_device(): lax.all_to_all(parts, 'gx', 0, 0, tiled=True)  8.15 us
    all_to_all x1, starting transfers between devices, per_device(): patches = lax.all_to_all(patches, 'gy', 0, 0, tiled=True)  4.92 us
    ppermute x4, starting transfers between devices, swap(): lax.ppermute(cells, axis, pairs + [(j, i) for i, j in pairs])  3.28 us
    ppermute x4, waiting for transfers between devices, swap(): lax.ppermute(cells, axis, pairs + [(j, i) for i, j in pairs])  2.92 us
    pallas_call x1, Pallas kernels, per_device(): pl.pallas_call(columns_kernel, out_shape=[shape(HALF, LANES)] * 2, in_spe...  2.39 us
  transfers between devices with their start and end apart: 5, of which 2 were waited for; matrix products, arithmetic and copies ran while one was open for 0% of the time, Pallas kernels for 2%

profile of v4, /device:TPU:0, one launch (start us, length us, event | category | flops | bytes accessed | tf_op | source)
XLA Modules:
  0.0 102.2 jit_solution(12245071848432827073)
XLA Ops:
  0.6 0.0 copy-start.3
  0.6 0.8 copy-done.3
  1.5 0.0 copy-start.4
  1.5 0.7 copy-done.4
  2.2 2.0 %patches.1 = f32[8,72,128]{2,1,0:T(8,128)} custom-call(s32[4,8]{1,0:T(4,128)S(1)} %bitcast.6, f32[4,4096]{1,0:T(4,128)S(1)} %copy-done.3), custom_call_target="tpu_custom_call" | custom-call | tf_op jit(solution)/shard_map/patches/pallas_call | solution.py:525
  4.1 4.9 %all-to-all-start = ((f32[8,72,128]{2,1,0:T(8,128)}), f32[8,72,128]{2,1,0:T(8,128)S(1)}, u32[]{:S(2)}, u32[]{:S(2)}) async-start(f32[8,72,128]{2,1,0:T(8,128)} %patches.1), calls=%async_computation | async-start | bytes 589824 | tf_op jit(solution)/shard_map/all_to_all | solution.py:534
  9.0 0.0 copy-start
  9.0 0.0 copy-start.1
  9.1 0.0 copy-start.2
  9.1 2.4 %columns.1 = (f32[128,128]{1,0:T(8,128)}, f32[128,128]{1,0:T(8,128)}) custom-call(f32[256,256]{1,0:T(8,128)} %thick.5, f32[2,256,256]{2,1,0:T(8,128)} %drive.5, f32[2,256,256]{2,1,0:T(8,128)} %obs.5), custom_call_target="tpu_custom_call" | custom-call | tf_op jit(solution)/shard_map/columns/pallas_call | solution.py:515
  11.5 1.9 %collective-permute-start = (f32[128,128]{1,0:T(8,128)}, f32[128,128]{1,0:T(8,128)S(1)}, u32[]{:S(2)}, u32[]{:S(2)}) collective-permute-start(f32[128,128]{1,0:T(8,128)} %get-tuple-element.10), channel_id=1, source_target_pairs={{0,8},{16,24},{8,0},{24,16},{1,9},{17,25},{9,1},{25,17},{2,10},{18... | collective-permute-start | bytes 196616 | tf_op jit(solution)/shard_map/ppermute | solution.py:511
  13.4 0.7 collective-permute-start.1
  14.0 2.3 %collective-permute-done.first_col = f32[128,128]{1,0:T(8,128)S(1)} collective-permute-done((f32[128,128]{1,0:T(8,128)}, f32[128,128]{1,0:T(8,128)S(1)}, u32[]{:S(2)}, u32[]{:S(2)}) %collective-permute-start) | collective-permute-done | bytes 65568 | tf_op jit(solution)/shard_map/ppermute | solution.py:511
  16.3 0.0 collective-permute-done.1.second_col
  16.3 0.0 copy-done
  16.3 0.0 copy-done.1
  16.3 0.0 copy-done.2
  16.3 0.1 rows.1
  16.5 0.0 copy-start.6
  16.5 0.1 collective-permute-start.2
  16.6 0.7 collective-permute-start.3
  17.3 0.6 collective-permute-done.2.first_row
  17.9 0.0 collective-permute-done.3.second_row
  17.9 0.0 all-to-all-done.patches
  17.9 0.0 copy-done.6
  17.9 52.7 %model.1 = (f32[256,256]{1,0:T(8,128)}, f32[256,256]{1,0:T(8,128)}, f32[4,8,8,128]{3,2,1,0:T(8,128)S(1)}) custom-call(s32[4,8]{1,0:T(4,128)S(1)} %bitcast.8, f32[8,72,128]{2,1,0:T(8,128)S(1)} %all-to-all-done.patches, f32[256,256]{1,0:T(8,128)S(1)} %copy-done.2, f32[2,256,256]{2,1,0:T(8,128)S(1)} %copy-done, f32[2,256,256]{2,1,0:T(8,128)S(1)} %copy-done.1, ...), custom_call_target="tpu_custom_call" | custom-call | tf_op jit(solution)/shard_map/model/pallas_call | solution.py:545
  70.6 0.0 copy-start.5
  70.6 22.0 %all_to_all.15.gathered = f32[32,8,128]{2,1,0:T(8,128)S(1)} all-to-all(f32[32,8,128]{2,1,0:T(8,128)S(1)} %bitcast.5), channel_id=1, replica_groups=mesh['gx'=4,'gy'=8] {'gx','gy'}, dimensions={0} | all-to-all | bytes 262144 | tf_op jit(solution)/shard_map/all_to_all | solution.py:565
  92.7 0.0 copy-done.5
  92.7 0.7 pick.1
  93.4 8.1 %all_to_all.16.parts = f32[4,4,8,128]{3,2,1,0:T(8,128)S(1)} all-to-all(f32[4,4,8,128]{3,2,1,0:T(8,128)S(1)} %pick.1), channel_id=1, replica_groups=mesh['gx'=4,'gy'=8] {'gx'}, dimensions={0} | all-to-all | bytes 131072 | tf_op jit(solution)/shard_map/all_to_all | solution.py:581
  101.5 0.7 join.1
Async XLA Ops:
  0.6 0.8 copy-start.3
  1.5 0.7 copy-start.4
  4.1 13.7 %all-to-all-start = ((f32[8,72,128]{2,1,0:T(8,128)}), f32[8,72,128]{2,1,0:T(8,128)S(1)}, u32[]{:S(2)}, u32[]{:S(2)}) async-start(f32[8,72,128]{2,1,0:T(8,128)} %patches.1), calls=%async_computation | async-start | bytes 589824 | tf_op jit(solution)/shard_map/all_to_all | solution.py:534
  9.0 7.3 %copy-start = (f32[2,256,256]{2,1,0:T(8,128)S(1)}, f32[2,256,256]{2,1,0:T(8,128)}, u32[]{:S(2)}) copy-start(f32[2,256,256]{2,1,0:T(8,128)} %drive.5) | copy-start | bytes 1572868
  9.0 7.3 %copy-start.1 = (f32[2,256,256]{2,1,0:T(8,128)S(1)}, f32[2,256,256]{2,1,0:T(8,128)}, u32[]{:S(2)}) copy-start(f32[2,256,256]{2,1,0:T(8,128)} %obs.5) | copy-start | bytes 1572868
  9.1 7.3 %copy-start.2 = (f32[256,256]{1,0:T(8,128)S(1)}, f32[256,256]{1,0:T(8,128)}, u32[]{:S(2)}) copy-start(f32[256,256]{1,0:T(8,128)} %thick.5) | copy-start | bytes 786436
  11.5 4.8 %collective-permute-start = (f32[128,128]{1,0:T(8,128)}, f32[128,128]{1,0:T(8,128)S(1)}, u32[]{:S(2)}, u32[]{:S(2)}) collective-permute-start(f32[128,128]{1,0:T(8,128)} %get-tuple-element.10), channel_id=1, source_target_pairs={{0,8},{16,24},{8,0},{24,16},{1,9},{17,25},{9,1},{25,17},{2,10},{18... | collective-permute-start | bytes 196616 | tf_op jit(solution)/shard_map/ppermute | solution.py:511
  13.4 3.0 %collective-permute-start.1 = (f32[128,128]{1,0:T(8,128)}, f32[128,128]{1,0:T(8,128)S(1)}, u32[]{:S(2)}, u32[]{:S(2)}) collective-permute-start(f32[128,128]{1,0:T(8,128)} %get-tuple-element.11), channel_id=1, source_target_pairs={{8,16},{16,8},{9,17},{17,9},{10,18},{18,10},{11,19},{19,11},{12,20... | collective-permute-start | bytes 196616 | tf_op jit(solution)/shard_map/ppermute | solution.py:511
  16.5 1.4 %copy-start.6 = (s32[8,4]{0,1:T(4,128)S(1)}, s32[8,4]{0,1:T(4,128)}, u32[]{:S(2)}) copy-start(s32[8,4]{0,1:T(4,128)} %param.10) | copy-start | bytes 388
  16.5 1.4 %collective-permute-start.2 = (f32[3,64,128]{2,1,0:T(8,128)S(1)}, f32[3,64,128]{2,1,0:T(8,128)S(1)}, u32[]{:S(2)}, u32[]{:S(2)}) collective-permute-start(f32[3,64,128]{2,1,0:T(8,128)S(1)} %get-tuple-element.12), channel_id=1, source_target_pairs={{0,1},{2,3},{4,5},{6,7},{1,0},{3,2},{5,4},{7,6},{8,9},{10,11},{12,... | collective-permute-start | bytes 294920 | tf_op jit(solution)/shard_map/ppermute | solution.py:511
  16.6 1.3 %collective-permute-start.3 = (f32[3,64,128]{2,1,0:T(8,128)S(1)}, f32[3,64,128]{2,1,0:T(8,128)S(1)}, u32[]{:S(2)}, u32[]{:S(2)}) collective-permute-start(f32[3,64,128]{2,1,0:T(8,128)S(1)} %get-tuple-element.13), channel_id=1, source_target_pairs={{1,2},{3,4},{5,6},{2,1},{4,3},{6,5},{9,10},{11,12},{13,14},{10,9},... | collective-permute-start | bytes 294920 | tf_op jit(solution)/shard_map/ppermute | solution.py:511
  70.6 22.1 %copy-start.5 = (s32[8,4,1]{0,2,1:T(1,128)S(1)}, s32[8,4,1]{0,2,1:T(1,128)}, u32[]{:S(2)}) copy-start(s32[8,4,1]{0,2,1:T(1,128)} %param.11) | copy-start | bytes 388

commit v5 on v4

--- a/solution.py
+++ b/solution.py
@@ -24,8 +24,8 @@
 ALL_ROWS = SIDE + HALF + 2 * TOP
 MAIN = (0, ROWS)
 SIDES = (SIDE,)
-GROUP = 8
 BLOCKS = 4
+AHEAD = 2
 PACK = COARSE // LANES
 VMEM_LIMIT = 40 * 1024 * 1024
 PACK_VMEM_LIMIT = 62 * 1024 * 1024
@@ -161,18 +161,25 @@
     return [jnp.where(lane == 0, rolled[1 - c], rolled[c]) for c in range(2)]
 
 
-def over_rows(framed, body):
+def over_rows(framed, read, work):
     start = MARGIN if framed else TOP
     wide = 2 * HALO if framed else 0
     main, side = (TILE + wide) // BLOCKS, (HALF + wide) // BLOCKS
+    step = 24 if framed else 32
+    groups = [(MAIN, g, step) for g in range(0, main, step)]
+    groups[1:1] = [(SIDES, 0, 16)]
+    groups[3:3] = [(SIDES, 16, side - 16)]
 
     def block(i, carry):
-        row = pl.multiple_of(start + i * main, 8)
-        side_row = pl.multiple_of(start + i * side, 8)
-        for g in range(0, main, GROUP):
-            body(MAIN, row + g)
-            if g < side:
-                body(SIDES, side_row + g)
+        first = {MAIN: pl.multiple_of(start + i * main, 8), SIDES: pl.multiple_of(start + i * side, 8)}
+        rows = [(part, first[part] + g, count) for part, g, count in groups]
+        pending = [read(*group) for group in rows[:AHEAD]]
+        for k, (part, row, count) in enumerate(rows):
+            if k + AHEAD < len(rows):
+                pending.append(read(*rows[k + AHEAD]))
+            for ref, lead, values in work(part, pending[k], lanes_of(count)):
+                for tile, value in zip(part, values):
+                    ref[(*lead, pl.ds(row + tile, count), slice(None))] = value
         return carry
 
     lax.fori_loop(0, BLOCKS, block, 0)
@@ -226,7 +233,7 @@
 def model_kernel(
     ice_mask, patches, thick, drive, obs, first_row, second_row, first_col, second_col,
     vel_u, vel_v, sums,
-    ext, fr, ice, visc, vel, coef, small, sems,
+    ext, fr, ice, visc, vel_a, vel_b, vel_c, coef, small, sems,
 ):
     tile_cols, tile_rows = ice_mask.shape
     row_tile = lax.axis_index("gy")
@@ -298,24 +305,27 @@
     ice[SIDE + MARGIN : SIDE + TOP, :] = jnp.where(upper, side_ice[0], side_ice[1])
     ice[SIDE + TOP + HALF : SIDE + TOP + HALF + HALO, :] = jnp.where(upper, side_ice[1], side_ice[2])
 
-    lane = lanes_of(GROUP)
-
-    def load(ref, part, row, *lead):
-        return [ref[(*lead, pl.ds(row + tile, GROUP), slice(None))] for tile in part]
-
-    def store(ref, part, row, values, *lead):
-        for tile, value in zip(part, values):
-            ref[(*lead, pl.ds(row + tile, GROUP), slice(None))] = value
-
-    def load_around(part, row, now):
-        return [load(vel, part, r, now, i) for i in range(2) for r in (row, row - 1, row + 1)]
-
-    def first_viscosity(part, row):
-        store(visc, part, row, [0.25 * visc_scale * strain_floor ** (-1.0 / 3.0) * t for t in load(ext, part, row, 0)])
-
-    def viscosity(part, row):
-        thickness = load(ext, part, row, 0)
-        u, u_n, u_s, v, v_n, v_s = load_around(part, row, 1)
+    def load(ref, part, row, count, *lead):
+        return [ref[(*lead, pl.ds(row + tile, count), slice(None))] for tile in part]
+
+    def load_around(part, row, count, now):
+        return [load(now, part, r, count, i) for i in range(2) for r in (row, row - 1, row + 1)]
+
+    def load_right(part, row, count):
+        return [load(ext, part, row, count, i) for i in (1, 2)]
+
+    def read_thickness(part, row, count):
+        return load(ext, part, row, count, 0)
+
+    def first_viscosity(part, thickness, lane):
+        factor = 0.25 * visc_scale * strain_floor ** (-1.0 / 3.0)
+        return [(visc, (), [factor * t for t in thickness])]
+
+    def read_viscosity(part, row, count):
+        return read_thickness(part, row, count), load_around(part, row, count, vel_b)
+
+    def viscosity(part, read, lane):
+        thickness, (u, u_n, u_s, v, v_n, v_s) = read
         u_e, u_w = shift_east(u, lane), shift_west(u, lane)
         v_e, v_w = shift_east(v, lane), shift_west(v, lane)
         result = []
@@ -325,21 +335,24 @@
             shear = uy + vx
             strain = 0.25 * (ux * (ux + vy) + vy * vy) + (0.0625 * (shear * shear) + strain_floor)
             result.append((0.25 * visc_scale) * thickness[c] * jnp.exp(jnp.log(strain) * (-1.0 / 3.0)))
-        store(visc, part, row, result)
+        return [(visc, (), result)]
 
     def inverse(x):
         near = pl.reciprocal(x, approx=True)
         return near * (2.0 - x * near)
 
-    def coefficients(part, row):
+    def read_coefficients(part, row, count):
+        around = [load(visc, part, r, count) for r in (row, row - 1, row + 1)]
+        return around + [load(fr, part, row, count), load(ice, part, row, count)]
+
+    def coefficients(part, read, lane):
         tiles = range(len(part))
-        q, q_n, q_s = load(visc, part, row), load(visc, part, row - 1), load(visc, part, row + 1)
+        q, q_n, q_s, friction, mask = read
         q_w = shift_west(q, lane)
         w = [q[c] + q_w[c] for c in tiles]
         e = shift_east(w, lane)
         s = [q[c] + q_s[c] for c in tiles]
         n = [q[c] + q_n[c] for c in tiles]
-        friction, mask = load(fr, part, row), load(ice, part, row)
         scale_u, scale_v = [], []
         for c in tiles:
             across, along = e[c] + w[c], s[c] + n[c]
@@ -352,15 +365,12 @@
         ):
             corners.append([q[c] + 0.5 * shifted[c] for c in tiles])
             corners.append([half[c] + shifted[c] for c in tiles])
-        k = [e, w, s, n, scale_u, scale_v] + corners
-        for i, values in enumerate(k):
-            store(coef, part, row, values, i)
-        return k
-
-    def relax(part, row, k, now, new):
+        return [e, w, s, n, scale_u, scale_v] + corners
+
+    def relax(part, k, around, right, lane):
         tiles = range(len(part))
         e, w, s, n, scale_u, scale_v, sw_u, sw_v, nw_u, nw_v, se_u, se_v, ne_u, ne_v = k
-        u, u_n, u_s, v, v_n, v_s = load_around(part, row, now)
+        u, u_n, u_s, v, v_n, v_s = around
         to_west_u, to_east_u, to_west_v, to_east_v = [], [], [], []
         for c in tiles:
             u4 = 4.0 * u[c]
@@ -370,76 +380,98 @@
             to_east_v.append(e[c] * v[c] + (ne_v[c] * u_n[c] - se_v[c] * u_s[c]))
         to_west_u, to_west_v = shift_east(to_west_u, lane), shift_east(to_west_v, lane)
         to_east_u, to_east_v = shift_west(to_east_u, lane), shift_west(to_east_v, lane)
-        right_u, right_v = load(ext, part, row, 1), load(ext, part, row, 2)
         new_u, new_v = [], []
         for c in tiles:
             mid_u = s[c] * u_s[c] + n[c] * u_n[c]
             mid_v = 4.0 * (s[c] * v_s[c] + n[c] * v_n[c])
-            new_u.append(scale_u[c] * (right_u[c] + mid_u + (to_west_u[c] + to_east_u[c])))
-            new_v.append(scale_v[c] * (right_v[c] + mid_v + (to_west_v[c] + to_east_v[c])))
-        store(vel, part, row, new_u, new, 0)
-        store(vel, part, row, new_v, new, 1)
+            new_u.append(scale_u[c] * (right[0][c] + mid_u + (to_west_u[c] + to_east_u[c])))
+            new_v.append(scale_v[c] * (right[1][c] + mid_v + (to_west_v[c] + to_east_v[c])))
+        return new_u, new_v
+
+    def put(new, values):
+        return [(new, (i,), values[i]) for i in range(2)]
+
+    def keep(k):
+        return [(coef, (i,), k[i]) for i in range(14)]
 
     def sweep(framed, now, new):
-        over_rows(framed, lambda part, row: relax(part, row, [load(coef, part, row, i) for i in range(14)], now, new))
-
-    def first_start(part, row):
-        k = coefficients(part, row)
-        for i in range(2):
-            right = load(ext, part, row, 1 + i)
-            store(vel, part, row, [a * b for a, b in zip(k[4 + i], right)], 0, i)
-
-    over_rows(True, first_viscosity)
-    over_rows(True, first_start)
-    sweep(True, 0, 1)
+        def read(part, row, count):
+            k = [load(coef, part, row, count, i) for i in range(14)]
+            return k, load_around(part, row, count, now), load_right(part, row, count)
+
+        over_rows(framed, read, lambda part, read, lane: put(new, relax(part, *read, lane)))
+
+    def read_first(part, row, count):
+        return read_coefficients(part, row, count), load_right(part, row, count)
+
+    def first_start(part, read, lane):
+        k = coefficients(part, read[0], lane)
+        return keep(k) + put(vel_a, [[a * b for a, b in zip(k[4 + i], read[1][i])] for i in range(2)])
+
+    def read_start(part, row, count):
+        return (*read_first(part, row, count), load_around(part, row, count, vel_b))
+
+    def start(part, read, lane):
+        k = coefficients(part, read[0], lane)
+        return keep(k) + put(vel_a, relax(part, k, read[2], read[1], lane))
+
+    over_rows(True, read_thickness, first_viscosity)
+    over_rows(True, read_first, first_start)
+    sweep(True, vel_a, vel_b)
 
     def iteration(i, carry):
         @pl.when(i == PIC - 1)
         def _():
-            join_parts(vel, ((1, 0), (1, 1)), True)
-
-        over_rows(True, viscosity)
-        over_rows(True, lambda part, row: relax(part, row, coefficients(part, row), 1, 0))
-        sweep(True, 0, 1)
+            join_parts(vel_b, ((0,), (1,)), True)
+
+        over_rows(True, read_viscosity, viscosity)
+        over_rows(True, read_start, start)
+        sweep(True, vel_a, vel_b)
         return carry
 
     lax.fori_loop(1, PIC, iteration, 0)
-    join_parts(vel, ((1, 0), (1, 1)), False)
+    join_parts(vel_b, ((0,), (1,)), False)
     copies = []
     for i, out in enumerate((vel_u, vel_v)):
         for c in range(2):
             copies.append(
                 pltpu.make_async_copy(
-                    vel.at[1, i, MAIN[c] + TOP : MAIN[c] + TOP + TILE, :],
+                    vel_b.at[i, MAIN[c] + TOP : MAIN[c] + TOP + TILE, :],
                     out.at[:, c * LANES : (c + 1) * LANES],
                     sems.at[2 * i + c],
                 )
             )
             copies[-1].start()
 
-    def first_adjoint(part, row):
-        for i in range(2):
-            u, seen, scale = load(vel, part, row, 1, i), load(ext, part, row, 3 + i), load(coef, part, row, 4 + i)
-            misfit = [0.5 * (a - b) for a, b in zip(u, seen)]
-            store(ext, part, row, misfit, 1 + i)
-            store(vel, part, row, [a * b for a, b in zip(scale, misfit)], 2, i)
-
-    over_rows(True, first_adjoint)
+    def read_misfit(part, row, count):
+        return [
+            [load(vel_b, part, row, count, i), load(ext, part, row, count, 3 + i), load(coef, part, row, count, 4 + i)]
+            for i in range(2)
+        ]
+
+    def first_adjoint(part, read, lane):
+        misfit = [[0.5 * (a - b) for a, b in zip(u, seen)] for u, seen, _ in read]
+        first = [[a * b for a, b in zip(read[i][2], misfit[i])] for i in range(2)]
+        return put(vel_c, first) + [(ext, (1 + i,), misfit[i]) for i in range(2)]
+
+    over_rows(True, read_misfit, first_adjoint)
 
     def two_sweeps(i, carry):
-        sweep(True, 2, 0)
-        sweep(True, 0, 2)
+        sweep(True, vel_c, vel_a)
+        sweep(True, vel_a, vel_c)
         return carry
 
     lax.fori_loop(0, (ADJ - 2) // 2, two_sweeps, 0)
-    sweep(False, 2, 0)
-
-    def gradient(part, row):
-        u, v, lu, lv = (load(vel, part, row, j, i) for j in (1, 0) for i in range(2))
-        friction = load(fr, part, row)
-        store(visc, part, row, [-2.0 * friction[c] * (u[c] * lu[c] + v[c] * lv[c]) for c in range(len(part))])
-
-    over_rows(False, gradient)
+    sweep(False, vel_c, vel_a)
+
+    def read_gradient(part, row, count):
+        return [load(ref, part, row, count, i) for ref in (vel_b, vel_a) for i in range(2)] + [load(fr, part, row, count)]
+
+    def gradient(part, read, lane):
+        u, v, lu, lv, friction = read
+        return [(visc, (), [-2.0 * friction[c] * (u[c] * lu[c] + v[c] * lv[c]) for c in range(len(part))])]
+
+    over_rows(False, read_gradient, gradient)
     join_parts(visc, ((),), False)
     down = [sum(visc[pl.ds(MAIN[c] + TOP + j, CT, stride=4), :] for j in range(4)) for c in range(2)]
     k = lax.broadcasted_iota(jnp.int32, (LANES, LANES), 0)
@@ -552,7 +584,9 @@
             pltpu.VMEM((ALL_ROWS, LANES), f32),
             pltpu.VMEM((ALL_ROWS, LANES), f32),
             pltpu.VMEM((ALL_ROWS, LANES), f32),
-            pltpu.VMEM((3, 2, ALL_ROWS, LANES), f32),
+            pltpu.VMEM((2, ALL_ROWS, LANES), f32),
+            pltpu.VMEM((2, ALL_ROWS, LANES), f32),
+            pltpu.VMEM((2, ALL_ROWS, LANES), f32),
             pltpu.VMEM((14, ALL_ROWS, LANES), f32),
             pltpu.VMEM((CT, LANES), f32),
             pltpu.SemaphoreType.DMA((4,)),

time: 102 us -> 69.9 us (0.69)
  Pallas kernels: 58.6 us -> 26 us
    pallas_call x1, Pallas kernels: 52.7 us -> 20.2 us  [per_device(): pl.pallas_call(model_kernel, out_shape=(shape(TILE, TILE), shape(TILE, TI...]
  transfers between devices with their start and end apart: 5 -> 5, of which waited for: 2 -> 2; matrix products, arithmetic and copies ran while one was open for 0% -> 0% of each run, Pallas kernels for 2% -> 4%
where the time goes in v5:
time: 69.9 us; the launch traced here: 69.6 us
  blocking collectives  30.1 us (43%)
  Pallas kernels  26 us (37%)
  starting transfers between devices  8.37 us (12%)
  waiting for transfers between devices  2.92 us (4%)
  local copies, waits for them, and re-layouts  1.54 us (2%)
  between operations  0.75 us (1%)
    all_to_all x1, blocking collectives, per_device(): lax.all_to_all(sums.reshape(cols * rows, *share[1:]), ('gx', 'gy'), 0, 0,...  22 us
    pallas_call x1, Pallas kernels, per_device(): pl.pallas_call(model_kernel, out_shape=(shape(TILE, TILE), shape(TILE, TI...  20.2 us
    all_to_all x1, blocking collectives, per_device(): lax.all_to_all(parts, 'gx', 0, 0, tiled=True)  8.15 us
    all_to_all x1, starting transfers between devices, per_device(): patches = lax.all_to_all(patches, 'gy', 0, 0, tiled=True)  5.14 us
    ppermute x4, starting transfers between devices, swap(): lax.ppermute(cells, axis, pairs + [(j, i) for i, j in pairs])  3.23 us
    ppermute x4, waiting for transfers between devices, swap(): lax.ppermute(cells, axis, pairs + [(j, i) for i, j in pairs])  2.92 us
    pallas_call x1, Pallas kernels, per_device(): pl.pallas_call(columns_kernel, out_shape=[shape(HALF, LANES)] * 2, in_spe...  2.39 us
    pallas_call x1, Pallas kernels, per_device(): pl.pallas_call(patches_kernel, out_shape=shape(rows, PATCH, LANES), in_sp...  1.83 us
  transfers between devices with their start and end apart: 5, of which 2 were waited for; matrix products, arithmetic and copies ran while one was open for 0% of the time, Pallas kernels for 4%

profile of v5, /device:TPU:0, one launch (start us, length us, event | category | flops | bytes accessed | tf_op | source)
XLA Modules:
  0.0 69.6 jit_solution(9785957843254301120)
XLA Ops:
  0.6 0.0 copy-start.3
  0.6 0.8 %copy-done.3 = f32[4,4096]{1,0:T(4,128)S(1)} copy-done((f32[4,4096]{1,0:T(4,128)S(1)}, f32[4,4096]{1,0:T(4,128)}, u32[]{:S(2)}) %copy-start.3) | copy-done | bytes 65560
  1.5 0.0 copy-start.4
  1.5 0.7 copy-done.4
  2.2 1.8 %patches.1 = f32[8,72,128]{2,1,0:T(8,128)} custom-call(s32[4,8]{1,0:T(4,128)S(1)} %bitcast.6, f32[4,4096]{1,0:T(4,128)S(1)} %copy-done.3), custom_call_target="tpu_custom_call" | custom-call | tf_op jit(solution)/shard_map/patches/pallas_call | solution.py:557
  4.0 5.1 %all-to-all-start = ((f32[8,72,128]{2,1,0:T(8,128)}), f32[8,72,128]{2,1,0:T(8,128)S(1)}, u32[]{:S(2)}, u32[]{:S(2)}) async-start(f32[8,72,128]{2,1,0:T(8,128)} %patches.1), calls=%async_computation | async-start | bytes 589824 | tf_op jit(solution)/shard_map/all_to_all | solution.py:566
  9.1 0.0 copy-start
  9.1 0.0 copy-start.1
  9.1 0.0 copy-start.2
  9.1 2.4 %columns.1 = (f32[128,128]{1,0:T(8,128)}, f32[128,128]{1,0:T(8,128)}) custom-call(f32[256,256]{1,0:T(8,128)} %thick.5, f32[2,256,256]{2,1,0:T(8,128)} %drive.5, f32[2,256,256]{2,1,0:T(8,128)} %obs.5), custom_call_target="tpu_custom_call" | custom-call | tf_op jit(solution)/shard_map/columns/pallas_call | solution.py:547
  11.5 1.8 %collective-permute-start = (f32[128,128]{1,0:T(8,128)}, f32[128,128]{1,0:T(8,128)S(1)}, u32[]{:S(2)}, u32[]{:S(2)}) collective-permute-start(f32[128,128]{1,0:T(8,128)} %get-tuple-element.10), channel_id=1, source_target_pairs={{0,8},{16,24},{8,0},{24,16},{1,9},{17,25},{9,1},{25,17},{2,10},{18... | collective-permute-start | bytes 196616 | tf_op jit(solution)/shard_map/ppermute | solution.py:543
  13.4 0.7 collective-permute-start.1
  14.0 2.3 %collective-permute-done.first_col = f32[128,128]{1,0:T(8,128)S(1)} collective-permute-done((f32[128,128]{1,0:T(8,128)}, f32[128,128]{1,0:T(8,128)S(1)}, u32[]{:S(2)}, u32[]{:S(2)}) %collective-permute-start) | collective-permute-done | bytes 65568 | tf_op jit(solution)/shard_map/ppermute | solution.py:543
  16.3 0.0 collective-permute-done.1.second_col
  16.3 0.0 copy-done
  16.3 0.0 copy-done.1
  16.4 0.0 copy-done.2
  16.4 0.1 rows.1
  16.5 0.0 copy-start.6
  16.5 0.1 collective-permute-start.2
  16.6 0.7 collective-permute-start.3
  17.3 0.6 collective-permute-done.2.first_row
  17.9 0.0 collective-permute-done.3.second_row
  17.9 0.0 all-to-all-done.patches
  17.9 0.0 copy-done.6
  17.9 20.2 %model.1 = (f32[256,256]{1,0:T(8,128)}, f32[256,256]{1,0:T(8,128)}, f32[4,8,8,128]{3,2,1,0:T(8,128)S(1)}) custom-call(s32[4,8]{1,0:T(4,128)S(1)} %bitcast.8, f32[8,72,128]{2,1,0:T(8,128)S(1)} %all-to-all-done.patches, f32[256,256]{1,0:T(8,128)S(1)} %copy-done.2, f32[2,256,256]{2,1,0:T(8,128)S(1)} %copy-done, f32[2,256,256]{2,1,0:T(8,128)S(1)} %copy-done.1, ...), custom_call_target="tpu_custom_call" | custom-call | tf_op jit(solution)/shard_map/model/pallas_call | solution.py:577
  38.1 0.0 copy-start.5
  38.1 22.0 %all_to_all.15.gathered = f32[32,8,128]{2,1,0:T(8,128)S(1)} all-to-all(f32[32,8,128]{2,1,0:T(8,128)S(1)} %bitcast.5), channel_id=1, replica_groups=mesh['gx'=4,'gy'=8] {'gx','gy'}, dimensions={0} | all-to-all | bytes 262144 | tf_op jit(solution)/shard_map/all_to_all | solution.py:599
  60.1 0.0 copy-done.5
  60.1 0.7 %pick.1 = f32[4,4,8,128]{3,2,1,0:T(8,128)S(1)} custom-call(s32[4,8]{1,0:T(4,128)S(1)} %bitcast.7, f32[32,8,128]{2,1,0:T(8,128)S(1)} %all_to_all.15.gathered), custom_call_target="tpu_custom_call" | custom-call | tf_op jit(solution)/shard_map/pick/pallas_call | solution.py:600
  60.8 8.1 %all_to_all.16.parts = f32[4,4,8,128]{3,2,1,0:T(8,128)S(1)} all-to-all(f32[4,4,8,128]{3,2,1,0:T(8,128)S(1)} %pick.1), channel_id=1, replica_groups=mesh['gx'=4,'gy'=8] {'gx'}, dimensions={0} | all-to-all | bytes 131072 | tf_op jit(solution)/shard_map/all_to_all | solution.py:615
  69.0 0.7 join.1
Async XLA Ops:
  0.6 0.8 %copy-start.3 = (f32[4,4096]{1,0:T(4,128)S(1)}, f32[4,4096]{1,0:T(4,128)}, u32[]{:S(2)}) copy-start(f32[4,4096]{1,0:T(4,128)} %control.1) | copy-start | bytes 196612
  1.5 0.7 copy-start.4
  4.0 13.9 %all-to-all-start = ((f32[8,72,128]{2,1,0:T(8,128)}), f32[8,72,128]{2,1,0:T(8,128)S(1)}, u32[]{:S(2)}, u32[]{:S(2)}) async-start(f32[8,72,128]{2,1,0:T(8,128)} %patches.1), calls=%async_computation | async-start | bytes 589824 | tf_op jit(solution)/shard_map/all_to_all | solution.py:566
  9.1 7.2 %copy-start = (f32[2,256,256]{2,1,0:T(8,128)S(1)}, f32[2,256,256]{2,1,0:T(8,128)}, u32[]{:S(2)}) copy-start(f32[2,256,256]{2,1,0:T(8,128)} %drive.5) | copy-start | bytes 1572868
  9.1 7.2 %copy-start.1 = (f32[2,256,256]{2,1,0:T(8,128)S(1)}, f32[2,256,256]{2,1,0:T(8,128)}, u32[]{:S(2)}) copy-start(f32[2,256,256]{2,1,0:T(8,128)} %obs.5) | copy-start | bytes 1572868
  9.1 7.2 %copy-start.2 = (f32[256,256]{1,0:T(8,128)S(1)}, f32[256,256]{1,0:T(8,128)}, u32[]{:S(2)}) copy-start(f32[256,256]{1,0:T(8,128)} %thick.5) | copy-start | bytes 786436
  11.5 4.8 %collective-permute-start = (f32[128,128]{1,0:T(8,128)}, f32[128,128]{1,0:T(8,128)S(1)}, u32[]{:S(2)}, u32[]{:S(2)}) collective-permute-start(f32[128,128]{1,0:T(8,128)} %get-tuple-element.10), channel_id=1, source_target_pairs={{0,8},{16,24},{8,0},{24,16},{1,9},{17,25},{9,1},{25,17},{2,10},{18... | collective-permute-start | bytes 196616 | tf_op jit(solution)/shard_map/ppermute | solution.py:543
  13.4 3.0 %collective-permute-start.1 = (f32[128,128]{1,0:T(8,128)}, f32[128,128]{1,0:T(8,128)S(1)}, u32[]{:S(2)}, u32[]{:S(2)}) collective-permute-start(f32[128,128]{1,0:T(8,128)} %get-tuple-element.11), channel_id=1, source_target_pairs={{8,16},{16,8},{9,17},{17,9},{10,18},{18,10},{11,19},{19,11},{12,20... | collective-permute-start | bytes 196616 | tf_op jit(solution)/shard_map/ppermute | solution.py:543
  16.5 1.4 %copy-start.6 = (s32[8,4]{0,1:T(4,128)S(1)}, s32[8,4]{0,1:T(4,128)}, u32[]{:S(2)}) copy-start(s32[8,4]{0,1:T(4,128)} %param.10) | copy-start | bytes 388
  16.5 1.4 %collective-permute-start.2 = (f32[3,64,128]{2,1,0:T(8,128)S(1)}, f32[3,64,128]{2,1,0:T(8,128)S(1)}, u32[]{:S(2)}, u32[]{:S(2)}) collective-permute-start(f32[3,64,128]{2,1,0:T(8,128)S(1)} %get-tuple-element.12), channel_id=1, source_target_pairs={{0,1},{2,3},{4,5},{6,7},{1,0},{3,2},{5,4},{7,6},{8,9},{10,11},{12,... | collective-permute-start | bytes 294920 | tf_op jit(solution)/shard_map/ppermute | solution.py:543
  16.6 1.3 %collective-permute-start.3 = (f32[3,64,128]{2,1,0:T(8,128)S(1)}, f32[3,64,128]{2,1,0:T(8,128)S(1)}, u32[]{:S(2)}, u32[]{:S(2)}) collective-permute-start(f32[3,64,128]{2,1,0:T(8,128)S(1)} %get-tuple-element.13), channel_id=1, source_target_pairs={{1,2},{3,4},{5,6},{2,1},{4,3},{6,5},{9,10},{11,12},{13,14},{10,9},... | collective-permute-start | bytes 294920 | tf_op jit(solution)/shard_map/ppermute | solution.py:543
  38.1 22.0 %copy-start.5 = (s32[8,4,1]{0,2,1:T(1,128)S(1)}, s32[8,4,1]{0,2,1:T(1,128)}, u32[]{:S(2)}) copy-start(s32[8,4,1]{0,2,1:T(1,128)} %param.11) | copy-start | bytes 388

commit v6 on v5

--- a/solution.py
+++ b/solution.py
@@ -24,7 +24,7 @@
 ALL_ROWS = SIDE + HALF + 2 * TOP
 MAIN = (0, ROWS)
 SIDES = (SIDE,)
-BLOCKS = 4
+BLOCKS = 2
 AHEAD = 2
 PACK = COARSE // LANES
 VMEM_LIMIT = 40 * 1024 * 1024
@@ -32,7 +32,10 @@
 
 STRIP = ((0, HALO), (HALO, HALO), (2 * HALO, HALO), (3 * HALO, OBS), (3 * HALO + OBS, OBS))
 
-PATCH_ROWS = ((-1, PACK - 2, 2, 0), (0, 0, PACK, 4), (1, 0, 2, CT + 4))
+CONTROL = ((0, 0, PACK, 0), (-1, PACK - 2, 2, PACK), (1, 0, 2, PACK + 2))
+FOLDED = 40
+CORNERS = 48
+PARCEL = 64
 PATCH = CT + 8
 
 visc_scale = 0.1
@@ -43,67 +46,111 @@
     return lax.broadcasted_iota(jnp.int32, (rows, LANES), 1)
 
 
-def patch_lanes(count, ds):
-    lane = lanes_of(count)
-    return (lane < CT) if ds == 0 else ((lane >= CT) & (lane < 96) if ds > 0 else lane >= 96)
-
-
 def is_even(axis):
     return lax.axis_index(axis) % 2 == 0
 
 
-def columns_kernel(thick, drive, obs, first_pair, second_pair, held, sems):
-    copies = []
+def side_lanes(rows, ds, group):
+    place = (lanes_of(rows) - 8 * group) % CT
+    return place < 4 if ds > 0 else place >= CT - 4
+
+
+def fill_parcels(tile_block, owned_blocks, parcels):
+    tile_cols, tile_rows = tile_block.shape
+    owned = owned_blocks.shape[0]
+    mine = lax.axis_index("gy") * owned
+    col_tile = lax.axis_index("gx")
+
+    def spread(row, carry):
+        for ds in (-1, 0, 1):
+            col = col_tile + ds
+            place = tile_block[jnp.clip(col, 0, tile_cols - 1), row] - mine
+
+            @pl.when((col >= 0) & (col < tile_cols) & (place >= 0) & (place < owned))
+            def _():
+                for dr, first, count, at in CONTROL:
+                    target = row - dr
+
+                    @pl.when((target >= 0) & (target < tile_rows))
+                    def _():
+                        if ds == 0:
+                            parcels[target, at : at + count, :] = owned_blocks[place, first : first + count, :]
+                            return
+                        start = FOLDED + at % 8
+                        rows = min(count, 8)
+                        folded = parcels[target, start : start + rows, :]
+                        for i in range(count // rows):
+                            group = at // 8 + i
+                            cells = owned_blocks[place, first + 8 * i : first + 8 * i + rows, :]
+                            folded = jnp.where(side_lanes(rows, ds, group), turn(cells, 0, 8 * group), folded)
+                        parcels[target, start : start + rows, :] = folded
+
+        return carry
+
+    lax.fori_loop(0, tile_rows, spread, 0)
+
+
+def pack_kernel(
+    tile_block, control, thick, drive, obs, first_col, second_col, first_row, second_row, parcels,
+    held, held_control, owned_blocks, sems,
+):
+    copies = [pltpu.make_async_copy(control, held_control, sems.at[5])]
     for f, field in enumerate((thick, drive.at[0], drive.at[1], obs.at[0], obs.at[1])):
         copies.append(pltpu.make_async_copy(field, held.at[f], sems.at[f]))
-        copies[-1].start()
+    for copy in copies:
+        copy.start()
+    parcels[...] = jnp.zeros_like(parcels)
+    copies[0].wait()
+    for j in range(PACK):
+        owned_blocks[:, j, :] = held_control[:, j * LANES : (j + 1) * LANES]
+    fill_parcels(tile_block, owned_blocks, parcels)
+
     lane = lanes_of(HALF)
     left = jnp.zeros((HALF, LANES), jnp.float32)
     right = jnp.zeros((HALF, LANES), jnp.float32)
+    even_row, even_col = is_even("gy"), is_even("gx")
     for f, (first, count) in enumerate(STRIP):
-        copies[f].wait()
+        copies[1 + f].wait()
+        for c in range(2):
+            cols = slice(c * LANES, (c + 1) * LANES)
+            top, bottom = held[f, 0:count, cols], held[f, TILE - count : TILE, cols]
+            first_row[c, first : first + count, :] = jnp.where(even_row, bottom, top)
+            second_row[c, first : first + count, :] = jnp.where(even_row, top, bottom)
         for part in range(2):
             rows = slice(part * HALF, (part + 1) * HALF)
             start = part * BAND + first
             inside = (lane >= start) & (lane < start + count)
-            left = jnp.where(inside, pltpu.roll(held[f, rows, :LANES], start, 1), left)
-            right = jnp.where(inside, pltpu.roll(held[f, rows, LANES:], (start + count) % LANES, 1), right)
-    even = is_even("gx")
-    first_pair[...] = jnp.where(even, right, left)
-    second_pair[...] = jnp.where(even, left, right)
-
-
-def patches_kernel(tile_block, control, patches, owned_blocks):
-    tile_cols, tile_rows = tile_block.shape
-    owned = control.shape[0]
-    mine = lax.axis_index("gy") * owned
-    col_tile = lax.axis_index("gx")
-    for j in range(PACK):
-        owned_blocks[:, j, :] = control[:, j * LANES : (j + 1) * LANES]
-    patches[...] = jnp.zeros_like(patches)
-
-    def spread(row, carry):
-        for ds in (-1, 0, 1):
-            col = col_tile + ds
-            place = tile_block[jnp.clip(col, 0, tile_cols - 1), row] - mine
-
-            @pl.when((col >= 0) & (col < tile_cols) & (place >= 0) & (place < owned))
-            def _():
-                for dr, first, count, at in PATCH_ROWS:
-                    target = row - dr
-
-                    @pl.when((target >= 0) & (target < tile_rows))
-                    def _():
-                        cells = owned_blocks[place, first : first + count, :]
-                        turned = pltpu.roll(cells, CT, 1)
-                        inside = patch_lanes(count, ds)
-                        for j, new in enumerate((cells, turned) if ds == 0 else (turned, cells)):
-                            rows = pl.ds(at + j, count, stride=2)
-                            patches[target, rows, :] = jnp.where(inside, new, patches[target, rows, :])
-
-        return carry
-
-    lax.fori_loop(0, tile_rows, spread, 0)
+            left = jnp.where(inside, turn(held[f, rows, :LANES], 0, start), left)
+            right = jnp.where(inside, turn(held[f, rows, LANES:], LANES - count, start), right)
+    first_col[...] = jnp.where(even_col, right, left)
+    second_col[...] = jnp.where(even_col, left, right)
+
+
+def corners_kernel(parcels_in, first_col, second_col, parcels):
+    west, east = sides("gx", first_col[...], second_col[...])
+    row_tile = lax.axis_index("gy")
+    lane = lanes_of(8)
+    parcels[...] = parcels_in[...]
+    for bottom, target, inside in (
+        (0, row_tile - 1, row_tile > 0),
+        (1, row_tile + 1, row_tile < parcels.shape[0] - 1),
+    ):
+        @pl.when(inside)
+        def _():
+            for half in range(2):
+                packed = jnp.zeros((8, LANES), jnp.float32)
+                for q, f in enumerate((0, 1, 2, 3 + half)):
+                    first, count = STRIP[f]
+                    row = 8 * half if q < 3 else 0
+                    row = HALF - count + row if bottom else row
+                    source = BAND * bottom + first
+                    start = 2 * HALO * q
+                    from_east = turn(east[row : row + 8], source, start)
+                    from_west = turn(west[row : row + 8], source, start + 2 * HALO - count)
+                    packed = jnp.where((lane >= start) & (lane < start + HALO), from_east, packed)
+                    packed = jnp.where((lane >= start + HALO) & (lane < start + 2 * HALO), from_west, packed)
+                at = CORNERS + 8 * half
+                parcels[target, at : at + 8, :] = packed
 
 
 def sides(axis, first_pair, second_pair):
@@ -123,30 +170,6 @@
     return pltpu.roll(cells, shift, 1) if shift else cells
 
 
-def rows_kernel(thick, drive, obs, first_col, second_col, first_pair, second_pair):
-    west, east = sides("gx", first_col[...], second_col[...])
-    even = is_even("gy")
-    for field, (first, count) in zip((thick, drive.at[0], drive.at[1], obs.at[0], obs.at[1]), STRIP):
-        strips = []
-        for rows, packed_rows, source, target in (
-            (slice(0, count), slice(0, count), first, BAND),
-            (slice(TILE - count, TILE), slice(HALF - count, HALF), BAND + first, 0),
-        ):
-            low, high = field[rows, :LANES], field[rows, LANES:]
-            sides_row = choose_side(
-                lanes_of(count),
-                turn(high, LANES - HALO, target),
-                turn(east[packed_rows], source, target + HALO),
-                turn(west[packed_rows], source, target + 3 * HALO - count),
-                turn(low, 0, target + 3 * HALO),
-            )
-            strips.append((low, high, sides_row))
-        for c in range(3):
-            top, bottom = strips[0][c], strips[1][c]
-            first_pair[c, first : first + count, :] = jnp.where(even, bottom, top)
-            second_pair[c, first : first + count, :] = jnp.where(even, top, bottom)
-
-
 def shift_east(tiles, lane):
     rolled = [pltpu.roll(t, LANES - 1, 1) for t in tiles]
     if len(tiles) == 1:
@@ -166,9 +189,9 @@
     wide = 2 * HALO if framed else 0
     main, side = (TILE + wide) // BLOCKS, (HALF + wide) // BLOCKS
     step = 24 if framed else 32
-    groups = [(MAIN, g, step) for g in range(0, main, step)]
-    groups[1:1] = [(SIDES, 0, 16)]
-    groups[3:3] = [(SIDES, 16, side - 16)]
+    groups = [(g / main, MAIN, g, step) for g in range(0, main, step)]
+    groups += [((g + 1) / side, SIDES, g, 16) for g in range(0, side, 16)]
+    groups = [group[1:] for group in sorted(groups)]
 
     def block(i, carry):
         first = {MAIN: pl.multiple_of(start + i * main, 8), SIDES: pl.multiple_of(start + i * side, 8)}
@@ -231,15 +254,28 @@
 
 
 def model_kernel(
-    ice_mask, patches, thick, drive, obs, first_row, second_row, first_col, second_col,
+    ice_mask, parcels, thick, drive, obs, first_row, second_row, first_col, second_col,
     vel_u, vel_v, sums,
-    ext, fr, ice, visc, vel_a, vel_b, vel_c, coef, small, sems,
+    ext, fr, ice, visc, vel_a, vel_b, vel_c, coef, small, patch, sems,
 ):
     tile_cols, tile_rows = ice_mask.shape
     row_tile = lax.axis_index("gy")
     col_tile = lax.axis_index("gx")
 
-    cells = 0.5 * jnp.exp(sum(patches[j] for j in range(tile_rows)))
+    flat = sum(parcels[j, :CORNERS, :] for j in range(tile_rows))
+    folded = flat[FOLDED:]
+    for dr, _, count, at in CONTROL:
+        cells = flat[at : at + count]
+        if dr == 0:
+            side = jnp.concatenate([turn(folded, 8 * g, 0) for g in range(PACK // 8)], axis=0)
+        else:
+            side = turn(folded, PACK, 0)[at % 8 : at % 8 + count]
+        inner = lanes_of(count) < CT
+        row = 4 + {-1: -4, 0: 0, 1: CT}[dr]
+        patch[pl.ds(row, count, stride=2), :] = jnp.where(inner, cells, turn(side, 0, CT))
+        patch[pl.ds(row + 1, count, stride=2), :] = jnp.where(inner, turn(cells, 0, CT), side)
+
+    cells = 0.5 * jnp.exp(patch[...])
     lane = lanes_of(PATCH)
     for c in range(2):
         wide = jnp.take_along_axis(cells, 32 * c + lane // 4, axis=1)
@@ -257,19 +293,23 @@
         fr[pl.ds(SIDE + MARGIN + j, 40, stride=4), :] = wide
 
     west, east = sides("gx", first_col[...], second_col[...])
+    corners = []
+    for target, inside in ((row_tile - 1, row_tile > 0), (row_tile + 1, row_tile < tile_rows - 1)):
+        cells = parcels[jnp.clip(target, 0, tile_rows - 1), CORNERS:, :]
+        corners.append(jnp.where(inside, cells, 0.0))
     even = is_even("gy")
     lane = lanes_of(HALF)
     upper = lane < BAND
     for f, (field, (first, count)) in enumerate(zip((thick, drive.at[0], drive.at[1], obs.at[0], obs.at[1]), STRIP)):
         scale = 0.5 if f in (1, 2) else 1.0
-        frames = []
-        for c in range(3):
+        north, south = [], []
+        for c in range(2):
             one, two = scale * first_row[c, first : first + count, :], scale * second_row[c, first : first + count, :]
-            frames.append((jnp.where(even, two, one), jnp.where(even, one, two)))
-        for c in range(2):
+            north.append(jnp.where(even, two, one))
+            south.append(jnp.where(even, one, two))
             ext[f, MAIN[c] + TOP : MAIN[c] + TOP + TILE, :] = scale * field[:, c * LANES : (c + 1) * LANES]
-            ext[f, MAIN[c] + TOP - count : MAIN[c] + TOP, :] = frames[c][0]
-            ext[f, MAIN[c] + TOP + TILE : MAIN[c] + TOP + TILE + count, :] = frames[c][1]
+            ext[f, MAIN[c] + TOP - count : MAIN[c] + TOP, :] = north[c]
+            ext[f, MAIN[c] + TOP + TILE : MAIN[c] + TOP + TILE + count, :] = south[c]
         halves = (slice(0, HALF), slice(HALF, TILE))
         high = [turn(field[halves[b], LANES:], LANES - HALO, BAND * b) for b in range(2)]
         low = [turn(field[halves[b], :LANES], 0, BAND * b + 3 * HALO) for b in range(2)]
@@ -281,11 +321,18 @@
             turn(west, first, 3 * HALO - count),
             jnp.where(upper, low[0], low[1]),
         )
-        upper_few = lanes_of(count) < BAND
+        few = lanes_of(count)
+        ends = []
+        for band, (low, high), cells in ((0, north, corners[0]), (BAND, south, corners[1])):
+            cells = cells if f < 3 else cells[8 * (f - 3) : 8 * (f - 2)]
+            frame = scale * turn(cells, 2 * HALO * min(f, 3), band + HALO)
+            ends.append(
+                choose_side(few, turn(high, LANES - HALO, band), frame, frame, turn(low, 0, band + 3 * HALO))
+            )
         above = turn(ext[f, here + HALF - count : here + HALF, :], 0, BAND)
         below = turn(ext[f, here : here + count, :], 0, BAND)
-        ext[f, here - count : here, :] = jnp.where(upper_few, frames[2][0], above)
-        ext[f, here + HALF : here + HALF + count, :] = jnp.where(upper_few, below, frames[2][1])
+        ext[f, here - count : here, :] = jnp.where(few < BAND, ends[0], above)
+        ext[f, here + HALF : here + HALF + count, :] = jnp.where(few < BAND, below, ends[1])
 
     side_ice = []
     for dr, first, count in ((-1, MARGIN, HALO), (0, TOP, TILE), (1, TOP + TILE, HALO)):
@@ -544,35 +591,32 @@
         return received[1], received[0]
 
     fields = thickness, driving, observed
-    columns = pl.pallas_call(
-        columns_kernel,
-        out_shape=[shape(HALF, LANES)] * 2,
-        in_specs=[pl.BlockSpec(memory_space=pltpu.HBM)] * 3,
-        out_specs=in_vmem(2),
-        scratch_shapes=[pltpu.VMEM((5, TILE, TILE), f32), pltpu.SemaphoreType.DMA((5,))],
+    owned = control.shape[0]
+    *edges, parcels = pl.pallas_call(
+        pack_kernel,
+        out_shape=[shape(HALF, LANES)] * 2 + [shape(2, 64, LANES)] * 2 + [shape(rows, PARCEL, LANES)],
+        in_specs=in_smem(1) + [pl.BlockSpec(memory_space=pltpu.HBM)] * 4,
+        out_specs=in_vmem(5),
+        scratch_shapes=[
+            pltpu.VMEM((5, TILE, TILE), f32),
+            pltpu.VMEM(control.shape, f32),
+            pltpu.VMEM((owned, PACK, LANES), f32),
+            pltpu.SemaphoreType.DMA((6,)),
+        ],
         compiler_params=pltpu.CompilerParams(vmem_limit_bytes=PACK_VMEM_LIMIT),
-        name="columns",
-    )(*fields)
-    columns_in = swap("gx", *columns)
-    patches = pl.pallas_call(
-        patches_kernel,
-        out_shape=shape(rows, PATCH, LANES),
-        in_specs=in_smem(1) + in_vmem(1),
+        name="pack",
+    )(tile_block, control, *fields)
+    columns_in = swap("gx", *edges[:2])
+    rows_in = swap("gy", *edges[2:])
+    parcels = pl.pallas_call(
+        corners_kernel,
+        out_shape=shape(*parcels.shape),
+        in_specs=in_vmem(3),
         out_specs=pl.BlockSpec(memory_space=pltpu.VMEM),
-        scratch_shapes=[pltpu.VMEM((control.shape[0], PACK, LANES), f32)],
         compiler_params=params,
-        name="patches",
-    )(tile_block, control)
-    patches = lax.all_to_all(patches, "gy", 0, 0, tiled=True)
-    strips = pl.pallas_call(
-        rows_kernel,
-        out_shape=[shape(3, 64, LANES)] * 2,
-        in_specs=in_vmem(5),
-        out_specs=in_vmem(2),
-        compiler_params=params,
-        name="rows",
-    )(*fields, *columns_in)
-    rows_in = swap("gy", *strips)
+        name="corners",
+    )(parcels, *columns_in)
+    parcels = lax.all_to_all(parcels, "gy", 0, 0, tiled=True)
 
     vel_u, vel_v, sums = pl.pallas_call(
         model_kernel,
@@ -589,11 +633,12 @@
             pltpu.VMEM((2, ALL_ROWS, LANES), f32),
             pltpu.VMEM((14, ALL_ROWS, LANES), f32),
             pltpu.VMEM((CT, LANES), f32),
+            pltpu.VMEM((PATCH, LANES), f32),
             pltpu.SemaphoreType.DMA((4,)),
         ],
         compiler_params=params,
         name="model",
-    )(ice_mask, patches, *fields, *rows_in, *columns_in)
+    )(ice_mask, parcels, *fields, *rows_in, *columns_in)
 
     share = (control.shape[0], PACK // cols, LANES)
     sums = lax.all_to_all(sums.reshape(cols * rows, *share[1:]), ("gx", "gy"), 0, 0, tiled=True)

time: 69.9 us -> 71.2 us (1.019)
  blocking collectives: 30.1 us -> 23.9 us
  waiting for transfers between devices: 2.92 us -> 7.5 us
  Pallas kernels: 26 us -> 28 us
  starting transfers between devices: 8.37 us -> 9.6 us
    all_to_all x1, blocking collectives: 22 us -> 15.7 us  [per_device(): lax.all_to_all(sums.reshape(cols * rows, *share[1:]), ('gx', 'gy'), 0, 0,...]
    all_to_all x1, waiting for transfers between devices: 0.01 us -> 5.46 us  [per_device(): parcels = lax.all_to_all(parcels, 'gy', 0, 0, tiled=True)]
    pallas_call x1, Pallas kernels: 20.2 us -> 22.3 us  [per_device(): pl.pallas_call(model_kernel, out_shape=(shape(TILE, TILE), shape(TILE, TI...]
    ppermute x4, starting transfers between devices: 3.23 us -> 5.13 us  [swap(): lax.ppermute(cells, axis, pairs + [(j, i) for i, j in pairs])]
    ppermute x4, waiting for transfers between devices: 2.92 us -> 2.04 us  [swap(): lax.ppermute(cells, axis, pairs + [(j, i) for i, j in pairs])]
    unnamed x14 -> x16, local copies, waits for them, and re-layouts: 1.54 us -> 0.98 us
    pallas_call x3 -> x2, Pallas kernels: 4.36 us -> 4.32 us  [the longest x1 3.52 us: per_device(): pl.pallas_call(pack_kernel, out_shape=[shape(HALF, LANES)] * 2 + [shape(2...]
  transfers between devices with their start and end apart: 5 -> 5, of which waited for: 2 -> 3; matrix products, arithmetic and copies ran while one was open for 0% -> 0% of each run, Pallas kernels for 4% -> 0%
where the time goes in v6:
time: 71.2 us; the launch traced here: 70.7 us
  Pallas kernels  28 us (39%)
  blocking collectives  23.9 us (34%)
  starting transfers between devices  9.6 us (13%)
  waiting for transfers between devices  7.5 us (11%)
  local copies, waits for them, and re-layouts  0.98 us (1%)
    pallas_call x1, Pallas kernels, per_device(): pl.pallas_call(model_kernel, out_shape=(shape(TILE, TILE), shape(TILE, TI...  22.3 us
    all_to_all x1, blocking collectives, per_device(): lax.all_to_all(sums.reshape(cols * rows, *share[1:]), ('gx', 'gy'), 0, 0,...  15.7 us
    all_to_all x1, blocking collectives, per_device(): lax.all_to_all(parts, 'gx', 0, 0, tiled=True)  8.15 us
    all_to_all x1, waiting for transfers between devices, per_device(): parcels = lax.all_to_all(parcels, 'gy', 0, 0, tiled=True)  5.46 us
    ppermute x4, starting transfers between devices, swap(): lax.ppermute(cells, axis, pairs + [(j, i) for i, j in pairs])  5.13 us
    all_to_all x1, starting transfers between devices, per_device(): parcels = lax.all_to_all(parcels, 'gy', 0, 0, tiled=True)  4.47 us
    pallas_call x1, Pallas kernels, per_device(): pl.pallas_call(pack_kernel, out_shape=[shape(HALF, LANES)] * 2 + [shape(2...  3.52 us
    ppermute x4, waiting for transfers between devices, swap(): lax.ppermute(cells, axis, pairs + [(j, i) for i, j in pairs])  2.04 us
  transfers between devices with their start and end apart: 5, of which 3 were waited for; matrix products, arithmetic and copies ran while one was open for 0% of the time, Pallas kernels for 0%

profile of v6, /device:TPU:0, one launch (start us, length us, event | category | flops | bytes accessed | tf_op | source)
XLA Modules:
  0.0 70.7 jit_solution(4144139257667168428)
XLA Ops:
  0.6 0.0 copy-start.2
  0.6 3.5 %pack.1 = (f32[128,128]{1,0:T(8,128)}, f32[128,128]{1,0:T(8,128)}, f32[2,64,128]{2,1,0:T(8,128)}, f32[2,64,128]{2,1,0:T(8,128)}, f32[8,64,128]{2,1,0:T(8,128)}) custom-call(s32[4,8]{1,0:T(4,128)} %bitcast.6, f32[4,4096]{1,0:T(4,128)} %control.1, f32[256,256]{1,0:T(8,128)} %thick.3, f32[2,256,256]{2,1,0:T(8,128)} %drive.3, f32[2,256,256]{2,1,0:T(8,128)} %obs.3), custom_call_target="tpu_custom_call" | custom-call | tf_op jit(solution)/shard_map/pack/pallas_call | solution.py:595
  4.2 3.3 %collective-permute-start = (f32[128,128]{1,0:T(8,128)}, f32[128,128]{1,0:T(8,128)S(1)}, u32[]{:S(2)}, u32[]{:S(2)}) collective-permute-start(f32[128,128]{1,0:T(8,128)} %get-tuple-element.12), channel_id=1, source_target_pairs={{0,8},{16,24},{8,0},{24,16},{1,9},{17,25},{9,1},{25,17},{2,10},{18... | collective-permute-start | bytes 196616 | tf_op jit(solution)/shard_map/ppermute | solution.py:590
  7.4 0.7 collective-permute-start.1
  8.1 1.8 %collective-permute-done.first_col = f32[128,128]{1,0:T(8,128)S(1)} collective-permute-done((f32[128,128]{1,0:T(8,128)}, f32[128,128]{1,0:T(8,128)S(1)}, u32[]{:S(2)}, u32[]{:S(2)}) %collective-permute-start) | collective-permute-done | bytes 65568 | tf_op jit(solution)/shard_map/ppermute | solution.py:590
  9.9 0.0 collective-permute-done.1.second_col
  9.9 0.0 copy-start.3
  9.9 0.9 %copy-done.3 = f32[8,64,128]{2,1,0:T(8,128)S(1)} copy-done((f32[8,64,128]{2,1,0:T(8,128)S(1)}, f32[8,64,128]{2,1,0:T(8,128)}, u32[]{:S(2)}) %copy-start.3) | copy-done | bytes 262168
  10.8 0.0 copy-start
  10.8 0.0 copy-start.1
  10.8 0.8 %corners.1 = f32[8,64,128]{2,1,0:T(8,128)} custom-call(f32[8,64,128]{2,1,0:T(8,128)S(1)} %copy-done.3, f32[128,128]{1,0:T(8,128)S(1)} %collective-permute-done.first_col, f32[128,128]{1,0:T(8,128)S(1)} %collective-permute-done.1.second_col), custom_call_target="tpu_custom_call" | custom-call | tf_op jit(solution)/shard_map/corners/pallas_call | solution.py:611
  11.7 0.0 copy-start.7
  11.7 0.0 copy-start.6
  11.7 4.5 %all-to-all-start = ((f32[8,64,128]{2,1,0:T(8,128)}), f32[8,64,128]{2,1,0:T(8,128)S(1)}, u32[]{:S(2)}, u32[]{:S(2)}) async-start(f32[8,64,128]{2,1,0:T(8,128)} %corners.1), calls=%async_computation | async-start | bytes 524288 | tf_op jit(solution)/shard_map/all_to_all | solution.py:619
  16.1 0.0 copy-done.7
  16.1 0.0 copy-start.5
  16.1 0.6 collective-permute-start.2
  16.7 0.0 copy-done.6
  16.7 0.7 collective-permute-start.3
  17.4 0.2 collective-permute-done.2.first_row
  17.6 0.0 collective-permute-done.3.second_row
  17.6 5.5 %all-to-all-done.parcels = f32[8,64,128]{2,1,0:T(8,128)S(1)} async-done(((f32[8,64,128]{2,1,0:T(8,128)}), f32[8,64,128]{2,1,0:T(8,128)S(1)}, u32[]{:S(2)}, u32[]{:S(2)}) %all-to-all-start) | async-done | bytes 262176 | tf_op jit(solution)/shard_map/all_to_all | solution.py:619
  23.1 0.0 copy-done.2
  23.1 0.0 copy-done
  23.1 0.0 copy-done.1
  23.1 0.0 copy-done.5
  23.1 22.3 %model.1 = (f32[256,256]{1,0:T(8,128)}, f32[256,256]{1,0:T(8,128)}, f32[4,8,8,128]{3,2,1,0:T(8,128)S(1)}) custom-call(s32[4,8]{1,0:T(4,128)S(1)} %bitcast.8, f32[8,64,128]{2,1,0:T(8,128)S(1)} %all-to-all-done.parcels, f32[256,256]{1,0:T(8,128)S(1)} %copy-done.2, f32[2,256,256]{2,1,0:T(8,128)S(1)} %copy-done, f32[2,256,256]{2,1,0:T(8,128)S(1)} %copy-done.1, ...), custom_call_target="tpu_custom_call" | custom-call | tf_op jit(solution)/shard_map/model/pallas_call | solution.py:621
  45.4 0.0 copy-start.4
  45.4 15.7 %all_to_all.15.gathered = f32[32,8,128]{2,1,0:T(8,128)S(1)} all-to-all(f32[32,8,128]{2,1,0:T(8,128)S(1)} %bitcast.5), channel_id=1, replica_groups=mesh['gx'=4,'gy'=8] {'gx','gy'}, dimensions={0} | all-to-all | bytes 262144 | tf_op jit(solution)/shard_map/all_to_all | solution.py:644
  61.1 0.0 copy-done.4
  61.2 0.7 %pick.1 = f32[4,4,8,128]{3,2,1,0:T(8,128)S(1)} custom-call(s32[4,8]{1,0:T(4,128)S(1)} %bitcast.7, f32[32,8,128]{2,1,0:T(8,128)S(1)} %all_to_all.15.gathered), custom_call_target="tpu_custom_call" | custom-call | tf_op jit(solution)/shard_map/pick/pallas_call | solution.py:645
  61.9 8.1 %all_to_all.16.parts = f32[4,4,8,128]{3,2,1,0:T(8,128)S(1)} all-to-all(f32[4,4,8,128]{3,2,1,0:T(8,128)S(1)} %pick.1), channel_id=1, replica_groups=mesh['gx'=4,'gy'=8] {'gx'}, dimensions={0} | all-to-all | bytes 131072 | tf_op jit(solution)/shard_map/all_to_all | solution.py:660
  70.0 0.7 join.1
Async XLA Ops:
  0.6 22.4 %copy-start.2 = (f32[256,256]{1,0:T(8,128)S(1)}, f32[256,256]{1,0:T(8,128)}, u32[]{:S(2)}) copy-start(f32[256,256]{1,0:T(8,128)} %thick.3) | copy-start | bytes 786436
  4.2 5.7 %collective-permute-start = (f32[128,128]{1,0:T(8,128)}, f32[128,128]{1,0:T(8,128)S(1)}, u32[]{:S(2)}, u32[]{:S(2)}) collective-permute-start(f32[128,128]{1,0:T(8,128)} %get-tuple-element.12), channel_id=1, source_target_pairs={{0,8},{16,24},{8,0},{24,16},{1,9},{17,25},{9,1},{25,17},{2,10},{18... | collective-permute-start | bytes 196616 | tf_op jit(solution)/shard_map/ppermute | solution.py:590
  7.4 2.5 %collective-permute-start.1 = (f32[128,128]{1,0:T(8,128)}, f32[128,128]{1,0:T(8,128)S(1)}, u32[]{:S(2)}, u32[]{:S(2)}) collective-permute-start(f32[128,128]{1,0:T(8,128)} %get-tuple-element.13), channel_id=1, source_target_pairs={{8,16},{16,8},{9,17},{17,9},{10,18},{18,10},{11,19},{19,11},{12,20... | collective-permute-start | bytes 196616 | tf_op jit(solution)/shard_map/ppermute | solution.py:590
  9.9 1.0 %copy-start.3 = (f32[8,64,128]{2,1,0:T(8,128)S(1)}, f32[8,64,128]{2,1,0:T(8,128)}, u32[]{:S(2)}) copy-start(f32[8,64,128]{2,1,0:T(8,128)} %get-tuple-element.11.parcels_in) | copy-start | bytes 786436
  10.8 12.2 %copy-start = (f32[2,256,256]{2,1,0:T(8,128)S(1)}, f32[2,256,256]{2,1,0:T(8,128)}, u32[]{:S(2)}) copy-start(f32[2,256,256]{2,1,0:T(8,128)} %drive.3) | copy-start | bytes 1572868
  10.8 12.2 %copy-start.1 = (f32[2,256,256]{2,1,0:T(8,128)S(1)}, f32[2,256,256]{2,1,0:T(8,128)}, u32[]{:S(2)}) copy-start(f32[2,256,256]{2,1,0:T(8,128)} %obs.3) | copy-start | bytes 1572868
  11.7 4.5 %copy-start.7 = (f32[2,64,128]{2,1,0:T(8,128)S(1)}, f32[2,64,128]{2,1,0:T(8,128)}, u32[]{:S(2)}) copy-start(f32[2,64,128]{2,1,0:T(8,128)} %get-tuple-element.14) | copy-start | bytes 196612
  11.7 5.0 %copy-start.6 = (f32[2,64,128]{2,1,0:T(8,128)S(1)}, f32[2,64,128]{2,1,0:T(8,128)}, u32[]{:S(2)}) copy-start(f32[2,64,128]{2,1,0:T(8,128)} %get-tuple-element.15) | copy-start | bytes 196612
  11.7 11.4 %all-to-all-start = ((f32[8,64,128]{2,1,0:T(8,128)}), f32[8,64,128]{2,1,0:T(8,128)S(1)}, u32[]{:S(2)}, u32[]{:S(2)}) async-start(f32[8,64,128]{2,1,0:T(8,128)} %corners.1), calls=%async_computation | async-start | bytes 524288 | tf_op jit(solution)/shard_map/all_to_all | solution.py:619
  16.1 6.9 %copy-start.5 = (s32[8,4]{0,1:T(4,128)S(1)}, s32[8,4]{0,1:T(4,128)}, u32[]{:S(2)}) copy-start(s32[8,4]{0,1:T(4,128)} %param.10) | copy-start | bytes 388
  16.1 1.5 %collective-permute-start.2 = (f32[2,64,128]{2,1,0:T(8,128)S(1)}, f32[2,64,128]{2,1,0:T(8,128)S(1)}, u32[]{:S(2)}, u32[]{:S(2)}) collective-permute-start(f32[2,64,128]{2,1,0:T(8,128)S(1)} %copy-done.7), channel_id=1, source_target_pairs={{0,1},{2,3},{4,5},{6,7},{1,0},{3,2},{5,4},{7,6},{8,9},{10,11},{12,... | collective-permute-start | bytes 196616 | tf_op jit(solution)/shard_map/ppermute | solution.py:590
  16.7 0.9 %collective-permute-start.3 = (f32[2,64,128]{2,1,0:T(8,128)S(1)}, f32[2,64,128]{2,1,0:T(8,128)S(1)}, u32[]{:S(2)}, u32[]{:S(2)}) collective-permute-start(f32[2,64,128]{2,1,0:T(8,128)S(1)} %copy-done.6), channel_id=1, source_target_pairs={{1,2},{3,4},{5,6},{2,1},{4,3},{6,5},{9,10},{11,12},{13,14},{10,9},... | collective-permute-start | bytes 196616 | tf_op jit(solution)/shard_map/ppermute | solution.py:590
  45.4 15.7 %copy-start.4 = (s32[8,4,1]{0,2,1:T(1,128)S(1)}, s32[8,4,1]{0,2,1:T(1,128)}, u32[]{:S(2)}) copy-start(s32[8,4,1]{0,2,1:T(1,128)} %param.11) | copy-start | bytes 388

commit v7 on v6

--- a/solution.py
+++ b/solution.py
@@ -24,7 +24,7 @@
 ALL_ROWS = SIDE + HALF + 2 * TOP
 MAIN = (0, ROWS)
 SIDES = (SIDE,)
-BLOCKS = 2
+BLOCKS = 4
 AHEAD = 2
 PACK = COARSE // LANES
 VMEM_LIMIT = 40 * 1024 * 1024
@@ -34,8 +34,7 @@
 
 CONTROL = ((0, 0, PACK, 0), (-1, PACK - 2, 2, PACK), (1, 0, 2, PACK + 2))
 FOLDED = 40
-CORNERS = 48
-PARCEL = 64
+PARCEL = 48
 PATCH = CT + 8
 
 visc_scale = 0.1
@@ -91,7 +90,7 @@
 
 
 def pack_kernel(
-    tile_block, control, thick, drive, obs, first_col, second_col, first_row, second_row, parcels,
+    tile_block, control, thick, drive, obs, first_col, second_col, parcels,
     held, held_control, owned_blocks, sems,
 ):
     copies = [pltpu.make_async_copy(control, held_control, sems.at[5])]
@@ -108,49 +107,17 @@
     lane = lanes_of(HALF)
     left = jnp.zeros((HALF, LANES), jnp.float32)
     right = jnp.zeros((HALF, LANES), jnp.float32)
-    even_row, even_col = is_even("gy"), is_even("gx")
     for f, (first, count) in enumerate(STRIP):
         copies[1 + f].wait()
-        for c in range(2):
-            cols = slice(c * LANES, (c + 1) * LANES)
-            top, bottom = held[f, 0:count, cols], held[f, TILE - count : TILE, cols]
-            first_row[c, first : first + count, :] = jnp.where(even_row, bottom, top)
-            second_row[c, first : first + count, :] = jnp.where(even_row, top, bottom)
         for part in range(2):
             rows = slice(part * HALF, (part + 1) * HALF)
             start = part * BAND + first
             inside = (lane >= start) & (lane < start + count)
             left = jnp.where(inside, turn(held[f, rows, :LANES], 0, start), left)
             right = jnp.where(inside, turn(held[f, rows, LANES:], LANES - count, start), right)
-    first_col[...] = jnp.where(even_col, right, left)
-    second_col[...] = jnp.where(even_col, left, right)
-
-
-def corners_kernel(parcels_in, first_col, second_col, parcels):
-    west, east = sides("gx", first_col[...], second_col[...])
-    row_tile = lax.axis_index("gy")
-    lane = lanes_of(8)
-    parcels[...] = parcels_in[...]
-    for bottom, target, inside in (
-        (0, row_tile - 1, row_tile > 0),
-        (1, row_tile + 1, row_tile < parcels.shape[0] - 1),
-    ):
-        @pl.when(inside)
-        def _():
-            for half in range(2):
-                packed = jnp.zeros((8, LANES), jnp.float32)
-                for q, f in enumerate((0, 1, 2, 3 + half)):
-                    first, count = STRIP[f]
-                    row = 8 * half if q < 3 else 0
-                    row = HALF - count + row if bottom else row
-                    source = BAND * bottom + first
-                    start = 2 * HALO * q
-                    from_east = turn(east[row : row + 8], source, start)
-                    from_west = turn(west[row : row + 8], source, start + 2 * HALO - count)
-                    packed = jnp.where((lane >= start) & (lane < start + HALO), from_east, packed)
-                    packed = jnp.where((lane >= start + HALO) & (lane < start + 2 * HALO), from_west, packed)
-                at = CORNERS + 8 * half
-                parcels[target, at : at + 8, :] = packed
+    even = is_even("gx")
+    first_col[...] = jnp.where(even, right, left)
+    second_col[...] = jnp.where(even, left, right)
 
 
 def sides(axis, first_pair, second_pair):
@@ -170,6 +137,30 @@
     return pltpu.roll(cells, shift, 1) if shift else cells
 
 
+def rows_kernel(thick, drive, obs, first_col, second_col, first_pair, second_pair):
+    west, east = sides("gx", first_col[...], second_col[...])
+    even = is_even("gy")
+    for field, (first, count) in zip((thick, drive.at[0], drive.at[1], obs.at[0], obs.at[1]), STRIP):
+        strips = []
+        for rows, packed_rows, source, target in (
+            (slice(0, count), slice(0, count), first, BAND),
+            (slice(TILE - count, TILE), slice(HALF - count, HALF), BAND + first, 0),
+        ):
+            low, high = field[rows, :LANES], field[rows, LANES:]
+            sides_row = choose_side(
+                lanes_of(count),
+                turn(high, LANES - HALO, target),
+                turn(east[packed_rows], source, target + HALO),
+                turn(west[packed_rows], source, target + 3 * HALO - count),
+                turn(low, 0, target + 3 * HALO),
+            )
+            strips.append((low, high, sides_row))
+        for c in range(3):
+            top, bottom = strips[0][c], strips[1][c]
+            first_pair[c, first : first + count, :] = jnp.where(even, bottom, top)
+            second_pair[c, first : first + count, :] = jnp.where(even, top, bottom)
+
+
 def shift_east(tiles, lane):
     rolled = [pltpu.roll(t, LANES - 1, 1) for t in tiles]
     if len(tiles) == 1:
@@ -189,9 +180,9 @@
     wide = 2 * HALO if framed else 0
     main, side = (TILE + wide) // BLOCKS, (HALF + wide) // BLOCKS
     step = 24 if framed else 32
-    groups = [(g / main, MAIN, g, step) for g in range(0, main, step)]
-    groups += [((g + 1) / side, SIDES, g, 16) for g in range(0, side, 16)]
-    groups = [group[1:] for group in sorted(groups)]
+    groups = [(MAIN, g, step) for g in range(0, main, step)]
+    groups[1:1] = [(SIDES, 0, 16)]
+    groups[3:3] = [(SIDES, 16, side - 16)]
 
     def block(i, carry):
         first = {MAIN: pl.multiple_of(start + i * main, 8), SIDES: pl.multiple_of(start + i * side, 8)}
@@ -253,16 +244,16 @@
         join(TOP + HALF, False, True, HALO)
 
 
-def model_kernel(
-    ice_mask, parcels, thick, drive, obs, first_row, second_row, first_col, second_col,
-    vel_u, vel_v, sums,
-    ext, fr, ice, visc, vel_a, vel_b, vel_c, coef, small, patch, sems,
+def setup_kernel(
+    ice_mask, parcels, thick, drive, obs, first_col, second_col,
+    fr, ice, middle,
+    patch,
 ):
     tile_cols, tile_rows = ice_mask.shape
     row_tile = lax.axis_index("gy")
     col_tile = lax.axis_index("gx")
 
-    flat = sum(parcels[j, :CORNERS, :] for j in range(tile_rows))
+    flat = sum(parcels[j] for j in range(tile_rows))
     folded = flat[FOLDED:]
     for dr, _, count, at in CONTROL:
         cells = flat[at : at + count]
@@ -293,46 +284,19 @@
         fr[pl.ds(SIDE + MARGIN + j, 40, stride=4), :] = wide
 
     west, east = sides("gx", first_col[...], second_col[...])
-    corners = []
-    for target, inside in ((row_tile - 1, row_tile > 0), (row_tile + 1, row_tile < tile_rows - 1)):
-        cells = parcels[jnp.clip(target, 0, tile_rows - 1), CORNERS:, :]
-        corners.append(jnp.where(inside, cells, 0.0))
-    even = is_even("gy")
     lane = lanes_of(HALF)
     upper = lane < BAND
     for f, (field, (first, count)) in enumerate(zip((thick, drive.at[0], drive.at[1], obs.at[0], obs.at[1]), STRIP)):
-        scale = 0.5 if f in (1, 2) else 1.0
-        north, south = [], []
-        for c in range(2):
-            one, two = scale * first_row[c, first : first + count, :], scale * second_row[c, first : first + count, :]
-            north.append(jnp.where(even, two, one))
-            south.append(jnp.where(even, one, two))
-            ext[f, MAIN[c] + TOP : MAIN[c] + TOP + TILE, :] = scale * field[:, c * LANES : (c + 1) * LANES]
-            ext[f, MAIN[c] + TOP - count : MAIN[c] + TOP, :] = north[c]
-            ext[f, MAIN[c] + TOP + TILE : MAIN[c] + TOP + TILE + count, :] = south[c]
         halves = (slice(0, HALF), slice(HALF, TILE))
         high = [turn(field[halves[b], LANES:], LANES - HALO, BAND * b) for b in range(2)]
         low = [turn(field[halves[b], :LANES], 0, BAND * b + 3 * HALO) for b in range(2)]
-        here = SIDE + TOP
-        ext[f, here : here + HALF, :] = scale * choose_side(
+        middle[f] = (0.5 if f in (1, 2) else 1.0) * choose_side(
             lane,
             jnp.where(upper, high[0], high[1]),
             turn(east, first, HALO),
             turn(west, first, 3 * HALO - count),
             jnp.where(upper, low[0], low[1]),
         )
-        few = lanes_of(count)
-        ends = []
-        for band, (low, high), cells in ((0, north, corners[0]), (BAND, south, corners[1])):
-            cells = cells if f < 3 else cells[8 * (f - 3) : 8 * (f - 2)]
-            frame = scale * turn(cells, 2 * HALO * min(f, 3), band + HALO)
-            ends.append(
-                choose_side(few, turn(high, LANES - HALO, band), frame, frame, turn(low, 0, band + 3 * HALO))
-            )
-        above = turn(ext[f, here + HALF - count : here + HALF, :], 0, BAND)
-        below = turn(ext[f, here : here + count, :], 0, BAND)
-        ext[f, here - count : here, :] = jnp.where(few < BAND, ends[0], above)
-        ext[f, here + HALF : here + HALF + count, :] = jnp.where(few < BAND, below, ends[1])
 
     side_ice = []
     for dr, first, count in ((-1, MARGIN, HALO), (0, TOP, TILE), (1, TOP + TILE, HALO)):
@@ -351,6 +315,31 @@
         ice[SIDE + TOP + i * HALO : SIDE + TOP + (i + 1) * HALO, :] = side_ice[1]
     ice[SIDE + MARGIN : SIDE + TOP, :] = jnp.where(upper, side_ice[0], side_ice[1])
     ice[SIDE + TOP + HALF : SIDE + TOP + HALF + HALO, :] = jnp.where(upper, side_ice[1], side_ice[2])
+
+
+def model_kernel(
+    fr, ice, middle, thick, drive, obs, first_row, second_row,
+    vel_u, vel_v, sums,
+    ext, visc, vel_a, vel_b, vel_c, coef, small, sems,
+):
+    even = is_even("gy")
+    for f, (field, (first, count)) in enumerate(zip((thick, drive.at[0], drive.at[1], obs.at[0], obs.at[1]), STRIP)):
+        scale = 0.5 if f in (1, 2) else 1.0
+        frames = []
+        for c in range(3):
+            one, two = scale * first_row[c, first : first + count, :], scale * second_row[c, first : first + count, :]
+            frames.append((jnp.where(even, two, one), jnp.where(even, one, two)))
+        for c in range(2):
+            ext[f, MAIN[c] + TOP : MAIN[c] + TOP + TILE, :] = scale * field[:, c * LANES : (c + 1) * LANES]
+            ext[f, MAIN[c] + TOP - count : MAIN[c] + TOP, :] = frames[c][0]
+            ext[f, MAIN[c] + TOP + TILE : MAIN[c] + TOP + TILE + count, :] = frames[c][1]
+        here = SIDE + TOP
+        ext[f, here : here + HALF, :] = middle[f]
+        upper = lanes_of(count) < BAND
+        above = turn(middle[f, HALF - count :, :], 0, BAND)
+        below = turn(middle[f, :count, :], 0, BAND)
+        ext[f, here - count : here, :] = jnp.where(upper, frames[2][0], above)
+        ext[f, here + HALF : here + HALF + count, :] = jnp.where(upper, below, frames[2][1])
 
     def load(ref, part, row, count, *lead):
         return [ref[(*lead, pl.ds(row + tile, count), slice(None))] for tile in part]
@@ -594,9 +583,9 @@
     owned = control.shape[0]
     *edges, parcels = pl.pallas_call(
         pack_kernel,
-        out_shape=[shape(HALF, LANES)] * 2 + [shape(2, 64, LANES)] * 2 + [shape(rows, PARCEL, LANES)],
+        out_shape=[shape(HALF, LANES)] * 2 + [shape(rows, PARCEL, LANES)],
         in_specs=in_smem(1) + [pl.BlockSpec(memory_space=pltpu.HBM)] * 4,
-        out_specs=in_vmem(5),
+        out_specs=in_vmem(3),
         scratch_shapes=[
             pltpu.VMEM((5, TILE, TILE), f32),
             pltpu.VMEM(control.shape, f32),
@@ -606,39 +595,45 @@
         compiler_params=pltpu.CompilerParams(vmem_limit_bytes=PACK_VMEM_LIMIT),
         name="pack",
     )(tile_block, control, *fields)
-    columns_in = swap("gx", *edges[:2])
-    rows_in = swap("gy", *edges[2:])
-    parcels = pl.pallas_call(
-        corners_kernel,
-        out_shape=shape(*parcels.shape),
-        in_specs=in_vmem(3),
-        out_specs=pl.BlockSpec(memory_space=pltpu.VMEM),
+    parcels = lax.all_to_all(parcels, "gy", 0, 0, tiled=True)
+    columns_in = swap("gx", *edges)
+    strips = pl.pallas_call(
+        rows_kernel,
+        out_shape=[shape(3, 64, LANES)] * 2,
+        in_specs=in_vmem(5),
+        out_specs=in_vmem(2),
         compiler_params=params,
-        name="corners",
-    )(parcels, *columns_in)
-    parcels = lax.all_to_all(parcels, "gy", 0, 0, tiled=True)
+        name="rows",
+    )(*fields, *columns_in)
+    rows_in = swap("gy", *strips)
+    prepared = pl.pallas_call(
+        setup_kernel,
+        out_shape=[shape(ALL_ROWS, LANES)] * 2 + [shape(5, HALF, LANES)],
+        in_specs=in_smem(1) + in_vmem(6),
+        out_specs=in_vmem(3),
+        scratch_shapes=[pltpu.VMEM((PATCH, LANES), f32)],
+        compiler_params=params,
+        name="setup",
+    )(ice_mask, parcels, *fields, *columns_in)
 
     vel_u, vel_v, sums = pl.pallas_call(
         model_kernel,
         out_shape=(shape(TILE, TILE), shape(TILE, TILE), shape(cols, rows, PACK // cols, LANES)),
-        in_specs=in_smem(1) + in_vmem(8),
+        in_specs=in_vmem(8),
         out_specs=[pl.BlockSpec(memory_space=pltpu.HBM)] * 2 + in_vmem(1),
         scratch_shapes=[
             pltpu.VMEM((5, ALL_ROWS, LANES), f32),
-            pltpu.VMEM((ALL_ROWS, LANES), f32),
-            pltpu.VMEM((ALL_ROWS, LANES), f32),
             pltpu.VMEM((ALL_ROWS, LANES), f32),
             pltpu.VMEM((2, ALL_ROWS, LANES), f32),
             pltpu.VMEM((2, ALL_ROWS, LANES), f32),
             pltpu.VMEM((2, ALL_ROWS, LANES), f32),
             pltpu.VMEM((14, ALL_ROWS, LANES), f32),
             pltpu.VMEM((CT, LANES), f32),
-            pltpu.VMEM((PATCH, LANES), f32),
             pltpu.SemaphoreType.DMA((4,)),
         ],
         compiler_params=params,
         name="model",
-    )(ice_mask, parcels, *fields, *rows_in, *columns_in)
+    )(*prepared, *fields, *rows_in)
 
     share = (control.shape[0], PACK // cols, LANES)
     sums = lax.all_to_all(sums.reshape(cols * rows, *share[1:]), ("gx", "gy"), 0, 0, tiled=True)

time: 71.2 us -> 66.4 us (0.933)
  waiting for transfers between devices: 7.5 us -> 2.97 us
  blocking collectives: 23.9 us -> 28.4 us
  Pallas kernels: 28 us -> 25.1 us
  starting transfers between devices: 9.6 us -> 8.6 us
  local copies, waits for them, and re-layouts: 0.98 us -> 0.04 us
    all_to_all x1, waiting for transfers between devices: 5.46 us -> 0.79 us  [per_device(): parcels = lax.all_to_all(parcels, 'gy', 0, 0, tiled=True)]
    all_to_all x1, blocking collectives: 15.7 us -> 20.3 us  [per_device(): lax.all_to_all(sums.reshape(cols * rows, *share[1:]), ('gx', 'gy'), 0, 0,...]
    pallas_call x1, Pallas kernels: 22.3 us -> 18.9 us  [per_device(): pl.pallas_call(model_kernel, out_shape=(shape(TILE, TILE), shape(TILE, TI...]
    ppermute x4, starting transfers between devices: 5.13 us -> 3.05 us  [swap(): lax.ppermute(cells, axis, pairs + [(j, i) for i, j in pairs])]
    all_to_all x1, starting transfers between devices: 4.47 us -> 5.55 us  [per_device(): parcels = lax.all_to_all(parcels, 'gy', 0, 0, tiled=True)]
    unnamed x16 -> x14, local copies, waits for them, and re-layouts: 0.98 us -> 0.04 us
    pallas_call x2 -> x3, Pallas kernels: 4.32 us -> 4.88 us  [the longest x1 3.54 us: per_device(): pl.pallas_call(pack_kernel, out_shape=[shape(HALF, LANES)] * 2 + [shape(r...]
  transfers between devices with their start and end apart: 5 -> 5, of which waited for: 3 -> 2; matrix products, arithmetic and copies ran while one was open for 0% -> 0% of each run, Pallas kernels for 0% -> 2%
where the time goes in v7:
time: 66.4 us; the launch traced here: 66 us
  blocking collectives  28.4 us (43%)
  Pallas kernels  25.1 us (38%)
  starting transfers between devices  8.6 us (13%)
  waiting for transfers between devices  2.97 us (4%)
  between operations  0.78 us (1%)
    all_to_all x1, blocking collectives, per_device(): lax.all_to_all(sums.reshape(cols * rows, *share[1:]), ('gx', 'gy'), 0, 0,...  20.3 us
    pallas_call x1, Pallas kernels, per_device(): pl.pallas_call(model_kernel, out_shape=(shape(TILE, TILE), shape(TILE, TI...  18.9 us
    all_to_all x1, blocking collectives, per_device(): lax.all_to_all(parts, 'gx', 0, 0, tiled=True)  8.15 us
    all_to_all x1, starting transfers between devices, per_device(): parcels = lax.all_to_all(parcels, 'gy', 0, 0, tiled=True)  5.55 us
    pallas_call x1, Pallas kernels, per_device(): pl.pallas_call(pack_kernel, out_shape=[shape(HALF, LANES)] * 2 + [shape(r...  3.54 us
    ppermute x4, starting transfers between devices, swap(): lax.ppermute(cells, axis, pairs + [(j, i) for i, j in pairs])  3.05 us
    ppermute x4, waiting for transfers between devices, swap(): lax.ppermute(cells, axis, pairs + [(j, i) for i, j in pairs])  2.18 us
  transfers between devices with their start and end apart: 5, of which 2 were waited for; matrix products, arithmetic and copies ran while one was open for 0% of the time, Pallas kernels for 2%

profile of v7, /device:TPU:0, one launch (start us, length us, event | category | flops | bytes accessed | tf_op | source)
XLA Modules:
  0.0 66.0 jit_solution(15941806690551844043)
XLA Ops:
  0.6 0.0 copy-start
  0.6 0.0 copy-start.1
  0.7 3.5 %pack.1 = (f32[128,128]{1,0:T(8,128)}, f32[128,128]{1,0:T(8,128)}, f32[8,48,128]{2,1,0:T(8,128)}) custom-call(s32[4,8]{1,0:T(4,128)} %bitcast.6, f32[4,4096]{1,0:T(4,128)} %control.1, f32[256,256]{1,0:T(8,128)} %thick.7, f32[2,256,256]{2,1,0:T(8,128)} %drive.7, f32[2,256,256]{2,1,0:T(8,128)} %obs.7), custom_call_target="tpu_custom_call" | custom-call | tf_op jit(solution)/shard_map/pack/pallas_call | solution.py:584
  4.2 0.0 copy-start.2
  4.2 0.0 copy-start.6
  4.2 0.0 copy-start.5
  4.2 5.5 %all-to-all-start = ((f32[8,48,128]{2,1,0:T(8,128)}), f32[8,48,128]{2,1,0:T(8,128)S(1)}, u32[]{:S(2)}, u32[]{:S(2)}) async-start(f32[8,48,128]{2,1,0:T(8,128)} %get-tuple-element.14), calls=%async_computation | async-start | bytes 393216 | tf_op jit(solution)/shard_map/all_to_all | solution.py:598
  9.8 0.0 copy-done.6
  9.8 1.7 %collective-permute-start = (f32[128,128]{1,0:T(8,128)S(1)}, f32[128,128]{1,0:T(8,128)S(1)}, u32[]{:S(2)}, u32[]{:S(2)}) collective-permute-start(f32[128,128]{1,0:T(8,128)S(1)} %copy-done.6), channel_id=1, source_target_pairs={{0,8},{16,24},{8,0},{24,16},{1,9},{17,25},{9,1},{25,17},{2,10},{18... | collective-permute-start | bytes 196616 | tf_op jit(solution)/shard_map/ppermute | solution.py:579
  11.4 0.0 copy-done.5
  11.5 0.7 collective-permute-start.1
  12.1 2.2 %collective-permute-done.first_col = f32[128,128]{1,0:T(8,128)S(1)} collective-permute-done((f32[128,128]{1,0:T(8,128)S(1)}, f32[128,128]{1,0:T(8,128)S(1)}, u32[]{:S(2)}, u32[]{:S(2)}) %collective-permute-start) | collective-permute-done | bytes 65568 | tf_op jit(solution)/shard_map/ppermute | solution.py:579
  14.3 0.0 collective-permute-done.1.second_col
  14.3 0.0 copy-done
  14.3 0.0 copy-done.1
  14.3 0.0 copy-done.2
  14.3 0.1 rows.1
  14.5 0.0 copy-start.4
  14.5 0.1 collective-permute-start.2
  14.5 0.7 %collective-permute-start.3 = (f32[3,64,128]{2,1,0:T(8,128)S(1)}, f32[3,64,128]{2,1,0:T(8,128)S(1)}, u32[]{:S(2)}, u32[]{:S(2)}) collective-permute-start(f32[3,64,128]{2,1,0:T(8,128)S(1)} %get-tuple-element.21), channel_id=1, source_target_pairs={{1,2},{3,4},{5,6},{2,1},{4,3},{6,5},{9,10},{11,12},{13,14},{10,9},... | collective-permute-start | bytes 294920 | tf_op jit(solution)/shard_map/ppermute | solution.py:579
  15.2 0.8 %all-to-all-done.parcels = f32[8,48,128]{2,1,0:T(8,128)S(1)} async-done(((f32[8,48,128]{2,1,0:T(8,128)}), f32[8,48,128]{2,1,0:T(8,128)S(1)}, u32[]{:S(2)}, u32[]{:S(2)}) %all-to-all-start) | async-done | bytes 196640 | tf_op jit(solution)/shard_map/all_to_all | solution.py:598
  16.0 0.0 copy-done.4
  16.0 1.2 %setup.1 = (f32[784,128]{1,0:T(8,128)S(1)}, f32[784,128]{1,0:T(8,128)S(1)}, f32[5,128,128]{2,1,0:T(8,128)S(1)}) custom-call(s32[4,8]{1,0:T(4,128)S(1)} %bitcast.8, f32[8,48,128]{2,1,0:T(8,128)S(1)} %all-to-all-done.parcels, f32[256,256]{1,0:T(8,128)S(1)} %copy-done.2, f32[2,256,256]{2,1,0:T(8,128)S(1)} %copy-done, f32[2,256,256]{2,1,0:T(8,128)S(1)} %copy-done.1, ...), custom_call_target="tpu_custom_call" | custom-call | tf_op jit(solution)/shard_map/setup/pallas_call | solution.py:609
  17.2 0.0 collective-permute-done.2.first_row
  17.2 0.0 collective-permute-done.3.second_row
  17.2 18.9 %model.1 = (f32[256,256]{1,0:T(8,128)}, f32[256,256]{1,0:T(8,128)}, f32[4,8,8,128]{3,2,1,0:T(8,128)S(1)}) custom-call(f32[784,128]{1,0:T(8,128)S(1)} %get-tuple-element.17.fr, f32[784,128]{1,0:T(8,128)S(1)} %get-tuple-element.18.ice, f32[5,128,128]{2,1,0:T(8,128)S(1)} %get-tuple-element.19.middle, f32[256,256]{1,0:T(8,128)S(1)} %copy-done.2, ...), custom_call_target="tpu_custom_call" | custom-call | tf_op jit(solution)/shard_map/model/pallas_call | solution.py:619
  36.1 0.0 copy-start.3
  36.2 20.3 %all_to_all.15.gathered = f32[32,8,128]{2,1,0:T(8,128)S(1)} all-to-all(f32[32,8,128]{2,1,0:T(8,128)S(1)} %bitcast.5), channel_id=1, replica_groups=mesh['gx'=4,'gy'=8] {'gx','gy'}, dimensions={0} | all-to-all | bytes 262144 | tf_op jit(solution)/shard_map/all_to_all | solution.py:639
  56.4 0.0 copy-done.3
  56.4 0.7 %pick.1 = f32[4,4,8,128]{3,2,1,0:T(8,128)S(1)} custom-call(s32[4,8]{1,0:T(4,128)S(1)} %bitcast.7, f32[32,8,128]{2,1,0:T(8,128)S(1)} %all_to_all.15.gathered), custom_call_target="tpu_custom_call" | custom-call | tf_op jit(solution)/shard_map/pick/pallas_call | solution.py:640
  57.1 8.1 %all_to_all.16.parts = f32[4,4,8,128]{3,2,1,0:T(8,128)S(1)} all-to-all(f32[4,4,8,128]{3,2,1,0:T(8,128)S(1)} %pick.1), channel_id=1, replica_groups=mesh['gx'=4,'gy'=8] {'gx'}, dimensions={0} | all-to-all | bytes 131072 | tf_op jit(solution)/shard_map/all_to_all | solution.py:655
  65.3 0.7 %join.1 = f32[4,4096]{1,0:T(4,128)} custom-call(f32[4,4,8,128]{3,2,1,0:T(8,128)S(1)} %all_to_all.16.parts), custom_call_target="tpu_custom_call" | custom-call | tf_op jit(solution)/shard_map/join/pallas_call | solution.py:648
Async XLA Ops:
  0.6 13.7 %copy-start = (f32[2,256,256]{2,1,0:T(8,128)S(1)}, f32[2,256,256]{2,1,0:T(8,128)}, u32[]{:S(2)}) copy-start(f32[2,256,256]{2,1,0:T(8,128)} %drive.7) | copy-start | bytes 1572868
  0.6 13.7 %copy-start.1 = (f32[2,256,256]{2,1,0:T(8,128)S(1)}, f32[2,256,256]{2,1,0:T(8,128)}, u32[]{:S(2)}) copy-start(f32[2,256,256]{2,1,0:T(8,128)} %obs.7) | copy-start | bytes 1572868
  4.2 10.1 %copy-start.2 = (f32[256,256]{1,0:T(8,128)S(1)}, f32[256,256]{1,0:T(8,128)}, u32[]{:S(2)}) copy-start(f32[256,256]{1,0:T(8,128)} %thick.7) | copy-start | bytes 786436
  4.2 5.6 %copy-start.6 = (f32[128,128]{1,0:T(8,128)S(1)}, f32[128,128]{1,0:T(8,128)}, u32[]{:S(2)}) copy-start(f32[128,128]{1,0:T(8,128)} %get-tuple-element.15) | copy-start | bytes 196612
  4.2 7.2 %copy-start.5 = (f32[128,128]{1,0:T(8,128)S(1)}, f32[128,128]{1,0:T(8,128)}, u32[]{:S(2)}) copy-start(f32[128,128]{1,0:T(8,128)} %get-tuple-element.16) | copy-start | bytes 196612
  4.2 11.8 %all-to-all-start = ((f32[8,48,128]{2,1,0:T(8,128)}), f32[8,48,128]{2,1,0:T(8,128)S(1)}, u32[]{:S(2)}, u32[]{:S(2)}) async-start(f32[8,48,128]{2,1,0:T(8,128)} %get-tuple-element.14), calls=%async_computation | async-start | bytes 393216 | tf_op jit(solution)/shard_map/all_to_all | solution.py:598
  9.8 4.5 %collective-permute-start = (f32[128,128]{1,0:T(8,128)S(1)}, f32[128,128]{1,0:T(8,128)S(1)}, u32[]{:S(2)}, u32[]{:S(2)}) collective-permute-start(f32[128,128]{1,0:T(8,128)S(1)} %copy-done.6), channel_id=1, source_target_pairs={{0,8},{16,24},{8,0},{24,16},{1,9},{17,25},{9,1},{25,17},{2,10},{18... | collective-permute-start | bytes 196616 | tf_op jit(solution)/shard_map/ppermute | solution.py:579
  11.5 2.8 %collective-permute-start.1 = (f32[128,128]{1,0:T(8,128)S(1)}, f32[128,128]{1,0:T(8,128)S(1)}, u32[]{:S(2)}, u32[]{:S(2)}) collective-permute-start(f32[128,128]{1,0:T(8,128)S(1)} %copy-done.5), channel_id=1, source_target_pairs={{8,16},{16,8},{9,17},{17,9},{10,18},{18,10},{11,19},{19,11},{12,20... | collective-permute-start | bytes 196616 | tf_op jit(solution)/shard_map/ppermute | solution.py:579
  14.5 1.6 %copy-start.4 = (s32[8,4]{0,1:T(4,128)S(1)}, s32[8,4]{0,1:T(4,128)}, u32[]{:S(2)}) copy-start(s32[8,4]{0,1:T(4,128)} %param.10) | copy-start | bytes 388
  14.5 2.8 %collective-permute-start.2 = (f32[3,64,128]{2,1,0:T(8,128)S(1)}, f32[3,64,128]{2,1,0:T(8,128)S(1)}, u32[]{:S(2)}, u32[]{:S(2)}) collective-permute-start(f32[3,64,128]{2,1,0:T(8,128)S(1)} %get-tuple-element.20), channel_id=1, source_target_pairs={{0,1},{2,3},{4,5},{6,7},{1,0},{3,2},{5,4},{7,6},{8,9},{10,11},{12,... | collective-permute-start | bytes 294920 | tf_op jit(solution)/shard_map/ppermute | solution.py:579
  14.5 2.7 %collective-permute-start.3 = (f32[3,64,128]{2,1,0:T(8,128)S(1)}, f32[3,64,128]{2,1,0:T(8,128)S(1)}, u32[]{:S(2)}, u32[]{:S(2)}) collective-permute-start(f32[3,64,128]{2,1,0:T(8,128)S(1)} %get-tuple-element.21), channel_id=1, source_target_pairs={{1,2},{3,4},{5,6},{2,1},{4,3},{6,5},{9,10},{11,12},{13,14},{10,9},... | collective-permute-start | bytes 294920 | tf_op jit(solution)/shard_map/ppermute | solution.py:579
  36.1 20.3 %copy-start.3 = (s32[8,4,1]{0,2,1:T(1,128)S(1)}, s32[8,4,1]{0,2,1:T(1,128)}, u32[]{:S(2)}) copy-start(s32[8,4,1]{0,2,1:T(1,128)} %param.11) | copy-start | bytes 388

commit v8 on v7

--- a/solution.py
+++ b/solution.py
@@ -25,6 +25,7 @@
 MAIN = (0, ROWS)
 SIDES = (SIDE,)
 BLOCKS = 4
+FACTORS = 10
 AHEAD = 2
 PACK = COARSE // LANES
 VMEM_LIMIT = 40 * 1024 * 1024
@@ -394,26 +395,23 @@
             across, along = e[c] + w[c], s[c] + n[c]
             scale_u.append(mask[c] * inverse(friction[c] + along + 4.0 * across))
             scale_v.append(mask[c] * inverse(friction[c] + across + 4.0 * along))
-        corners = []
-        half = [0.5 * q[c] for c in tiles]
-        for shifted in (
+        turned = [
             shift_west(q_s, lane), shift_west(q_n, lane), shift_east(q_s, lane), shift_east(q_n, lane),
-        ):
-            corners.append([q[c] + 0.5 * shifted[c] for c in tiles])
-            corners.append([half[c] + shifted[c] for c in tiles])
-        return [e, w, s, n, scale_u, scale_v] + corners
-
-    def relax(part, k, around, right, lane):
+        ]
+        return [e, w, s, n, scale_u, scale_v] + turned
+
+    def relax(part, q, k, around, right, lane):
         tiles = range(len(part))
-        e, w, s, n, scale_u, scale_v, sw_u, sw_v, nw_u, nw_v, se_u, se_v, ne_u, ne_v = k
+        e, w, s, n, scale_u, scale_v, q_sw, q_nw, q_se, q_ne = k
         u, u_n, u_s, v, v_n, v_s = around
         to_west_u, to_east_u, to_west_v, to_east_v = [], [], [], []
         for c in tiles:
             u4 = 4.0 * u[c]
-            to_west_u.append(w[c] * u4 + (sw_u[c] * v_s[c] - nw_u[c] * v_n[c]))
-            to_east_u.append(e[c] * u4 + (ne_u[c] * v_n[c] - se_u[c] * v_s[c]))
-            to_west_v.append(w[c] * v[c] + (sw_v[c] * u_s[c] - nw_v[c] * u_n[c]))
-            to_east_v.append(e[c] * v[c] + (ne_v[c] * u_n[c] - se_v[c] * u_s[c]))
+            cross_u, cross_v = q[c] * (v_s[c] - v_n[c]), 0.5 * q[c] * (u_s[c] - u_n[c])
+            to_west_u.append((w[c] * u4 + cross_u) + 0.5 * (q_sw[c] * v_s[c] - q_nw[c] * v_n[c]))
+            to_east_u.append((e[c] * u4 - cross_u) + 0.5 * (q_ne[c] * v_n[c] - q_se[c] * v_s[c]))
+            to_west_v.append((w[c] * v[c] + cross_v) + (q_sw[c] * u_s[c] - q_nw[c] * u_n[c]))
+            to_east_v.append((e[c] * v[c] - cross_v) + (q_ne[c] * u_n[c] - q_se[c] * u_s[c]))
         to_west_u, to_west_v = shift_east(to_west_u, lane), shift_east(to_west_v, lane)
         to_east_u, to_east_v = shift_west(to_east_u, lane), shift_west(to_east_v, lane)
         new_u, new_v = [], []
@@ -428,12 +426,12 @@
         return [(new, (i,), values[i]) for i in range(2)]
 
     def keep(k):
-        return [(coef, (i,), k[i]) for i in range(14)]
+        return [(coef, (i,), k[i]) for i in range(FACTORS)]
 
     def sweep(framed, now, new):
         def read(part, row, count):
-            k = [load(coef, part, row, count, i) for i in range(14)]
-            return k, load_around(part, row, count, now), load_right(part, row, count)
+            k = [load(coef, part, row, count, i) for i in range(FACTORS)]
+            return load(visc, part, row, count), k, load_around(part, row, count, now), load_right(part, row, count)
 
         over_rows(framed, read, lambda part, read, lane: put(new, relax(part, *read, lane)))
 
@@ -449,7 +447,7 @@
 
     def start(part, read, lane):
         k = coefficients(part, read[0], lane)
-        return keep(k) + put(vel_a, relax(part, k, read[2], read[1], lane))
+        return keep(k) + put(vel_a, relax(part, read[0][0], k, read[2], read[1], lane))
 
     over_rows(True, read_thickness, first_viscosity)
     over_rows(True, read_first, first_start)
@@ -524,34 +522,34 @@
     packed = jnp.where(
         lanes_of(PACK) < CT, small[pl.ds(0, PACK, stride=2), :], small[pl.ds(1, PACK, stride=2), :]
     )
-    part = PACK // sums.shape[0]
-    for i in range(sums.shape[0]):
-        for j in range(sums.shape[1]):
-            sums[i, j] = packed[i * part : (i + 1) * part]
+    for j in range(sums.shape[0]):
+        sums[j] = packed
     for copy in copies:
         copy.wait()
 
 
-def pick_kernel(tile_block, gathered, out):
-    owned = out.shape[1]
-    first = lax.axis_index("gy") * owned
+def pick_kernel(tile_block, gathered, own, other, total):
+    owned = own.shape[0]
+    row_tile = lax.axis_index("gy")
+    core = row_tile % 2
+    first = (row_tile - core) * owned
     tile_cols, tile_rows = tile_block.shape
-    total = [jnp.zeros(out.shape[2:], jnp.float32) for _ in range(owned)]
-    for t in range(tile_cols * tile_rows):
-        place = tile_block[t // tile_rows, t % tile_rows] - first
-        cells = gathered[t]
-        total = [total[b] + jnp.where(place == b, cells, 0.0) for b in range(owned)]
-    for b in range(owned):
-        for j in range(out.shape[0]):
-            out[j, b] = total[b]
-
-
-def join_kernel(parts, out):
-    share = parts.shape[2]
-    for i in range(parts.shape[0]):
-        for j in range(share):
-            at = (i * share + j) * LANES
-            out[:, at : at + LANES] = parts[i, :, j, :]
+    total[...] = jnp.zeros_like(total)
+    for t in range(tile_cols * tile_rows // 2):
+        place = tile_block[t // (tile_rows // 2), t % (tile_rows // 2) * 2 + core] - first
+
+        @pl.when((place >= 0) & (place < 2 * owned))
+        def _():
+            total[place] += gathered[t]
+
+    own[...] = total[pl.ds(core * owned, owned)]
+    other[...] = total[pl.ds((1 - core) * owned, owned)]
+
+
+def join_kernel(own, received, out):
+    total = own[...] + received[...]
+    for j in range(PACK):
+        out[:, j * LANES : (j + 1) * LANES] = total[:, j, :]
 
 
 def in_vmem(count):
@@ -618,7 +616,7 @@
 
     vel_u, vel_v, sums = pl.pallas_call(
         model_kernel,
-        out_shape=(shape(TILE, TILE), shape(TILE, TILE), shape(cols, rows, PACK // cols, LANES)),
+        out_shape=(shape(TILE, TILE), shape(TILE, TILE), shape(cols * rows // 2, PACK, LANES)),
         in_specs=in_vmem(8),
         out_specs=[pl.BlockSpec(memory_space=pltpu.HBM)] * 2 + in_vmem(1),
         scratch_shapes=[
@@ -627,7 +625,7 @@
             pltpu.VMEM((2, ALL_ROWS, LANES), f32),
             pltpu.VMEM((2, ALL_ROWS, LANES), f32),
             pltpu.VMEM((2, ALL_ROWS, LANES), f32),
-            pltpu.VMEM((14, ALL_ROWS, LANES), f32),
+            pltpu.VMEM((FACTORS, ALL_ROWS, LANES), f32),
             pltpu.VMEM((CT, LANES), f32),
             pltpu.SemaphoreType.DMA((4,)),
         ],
@@ -635,24 +633,26 @@
         name="model",
     )(*prepared, *fields, *rows_in)
 
-    share = (control.shape[0], PACK // cols, LANES)
-    sums = lax.all_to_all(sums.reshape(cols * rows, *share[1:]), ("gx", "gy"), 0, 0, tiled=True)
-    parts = pl.pallas_call(
+    same_core = [[i * rows + j for i in range(cols) for j in range(core, rows, 2)] for core in range(2)]
+    sums = lax.all_to_all(sums, ("gx", "gy"), 0, 0, tiled=True, axis_index_groups=same_core)
+    own, other = pl.pallas_call(
         pick_kernel,
-        out_shape=shape(cols, *share),
+        out_shape=[shape(owned, PACK, LANES)] * 2,
         in_specs=in_smem(1) + in_vmem(1),
-        out_specs=pl.BlockSpec(memory_space=pltpu.VMEM),
+        out_specs=in_vmem(2),
+        scratch_shapes=[pltpu.VMEM((2 * owned, PACK, LANES), f32)],
         compiler_params=params,
         name="pick",
     )(tile_block, sums)
+    received = lax.ppermute(other, "gy", [(j, j ^ 1) for j in range(rows)])
     gradient = pl.pallas_call(
         join_kernel,
         out_shape=shape(*control.shape),
-        in_specs=in_vmem(1),
+        in_specs=in_vmem(2),
         out_specs=pl.BlockSpec(memory_space=pltpu.VMEM),
         compiler_params=params,
         name="join",
-    )(lax.all_to_all(parts, "gx", 0, 0, tiled=True))
+    )(own, received)
     return vel_u, vel_v, gradient
 
 

time: 66.4 us -> 63.5 us (0.956)
  blocking collectives: 28.4 us -> 23.6 us
  Pallas kernels: 25.1 us -> 26.2 us
  waiting for transfers between devices: 2.97 us -> 3.99 us
    all_to_all x2 -> x1, blocking collectives: 28.4 us -> 23.6 us  [per_device(): lax.all_to_all(sums, ('gx', 'gy'), 0, 0, tiled=True, axis_index_groups=sa...]
    ppermute x0 -> x1, waiting for transfers between devices: none -> 1.24 us  [per_device(): received = lax.ppermute(other, 'gy', [(j, j ^ 1) for j in range(rows)])]
    pallas_call x1, Pallas kernels: 18.9 us -> 19.8 us  [per_device(): pl.pallas_call(model_kernel, out_shape=(shape(TILE, TILE), shape(TILE, TI...]
  transfers between devices with their start and end apart: 5 -> 6, of which waited for: 2 -> 3; matrix products, arithmetic and copies ran while one was open for 0% -> 0% of each run, Pallas kernels for 2% -> 2%
where the time goes in v8:
time: 63.5 us; the launch traced here: 63.3 us
  Pallas kernels  26.2 us (41%)
  blocking collectives  23.6 us (37%)
  starting transfers between devices  8.66 us (14%)
  waiting for transfers between devices  3.99 us (6%)
  between operations  0.79 us (1%)
    all_to_all x1, blocking collectives, per_device(): lax.all_to_all(sums, ('gx', 'gy'), 0, 0, tiled=True, axis_index_groups=sa...  23.6 us
    pallas_call x1, Pallas kernels, per_device(): pl.pallas_call(model_kernel, out_shape=(shape(TILE, TILE), shape(TILE, TI...  19.8 us
    all_to_all x1, starting transfers between devices, per_device(): parcels = lax.all_to_all(parcels, 'gy', 0, 0, tiled=True)  5.31 us
    pallas_call x1, Pallas kernels, per_device(): pl.pallas_call(pack_kernel, out_shape=[shape(HALF, LANES)] * 2 + [shape(r...  3.66 us
    ppermute x4, starting transfers between devices, swap(): lax.ppermute(cells, axis, pairs + [(j, i) for i, j in pairs])  3.28 us
    ppermute x4, waiting for transfers between devices, swap(): lax.ppermute(cells, axis, pairs + [(j, i) for i, j in pairs])  2.04 us
  transfers between devices with their start and end apart: 6, of which 3 were waited for; matrix products, arithmetic and copies ran while one was open for 0% of the time, Pallas kernels for 2%

profile of v8, /device:TPU:0, one launch (start us, length us, event | category | flops | bytes accessed | tf_op | source)
XLA Modules:
  0.0 63.3 jit_solution(11459539084616273206)
XLA Ops:
  0.6 0.0 copy-start
  0.6 0.0 copy-start.1
  0.7 3.7 %pack.1 = (f32[128,128]{1,0:T(8,128)}, f32[128,128]{1,0:T(8,128)}, f32[8,48,128]{2,1,0:T(8,128)}) custom-call(s32[4,8]{1,0:T(4,128)} %bitcast.4, f32[4,4096]{1,0:T(4,128)} %control.1, f32[256,256]{1,0:T(8,128)} %thick.7, f32[2,256,256]{2,1,0:T(8,128)} %drive.7, f32[2,256,256]{2,1,0:T(8,128)} %obs.7), custom_call_target="tpu_custom_call" | custom-call | tf_op jit(solution)/shard_map/pack/pallas_call | solution.py:582
  4.3 0.0 copy-start.2
  4.3 0.0 copy-start.6
  4.3 0.0 copy-start.5
  4.3 5.3 %all-to-all-start = ((f32[8,48,128]{2,1,0:T(8,128)}), f32[8,48,128]{2,1,0:T(8,128)S(1)}, u32[]{:S(2)}, u32[]{:S(2)}) async-start(f32[8,48,128]{2,1,0:T(8,128)} %get-tuple-element.16), calls=%async_computation | async-start | bytes 393216 | tf_op jit(solution)/shard_map/all_to_all | solution.py:596
  9.7 0.0 copy-done.6
  9.7 1.9 %collective-permute-start = (f32[128,128]{1,0:T(8,128)S(1)}, f32[128,128]{1,0:T(8,128)S(1)}, u32[]{:S(2)}, u32[]{:S(2)}) collective-permute-start(f32[128,128]{1,0:T(8,128)S(1)} %copy-done.6), channel_id=1, source_target_pairs={{0,8},{16,24},{8,0},{24,16},{1,9},{17,25},{9,1},{25,17},{2,10},{18... | collective-permute-start | bytes 196616 | tf_op jit(solution)/shard_map/ppermute | solution.py:577
  11.6 0.0 copy-done.5
  11.6 0.7 %collective-permute-start.1 = (f32[128,128]{1,0:T(8,128)S(1)}, f32[128,128]{1,0:T(8,128)S(1)}, u32[]{:S(2)}, u32[]{:S(2)}) collective-permute-start(f32[128,128]{1,0:T(8,128)S(1)} %copy-done.5), channel_id=1, source_target_pairs={{8,16},{16,8},{9,17},{17,9},{10,18},{18,10},{11,19},{19,11},{12,20... | collective-permute-start | bytes 196616 | tf_op jit(solution)/shard_map/ppermute | solution.py:577
  12.2 2.0 %collective-permute-done.first_col = f32[128,128]{1,0:T(8,128)S(1)} collective-permute-done((f32[128,128]{1,0:T(8,128)S(1)}, f32[128,128]{1,0:T(8,128)S(1)}, u32[]{:S(2)}, u32[]{:S(2)}) %collective-permute-start) | collective-permute-done | bytes 65568 | tf_op jit(solution)/shard_map/ppermute | solution.py:577
  14.2 0.0 collective-permute-done.1.second_col
  14.3 0.0 copy-done
  14.3 0.0 copy-done.1
  14.3 0.0 copy-done.2
  14.3 0.1 rows.1
  14.4 0.0 copy-start.4
  14.4 0.1 collective-permute-start.2
  14.5 0.7 %collective-permute-start.3 = (f32[3,64,128]{2,1,0:T(8,128)S(1)}, f32[3,64,128]{2,1,0:T(8,128)S(1)}, u32[]{:S(2)}, u32[]{:S(2)}) collective-permute-start(f32[3,64,128]{2,1,0:T(8,128)S(1)} %get-tuple-element.23), channel_id=1, source_target_pairs={{1,2},{3,4},{5,6},{2,1},{4,3},{6,5},{9,10},{11,12},{13,14},{10,9},... | collective-permute-start | bytes 294920 | tf_op jit(solution)/shard_map/ppermute | solution.py:577
  15.2 0.7 %all-to-all-done.parcels = f32[8,48,128]{2,1,0:T(8,128)S(1)} async-done(((f32[8,48,128]{2,1,0:T(8,128)}), f32[8,48,128]{2,1,0:T(8,128)S(1)}, u32[]{:S(2)}, u32[]{:S(2)}) %all-to-all-start) | async-done | bytes 196640 | tf_op jit(solution)/shard_map/all_to_all | solution.py:596
  15.9 0.0 copy-done.4
  15.9 1.2 %setup.1 = (f32[784,128]{1,0:T(8,128)S(1)}, f32[784,128]{1,0:T(8,128)S(1)}, f32[5,128,128]{2,1,0:T(8,128)S(1)}) custom-call(s32[4,8]{1,0:T(4,128)S(1)} %bitcast.6, f32[8,48,128]{2,1,0:T(8,128)S(1)} %all-to-all-done.parcels, f32[256,256]{1,0:T(8,128)S(1)} %copy-done.2, f32[2,256,256]{2,1,0:T(8,128)S(1)} %copy-done, f32[2,256,256]{2,1,0:T(8,128)S(1)} %copy-done.1, ...), custom_call_target="tpu_custom_call" | custom-call | tf_op jit(solution)/shard_map/setup/pallas_call | solution.py:607
  17.1 0.0 collective-permute-done.2.first_row
  17.1 0.0 collective-permute-done.3.second_row
  17.1 19.8 %model.1 = (f32[256,256]{1,0:T(8,128)}, f32[256,256]{1,0:T(8,128)}, f32[16,32,128]{2,1,0:T(8,128)S(1)}) custom-call(f32[784,128]{1,0:T(8,128)S(1)} %get-tuple-element.19.fr, f32[784,128]{1,0:T(8,128)S(1)} %get-tuple-element.20.ice, f32[5,128,128]{2,1,0:T(8,128)S(1)} %get-tuple-element.21.middle, f32[256,256]{1,0:T(8,128)S(1)} %copy-done.2, ...), custom_call_target="tpu_custom_call" | custom-call | tf_op jit(solution)/shard_map/model/pallas_call | solution.py:617
  36.9 0.0 copy-start.3
  36.9 23.6 %all_to_all.10.gathered = f32[16,32,128]{2,1,0:T(8,128)S(1)} all-to-all(f32[16,32,128]{2,1,0:T(8,128)S(1)} %get-tuple-element.26), channel_id=1, replica_groups={{0,2,4,6,8,10,12,14,16,18,20,22,24,26,28,30},{1,3,5,7,9,11,13,15,17,19,..., dimensions={0} | all-to-all | bytes 524288 | tf_op jit(solution)/shard_map/all_to_all | solution.py:637
  60.5 0.0 copy-done.3
  60.5 0.8 %pick.1 = (f32[4,32,128]{2,1,0:T(8,128)S(1)}, f32[4,32,128]{2,1,0:T(8,128)S(1)}) custom-call(s32[4,8]{1,0:T(4,128)S(1)} %bitcast.5, f32[16,32,128]{2,1,0:T(8,128)S(1)} %all_to_all.10.gathered), custom_call_target="tpu_custom_call" | custom-call | tf_op jit(solution)/shard_map/pick/pallas_call | solution.py:638
  61.3 0.1 collective-permute-start.4
  61.4 1.2 %collective-permute-done.4.received = f32[4,32,128]{2,1,0:T(8,128)S(1)} collective-permute-done((f32[4,32,128]{2,1,0:T(8,128)S(1)}, f32[4,32,128]{2,1,0:T(8,128)S(1)}, u32[]{:S(2)}, u32[]{:S(2)}) %collective-permute-start.4) | collective-permute-done | bytes 65568 | tf_op jit(solution)/shard_map/ppermute | solution.py:647
  62.6 0.7 %join.1 = f32[4,4096]{1,0:T(4,128)} custom-call(f32[4,32,128]{2,1,0:T(8,128)S(1)} %get-tuple-element.27.own, f32[4,32,128]{2,1,0:T(8,128)S(1)} %collective-permute-done.4.received), custom_call_target="tpu_custom_call" | custom-call | tf_op jit(solution)/shard_map/join/pallas_call | solution.py:648
Async XLA Ops:
  0.6 13.6 %copy-start = (f32[2,256,256]{2,1,0:T(8,128)S(1)}, f32[2,256,256]{2,1,0:T(8,128)}, u32[]{:S(2)}) copy-start(f32[2,256,256]{2,1,0:T(8,128)} %drive.7) | copy-start | bytes 1572868
  0.6 13.6 %copy-start.1 = (f32[2,256,256]{2,1,0:T(8,128)S(1)}, f32[2,256,256]{2,1,0:T(8,128)}, u32[]{:S(2)}) copy-start(f32[2,256,256]{2,1,0:T(8,128)} %obs.7) | copy-start | bytes 1572868
  4.3 9.9 %copy-start.2 = (f32[256,256]{1,0:T(8,128)S(1)}, f32[256,256]{1,0:T(8,128)}, u32[]{:S(2)}) copy-start(f32[256,256]{1,0:T(8,128)} %thick.7) | copy-start | bytes 786436
  4.3 5.3 %copy-start.6 = (f32[128,128]{1,0:T(8,128)S(1)}, f32[128,128]{1,0:T(8,128)}, u32[]{:S(2)}) copy-start(f32[128,128]{1,0:T(8,128)} %get-tuple-element.17) | copy-start | bytes 196612
  4.3 7.2 %copy-start.5 = (f32[128,128]{1,0:T(8,128)S(1)}, f32[128,128]{1,0:T(8,128)}, u32[]{:S(2)}) copy-start(f32[128,128]{1,0:T(8,128)} %get-tuple-element.18) | copy-start | bytes 196612
  4.3 11.5 %all-to-all-start = ((f32[8,48,128]{2,1,0:T(8,128)}), f32[8,48,128]{2,1,0:T(8,128)S(1)}, u32[]{:S(2)}, u32[]{:S(2)}) async-start(f32[8,48,128]{2,1,0:T(8,128)} %get-tuple-element.16), calls=%async_computation | async-start | bytes 393216 | tf_op jit(solution)/shard_map/all_to_all | solution.py:596
  9.7 4.6 %collective-permute-start = (f32[128,128]{1,0:T(8,128)S(1)}, f32[128,128]{1,0:T(8,128)S(1)}, u32[]{:S(2)}, u32[]{:S(2)}) collective-permute-start(f32[128,128]{1,0:T(8,128)S(1)} %copy-done.6), channel_id=1, source_target_pairs={{0,8},{16,24},{8,0},{24,16},{1,9},{17,25},{9,1},{25,17},{2,10},{18... | collective-permute-start | bytes 196616 | tf_op jit(solution)/shard_map/ppermute | solution.py:577
  11.6 2.7 %collective-permute-start.1 = (f32[128,128]{1,0:T(8,128)S(1)}, f32[128,128]{1,0:T(8,128)S(1)}, u32[]{:S(2)}, u32[]{:S(2)}) collective-permute-start(f32[128,128]{1,0:T(8,128)S(1)} %copy-done.5), channel_id=1, source_target_pairs={{8,16},{16,8},{9,17},{17,9},{10,18},{18,10},{11,19},{19,11},{12,20... | collective-permute-start | bytes 196616 | tf_op jit(solution)/shard_map/ppermute | solution.py:577
  14.4 1.5 %copy-start.4 = (s32[8,4]{0,1:T(4,128)S(1)}, s32[8,4]{0,1:T(4,128)}, u32[]{:S(2)}) copy-start(s32[8,4]{0,1:T(4,128)} %param.10) | copy-start | bytes 388
  14.4 2.7 %collective-permute-start.2 = (f32[3,64,128]{2,1,0:T(8,128)S(1)}, f32[3,64,128]{2,1,0:T(8,128)S(1)}, u32[]{:S(2)}, u32[]{:S(2)}) collective-permute-start(f32[3,64,128]{2,1,0:T(8,128)S(1)} %get-tuple-element.22), channel_id=1, source_target_pairs={{0,1},{2,3},{4,5},{6,7},{1,0},{3,2},{5,4},{7,6},{8,9},{10,11},{12,... | collective-permute-start | bytes 294920 | tf_op jit(solution)/shard_map/ppermute | solution.py:577
  14.5 2.6 %collective-permute-start.3 = (f32[3,64,128]{2,1,0:T(8,128)S(1)}, f32[3,64,128]{2,1,0:T(8,128)S(1)}, u32[]{:S(2)}, u32[]{:S(2)}) collective-permute-start(f32[3,64,128]{2,1,0:T(8,128)S(1)} %get-tuple-element.23), channel_id=1, source_target_pairs={{1,2},{3,4},{5,6},{2,1},{4,3},{6,5},{9,10},{11,12},{13,14},{10,9},... | collective-permute-start | bytes 294920 | tf_op jit(solution)/shard_map/ppermute | solution.py:577
  36.9 23.6 %copy-start.3 = (s32[8,4,1]{0,2,1:T(1,128)S(1)}, s32[8,4,1]{0,2,1:T(1,128)}, u32[]{:S(2)}) copy-start(s32[8,4,1]{0,2,1:T(1,128)} %param.11) | copy-start | bytes 388
  61.3 1.3 %collective-permute-start.4 = (f32[4,32,128]{2,1,0:T(8,128)S(1)}, f32[4,32,128]{2,1,0:T(8,128)S(1)}, u32[]{:S(2)}, u32[]{:S(2)}) collective-permute-start(f32[4,32,128]{2,1,0:T(8,128)S(1)} %get-tuple-element.28), channel_id=1, source_target_pairs={{0,1},{1,0},{2,3},{3,2},{4,5},{5,4},{6,7},{7,6},{8,9},{9,8},{10,11... | collective-permute-start | bytes 196616 | tf_op jit(solution)/shard_map/ppermute | solution.py:647

commit v9 on v8

--- a/solution.py
+++ b/solution.py
@@ -25,7 +25,7 @@
 MAIN = (0, ROWS)
 SIDES = (SIDE,)
 BLOCKS = 4
-FACTORS = 10
+FACTORS = 14
 AHEAD = 2
 PACK = COARSE // LANES
 VMEM_LIMIT = 40 * 1024 * 1024
@@ -90,32 +90,27 @@
     lax.fori_loop(0, tile_rows, spread, 0)
 
 
-def pack_kernel(
-    tile_block, control, thick, drive, obs, first_col, second_col, parcels,
-    held, held_control, owned_blocks, sems,
-):
-    copies = [pltpu.make_async_copy(control, held_control, sems.at[5])]
-    for f, field in enumerate((thick, drive.at[0], drive.at[1], obs.at[0], obs.at[1])):
-        copies.append(pltpu.make_async_copy(field, held.at[f], sems.at[f]))
-    for copy in copies:
-        copy.start()
+def parcels_kernel(tile_block, control, parcels, held, owned_blocks, sem):
+    copy = pltpu.make_async_copy(control, held, sem)
+    copy.start()
     parcels[...] = jnp.zeros_like(parcels)
-    copies[0].wait()
+    copy.wait()
     for j in range(PACK):
-        owned_blocks[:, j, :] = held_control[:, j * LANES : (j + 1) * LANES]
+        owned_blocks[:, j, :] = held[:, j * LANES : (j + 1) * LANES]
     fill_parcels(tile_block, owned_blocks, parcels)
 
+
+def columns_kernel(thick, drive, obs, first_col, second_col):
     lane = lanes_of(HALF)
     left = jnp.zeros((HALF, LANES), jnp.float32)
     right = jnp.zeros((HALF, LANES), jnp.float32)
-    for f, (first, count) in enumerate(STRIP):
-        copies[1 + f].wait()
+    for field, (first, count) in zip((thick, drive.at[0], drive.at[1], obs.at[0], obs.at[1]), STRIP):
         for part in range(2):
             rows = slice(part * HALF, (part + 1) * HALF)
             start = part * BAND + first
             inside = (lane >= start) & (lane < start + count)
-            left = jnp.where(inside, turn(held[f, rows, :LANES], 0, start), left)
-            right = jnp.where(inside, turn(held[f, rows, LANES:], LANES - count, start), right)
+            left = jnp.where(inside, turn(field[rows, :LANES], 0, start), left)
+            right = jnp.where(inside, turn(field[rows, LANES:], LANES - count, start), right)
     even = is_even("gx")
     first_col[...] = jnp.where(even, right, left)
     second_col[...] = jnp.where(even, left, right)
@@ -354,9 +349,12 @@
     def read_thickness(part, row, count):
         return load(ext, part, row, count, 0)
 
+    def keep_viscosity(q, lane):
+        return [(visc, (0,), q), (visc, (1,), shift_west(q, lane)), (visc, (2,), shift_east(q, lane))]
+
     def first_viscosity(part, thickness, lane):
         factor = 0.25 * visc_scale * strain_floor ** (-1.0 / 3.0)
-        return [(visc, (), [factor * t for t in thickness])]
+        return keep_viscosity([factor * t for t in thickness], lane)
 
     def read_viscosity(part, row, count):
         return read_thickness(part, row, count), load_around(part, row, count, vel_b)
@@ -372,22 +370,21 @@
             shear = uy + vx
             strain = 0.25 * (ux * (ux + vy) + vy * vy) + (0.0625 * (shear * shear) + strain_floor)
             result.append((0.25 * visc_scale) * thickness[c] * jnp.exp(jnp.log(strain) * (-1.0 / 3.0)))
-        return [(visc, (), result)]
+        return keep_viscosity(result, lane)
 
     def inverse(x):
         near = pl.reciprocal(x, approx=True)
         return near * (2.0 - x * near)
 
     def read_coefficients(part, row, count):
-        around = [load(visc, part, r, count) for r in (row, row - 1, row + 1)]
+        around = [load(visc, part, r, count, i) for i in range(3) for r in (row, row - 1, row + 1)]
         return around + [load(fr, part, row, count), load(ice, part, row, count)]
 
-    def coefficients(part, read, lane):
+    def coefficients(part, read):
         tiles = range(len(part))
-        q, q_n, q_s, friction, mask = read
-        q_w = shift_west(q, lane)
+        q, q_n, q_s, q_w, q_nw, q_sw, q_e, q_ne, q_se, friction, mask = read
         w = [q[c] + q_w[c] for c in tiles]
-        e = shift_east(w, lane)
+        e = [q[c] + q_e[c] for c in tiles]
         s = [q[c] + q_s[c] for c in tiles]
         n = [q[c] + q_n[c] for c in tiles]
         scale_u, scale_v = [], []
@@ -395,23 +392,24 @@
             across, along = e[c] + w[c], s[c] + n[c]
             scale_u.append(mask[c] * inverse(friction[c] + along + 4.0 * across))
             scale_v.append(mask[c] * inverse(friction[c] + across + 4.0 * along))
-        turned = [
-            shift_west(q_s, lane), shift_west(q_n, lane), shift_east(q_s, lane), shift_east(q_n, lane),
-        ]
-        return [e, w, s, n, scale_u, scale_v] + turned
-
-    def relax(part, q, k, around, right, lane):
+        corners = []
+        half = [0.5 * q[c] for c in tiles]
+        for shifted in (q_sw, q_nw, q_se, q_ne):
+            corners.append([q[c] + 0.5 * shifted[c] for c in tiles])
+            corners.append([half[c] + shifted[c] for c in tiles])
+        return [e, w, s, n, scale_u, scale_v] + corners
+
+    def relax(part, k, around, right, lane):
         tiles = range(len(part))
-        e, w, s, n, scale_u, scale_v, q_sw, q_nw, q_se, q_ne = k
+        e, w, s, n, scale_u, scale_v, sw_u, sw_v, nw_u, nw_v, se_u, se_v, ne_u, ne_v = k
         u, u_n, u_s, v, v_n, v_s = around
         to_west_u, to_east_u, to_west_v, to_east_v = [], [], [], []
         for c in tiles:
             u4 = 4.0 * u[c]
-            cross_u, cross_v = q[c] * (v_s[c] - v_n[c]), 0.5 * q[c] * (u_s[c] - u_n[c])
-            to_west_u.append((w[c] * u4 + cross_u) + 0.5 * (q_sw[c] * v_s[c] - q_nw[c] * v_n[c]))
-            to_east_u.append((e[c] * u4 - cross_u) + 0.5 * (q_ne[c] * v_n[c] - q_se[c] * v_s[c]))
-            to_west_v.append((w[c] * v[c] + cross_v) + (q_sw[c] * u_s[c] - q_nw[c] * u_n[c]))
-            to_east_v.append((e[c] * v[c] - cross_v) + (q_ne[c] * u_n[c] - q_se[c] * u_s[c]))
+            to_west_u.append(w[c] * u4 + (sw_u[c] * v_s[c] - nw_u[c] * v_n[c]))
+            to_east_u.append(e[c] * u4 + (ne_u[c] * v_n[c] - se_u[c] * v_s[c]))
+            to_west_v.append(w[c] * v[c] + (sw_v[c] * u_s[c] - nw_v[c] * u_n[c]))
+            to_east_v.append(e[c] * v[c] + (ne_v[c] * u_n[c] - se_v[c] * u_s[c]))
         to_west_u, to_west_v = shift_east(to_west_u, lane), shift_east(to_west_v, lane)
         to_east_u, to_east_v = shift_west(to_east_u, lane), shift_west(to_east_v, lane)
         new_u, new_v = [], []
@@ -431,7 +429,7 @@
     def sweep(framed, now, new):
         def read(part, row, count):
             k = [load(coef, part, row, count, i) for i in range(FACTORS)]
-            return load(visc, part, row, count), k, load_around(part, row, count, now), load_right(part, row, count)
+            return k, load_around(part, row, count, now), load_right(part, row, count)
 
         over_rows(framed, read, lambda part, read, lane: put(new, relax(part, *read, lane)))
 
@@ -439,15 +437,15 @@
         return read_coefficients(part, row, count), load_right(part, row, count)
 
     def first_start(part, read, lane):
-        k = coefficients(part, read[0], lane)
+        k = coefficients(part, read[0])
         return keep(k) + put(vel_a, [[a * b for a, b in zip(k[4 + i], read[1][i])] for i in range(2)])
 
     def read_start(part, row, count):
         return (*read_first(part, row, count), load_around(part, row, count, vel_b))
 
     def start(part, read, lane):
-        k = coefficients(part, read[0], lane)
-        return keep(k) + put(vel_a, relax(part, read[0][0], k, read[2], read[1], lane))
+        k = coefficients(part, read[0])
+        return keep(k) + put(vel_a, relax(part, k, read[2], read[1], lane))
 
     over_rows(True, read_thickness, first_viscosity)
     over_rows(True, read_first, first_start)
@@ -503,11 +501,11 @@
 
     def gradient(part, read, lane):
         u, v, lu, lv, friction = read
-        return [(visc, (), [-2.0 * friction[c] * (u[c] * lu[c] + v[c] * lv[c]) for c in range(len(part))])]
+        return [(visc, (0,), [-2.0 * friction[c] * (u[c] * lu[c] + v[c] * lv[c]) for c in range(len(part))])]
 
     over_rows(False, read_gradient, gradient)
-    join_parts(visc, ((),), False)
-    down = [sum(visc[pl.ds(MAIN[c] + TOP + j, CT, stride=4), :] for j in range(4)) for c in range(2)]
+    join_parts(visc, ((0,),), False)
+    down = [sum(visc[0, pl.ds(MAIN[c] + TOP + j, CT, stride=4), :] for j in range(4)) for c in range(2)]
     k = lax.broadcasted_iota(jnp.int32, (LANES, LANES), 0)
     l = lanes_of(LANES) % CT
     total = jnp.zeros((CT, LANES), jnp.float32)
@@ -579,21 +577,28 @@
 
     fields = thickness, driving, observed
     owned = control.shape[0]
-    *edges, parcels = pl.pallas_call(
-        pack_kernel,
-        out_shape=[shape(HALF, LANES)] * 2 + [shape(rows, PARCEL, LANES)],
-        in_specs=in_smem(1) + [pl.BlockSpec(memory_space=pltpu.HBM)] * 4,
-        out_specs=in_vmem(3),
+    parcels = pl.pallas_call(
+        parcels_kernel,
+        out_shape=shape(rows, PARCEL, LANES),
+        in_specs=in_smem(1) + [pl.BlockSpec(memory_space=pltpu.HBM)],
+        out_specs=pl.BlockSpec(memory_space=pltpu.VMEM),
         scratch_shapes=[
-            pltpu.VMEM((5, TILE, TILE), f32),
             pltpu.VMEM(control.shape, f32),
             pltpu.VMEM((owned, PACK, LANES), f32),
-            pltpu.SemaphoreType.DMA((6,)),
+            pltpu.SemaphoreType.DMA,
         ],
         compiler_params=pltpu.CompilerParams(vmem_limit_bytes=PACK_VMEM_LIMIT),
-        name="pack",
-    )(tile_block, control, *fields)
+        name="parcels",
+    )(tile_block, control)
     parcels = lax.all_to_all(parcels, "gy", 0, 0, tiled=True)
+    edges = pl.pallas_call(
+        columns_kernel,
+        out_shape=[shape(HALF, LANES)] * 2,
+        in_specs=in_vmem(3),
+        out_specs=in_vmem(2),
+        compiler_params=params,
+        name="columns",
+    )(*fields)
     columns_in = swap("gx", *edges)
     strips = pl.pallas_call(
         rows_kernel,
@@ -621,7 +626,7 @@
         out_specs=[pl.BlockSpec(memory_space=pltpu.HBM)] * 2 + in_vmem(1),
         scratch_shapes=[
             pltpu.VMEM((5, ALL_ROWS, LANES), f32),
-            pltpu.VMEM((ALL_ROWS, LANES), f32),
+            pltpu.VMEM((3, ALL_ROWS, LANES), f32),
             pltpu.VMEM((2, ALL_ROWS, LANES), f32),
             pltpu.VMEM((2, ALL_ROWS, LANES), f32),
             pltpu.VMEM((2, ALL_ROWS, LANES), f32),

time: 63.5 us -> 63.2 us (level)
  Pallas kernels: 26.2 us -> 23.8 us
  local copies, waits for them, and re-layouts: 0.04 us -> 2.01 us
  blocking collectives: 23.6 us -> 24.4 us
    pallas_call x1, Pallas kernels: 19.8 us -> 17.8 us  [per_device(): pl.pallas_call(model_kernel, out_shape=(shape(TILE, TILE), shape(TILE, TI...]
    unnamed x14, local copies, waits for them, and re-layouts: 0.04 us -> 2.01 us
    all_to_all x1, blocking collectives: 23.6 us -> 24.4 us  [per_device(): lax.all_to_all(sums, ('gx', 'gy'), 0, 0, tiled=True, axis_index_groups=sa...]
    all_to_all x1, waiting for transfers between devices: 0.71 us -> 0.01 us  [per_device(): parcels = lax.all_to_all(parcels, 'gy', 0, 0, tiled=True)]
    pallas_call x1 -> x2, Pallas kernels: 3.66 us -> 3.26 us  [the longest x1 2.89 us: per_device(): pl.pallas_call(parcels_kernel, out_shape=shape(rows, PARCEL, LANES), in_s...]
  transfers between devices with their start and end apart: 6 -> 6, of which waited for: 3 -> 2; matrix products, arithmetic and copies ran while one was open for 0% -> 0% of each run, Pallas kernels for 2% -> 3%
where the time goes in v9:
time: 63.2 us; the launch traced here: 62.8 us
  blocking collectives  24.4 us (39%)
  Pallas kernels  23.8 us (38%)
  starting transfers between devices  8.45 us (13%)
  waiting for transfers between devices  3.37 us (5%)
  local copies, waits for them, and re-layouts  2.01 us (3%)
  between operations  0.8 us (1%)
    all_to_all x1, blocking collectives, per_device(): lax.all_to_all(sums, ('gx', 'gy'), 0, 0, tiled=True, axis_index_groups=sa...  24.4 us
    pallas_call x1, Pallas kernels, per_device(): pl.pallas_call(model_kernel, out_shape=(shape(TILE, TILE), shape(TILE, TI...  17.8 us
    all_to_all x1, starting transfers between devices, per_device(): parcels = lax.all_to_all(parcels, 'gy', 0, 0, tiled=True)  5.21 us
    ppermute x4, starting transfers between devices, swap(): lax.ppermute(cells, axis, pairs + [(j, i) for i, j in pairs])  3.17 us
    pallas_call x1, Pallas kernels, per_device(): pl.pallas_call(parcels_kernel, out_shape=shape(rows, PARCEL, LANES), in_s...  2.89 us
    ppermute x4, waiting for transfers between devices, swap(): lax.ppermute(cells, axis, pairs + [(j, i) for i, j in pairs])  2.12 us
    unnamed x14, local copies, waits for them, and re-layouts  2.01 us
  transfers between devices with their start and end apart: 6, of which 2 were waited for; matrix products, arithmetic and copies ran while one was open for 0% of the time, Pallas kernels for 3%

profile of v9, /device:TPU:0, one launch (start us, length us, event | category | flops | bytes accessed | tf_op | source)
XLA Modules:
  0.0 62.8 jit_solution(13370345717141126776)
XLA Ops:
  0.6 0.0 copy-start
  0.6 2.9 %parcels.1 = f32[8,48,128]{2,1,0:T(8,128)} custom-call(s32[4,8]{1,0:T(4,128)} %bitcast.4, f32[4,4096]{1,0:T(4,128)} %control.1), custom_call_target="tpu_custom_call" | custom-call | tf_op jit(solution)/shard_map/parcels/pallas_call | solution.py:580
  3.5 5.2 %all-to-all-start = ((f32[8,48,128]{2,1,0:T(8,128)}), f32[8,48,128]{2,1,0:T(8,128)S(1)}, u32[]{:S(2)}, u32[]{:S(2)}) async-start(f32[8,48,128]{2,1,0:T(8,128)} %parcels.1), calls=%async_computation | async-start | bytes 393216 | tf_op jit(solution)/shard_map/all_to_all | solution.py:593
  8.7 0.0 copy-done
  8.7 0.0 copy-start.1
  8.8 1.0 %copy-done.1 = f32[2,256,256]{2,1,0:T(8,128)S(1)} copy-done((f32[2,256,256]{2,1,0:T(8,128)S(1)}, f32[2,256,256]{2,1,0:T(8,128)}, u32[]{:S(2)}) %copy-start.1) | copy-done | bytes 524312
  9.8 0.0 copy-start.3
  9.8 0.9 %copy-done.3 = f32[256,256]{1,0:T(8,128)S(1)} copy-done((f32[256,256]{1,0:T(8,128)S(1)}, f32[256,256]{1,0:T(8,128)}, u32[]{:S(2)}) %copy-start.3) | copy-done | bytes 262168
  10.7 0.4 columns.1
  11.1 1.7 %collective-permute-start = (f32[128,128]{1,0:T(8,128)S(1)}, f32[128,128]{1,0:T(8,128)S(1)}, u32[]{:S(2)}, u32[]{:S(2)}) collective-permute-start(f32[128,128]{1,0:T(8,128)S(1)} %get-tuple-element.15), channel_id=1, source_target_pairs={{0,8},{16,24},{8,0},{24,16},{1,9},{17,25},{9,1},{25,17},{2,10},{18... | collective-permute-start | bytes 196616 | tf_op jit(solution)/shard_map/ppermute | solution.py:575
  12.8 0.0 copy-start.2
  12.8 0.0 copy-start.4
  12.8 0.8 %collective-permute-start.1 = (f32[128,128]{1,0:T(8,128)S(1)}, f32[128,128]{1,0:T(8,128)S(1)}, u32[]{:S(2)}, u32[]{:S(2)}) collective-permute-start(f32[128,128]{1,0:T(8,128)S(1)} %get-tuple-element.16), channel_id=1, source_target_pairs={{8,16},{16,8},{9,17},{17,9},{10,18},{18,10},{11,19},{19,11},{12,20... | collective-permute-start | bytes 196616 | tf_op jit(solution)/shard_map/ppermute | solution.py:575
  13.6 2.1 %collective-permute-done.first_col = f32[128,128]{1,0:T(8,128)S(1)} collective-permute-done((f32[128,128]{1,0:T(8,128)S(1)}, f32[128,128]{1,0:T(8,128)S(1)}, u32[]{:S(2)}, u32[]{:S(2)}) %collective-permute-start) | collective-permute-done | bytes 65568 | tf_op jit(solution)/shard_map/ppermute | solution.py:575
  15.7 0.0 collective-permute-done.1.second_col
  15.7 0.1 rows.1
  15.8 0.0 copy-start.6
  15.8 0.1 collective-permute-start.2
  15.9 0.7 %collective-permute-start.3 = (f32[3,64,128]{2,1,0:T(8,128)S(1)}, f32[3,64,128]{2,1,0:T(8,128)S(1)}, u32[]{:S(2)}, u32[]{:S(2)}) collective-permute-start(f32[3,64,128]{2,1,0:T(8,128)S(1)} %get-tuple-element.21), channel_id=1, source_target_pairs={{1,2},{3,4},{5,6},{2,1},{4,3},{6,5},{9,10},{11,12},{13,14},{10,9},... | collective-permute-start | bytes 294920 | tf_op jit(solution)/shard_map/ppermute | solution.py:575
  16.6 0.0 all-to-all-done.parcels
  16.6 0.0 copy-done.2
  16.6 0.0 copy-done.4
  16.6 0.0 copy-done.6
  16.6 1.2 %setup.1 = (f32[784,128]{1,0:T(8,128)S(1)}, f32[784,128]{1,0:T(8,128)S(1)}, f32[5,128,128]{2,1,0:T(8,128)S(1)}) custom-call(s32[4,8]{1,0:T(4,128)S(1)} %bitcast.6, f32[8,48,128]{2,1,0:T(8,128)S(1)} %all-to-all-done.parcels, f32[256,256]{1,0:T(8,128)S(1)} %copy-done.4, f32[2,256,256]{2,1,0:T(8,128)S(1)} %copy-done, f32[2,256,256]{2,1,0:T(8,128)S(1)} %copy-done.2, ...), custom_call_target="tpu_custom_call" | custom-call | tf_op jit(solution)/shard_map/setup/pallas_call | solution.py:612
  17.9 0.0 collective-permute-done.2.first_row
  17.9 0.0 collective-permute-done.3.second_row
  17.9 17.8 %model.1 = (f32[256,256]{1,0:T(8,128)}, f32[256,256]{1,0:T(8,128)}, f32[16,32,128]{2,1,0:T(8,128)S(1)}) custom-call(f32[784,128]{1,0:T(8,128)S(1)} %get-tuple-element.17.fr, f32[784,128]{1,0:T(8,128)S(1)} %get-tuple-element.18.ice, f32[5,128,128]{2,1,0:T(8,128)S(1)} %get-tuple-element.19.middle, f32[256,256]{1,0:T(8,128)S(1)} %copy-done.4, ...), custom_call_target="tpu_custom_call" | custom-call | tf_op jit(solution)/shard_map/model/pallas_call | solution.py:622
  35.6 0.0 copy-start.5
  35.6 24.4 %all_to_all.10.gathered = f32[16,32,128]{2,1,0:T(8,128)S(1)} all-to-all(f32[16,32,128]{2,1,0:T(8,128)S(1)} %get-tuple-element.24), channel_id=1, replica_groups={{0,2,4,6,8,10,12,14,16,18,20,22,24,26,28,30},{1,3,5,7,9,11,13,15,17,19,..., dimensions={0} | all-to-all | bytes 524288 | tf_op jit(solution)/shard_map/all_to_all | solution.py:642
  60.0 0.0 copy-done.5
  60.0 0.8 %pick.1 = (f32[4,32,128]{2,1,0:T(8,128)S(1)}, f32[4,32,128]{2,1,0:T(8,128)S(1)}) custom-call(s32[4,8]{1,0:T(4,128)S(1)} %bitcast.5, f32[16,32,128]{2,1,0:T(8,128)S(1)} %all_to_all.10.gathered), custom_call_target="tpu_custom_call" | custom-call | tf_op jit(solution)/shard_map/pick/pallas_call | solution.py:643
  60.8 0.1 collective-permute-start.4
  60.9 1.2 %collective-permute-done.4.received = f32[4,32,128]{2,1,0:T(8,128)S(1)} collective-permute-done((f32[4,32,128]{2,1,0:T(8,128)S(1)}, f32[4,32,128]{2,1,0:T(8,128)S(1)}, u32[]{:S(2)}, u32[]{:S(2)}) %collective-permute-start.4) | collective-permute-done | bytes 65568 | tf_op jit(solution)/shard_map/ppermute | solution.py:652
  62.1 0.7 %join.1 = f32[4,4096]{1,0:T(4,128)} custom-call(f32[4,32,128]{2,1,0:T(8,128)S(1)} %get-tuple-element.25.own, f32[4,32,128]{2,1,0:T(8,128)S(1)} %collective-permute-done.4.received), custom_call_target="tpu_custom_call" | custom-call | tf_op jit(solution)/shard_map/join/pallas_call | solution.py:653
Async XLA Ops:
  0.6 8.1 %copy-start = (f32[2,256,256]{2,1,0:T(8,128)S(1)}, f32[2,256,256]{2,1,0:T(8,128)}, u32[]{:S(2)}) copy-start(f32[2,256,256]{2,1,0:T(8,128)} %drive.7) | copy-start | bytes 1572868
  3.5 13.1 %all-to-all-start = ((f32[8,48,128]{2,1,0:T(8,128)}), f32[8,48,128]{2,1,0:T(8,128)S(1)}, u32[]{:S(2)}, u32[]{:S(2)}) async-start(f32[8,48,128]{2,1,0:T(8,128)} %parcels.1), calls=%async_computation | async-start | bytes 393216 | tf_op jit(solution)/shard_map/all_to_all | solution.py:593
  8.7 1.0 %copy-start.1 = (f32[2,256,256]{2,1,0:T(8,128)S(1)}, f32[2,256,256]{2,1,0:T(8,128)}, u32[]{:S(2)}) copy-start(f32[2,256,256]{2,1,0:T(8,128)} %obs.7) | copy-start | bytes 1572868
  9.8 0.9 %copy-start.3 = (f32[256,256]{1,0:T(8,128)S(1)}, f32[256,256]{1,0:T(8,128)}, u32[]{:S(2)}) copy-start(f32[256,256]{1,0:T(8,128)} %thick.7) | copy-start | bytes 786436
  11.1 4.6 %collective-permute-start = (f32[128,128]{1,0:T(8,128)S(1)}, f32[128,128]{1,0:T(8,128)S(1)}, u32[]{:S(2)}, u32[]{:S(2)}) collective-permute-start(f32[128,128]{1,0:T(8,128)S(1)} %get-tuple-element.15), channel_id=1, source_target_pairs={{0,8},{16,24},{8,0},{24,16},{1,9},{17,25},{9,1},{25,17},{2,10},{18... | collective-permute-start | bytes 196616 | tf_op jit(solution)/shard_map/ppermute | solution.py:575
  12.8 3.8 %copy-start.2 = (f32[2,256,256]{2,1,0:T(8,128)S(1)}, f32[2,256,256]{2,1,0:T(8,128)}, u32[]{:S(2)}) copy-start(f32[2,256,256]{2,1,0:T(8,128)} %obs.7) | copy-start | bytes 1572868
  12.8 3.8 %copy-start.4 = (f32[256,256]{1,0:T(8,128)S(1)}, f32[256,256]{1,0:T(8,128)}, u32[]{:S(2)}) copy-start(f32[256,256]{1,0:T(8,128)} %thick.7) | copy-start | bytes 786436
  12.8 2.9 %collective-permute-start.1 = (f32[128,128]{1,0:T(8,128)S(1)}, f32[128,128]{1,0:T(8,128)S(1)}, u32[]{:S(2)}, u32[]{:S(2)}) collective-permute-start(f32[128,128]{1,0:T(8,128)S(1)} %get-tuple-element.16), channel_id=1, source_target_pairs={{8,16},{16,8},{9,17},{17,9},{10,18},{18,10},{11,19},{19,11},{12,20... | collective-permute-start | bytes 196616 | tf_op jit(solution)/shard_map/ppermute | solution.py:575
  15.8 0.8 %copy-start.6 = (s32[8,4]{0,1:T(4,128)S(1)}, s32[8,4]{0,1:T(4,128)}, u32[]{:S(2)}) copy-start(s32[8,4]{0,1:T(4,128)} %param.10) | copy-start | bytes 388
  15.8 2.0 %collective-permute-start.2 = (f32[3,64,128]{2,1,0:T(8,128)S(1)}, f32[3,64,128]{2,1,0:T(8,128)S(1)}, u32[]{:S(2)}, u32[]{:S(2)}) collective-permute-start(f32[3,64,128]{2,1,0:T(8,128)S(1)} %get-tuple-element.20), channel_id=1, source_target_pairs={{0,1},{2,3},{4,5},{6,7},{1,0},{3,2},{5,4},{7,6},{8,9},{10,11},{12,... | collective-permute-start | bytes 294920 | tf_op jit(solution)/shard_map/ppermute | solution.py:575
  15.9 1.9 %collective-permute-start.3 = (f32[3,64,128]{2,1,0:T(8,128)S(1)}, f32[3,64,128]{2,1,0:T(8,128)S(1)}, u32[]{:S(2)}, u32[]{:S(2)}) collective-permute-start(f32[3,64,128]{2,1,0:T(8,128)S(1)} %get-tuple-element.21), channel_id=1, source_target_pairs={{1,2},{3,4},{5,6},{2,1},{4,3},{6,5},{9,10},{11,12},{13,14},{10,9},... | collective-permute-start | bytes 294920 | tf_op jit(solution)/shard_map/ppermute | solution.py:575
  35.6 24.4 %copy-start.5 = (s32[8,4,1]{0,2,1:T(1,128)S(1)}, s32[8,4,1]{0,2,1:T(1,128)}, u32[]{:S(2)}) copy-start(s32[8,4,1]{0,2,1:T(1,128)} %param.11) | copy-start | bytes 388
  60.8 1.3 %collective-permute-start.4 = (f32[4,32,128]{2,1,0:T(8,128)S(1)}, f32[4,32,128]{2,1,0:T(8,128)S(1)}, u32[]{:S(2)}, u32[]{:S(2)}) collective-permute-start(f32[4,32,128]{2,1,0:T(8,128)S(1)} %get-tuple-element.26), channel_id=1, source_target_pairs={{0,1},{1,0},{2,3},{3,2},{4,5},{5,4},{6,7},{7,6},{8,9},{9,8},{10,11... | collective-permute-start | bytes 196616 | tf_op jit(solution)/shard_map/ppermute | solution.py:652

commit v10 on v9

--- a/solution.py
+++ b/solution.py
@@ -1,3 +1,5 @@
+from types import SimpleNamespace
+
 import jax
 import jax.numpy as jnp
 from jax import lax
@@ -24,7 +26,11 @@
 ALL_ROWS = SIDE + HALF + 2 * TOP
 MAIN = (0, ROWS)
 SIDES = (SIDE,)
-BLOCKS = 4
+SPANS = {
+    "frame": (MARGIN, 4, 72, MARGIN, 40, 0, 0),
+    "inner": (MARGIN + 8, 3, 72, MARGIN + 8, 40, 56, 24),
+    "tile": (TOP, 4, 64, TOP, 32, 0, 0),
+}
 FACTORS = 14
 AHEAD = 2
 PACK = COARSE // LANES
@@ -90,30 +96,42 @@
     lax.fori_loop(0, tile_rows, spread, 0)
 
 
-def parcels_kernel(tile_block, control, parcels, held, owned_blocks, sem):
-    copy = pltpu.make_async_copy(control, held, sem)
-    copy.start()
-    parcels[...] = jnp.zeros_like(parcels)
-    copy.wait()
+def pack_kernel(
+    tile_block, control, thick, drive, obs, first_col, second_col, parcels,
+    held, held_control, owned_blocks, packed_parcels, packed_cols, sems,
+):
+    copies = [pltpu.make_async_copy(control, held_control, sems.at[5])]
+    for f, field in enumerate((thick, drive.at[0], drive.at[1], obs.at[0], obs.at[1])):
+        copies.append(pltpu.make_async_copy(field, held.at[f], sems.at[f]))
+    for copy in copies:
+        copy.start()
+    packed_parcels[...] = jnp.zeros_like(packed_parcels)
+    copies[0].wait()
     for j in range(PACK):
-        owned_blocks[:, j, :] = held[:, j * LANES : (j + 1) * LANES]
-    fill_parcels(tile_block, owned_blocks, parcels)
-
-
-def columns_kernel(thick, drive, obs, first_col, second_col):
+        owned_blocks[:, j, :] = held_control[:, j * LANES : (j + 1) * LANES]
+    fill_parcels(tile_block, owned_blocks, packed_parcels)
+    results = [pltpu.make_async_copy(packed_parcels, parcels, sems.at[6])]
+    results[0].start()
+
     lane = lanes_of(HALF)
     left = jnp.zeros((HALF, LANES), jnp.float32)
     right = jnp.zeros((HALF, LANES), jnp.float32)
-    for field, (first, count) in zip((thick, drive.at[0], drive.at[1], obs.at[0], obs.at[1]), STRIP):
+    for f, (first, count) in enumerate(STRIP):
+        copies[1 + f].wait()
         for part in range(2):
             rows = slice(part * HALF, (part + 1) * HALF)
             start = part * BAND + first
             inside = (lane >= start) & (lane < start + count)
-            left = jnp.where(inside, turn(field[rows, :LANES], 0, start), left)
-            right = jnp.where(inside, turn(field[rows, LANES:], LANES - count, start), right)
+            left = jnp.where(inside, turn(held[f, rows, :LANES], 0, start), left)
+            right = jnp.where(inside, turn(held[f, rows, LANES:], LANES - count, start), right)
     even = is_even("gx")
-    first_col[...] = jnp.where(even, right, left)
-    second_col[...] = jnp.where(even, left, right)
+    packed_cols[0] = jnp.where(even, right, left)
+    packed_cols[1] = jnp.where(even, left, right)
+    for i, out in enumerate((first_col, second_col)):
+        results.append(pltpu.make_async_copy(packed_cols.at[i], out, sems.at[7 + i]))
+        results[-1].start()
+    for copy in results:
+        copy.wait()
 
 
 def sides(axis, first_pair, second_pair):
@@ -171,28 +189,50 @@
     return [jnp.where(lane == 0, rolled[1 - c], rolled[c]) for c in range(2)]
 
 
-def over_rows(framed, read, work):
-    start = MARGIN if framed else TOP
-    wide = 2 * HALO if framed else 0
-    main, side = (TILE + wide) // BLOCKS, (HALF + wide) // BLOCKS
-    step = 24 if framed else 32
-    groups = [(MAIN, g, step) for g in range(0, main, step)]
-    groups[1:1] = [(SIDES, 0, 16)]
-    groups[3:3] = [(SIDES, 16, side - 16)]
+def run_groups(groups, read, work):
+    pending = [read(*group) for group in groups[:AHEAD]]
+    for k, (part, row, count) in enumerate(groups):
+        if k + AHEAD < len(groups):
+            pending.append(read(*groups[k + AHEAD]))
+        for ref, lead, values in work(part, pending[k], lanes_of(count)):
+            for tile, value in zip(part, values):
+                ref[(*lead, pl.ds(row + tile, count), slice(None))] = value
+
+
+def block_groups(row, main, side_row, side):
+    step = 32 if main % 32 == 0 else 24
+    first = side // 16 * 8 if side > 24 else side
+    groups = [(MAIN, row + g, min(step, main - g)) for g in range(0, main, step)]
+    groups[1:1] = [(SIDES, side_row, first)]
+    if first < side:
+        groups[3:3] = [(SIDES, side_row + first, side - first)]
+    return groups
+
+
+def over_rows(span, read, work):
+    start, blocks, main, side_start, side, main_rest, side_rest = SPANS[span]
 
     def block(i, carry):
-        first = {MAIN: pl.multiple_of(start + i * main, 8), SIDES: pl.multiple_of(start + i * side, 8)}
-        rows = [(part, first[part] + g, count) for part, g, count in groups]
-        pending = [read(*group) for group in rows[:AHEAD]]
-        for k, (part, row, count) in enumerate(rows):
-            if k + AHEAD < len(rows):
-                pending.append(read(*rows[k + AHEAD]))
-            for ref, lead, values in work(part, pending[k], lanes_of(count)):
-                for tile, value in zip(part, values):
-                    ref[(*lead, pl.ds(row + tile, count), slice(None))] = value
+        row, side_row = pl.multiple_of(start + i * main, 8), pl.multiple_of(side_start + i * side, 8)
+        run_groups(block_groups(row, main, side_row, side), read, work)
         return carry
 
-    lax.fori_loop(0, BLOCKS, block, 0)
+    lax.fori_loop(0, blocks, block, 0)
+    if main_rest:
+        none = 8 * jnp.minimum(lax.axis_index("gx"), 0)
+        row = pl.multiple_of(none + start + blocks * main, 8)
+        side_row = pl.multiple_of(none + side_start + blocks * side, 8)
+        run_groups(block_groups(row, main_rest, side_row, side_rest), read, work)
+
+
+def over_ends(count, read, work):
+    def block(i, carry):
+        row = pl.multiple_of(MARGIN + i * (TILE + 2 * HALO - count), 8)
+        side_row = pl.multiple_of(MARGIN + i * (HALF + 2 * HALO - count), 8)
+        run_groups([(MAIN, row, count), (SIDES, side_row, count)], read, work)
+        return carry
+
+    lax.fori_loop(0, 2, block, 0)
 
 
 def join_parts(ref, leads, whole):
@@ -240,11 +280,7 @@
         join(TOP + HALF, False, True, HALO)
 
 
-def setup_kernel(
-    ice_mask, parcels, thick, drive, obs, first_col, second_col,
-    fr, ice, middle,
-    patch,
-):
+def friction_kernel(ice_mask, parcels, fr, ice, patch):
     tile_cols, tile_rows = ice_mask.shape
     row_tile = lax.axis_index("gy")
     col_tile = lax.axis_index("gx")
@@ -278,21 +314,6 @@
     )
     for j in range(4):
         fr[pl.ds(SIDE + MARGIN + j, 40, stride=4), :] = wide
-
-    west, east = sides("gx", first_col[...], second_col[...])
-    lane = lanes_of(HALF)
-    upper = lane < BAND
-    for f, (field, (first, count)) in enumerate(zip((thick, drive.at[0], drive.at[1], obs.at[0], obs.at[1]), STRIP)):
-        halves = (slice(0, HALF), slice(HALF, TILE))
-        high = [turn(field[halves[b], LANES:], LANES - HALO, BAND * b) for b in range(2)]
-        low = [turn(field[halves[b], :LANES], 0, BAND * b + 3 * HALO) for b in range(2)]
-        middle[f] = (0.5 if f in (1, 2) else 1.0) * choose_side(
-            lane,
-            jnp.where(upper, high[0], high[1]),
-            turn(east, first, HALO),
-            turn(west, first, 3 * HALO - count),
-            jnp.where(upper, low[0], low[1]),
-        )
 
     side_ice = []
     for dr, first, count in ((-1, MARGIN, HALO), (0, TOP, TILE), (1, TOP + TILE, HALO)):
@@ -313,30 +334,7 @@
     ice[SIDE + TOP + HALF : SIDE + TOP + HALF + HALO, :] = jnp.where(upper, side_ice[1], side_ice[2])
 
 
-def model_kernel(
-    fr, ice, middle, thick, drive, obs, first_row, second_row,
-    vel_u, vel_v, sums,
-    ext, visc, vel_a, vel_b, vel_c, coef, small, sems,
-):
-    even = is_even("gy")
-    for f, (field, (first, count)) in enumerate(zip((thick, drive.at[0], drive.at[1], obs.at[0], obs.at[1]), STRIP)):
-        scale = 0.5 if f in (1, 2) else 1.0
-        frames = []
-        for c in range(3):
-            one, two = scale * first_row[c, first : first + count, :], scale * second_row[c, first : first + count, :]
-            frames.append((jnp.where(even, two, one), jnp.where(even, one, two)))
-        for c in range(2):
-            ext[f, MAIN[c] + TOP : MAIN[c] + TOP + TILE, :] = scale * field[:, c * LANES : (c + 1) * LANES]
-            ext[f, MAIN[c] + TOP - count : MAIN[c] + TOP, :] = frames[c][0]
-            ext[f, MAIN[c] + TOP + TILE : MAIN[c] + TOP + TILE + count, :] = frames[c][1]
-        here = SIDE + TOP
-        ext[f, here : here + HALF, :] = middle[f]
-        upper = lanes_of(count) < BAND
-        above = turn(middle[f, HALF - count :, :], 0, BAND)
-        below = turn(middle[f, :count, :], 0, BAND)
-        ext[f, here - count : here, :] = jnp.where(upper, frames[2][0], above)
-        ext[f, here + HALF : here + HALF + count, :] = jnp.where(upper, below, frames[2][1])
-
+def make_stages(ext, fr, ice, visc, vel_a, vel_b, coef):
     def load(ref, part, row, count, *lead):
         return [ref[(*lead, pl.ds(row + tile, count), slice(None))] for tile in part]
 
@@ -426,12 +424,15 @@
     def keep(k):
         return [(coef, (i,), k[i]) for i in range(FACTORS)]
 
-    def sweep(framed, now, new):
+    def read_sweep(now):
         def read(part, row, count):
             k = [load(coef, part, row, count, i) for i in range(FACTORS)]
             return k, load_around(part, row, count, now), load_right(part, row, count)
 
-        over_rows(framed, read, lambda part, read, lane: put(new, relax(part, *read, lane)))
+        return read
+
+    def sweep(new):
+        return lambda part, read, lane: put(new, relax(part, *read, lane))
 
     def read_first(part, row, count):
         return read_coefficients(part, row, count), load_right(part, row, count)
@@ -447,21 +448,78 @@
         k = coefficients(part, read[0])
         return keep(k) + put(vel_a, relax(part, k, read[2], read[1], lane))
 
-    over_rows(True, read_thickness, first_viscosity)
-    over_rows(True, read_first, first_start)
-    sweep(True, vel_a, vel_b)
+    return SimpleNamespace(**locals())
+
+
+def setup_kernel(
+    fr, ice, thick, drive, obs, first_col, second_col,
+    ext, vel_b,
+    visc, vel_a, coef,
+):
+    west, east = sides("gx", first_col[...], second_col[...])
+    lane = lanes_of(HALF)
+    upper = lane < BAND
+    for f, (field, (first, count)) in enumerate(zip((thick, drive.at[0], drive.at[1], obs.at[0], obs.at[1]), STRIP)):
+        scale = 0.5 if f in (1, 2) else 1.0
+        for c in range(2):
+            ext[f, MAIN[c] + TOP : MAIN[c] + TOP + TILE, :] = scale * field[:, c * LANES : (c + 1) * LANES]
+        halves = (slice(0, HALF), slice(HALF, TILE))
+        high = [turn(field[halves[b], LANES:], LANES - HALO, BAND * b) for b in range(2)]
+        low = [turn(field[halves[b], :LANES], 0, BAND * b + 3 * HALO) for b in range(2)]
+        ext[f, SIDE + TOP : SIDE + TOP + HALF, :] = scale * choose_side(
+            lane,
+            jnp.where(upper, high[0], high[1]),
+            turn(east, first, HALO),
+            turn(west, first, 3 * HALO - count),
+            jnp.where(upper, low[0], low[1]),
+        )
+    step = make_stages(ext, fr, ice, visc, vel_a, vel_b, coef)
+    over_rows("tile", step.read_thickness, step.first_viscosity)
+    over_rows("tile", step.read_first, step.first_start)
+    over_rows("tile", step.read_sweep(vel_a), step.sweep(vel_b))
+
+
+def model_kernel(
+    fr, ice, ext_in, vel_in, first_row, second_row,
+    vel_u, vel_v, sums,
+    ext, visc, vel_a, vel_b, vel_c, coef, small, sems,
+):
+    ext[...] = ext_in[...]
+    vel_b[...] = vel_in[...]
+    even = is_even("gy")
+    here = SIDE + TOP
+    for f, (first, count) in enumerate(STRIP):
+        scale = 0.5 if f in (1, 2) else 1.0
+        frames = []
+        for c in range(3):
+            one, two = scale * first_row[c, first : first + count, :], scale * second_row[c, first : first + count, :]
+            frames.append((jnp.where(even, two, one), jnp.where(even, one, two)))
+        for c in range(2):
+            ext[f, MAIN[c] + TOP - count : MAIN[c] + TOP, :] = frames[c][0]
+            ext[f, MAIN[c] + TOP + TILE : MAIN[c] + TOP + TILE + count, :] = frames[c][1]
+        upper = lanes_of(count) < BAND
+        above = turn(ext_in[f, here + HALF - count : here + HALF, :], 0, BAND)
+        below = turn(ext_in[f, here : here + count, :], 0, BAND)
+        ext[f, here - count : here, :] = jnp.where(upper, frames[2][0], above)
+        ext[f, here + HALF : here + HALF + count, :] = jnp.where(upper, below, frames[2][1])
+
+    step = make_stages(ext, fr, ice, visc, vel_a, vel_b, coef)
+    over_ends(32, step.read_thickness, step.first_viscosity)
+    over_ends(32, step.read_first, step.first_start)
+    over_ends(24, step.read_sweep(vel_a), step.sweep(vel_b))
+
+    def iterate(span):
+        over_rows(span, step.read_viscosity, step.viscosity)
+        over_rows(span, step.read_start, step.start)
+        over_rows(span, step.read_sweep(vel_a), step.sweep(vel_b))
 
     def iteration(i, carry):
-        @pl.when(i == PIC - 1)
-        def _():
-            join_parts(vel_b, ((0,), (1,)), True)
-
-        over_rows(True, read_viscosity, viscosity)
-        over_rows(True, read_start, start)
-        sweep(True, vel_a, vel_b)
+        iterate("frame")
         return carry
 
-    lax.fori_loop(1, PIC, iteration, 0)
+    lax.fori_loop(1, PIC - 1, iteration, 0)
+    join_parts(vel_b, ((0,), (1,)), True)
+    iterate("inner")
     join_parts(vel_b, ((0,), (1,)), False)
     copies = []
     for i, out in enumerate((vel_u, vel_v)):
@@ -475,6 +533,8 @@
             )
             copies[-1].start()
 
+    load = step.load
+
     def read_misfit(part, row, count):
         return [
             [load(vel_b, part, row, count, i), load(ext, part, row, count, 3 + i), load(coef, part, row, count, 4 + i)]
@@ -484,17 +544,17 @@
     def first_adjoint(part, read, lane):
         misfit = [[0.5 * (a - b) for a, b in zip(u, seen)] for u, seen, _ in read]
         first = [[a * b for a, b in zip(read[i][2], misfit[i])] for i in range(2)]
-        return put(vel_c, first) + [(ext, (1 + i,), misfit[i]) for i in range(2)]
-
-    over_rows(True, read_misfit, first_adjoint)
+        return step.put(vel_c, first) + [(ext, (1 + i,), misfit[i]) for i in range(2)]
+
+    over_rows("inner", read_misfit, first_adjoint)
 
     def two_sweeps(i, carry):
-        sweep(True, vel_c, vel_a)
-        sweep(True, vel_a, vel_c)
+        over_rows("inner", step.read_sweep(vel_c), step.sweep(vel_a))
+        over_rows("inner", step.read_sweep(vel_a), step.sweep(vel_c))
         return carry
 
     lax.fori_loop(0, (ADJ - 2) // 2, two_sweeps, 0)
-    sweep(False, vel_c, vel_a)
+    over_rows("tile", step.read_sweep(vel_c), step.sweep(vel_a))
 
     def read_gradient(part, row, count):
         return [load(ref, part, row, count, i) for ref in (vel_b, vel_a) for i in range(2)] + [load(fr, part, row, count)]
@@ -503,7 +563,7 @@
         u, v, lu, lv, friction = read
         return [(visc, (0,), [-2.0 * friction[c] * (u[c] * lu[c] + v[c] * lv[c]) for c in range(len(part))])]
 
-    over_rows(False, read_gradient, gradient)
+    over_rows("tile", read_gradient, gradient)
     join_parts(visc, ((0,),), False)
     down = [sum(visc[0, pl.ds(MAIN[c] + TOP + j, CT, stride=4), :] for j in range(4)) for c in range(2)]
     k = lax.broadcasted_iota(jnp.int32, (LANES, LANES), 0)
@@ -577,28 +637,23 @@
 
     fields = thickness, driving, observed
     owned = control.shape[0]
-    parcels = pl.pallas_call(
-        parcels_kernel,
-        out_shape=shape(rows, PARCEL, LANES),
-        in_specs=in_smem(1) + [pl.BlockSpec(memory_space=pltpu.HBM)],
-        out_specs=pl.BlockSpec(memory_space=pltpu.VMEM),
+    *edges, parcels = pl.pallas_call(
+        pack_kernel,
+        out_shape=[shape(HALF, LANES)] * 2 + [shape(rows, PARCEL, LANES)],
+        in_specs=in_smem(1) + [pl.BlockSpec(memory_space=pltpu.HBM)] * 4,
+        out_specs=[pl.BlockSpec(memory_space=pltpu.HBM)] * 3,
         scratch_shapes=[
+            pltpu.VMEM((5, TILE, TILE), f32),
             pltpu.VMEM(control.shape, f32),
             pltpu.VMEM((owned, PACK, LANES), f32),
-            pltpu.SemaphoreType.DMA,
+            pltpu.VMEM((rows, PARCEL, LANES), f32),
+            pltpu.VMEM((2, HALF, LANES), f32),
+            pltpu.SemaphoreType.DMA((9,)),
         ],
         compiler_params=pltpu.CompilerParams(vmem_limit_bytes=PACK_VMEM_LIMIT),
-        name="parcels",
-    )(tile_block, control)
+        name="pack",
+    )(tile_block, control, *fields)
     parcels = lax.all_to_all(parcels, "gy", 0, 0, tiled=True)
-    edges = pl.pallas_call(
-        columns_kernel,
-        out_shape=[shape(HALF, LANES)] * 2,
-        in_specs=in_vmem(3),
-        out_specs=in_vmem(2),
-        compiler_params=params,
-        name="columns",
-    )(*fields)
     columns_in = swap("gx", *edges)
     strips = pl.pallas_call(
         rows_kernel,
@@ -609,20 +664,33 @@
         name="rows",
     )(*fields, *columns_in)
     rows_in = swap("gy", *strips)
+    friction = pl.pallas_call(
+        friction_kernel,
+        out_shape=[shape(ALL_ROWS, LANES)] * 2,
+        in_specs=in_smem(1) + in_vmem(1),
+        out_specs=in_vmem(2),
+        scratch_shapes=[pltpu.VMEM((PATCH, LANES), f32)],
+        compiler_params=params,
+        name="friction",
+    )(ice_mask, parcels)
     prepared = pl.pallas_call(
         setup_kernel,
-        out_shape=[shape(ALL_ROWS, LANES)] * 2 + [shape(5, HALF, LANES)],
-        in_specs=in_smem(1) + in_vmem(6),
-        out_specs=in_vmem(3),
-        scratch_shapes=[pltpu.VMEM((PATCH, LANES), f32)],
+        out_shape=[shape(5, ALL_ROWS, LANES), shape(2, ALL_ROWS, LANES)],
+        in_specs=in_vmem(7),
+        out_specs=in_vmem(2),
+        scratch_shapes=[
+            pltpu.VMEM((3, ALL_ROWS, LANES), f32),
+            pltpu.VMEM((2, ALL_ROWS, LANES), f32),
+            pltpu.VMEM((FACTORS, ALL_ROWS, LANES), f32),
+        ],
         compiler_params=params,
         name="setup",
-    )(ice_mask, parcels, *fields, *columns_in)
+    )(*friction, *fields, *columns_in)
 
     vel_u, vel_v, sums = pl.pallas_call(
         model_kernel,
         out_shape=(shape(TILE, TILE), shape(TILE, TILE), shape(cols * rows // 2, PACK, LANES)),
-        in_specs=in_vmem(8),
+        in_specs=in_vmem(6),
         out_specs=[pl.BlockSpec(memory_space=pltpu.HBM)] * 2 + in_vmem(1),
         scratch_shapes=[
             pltpu.VMEM((5, ALL_ROWS, LANES), f32),
@@ -636,7 +704,7 @@
         ],
         compiler_params=params,
         name="model",
-    )(*prepared, *fields, *rows_in)
+    )(*friction, *prepared, *rows_in)
 
     same_core = [[i * rows + j for i in range(cols) for j in range(core, rows, 2)] for core in range(2)]
     sums = lax.all_to_all(sums, ("gx", "gy"), 0, 0, tiled=True, axis_index_groups=same_core)

time: 63.2 us -> 60.8 us (0.962)
  blocking collectives: 24.4 us -> 22.3 us
  local copies, waits for them, and re-layouts: 2.01 us -> 0.97 us
  Pallas kernels: 23.8 us -> 24.5 us
    pallas_call x3, Pallas kernels: 4.46 us -> 6.84 us  [the longest x1 3.7 us: per_device(): pl.pallas_call(pack_kernel, out_shape=[shape(HALF, LANES)] * 2 + [shape(r...]
    all_to_all x1, blocking collectives: 24.4 us -> 22.3 us  [per_device(): lax.all_to_all(sums, ('gx', 'gy'), 0, 0, tiled=True, axis_index_groups=sa...]
    pallas_call x1, Pallas kernels: 17.8 us -> 16.1 us  [per_device(): pl.pallas_call(model_kernel, out_shape=(shape(TILE, TILE), shape(TILE, TI...]
    unnamed x14 -> x12, local copies, waits for them, and re-layouts: 2.01 us -> 0.97 us
  transfers between devices with their start and end apart: 6 -> 6, of which waited for: 2 -> 2; matrix products, arithmetic and copies ran while one was open for 0% -> 0% of each run, Pallas kernels for 3% -> 5%
where the time goes in v10:
time: 60.8 us; the launch traced here: 60.4 us
  Pallas kernels  24.5 us (40%)
  blocking collectives  22.3 us (37%)
  starting transfers between devices  8.27 us (14%)
  waiting for transfers between devices  3.63 us (6%)
  local copies, waits for them, and re-layouts  0.97 us (2%)
  between operations  0.8 us (1%)
    all_to_all x1, blocking collectives, per_device(): lax.all_to_all(sums, ('gx', 'gy'), 0, 0, tiled=True, axis_index_groups=sa...  22.3 us
    pallas_call x1, Pallas kernels, per_device(): pl.pallas_call(model_kernel, out_shape=(shape(TILE, TILE), shape(TILE, TI...  16.1 us
    all_to_all x1, starting transfers between devices, per_device(): parcels = lax.all_to_all(parcels, 'gy', 0, 0, tiled=True)  5.13 us
    pallas_call x1, Pallas kernels, per_device(): pl.pallas_call(pack_kernel, out_shape=[shape(HALF, LANES)] * 2 + [shape(r...  3.7 us
    ppermute x4, starting transfers between devices, swap(): lax.ppermute(cells, axis, pairs + [(j, i) for i, j in pairs])  3.07 us
    ppermute x4, waiting for transfers between devices, swap(): lax.ppermute(cells, axis, pairs + [(j, i) for i, j in pairs])  2.38 us
    pallas_call x1, Pallas kernels, per_device(): pl.pallas_call(setup_kernel, out_shape=[shape(5, ALL_ROWS, LANES), shape(...  2.31 us
    ppermute x1, waiting for transfers between devices, per_device(): received = lax.ppermute(other, 'gy', [(j, j ^ 1) for j in range(rows)])  1.24 us
  transfers between devices with their start and end apart: 6, of which 2 were waited for; matrix products, arithmetic and copies ran while one was open for 0% of the time, Pallas kernels for 5%

profile of v10, /device:TPU:0, one launch (start us, length us, event | category | flops | bytes accessed | tf_op | source)
XLA Modules:
  0.0 60.4 jit_solution(12464858848925272234)
XLA Ops:
  0.6 0.0 copy-start.1
  0.6 0.0 copy-start
  0.7 0.0 copy-start.3
  0.7 0.0 copy-start.5
  0.7 3.7 %pack.1 = (f32[128,128]{1,0:T(8,128)}, f32[128,128]{1,0:T(8,128)}, f32[8,48,128]{2,1,0:T(8,128)}) custom-call(s32[4,8]{1,0:T(4,128)} %bitcast.4, f32[4,4096]{1,0:T(4,128)} %control.1, f32[256,256]{1,0:T(8,128)} %thick.5, f32[2,256,256]{2,1,0:T(8,128)} %drive.5, f32[2,256,256]{2,1,0:T(8,128)} %obs.5), custom_call_target="tpu_custom_call" | custom-call | tf_op jit(solution)/shard_map/pack/pallas_call | solution.py:640
  4.4 5.1 %all-to-all-start = ((f32[8,48,128]{2,1,0:T(8,128)}), f32[8,48,128]{2,1,0:T(8,128)S(1)}, u32[]{:S(2)}, u32[]{:S(2)}) async-start(f32[8,48,128]{2,1,0:T(8,128)} %get-tuple-element.17), calls=%async_computation | async-start | bytes 393216 | tf_op jit(solution)/shard_map/all_to_all | solution.py:656
  9.5 1.7 %collective-permute-start = (f32[128,128]{1,0:T(8,128)}, f32[128,128]{1,0:T(8,128)S(1)}, u32[]{:S(2)}, u32[]{:S(2)}) collective-permute-start(f32[128,128]{1,0:T(8,128)} %get-tuple-element.20), channel_id=1, source_target_pairs={{0,8},{16,24},{8,0},{24,16},{1,9},{17,25},{9,1},{25,17},{2,10},{18... | collective-permute-start | bytes 196616 | tf_op jit(solution)/shard_map/ppermute | solution.py:635
  11.2 0.7 %collective-permute-start.1 = (f32[128,128]{1,0:T(8,128)}, f32[128,128]{1,0:T(8,128)S(1)}, u32[]{:S(2)}, u32[]{:S(2)}) collective-permute-start(f32[128,128]{1,0:T(8,128)} %get-tuple-element.21), channel_id=1, source_target_pairs={{8,16},{16,8},{9,17},{17,9},{10,18},{18,10},{11,19},{19,11},{12,20... | collective-permute-start | bytes 196616 | tf_op jit(solution)/shard_map/ppermute | solution.py:635
  11.8 2.4 %collective-permute-done.first_col = f32[128,128]{1,0:T(8,128)S(1)} collective-permute-done((f32[128,128]{1,0:T(8,128)}, f32[128,128]{1,0:T(8,128)S(1)}, u32[]{:S(2)}, u32[]{:S(2)}) %collective-permute-start) | collective-permute-done | bytes 65568 | tf_op jit(solution)/shard_map/ppermute | solution.py:635
  14.2 0.0 collective-permute-done.1.second_col
  14.2 0.0 copy-done.1
  14.2 0.0 copy-done
  14.2 0.0 copy-start.2
  14.2 0.9 %copy-done.2 = f32[256,256]{1,0:T(8,128)S(1)} copy-done((f32[256,256]{1,0:T(8,128)S(1)}, f32[256,256]{1,0:T(8,128)}, u32[]{:S(2)}) %copy-start.2) | copy-done | bytes 262168
  15.2 0.1 rows.1
  15.3 0.1 collective-permute-start.2
  15.4 0.7 %collective-permute-start.3 = (f32[3,64,128]{2,1,0:T(8,128)S(1)}, f32[3,64,128]{2,1,0:T(8,128)S(1)}, u32[]{:S(2)}, u32[]{:S(2)}) collective-permute-start(f32[3,64,128]{2,1,0:T(8,128)S(1)} %get-tuple-element.25), channel_id=1, source_target_pairs={{1,2},{3,4},{5,6},{2,1},{4,3},{6,5},{9,10},{11,12},{13,14},{10,9},... | collective-permute-start | bytes 294920 | tf_op jit(solution)/shard_map/ppermute | solution.py:635
  16.1 0.0 all-to-all-done.parcels
  16.1 0.0 copy-done.5
  16.1 0.8 %friction.1 = (f32[784,128]{1,0:T(8,128)S(1)}, f32[784,128]{1,0:T(8,128)S(1)}) custom-call(s32[4,8]{1,0:T(4,128)S(1)} %bitcast.6, f32[8,48,128]{2,1,0:T(8,128)S(1)} %all-to-all-done.parcels), custom_call_target="tpu_custom_call" | custom-call | tf_op jit(solution)/shard_map/friction/pallas_call | solution.py:667
  16.9 0.0 copy-done.3
  17.0 2.3 %setup.1 = (f32[5,784,128]{2,1,0:T(8,128)S(1)}, f32[2,784,128]{2,1,0:T(8,128)S(1)}) custom-call(f32[784,128]{1,0:T(8,128)S(1)} %get-tuple-element.18.fr, f32[784,128]{1,0:T(8,128)S(1)} %get-tuple-element.19.ice, f32[256,256]{1,0:T(8,128)S(1)} %copy-done.3, f32[2,256,256]{2,1,0:T(8,128)S(1)} %copy-done, f32[2,256,256]{2,1,0:T(8,128)S(1)} %copy-done.1, ...), custom_call_target="tpu_custom_call" | custom-call | tf_op jit(solution)/shard_map/setup/pallas_call | solution.py:676
  19.3 0.0 collective-permute-done.2.first_row
  19.3 0.0 collective-permute-done.3.second_row
  19.3 0.0 copy-start.4
  19.3 16.1 %model.1 = (f32[256,256]{1,0:T(8,128)}, f32[256,256]{1,0:T(8,128)}, f32[16,32,128]{2,1,0:T(8,128)S(1)}) custom-call(f32[784,128]{1,0:T(8,128)S(1)} %get-tuple-element.18.fr, f32[784,128]{1,0:T(8,128)S(1)} %get-tuple-element.19.ice, f32[5,784,128]{2,1,0:T(8,128)S(1)} %get-tuple-element.22.ext_in, f32[2,784,128]{2,1,0:T(8,128)S(1)} %get-tuple-element.23.vel_in, ...), custom_call_target="tpu_custom_call" | custom-call | tf_op jit(solution)/shard_map/model/pallas_call | solution.py:690
  35.4 22.3 %all_to_all.10.gathered = f32[16,32,128]{2,1,0:T(8,128)S(1)} all-to-all(f32[16,32,128]{2,1,0:T(8,128)S(1)} %get-tuple-element.28), channel_id=1, replica_groups={{0,2,4,6,8,10,12,14,16,18,20,22,24,26,28,30},{1,3,5,7,9,11,13,15,17,19,..., dimensions={0} | all-to-all | bytes 524288 | tf_op jit(solution)/shard_map/all_to_all | solution.py:710
  57.7 0.0 copy-done.4
  57.7 0.8 %pick.1 = (f32[4,32,128]{2,1,0:T(8,128)S(1)}, f32[4,32,128]{2,1,0:T(8,128)S(1)}) custom-call(s32[4,8]{1,0:T(4,128)S(1)} %bitcast.5, f32[16,32,128]{2,1,0:T(8,128)S(1)} %all_to_all.10.gathered), custom_call_target="tpu_custom_call" | custom-call | tf_op jit(solution)/shard_map/pick/pallas_call | solution.py:711
  58.5 0.1 collective-permute-start.4
  58.5 1.2 %collective-permute-done.4.received = f32[4,32,128]{2,1,0:T(8,128)S(1)} collective-permute-done((f32[4,32,128]{2,1,0:T(8,128)S(1)}, f32[4,32,128]{2,1,0:T(8,128)S(1)}, u32[]{:S(2)}, u32[]{:S(2)}) %collective-permute-start.4) | collective-permute-done | bytes 65568 | tf_op jit(solution)/shard_map/ppermute | solution.py:720
  59.8 0.7 %join.1 = f32[4,4096]{1,0:T(4,128)} custom-call(f32[4,32,128]{2,1,0:T(8,128)S(1)} %get-tuple-element.29.own, f32[4,32,128]{2,1,0:T(8,128)S(1)} %collective-permute-done.4.received), custom_call_target="tpu_custom_call" | custom-call | tf_op jit(solution)/shard_map/join/pallas_call | solution.py:721
Async XLA Ops:
  0.6 13.6 %copy-start.1 = (f32[2,256,256]{2,1,0:T(8,128)S(1)}, f32[2,256,256]{2,1,0:T(8,128)}, u32[]{:S(2)}) copy-start(f32[2,256,256]{2,1,0:T(8,128)} %obs.5) | copy-start | bytes 1572868
  0.6 13.6 %copy-start = (f32[2,256,256]{2,1,0:T(8,128)S(1)}, f32[2,256,256]{2,1,0:T(8,128)}, u32[]{:S(2)}) copy-start(f32[2,256,256]{2,1,0:T(8,128)} %drive.5) | copy-start | bytes 1572868
  0.7 16.3 %copy-start.3 = (f32[256,256]{1,0:T(8,128)S(1)}, f32[256,256]{1,0:T(8,128)}, u32[]{:S(2)}) copy-start(f32[256,256]{1,0:T(8,128)} %thick.5) | copy-start | bytes 786436
  0.7 15.4 %copy-start.5 = (s32[8,4]{0,1:T(4,128)S(1)}, s32[8,4]{0,1:T(4,128)}, u32[]{:S(2)}) copy-start(s32[8,4]{0,1:T(4,128)} %param.10) | copy-start | bytes 388
  4.4 11.7 %all-to-all-start = ((f32[8,48,128]{2,1,0:T(8,128)}), f32[8,48,128]{2,1,0:T(8,128)S(1)}, u32[]{:S(2)}, u32[]{:S(2)}) async-start(f32[8,48,128]{2,1,0:T(8,128)} %get-tuple-element.17), calls=%async_computation | async-start | bytes 393216 | tf_op jit(solution)/shard_map/all_to_all | solution.py:656
  9.5 4.7 %collective-permute-start = (f32[128,128]{1,0:T(8,128)}, f32[128,128]{1,0:T(8,128)S(1)}, u32[]{:S(2)}, u32[]{:S(2)}) collective-permute-start(f32[128,128]{1,0:T(8,128)} %get-tuple-element.20), channel_id=1, source_target_pairs={{0,8},{16,24},{8,0},{24,16},{1,9},{17,25},{9,1},{25,17},{2,10},{18... | collective-permute-start | bytes 196616 | tf_op jit(solution)/shard_map/ppermute | solution.py:635
  11.2 3.0 %collective-permute-start.1 = (f32[128,128]{1,0:T(8,128)}, f32[128,128]{1,0:T(8,128)S(1)}, u32[]{:S(2)}, u32[]{:S(2)}) collective-permute-start(f32[128,128]{1,0:T(8,128)} %get-tuple-element.21), channel_id=1, source_target_pairs={{8,16},{16,8},{9,17},{17,9},{10,18},{18,10},{11,19},{19,11},{12,20... | collective-permute-start | bytes 196616 | tf_op jit(solution)/shard_map/ppermute | solution.py:635
  14.2 1.0 %copy-start.2 = (f32[256,256]{1,0:T(8,128)S(1)}, f32[256,256]{1,0:T(8,128)}, u32[]{:S(2)}) copy-start(f32[256,256]{1,0:T(8,128)} %thick.5) | copy-start | bytes 786436
  15.3 3.9 %collective-permute-start.2 = (f32[3,64,128]{2,1,0:T(8,128)S(1)}, f32[3,64,128]{2,1,0:T(8,128)S(1)}, u32[]{:S(2)}, u32[]{:S(2)}) collective-permute-start(f32[3,64,128]{2,1,0:T(8,128)S(1)} %get-tuple-element.24), channel_id=1, source_target_pairs={{0,1},{2,3},{4,5},{6,7},{1,0},{3,2},{5,4},{7,6},{8,9},{10,11},{12,... | collective-permute-start | bytes 294920 | tf_op jit(solution)/shard_map/ppermute | solution.py:635
  15.4 3.9 %collective-permute-start.3 = (f32[3,64,128]{2,1,0:T(8,128)S(1)}, f32[3,64,128]{2,1,0:T(8,128)S(1)}, u32[]{:S(2)}, u32[]{:S(2)}) collective-permute-start(f32[3,64,128]{2,1,0:T(8,128)S(1)} %get-tuple-element.25), channel_id=1, source_target_pairs={{1,2},{3,4},{5,6},{2,1},{4,3},{6,5},{9,10},{11,12},{13,14},{10,9},... | collective-permute-start | bytes 294920 | tf_op jit(solution)/shard_map/ppermute | solution.py:635
  19.3 38.4 %copy-start.4 = (s32[8,4,1]{0,2,1:T(1,128)S(1)}, s32[8,4,1]{0,2,1:T(1,128)}, u32[]{:S(2)}) copy-start(s32[8,4,1]{0,2,1:T(1,128)} %param.11) | copy-start | bytes 388
  58.5 1.3 %collective-permute-start.4 = (f32[4,32,128]{2,1,0:T(8,128)S(1)}, f32[4,32,128]{2,1,0:T(8,128)S(1)}, u32[]{:S(2)}, u32[]{:S(2)}) collective-permute-start(f32[4,32,128]{2,1,0:T(8,128)S(1)} %get-tuple-element.30), channel_id=1, source_target_pairs={{0,1},{1,0},{2,3},{3,2},{4,5},{5,4},{6,7},{7,6},{8,9},{9,8},{10,11... | collective-permute-start | bytes 196616 | tf_op jit(solution)/shard_map/ppermute | solution.py:720

commit v11 on v10

--- a/solution.py
+++ b/solution.py
@@ -34,7 +34,7 @@
 FACTORS = 14
 AHEAD = 2
 PACK = COARSE // LANES
-VMEM_LIMIT = 40 * 1024 * 1024
+VMEM_LIMIT = 24 * 1024 * 1024
 PACK_VMEM_LIMIT = 62 * 1024 * 1024
 
 STRIP = ((0, HALO), (HALO, HALO), (2 * HALO, HALO), (3 * HALO, OBS), (3 * HALO + OBS, OBS))
@@ -151,42 +151,64 @@
     return pltpu.roll(cells, shift, 1) if shift else cells
 
 
-def rows_kernel(thick, drive, obs, first_col, second_col, first_pair, second_pair):
+def gather(cells, source):
+    return jnp.take_along_axis(cells, source, axis=1)
+
+
+def scale_of(f):
+    return 0.5 if f in (1, 2) else 1.0
+
+
+def weave_kernel(thick, drive, obs, woven, own_sides, edges):
+    lane, half_lane = lanes_of(TILE), lanes_of(HALF)
+    source = 2 * lane % LANES
+    for f, (field, (first, count)) in enumerate(zip((thick, drive.at[0], drive.at[1], obs.at[0], obs.at[1]), STRIP)):
+        low, high = scale_of(f) * field[:, :LANES], scale_of(f) * field[:, LANES:]
+        tiles = [jnp.where(lane < BAND, gather(low, source + i), gather(high, source + i)) for i in range(2)]
+        bands = []
+        for band in (0, BAND):
+            bands.append(
+                jnp.where(lane % BAND < BAND // 2, turn(high, LANES - HALO, band), turn(low, 0, band + 3 * HALO))
+            )
+        own_sides[f] = jnp.where(half_lane < BAND, bands[0][:HALF], bands[1][HALF:])
+        for c in range(2):
+            woven[f, c] = tiles[c]
+        for c, tile in enumerate(tiles + [bands[1]]):
+            edges[0, c, first : first + count, :] = tile[:count]
+        for c, tile in enumerate(tiles + [bands[0]]):
+            edges[1, c, first : first + count, :] = tile[TILE - count :]
+
+
+def rows_kernel(edges, first_col, second_col, first_pair, second_pair):
     west, east = sides("gx", first_col[...], second_col[...])
     even = is_even("gy")
-    for field, (first, count) in zip((thick, drive.at[0], drive.at[1], obs.at[0], obs.at[1]), STRIP):
+    for c in range(2):
+        top, bottom = edges[0, c], edges[1, c]
+        first_pair[c] = jnp.where(even, bottom, top)
+        second_pair[c] = jnp.where(even, top, bottom)
+    for f, (first, count) in enumerate(STRIP):
         strips = []
-        for rows, packed_rows, source, target in (
-            (slice(0, count), slice(0, count), first, BAND),
-            (slice(TILE - count, TILE), slice(HALF - count, HALF), BAND + first, 0),
+        for i, packed, source, target in (
+            (0, slice(0, count), first, BAND),
+            (1, slice(HALF - count, HALF), BAND + first, 0),
         ):
-            low, high = field[rows, :LANES], field[rows, LANES:]
-            sides_row = choose_side(
-                lanes_of(count),
-                turn(high, LANES - HALO, target),
-                turn(east[packed_rows], source, target + HALO),
-                turn(west[packed_rows], source, target + 3 * HALO - count),
-                turn(low, 0, target + 3 * HALO),
-            )
-            strips.append((low, high, sides_row))
-        for c in range(3):
-            top, bottom = strips[0][c], strips[1][c]
-            first_pair[c, first : first + count, :] = jnp.where(even, bottom, top)
-            second_pair[c, first : first + count, :] = jnp.where(even, top, bottom)
-
-
-def shift_east(tiles, lane):
-    rolled = [pltpu.roll(t, LANES - 1, 1) for t in tiles]
-    if len(tiles) == 1:
-        return rolled
-    return [jnp.where(lane == LANES - 1, rolled[1 - c], rolled[c]) for c in range(2)]
-
-
-def shift_west(tiles, lane):
-    rolled = [pltpu.roll(t, 1, 1) for t in tiles]
-    if len(tiles) == 1:
-        return rolled
-    return [jnp.where(lane == 0, rolled[1 - c], rolled[c]) for c in range(2)]
+            own = edges[i, 2, first : first + count, :]
+            from_east = scale_of(f) * turn(east[packed], source, target + HALO)
+            from_west = scale_of(f) * turn(west[packed], source, target + 3 * HALO - count)
+            strips.append(choose_side(lanes_of(count), own, from_east, from_west, own))
+        top, bottom = strips
+        first_pair[2, first : first + count, :] = jnp.where(even, bottom, top)
+        second_pair[2, first : first + count, :] = jnp.where(even, top, bottom)
+
+
+def shift_east(tiles):
+    turned = pltpu.roll(tiles[0], LANES - 1, 1)
+    return [turned] if len(tiles) == 1 else [tiles[1], turned]
+
+
+def shift_west(tiles):
+    turned = pltpu.roll(tiles[-1], 1, 1)
+    return [turned] if len(tiles) == 1 else [turned, tiles[0]]
 
 
 def run_groups(groups, read, work):
@@ -194,7 +216,7 @@
     for k, (part, row, count) in enumerate(groups):
         if k + AHEAD < len(groups):
             pending.append(read(*groups[k + AHEAD]))
-        for ref, lead, values in work(part, pending[k], lanes_of(count)):
+        for ref, lead, values in work(part, pending[k]):
             for tile, value in zip(part, values):
                 ref[(*lead, pl.ds(row + tile, count), slice(None))] = value
 
@@ -240,33 +262,29 @@
 
     def join(row, upper, lower, count):
         lane = lanes_of(count)
+        place = lane % BAND
         for lead in leads:
             def at(tile_row):
                 return (*lead, pl.ds(tile_row, count), slice(None))
 
             mixed = ref[at(SIDE + row)]
             if whole:
-                place = lane % BAND
-                upper_lane = lane < BAND
-                from_high = jnp.where(
-                    upper_lane,
-                    turn(ref[at(ROWS + row)], LANES - HALO, 0),
-                    turn(ref[at(ROWS + row + HALF)], LANES - HALO, BAND),
-                )
-                from_low = jnp.where(
-                    upper_lane,
-                    turn(ref[at(row)], edge, BAND - edge),
-                    turn(ref[at(row + HALF)], edge, LANES - edge),
-                )
-                ref[at(SIDE + row)] = jnp.where(
-                    place < edge, from_high, jnp.where(place >= BAND - edge, from_low, mixed)
-                )
+                source = jnp.where(place < edge, LANES - edge + place // 2, place // 2 - 24)
+                source = jnp.clip(source, 0, LANES - 1)
+                halves = []
+                for main_row in (row, row + HALF):
+                    even, odd = (gather(ref[at(tile + main_row)], source) for tile in MAIN)
+                    halves.append(jnp.where(lane % 2 == 0, even, odd))
+                outer = (place < edge) | (place >= BAND - edge)
+                ref[at(SIDE + row)] = jnp.where(outer, jnp.where(lane < BAND, halves[0], halves[1]), mixed)
             for wanted, band, main_row in ((upper, 0, row), (lower, BAND, row + HALF)):
                 if wanted:
-                    low = turn(mixed, band + 3 * HALO, 0)
-                    high = turn(mixed, band + edge, LANES - edge)
-                    ref[at(main_row)] = jnp.where(lane < edge, low, ref[at(main_row)])
-                    ref[at(ROWS + main_row)] = jnp.where(lane >= LANES - edge, high, ref[at(ROWS + main_row)])
+                    few = edge // 2
+                    source = band + jnp.where(lane < few, 3 * HALO + 2 * lane, edge + 2 * (lane - LANES + few))
+                    source = jnp.clip(source, 0, LANES - 2)
+                    outer = (lane < few) | (lane >= LANES - few)
+                    for c, tile in enumerate(MAIN):
+                        ref[at(tile + main_row)] = jnp.where(outer, gather(mixed, source + c), ref[at(tile + main_row)])
 
     step = 32
 
@@ -300,17 +318,17 @@
 
     cells = 0.5 * jnp.exp(patch[...])
     lane = lanes_of(PATCH)
-    for c in range(2):
-        wide = jnp.take_along_axis(cells, 32 * c + lane // 4, axis=1)
+    wide = gather(cells, lane // 2)
+    for tile in MAIN:
         for j in range(4):
-            fr[pl.ds(MAIN[c] + MARGIN + j, PATCH, stride=4), :] = wide
+            fr[pl.ds(tile + MARGIN + j, PATCH, stride=4), :] = wide
     lane = lanes_of(40)
     place = lane % BAND // 4
     source = jnp.where(place < 8, 60 + place, (116 + place) % LANES)
     wide = jnp.where(
         lane < BAND,
-        jnp.take_along_axis(cells[:40], source, axis=1),
-        jnp.take_along_axis(cells[PATCH - 40 :], source, axis=1),
+        gather(cells[:40], source),
+        gather(cells[PATCH - 40 :], source),
     )
     for j in range(4):
         fr[pl.ds(SIDE + MARGIN + j, 40, stride=4), :] = wide
@@ -347,20 +365,20 @@
     def read_thickness(part, row, count):
         return load(ext, part, row, count, 0)
 
-    def keep_viscosity(q, lane):
-        return [(visc, (0,), q), (visc, (1,), shift_west(q, lane)), (visc, (2,), shift_east(q, lane))]
-
-    def first_viscosity(part, thickness, lane):
+    def keep_viscosity(q):
+        return [(visc, (0,), q), (visc, (1,), shift_west(q)), (visc, (2,), shift_east(q))]
+
+    def first_viscosity(part, thickness):
         factor = 0.25 * visc_scale * strain_floor ** (-1.0 / 3.0)
-        return keep_viscosity([factor * t for t in thickness], lane)
+        return keep_viscosity([factor * t for t in thickness])
 
     def read_viscosity(part, row, count):
         return read_thickness(part, row, count), load_around(part, row, count, vel_b)
 
-    def viscosity(part, read, lane):
+    def viscosity(part, read):
         thickness, (u, u_n, u_s, v, v_n, v_s) = read
-        u_e, u_w = shift_east(u, lane), shift_west(u, lane)
-        v_e, v_w = shift_east(v, lane), shift_west(v, lane)
+        u_e, u_w = shift_east(u), shift_west(u)
+        v_e, v_w = shift_east(v), shift_west(v)
         result = []
         for c in range(len(part)):
             ux, vx = u_e[c] - u_w[c], v_e[c] - v_w[c]
@@ -368,7 +386,7 @@
             shear = uy + vx
             strain = 0.25 * (ux * (ux + vy) + vy * vy) + (0.0625 * (shear * shear) + strain_floor)
             result.append((0.25 * visc_scale) * thickness[c] * jnp.exp(jnp.log(strain) * (-1.0 / 3.0)))
-        return keep_viscosity(result, lane)
+        return keep_viscosity(result)
 
     def inverse(x):
         near = pl.reciprocal(x, approx=True)
@@ -397,7 +415,7 @@
             corners.append([half[c] + shifted[c] for c in tiles])
         return [e, w, s, n, scale_u, scale_v] + corners
 
-    def relax(part, k, around, right, lane):
+    def relax(part, k, around, right):
         tiles = range(len(part))
         e, w, s, n, scale_u, scale_v, sw_u, sw_v, nw_u, nw_v, se_u, se_v, ne_u, ne_v = k
         u, u_n, u_s, v, v_n, v_s = around
@@ -408,8 +426,8 @@
             to_east_u.append(e[c] * u4 + (ne_u[c] * v_n[c] - se_u[c] * v_s[c]))
             to_west_v.append(w[c] * v[c] + (sw_v[c] * u_s[c] - nw_v[c] * u_n[c]))
             to_east_v.append(e[c] * v[c] + (ne_v[c] * u_n[c] - se_v[c] * u_s[c]))
-        to_west_u, to_west_v = shift_east(to_west_u, lane), shift_east(to_west_v, lane)
-        to_east_u, to_east_v = shift_west(to_east_u, lane), shift_west(to_east_v, lane)
+        to_west_u, to_west_v = shift_east(to_west_u), shift_east(to_west_v)
+        to_east_u, to_east_v = shift_west(to_east_u), shift_west(to_east_v)
         new_u, new_v = [], []
         for c in tiles:
             mid_u = s[c] * u_s[c] + n[c] * u_n[c]
@@ -432,47 +450,39 @@
         return read
 
     def sweep(new):
-        return lambda part, read, lane: put(new, relax(part, *read, lane))
+        return lambda part, read: put(new, relax(part, *read))
 
     def read_first(part, row, count):
         return read_coefficients(part, row, count), load_right(part, row, count)
 
-    def first_start(part, read, lane):
+    def first_start(part, read):
         k = coefficients(part, read[0])
         return keep(k) + put(vel_a, [[a * b for a, b in zip(k[4 + i], read[1][i])] for i in range(2)])
 
     def read_start(part, row, count):
         return (*read_first(part, row, count), load_around(part, row, count, vel_b))
 
-    def start(part, read, lane):
+    def start(part, read):
         k = coefficients(part, read[0])
-        return keep(k) + put(vel_a, relax(part, k, read[2], read[1], lane))
+        return keep(k) + put(vel_a, relax(part, k, read[2], read[1]))
 
     return SimpleNamespace(**locals())
 
 
 def setup_kernel(
-    fr, ice, thick, drive, obs, first_col, second_col,
+    fr, ice, woven, own_sides, first_col, second_col,
     ext, vel_b,
     visc, vel_a, coef,
 ):
     west, east = sides("gx", first_col[...], second_col[...])
     lane = lanes_of(HALF)
-    upper = lane < BAND
-    for f, (field, (first, count)) in enumerate(zip((thick, drive.at[0], drive.at[1], obs.at[0], obs.at[1]), STRIP)):
-        scale = 0.5 if f in (1, 2) else 1.0
+    for f, (first, count) in enumerate(STRIP):
         for c in range(2):
-            ext[f, MAIN[c] + TOP : MAIN[c] + TOP + TILE, :] = scale * field[:, c * LANES : (c + 1) * LANES]
-        halves = (slice(0, HALF), slice(HALF, TILE))
-        high = [turn(field[halves[b], LANES:], LANES - HALO, BAND * b) for b in range(2)]
-        low = [turn(field[halves[b], :LANES], 0, BAND * b + 3 * HALO) for b in range(2)]
-        ext[f, SIDE + TOP : SIDE + TOP + HALF, :] = scale * choose_side(
-            lane,
-            jnp.where(upper, high[0], high[1]),
-            turn(east, first, HALO),
-            turn(west, first, 3 * HALO - count),
-            jnp.where(upper, low[0], low[1]),
-        )
+            ext[f, MAIN[c] + TOP : MAIN[c] + TOP + TILE, :] = woven[f, c]
+        from_east = scale_of(f) * turn(east, first, HALO)
+        from_west = scale_of(f) * turn(west, first, 3 * HALO - count)
+        own = own_sides[f]
+        ext[f, SIDE + TOP : SIDE + TOP + HALF, :] = choose_side(lane, own, from_east, from_west, own)
     step = make_stages(ext, fr, ice, visc, vel_a, vel_b, coef)
     over_rows("tile", step.read_thickness, step.first_viscosity)
     over_rows("tile", step.read_first, step.first_start)
@@ -482,17 +492,16 @@
 def model_kernel(
     fr, ice, ext_in, vel_in, first_row, second_row,
     vel_u, vel_v, sums,
-    ext, visc, vel_a, vel_b, vel_c, coef, small, sems,
+    ext, visc, vel_a, vel_b, vel_c, coef, plain, small, sems,
 ):
     ext[...] = ext_in[...]
     vel_b[...] = vel_in[...]
     even = is_even("gy")
     here = SIDE + TOP
     for f, (first, count) in enumerate(STRIP):
-        scale = 0.5 if f in (1, 2) else 1.0
         frames = []
         for c in range(3):
-            one, two = scale * first_row[c, first : first + count, :], scale * second_row[c, first : first + count, :]
+            one, two = first_row[c, first : first + count, :], second_row[c, first : first + count, :]
             frames.append((jnp.where(even, two, one), jnp.where(even, one, two)))
         for c in range(2):
             ext[f, MAIN[c] + TOP - count : MAIN[c] + TOP, :] = frames[c][0]
@@ -521,15 +530,15 @@
     join_parts(vel_b, ((0,), (1,)), True)
     iterate("inner")
     join_parts(vel_b, ((0,), (1,)), False)
+    lane = lanes_of(TILE)
     copies = []
     for i, out in enumerate((vel_u, vel_v)):
+        even, odd = (vel_b[i, tile + TOP : tile + TOP + TILE, :] for tile in MAIN)
         for c in range(2):
+            source = BAND * c + lane // 2
+            plain[i, c] = jnp.where(lane % 2 == 0, gather(even, source), gather(odd, source))
             copies.append(
-                pltpu.make_async_copy(
-                    vel_b.at[i, MAIN[c] + TOP : MAIN[c] + TOP + TILE, :],
-                    out.at[:, c * LANES : (c + 1) * LANES],
-                    sems.at[2 * i + c],
-                )
+                pltpu.make_async_copy(plain.at[i, c], out.at[:, c * LANES : (c + 1) * LANES], sems.at[2 * i + c])
             )
             copies[-1].start()
 
@@ -541,7 +550,7 @@
             for i in range(2)
         ]
 
-    def first_adjoint(part, read, lane):
+    def first_adjoint(part, read):
         misfit = [[0.5 * (a - b) for a, b in zip(u, seen)] for u, seen, _ in read]
         first = [[a * b for a, b in zip(read[i][2], misfit[i])] for i in range(2)]
         return step.put(vel_c, first) + [(ext, (1 + i,), misfit[i]) for i in range(2)]
@@ -559,23 +568,20 @@
     def read_gradient(part, row, count):
         return [load(ref, part, row, count, i) for ref in (vel_b, vel_a) for i in range(2)] + [load(fr, part, row, count)]
 
-    def gradient(part, read, lane):
+    def gradient(part, read):
         u, v, lu, lv, friction = read
         return [(visc, (0,), [-2.0 * friction[c] * (u[c] * lu[c] + v[c] * lv[c]) for c in range(len(part))])]
 
     over_rows("tile", read_gradient, gradient)
     join_parts(visc, ((0,),), False)
-    down = [sum(visc[0, pl.ds(MAIN[c] + TOP + j, CT, stride=4), :] for j in range(4)) for c in range(2)]
+    down = sum(visc[0, pl.ds(tile + TOP + j, CT, stride=4), :] for tile in MAIN for j in range(4))
     k = lax.broadcasted_iota(jnp.int32, (LANES, LANES), 0)
-    l = lanes_of(LANES) % CT
-    total = jnp.zeros((CT, LANES), jnp.float32)
-    for c in range(2):
-        total += jnp.dot(
-            down[c],
-            (k // 4 + 32 * c == l).astype(jnp.float32),
-            precision=lax.Precision.HIGHEST,
-            preferred_element_type=jnp.float32,
-        )
+    total = jnp.dot(
+        down,
+        (k // 2 == lanes_of(LANES) % CT).astype(jnp.float32),
+        precision=lax.Precision.HIGHEST,
+        preferred_element_type=jnp.float32,
+    )
     small[...] = total
     packed = jnp.where(
         lanes_of(PACK) < CT, small[pl.ds(0, PACK, stride=2), :], small[pl.ds(1, PACK, stride=2), :]
@@ -655,14 +661,22 @@
     )(tile_block, control, *fields)
     parcels = lax.all_to_all(parcels, "gy", 0, 0, tiled=True)
     columns_in = swap("gx", *edges)
+    woven, own_sides, strips = pl.pallas_call(
+        weave_kernel,
+        out_shape=[shape(5, 2, TILE, LANES), shape(5, HALF, LANES), shape(2, 3, 64, LANES)],
+        in_specs=in_vmem(3),
+        out_specs=in_vmem(3),
+        compiler_params=params,
+        name="weave",
+    )(*fields)
     strips = pl.pallas_call(
         rows_kernel,
         out_shape=[shape(3, 64, LANES)] * 2,
-        in_specs=in_vmem(5),
+        in_specs=in_vmem(3),
         out_specs=in_vmem(2),
         compiler_params=params,
         name="rows",
-    )(*fields, *columns_in)
+    )(strips, *columns_in)
     rows_in = swap("gy", *strips)
     friction = pl.pallas_call(
         friction_kernel,
@@ -676,7 +690,7 @@
     prepared = pl.pallas_call(
         setup_kernel,
         out_shape=[shape(5, ALL_ROWS, LANES), shape(2, ALL_ROWS, LANES)],
-        in_specs=in_vmem(7),
+        in_specs=in_vmem(6),
         out_specs=in_vmem(2),
         scratch_shapes=[
             pltpu.VMEM((3, ALL_ROWS, LANES), f32),
@@ -685,7 +699,7 @@
         ],
         compiler_params=params,
         name="setup",
-    )(*friction, *fields, *columns_in)
+    )(*friction, woven, own_sides, *columns_in)
 
     vel_u, vel_v, sums = pl.pallas_call(
         model_kernel,
@@ -699,6 +713,7 @@
             pltpu.VMEM((2, ALL_ROWS, LANES), f32),
             pltpu.VMEM((2, ALL_ROWS, LANES), f32),
             pltpu.VMEM((FACTORS, ALL_ROWS, LANES), f32),
+            pltpu.VMEM((2, 2, TILE, LANES), f32),
             pltpu.VMEM((CT, LANES), f32),
             pltpu.SemaphoreType.DMA((4,)),
         ],

time: 60.8 us -> 57.4 us (0.944)
  waiting for transfers between devices: 3.63 us -> 1.76 us
  Pallas kernels: 24.5 us -> 22.7 us
    pallas_call x1, Pallas kernels: 16.1 us -> 13.8 us  [per_device(): pl.pallas_call(model_kernel, out_shape=(shape(TILE, TILE), shape(TILE, TI...]
    ppermute x4, waiting for transfers between devices: 2.38 us -> 0.18 us  [swap(): lax.ppermute(cells, axis, pairs + [(j, i) for i, j in pairs])]
    pallas_call x0 -> x1, Pallas kernels: none -> 1.15 us  [per_device(): pl.pallas_call(weave_kernel, out_shape=[shape(5, 2, TILE, LANES), shape(5...]
  transfers between devices with their start and end apart: 6 -> 6, of which waited for: 2 -> 3; matrix products, arithmetic and copies ran while one was open for 0% -> 0% of each run, Pallas kernels for 5% -> 7%
where the time goes in v11:
time: 57.4 us; the launch traced here: 57.1 us
  Pallas kernels  22.7 us (40%)
  blocking collectives  22.3 us (39%)
  starting transfers between devices  8.6 us (15%)
  waiting for transfers between devices  1.76 us (3%)
  local copies, waits for them, and re-layouts  0.96 us (2%)
  between operations  0.78 us (1%)
    all_to_all x1, blocking collectives, per_device(): lax.all_to_all(sums, ('gx', 'gy'), 0, 0, tiled=True, axis_index_groups=sa...  22.3 us
    pallas_call x1, Pallas kernels, per_device(): pl.pallas_call(model_kernel, out_shape=(shape(TILE, TILE), shape(TILE, TI...  13.8 us
    all_to_all x1, starting transfers between devices, per_device(): parcels = lax.all_to_all(parcels, 'gy', 0, 0, tiled=True)  5.08 us
    pallas_call x1, Pallas kernels, per_device(): pl.pallas_call(pack_kernel, out_shape=[shape(HALF, LANES)] * 2 + [shape(r...  3.6 us
    ppermute x4, starting transfers between devices, swap(): lax.ppermute(cells, axis, pairs + [(j, i) for i, j in pairs])  3.45 us
    pallas_call x1, Pallas kernels, per_device(): pl.pallas_call(setup_kernel, out_shape=[shape(5, ALL_ROWS, LANES), shape(...  1.82 us
    ppermute x1, waiting for transfers between devices, per_device(): received = lax.ppermute(other, 'gy', [(j, j ^ 1) for j in range(rows)])  1.24 us
    pallas_call x1, Pallas kernels, per_device(): pl.pallas_call(weave_kernel, out_shape=[shape(5, 2, TILE, LANES), shape(5...  1.15 us
  transfers between devices with their start and end apart: 6, of which 3 were waited for; matrix products, arithmetic and copies ran while one was open for 0% of the time, Pallas kernels for 7%

profile of v11, /device:TPU:0, one launch (start us, length us, event | category | flops | bytes accessed | tf_op | source)
XLA Modules:
  0.0 57.1 jit_solution(7030678664268490806)
XLA Ops:
  0.6 0.0 copy-start.1
  0.6 0.0 copy-start
  0.7 0.0 copy-start.4
  0.7 3.6 %pack.1 = (f32[128,128]{1,0:T(8,128)}, f32[128,128]{1,0:T(8,128)}, f32[8,48,128]{2,1,0:T(8,128)}) custom-call(s32[4,8]{1,0:T(4,128)} %bitcast.4, f32[4,4096]{1,0:T(4,128)} %control.1, f32[256,256]{1,0:T(8,128)} %thick.3, f32[2,256,256]{2,1,0:T(8,128)} %drive.3, f32[2,256,256]{2,1,0:T(8,128)} %obs.3), custom_call_target="tpu_custom_call" | custom-call | tf_op jit(solution)/shard_map/pack/pallas_call | solution.py:646
  4.3 5.1 %all-to-all-start = ((f32[8,48,128]{2,1,0:T(8,128)}), f32[8,48,128]{2,1,0:T(8,128)S(1)}, u32[]{:S(2)}, u32[]{:S(2)}) async-start(f32[8,48,128]{2,1,0:T(8,128)} %get-tuple-element.20), calls=%async_computation | async-start | bytes 393216 | tf_op jit(solution)/shard_map/all_to_all | solution.py:662
  9.4 2.0 %collective-permute-start = (f32[128,128]{1,0:T(8,128)}, f32[128,128]{1,0:T(8,128)S(1)}, u32[]{:S(2)}, u32[]{:S(2)}) collective-permute-start(f32[128,128]{1,0:T(8,128)} %get-tuple-element.25), channel_id=1, source_target_pairs={{0,8},{16,24},{8,0},{24,16},{1,9},{17,25},{9,1},{25,17},{2,10},{18... | collective-permute-start | bytes 196616 | tf_op jit(solution)/shard_map/ppermute | solution.py:641
  11.4 0.7 %collective-permute-start.1 = (f32[128,128]{1,0:T(8,128)}, f32[128,128]{1,0:T(8,128)S(1)}, u32[]{:S(2)}, u32[]{:S(2)}) collective-permute-start(f32[128,128]{1,0:T(8,128)} %get-tuple-element.26), channel_id=1, source_target_pairs={{8,16},{16,8},{9,17},{17,9},{10,18},{18,10},{11,19},{19,11},{12,20... | collective-permute-start | bytes 196616 | tf_op jit(solution)/shard_map/ppermute | solution.py:641
  12.0 0.0 copy-done.1
  12.0 0.0 copy-done
  12.0 0.0 copy-start.2
  12.0 0.9 %copy-done.2 = f32[256,256]{1,0:T(8,128)S(1)} copy-done((f32[256,256]{1,0:T(8,128)S(1)}, f32[256,256]{1,0:T(8,128)}, u32[]{:S(2)}) %copy-start.2) | copy-done | bytes 262168
  13.0 1.2 %weave.1 = (f32[5,2,256,128]{3,2,1,0:T(8,128)S(1)}, f32[5,128,128]{2,1,0:T(8,128)S(1)}, f32[2,3,64,128]{3,2,1,0:T(8,128)S(1)}) custom-call(f32[256,256]{1,0:T(8,128)S(1)} %copy-done.2, f32[2,256,256]{2,1,0:T(8,128)S(1)} %copy-done, f32[2,256,256]{2,1,0:T(8,128)S(1)} %copy-done.1), custom_call_target="tpu_custom_call" | custom-call | tf_op jit(solution)/shard_map/weave/pallas_call | solution.py:664
  14.2 0.2 collective-permute-done.first_col
  14.3 0.0 collective-permute-done.1.second_col
  14.3 0.1 rows.1
  14.4 0.1 collective-permute-start.2
  14.6 0.7 %collective-permute-start.3 = (f32[3,64,128]{2,1,0:T(8,128)S(1)}, f32[3,64,128]{2,1,0:T(8,128)S(1)}, u32[]{:S(2)}, u32[]{:S(2)}) collective-permute-start(f32[3,64,128]{2,1,0:T(8,128)S(1)} %get-tuple-element.31), channel_id=1, source_target_pairs={{1,2},{3,4},{5,6},{2,1},{4,3},{6,5},{9,10},{11,12},{13,14},{10,9},... | collective-permute-start | bytes 294920 | tf_op jit(solution)/shard_map/ppermute | solution.py:641
  15.2 0.3 all-to-all-done.parcels
  15.6 0.0 copy-done.4
  15.6 0.8 %friction.1 = (f32[784,128]{1,0:T(8,128)S(1)}, f32[784,128]{1,0:T(8,128)S(1)}) custom-call(s32[4,8]{1,0:T(4,128)S(1)} %bitcast.6, f32[8,48,128]{2,1,0:T(8,128)S(1)} %all-to-all-done.parcels), custom_call_target="tpu_custom_call" | custom-call | tf_op jit(solution)/shard_map/friction/pallas_call | solution.py:681
  16.4 1.8 %setup.1 = (f32[5,784,128]{2,1,0:T(8,128)S(1)}, f32[2,784,128]{2,1,0:T(8,128)S(1)}) custom-call(f32[784,128]{1,0:T(8,128)S(1)} %get-tuple-element.21.fr, f32[784,128]{1,0:T(8,128)S(1)} %get-tuple-element.22.ice, f32[5,2,256,128]{3,2,1,0:T(8,128)S(1)} %get-tuple-element.23.woven, f32[5,128,128]{2,1,0:T(8,128)S(1)} %get-tuple-element.24.own_sides, ...), custom_call_target="tpu_custom_call" | custom-call | tf_op jit(solution)/shard_map/setup/pallas_call | solution.py:690
  18.2 0.0 collective-permute-done.2.first_row
  18.3 0.0 collective-permute-done.3.second_row
  18.3 0.0 copy-start.3
  18.3 13.8 %model.1 = (f32[256,256]{1,0:T(8,128)}, f32[256,256]{1,0:T(8,128)}, f32[16,32,128]{2,1,0:T(8,128)S(1)}) custom-call(f32[784,128]{1,0:T(8,128)S(1)} %get-tuple-element.21.fr, f32[784,128]{1,0:T(8,128)S(1)} %get-tuple-element.22.ice, f32[5,784,128]{2,1,0:T(8,128)S(1)} %get-tuple-element.27.ext_in, f32[2,784,128]{2,1,0:T(8,128)S(1)} %get-tuple-element.28.vel_in, ...), custom_call_target="tpu_custom_call" | custom-call | tf_op jit(solution)/shard_map/model/pallas_call | solution.py:704
  32.1 22.3 %all_to_all.10.gathered = f32[16,32,128]{2,1,0:T(8,128)S(1)} all-to-all(f32[16,32,128]{2,1,0:T(8,128)S(1)} %get-tuple-element.34), channel_id=1, replica_groups={{0,2,4,6,8,10,12,14,16,18,20,22,24,26,28,30},{1,3,5,7,9,11,13,15,17,19,..., dimensions={0} | all-to-all | bytes 524288 | tf_op jit(solution)/shard_map/all_to_all | solution.py:725
  54.4 0.0 copy-done.3
  54.4 0.8 %pick.1 = (f32[4,32,128]{2,1,0:T(8,128)S(1)}, f32[4,32,128]{2,1,0:T(8,128)S(1)}) custom-call(s32[4,8]{1,0:T(4,128)S(1)} %bitcast.5, f32[16,32,128]{2,1,0:T(8,128)S(1)} %all_to_all.10.gathered), custom_call_target="tpu_custom_call" | custom-call | tf_op jit(solution)/shard_map/pick/pallas_call | solution.py:726
  55.1 0.1 collective-permute-start.4
  55.2 1.2 %collective-permute-done.4.received = f32[4,32,128]{2,1,0:T(8,128)S(1)} collective-permute-done((f32[4,32,128]{2,1,0:T(8,128)S(1)}, f32[4,32,128]{2,1,0:T(8,128)S(1)}, u32[]{:S(2)}, u32[]{:S(2)}) %collective-permute-start.4) | collective-permute-done | bytes 65568 | tf_op jit(solution)/shard_map/ppermute | solution.py:735
  56.5 0.7 %join.1 = f32[4,4096]{1,0:T(4,128)} custom-call(f32[4,32,128]{2,1,0:T(8,128)S(1)} %get-tuple-element.35.own, f32[4,32,128]{2,1,0:T(8,128)S(1)} %collective-permute-done.4.received), custom_call_target="tpu_custom_call" | custom-call | tf_op jit(solution)/shard_map/join/pallas_call | solution.py:736
Async XLA Ops:
  0.6 11.4 %copy-start.1 = (f32[2,256,256]{2,1,0:T(8,128)S(1)}, f32[2,256,256]{2,1,0:T(8,128)}, u32[]{:S(2)}) copy-start(f32[2,256,256]{2,1,0:T(8,128)} %obs.3) | copy-start | bytes 1572868
  0.6 11.4 %copy-start = (f32[2,256,256]{2,1,0:T(8,128)S(1)}, f32[2,256,256]{2,1,0:T(8,128)}, u32[]{:S(2)}) copy-start(f32[2,256,256]{2,1,0:T(8,128)} %drive.3) | copy-start | bytes 1572868
  0.7 14.9 %copy-start.4 = (s32[8,4]{0,1:T(4,128)S(1)}, s32[8,4]{0,1:T(4,128)}, u32[]{:S(2)}) copy-start(s32[8,4]{0,1:T(4,128)} %param.10) | copy-start | bytes 388
  4.3 11.3 %all-to-all-start = ((f32[8,48,128]{2,1,0:T(8,128)}), f32[8,48,128]{2,1,0:T(8,128)S(1)}, u32[]{:S(2)}, u32[]{:S(2)}) async-start(f32[8,48,128]{2,1,0:T(8,128)} %get-tuple-element.20), calls=%async_computation | async-start | bytes 393216 | tf_op jit(solution)/shard_map/all_to_all | solution.py:662
  9.4 5.0 %collective-permute-start = (f32[128,128]{1,0:T(8,128)}, f32[128,128]{1,0:T(8,128)S(1)}, u32[]{:S(2)}, u32[]{:S(2)}) collective-permute-start(f32[128,128]{1,0:T(8,128)} %get-tuple-element.25), channel_id=1, source_target_pairs={{0,8},{16,24},{8,0},{24,16},{1,9},{17,25},{9,1},{25,17},{2,10},{18... | collective-permute-start | bytes 196616 | tf_op jit(solution)/shard_map/ppermute | solution.py:641
  11.4 3.0 %collective-permute-start.1 = (f32[128,128]{1,0:T(8,128)}, f32[128,128]{1,0:T(8,128)S(1)}, u32[]{:S(2)}, u32[]{:S(2)}) collective-permute-start(f32[128,128]{1,0:T(8,128)} %get-tuple-element.26), channel_id=1, source_target_pairs={{8,16},{16,8},{9,17},{17,9},{10,18},{18,10},{11,19},{19,11},{12,20... | collective-permute-start | bytes 196616 | tf_op jit(solution)/shard_map/ppermute | solution.py:641
  12.0 1.0 %copy-start.2 = (f32[256,256]{1,0:T(8,128)S(1)}, f32[256,256]{1,0:T(8,128)}, u32[]{:S(2)}) copy-start(f32[256,256]{1,0:T(8,128)} %thick.3) | copy-start | bytes 786436
  14.4 3.8 %collective-permute-start.2 = (f32[3,64,128]{2,1,0:T(8,128)S(1)}, f32[3,64,128]{2,1,0:T(8,128)S(1)}, u32[]{:S(2)}, u32[]{:S(2)}) collective-permute-start(f32[3,64,128]{2,1,0:T(8,128)S(1)} %get-tuple-element.30), channel_id=1, source_target_pairs={{0,1},{2,3},{4,5},{6,7},{1,0},{3,2},{5,4},{7,6},{8,9},{10,11},{12,... | collective-permute-start | bytes 294920 | tf_op jit(solution)/shard_map/ppermute | solution.py:641
  14.6 3.7 %collective-permute-start.3 = (f32[3,64,128]{2,1,0:T(8,128)S(1)}, f32[3,64,128]{2,1,0:T(8,128)S(1)}, u32[]{:S(2)}, u32[]{:S(2)}) collective-permute-start(f32[3,64,128]{2,1,0:T(8,128)S(1)} %get-tuple-element.31), channel_id=1, source_target_pairs={{1,2},{3,4},{5,6},{2,1},{4,3},{6,5},{9,10},{11,12},{13,14},{10,9},... | collective-permute-start | bytes 294920 | tf_op jit(solution)/shard_map/ppermute | solution.py:641
  18.3 36.1 %copy-start.3 = (s32[8,4,1]{0,2,1:T(1,128)S(1)}, s32[8,4,1]{0,2,1:T(1,128)}, u32[]{:S(2)}) copy-start(s32[8,4,1]{0,2,1:T(1,128)} %param.11) | copy-start | bytes 388
  55.1 1.3 %collective-permute-start.4 = (f32[4,32,128]{2,1,0:T(8,128)S(1)}, f32[4,32,128]{2,1,0:T(8,128)S(1)}, u32[]{:S(2)}, u32[]{:S(2)}) collective-permute-start(f32[4,32,128]{2,1,0:T(8,128)S(1)} %get-tuple-element.36), channel_id=1, source_target_pairs={{0,1},{1,0},{2,3},{3,2},{4,5},{5,4},{6,7},{7,6},{8,9},{9,8},{10,11... | collective-permute-start | bytes 196616 | tf_op jit(solution)/shard_map/ppermute | solution.py:735

commit v12 on v11

--- a/solution.py
+++ b/solution.py
@@ -32,7 +32,7 @@
     "tile": (TOP, 4, 64, TOP, 32, 0, 0),
 }
 FACTORS = 14
-AHEAD = 2
+AHEAD = 5
 PACK = COARSE // LANES
 VMEM_LIMIT = 24 * 1024 * 1024
 PACK_VMEM_LIMIT = 62 * 1024 * 1024
@@ -132,6 +132,10 @@
         results[-1].start()
     for copy in results:
         copy.wait()
+
+
+def pass_kernel(parcels, after, out):
+    pass
 
 
 def sides(axis, first_pair, second_pair):
@@ -659,8 +663,17 @@
         compiler_params=pltpu.CompilerParams(vmem_limit_bytes=PACK_VMEM_LIMIT),
         name="pack",
     )(tile_block, control, *fields)
+    columns_in = swap("gx", *edges)
+    parcels = pl.pallas_call(
+        pass_kernel,
+        out_shape=shape(*parcels.shape),
+        in_specs=[pl.BlockSpec(memory_space=pl.ANY)] * 2,
+        out_specs=pl.BlockSpec(memory_space=pl.ANY),
+        input_output_aliases={0: 0},
+        compiler_params=pltpu.CompilerParams(vmem_limit_bytes=1024 * 1024),
+        name="pass",
+    )(parcels, columns_in[0])
     parcels = lax.all_to_all(parcels, "gy", 0, 0, tiled=True)
-    columns_in = swap("gx", *edges)
     woven, own_sides, strips = pl.pallas_call(
         weave_kernel,
         out_shape=[shape(5, 2, TILE, LANES), shape(5, HALF, LANES), shape(2, 3, 64, LANES)],

time: 57.4 us -> 62 us (1.080)
  waiting for transfers between devices: 1.76 us -> 6.75 us
  blocking collectives: 22.3 us -> 20.6 us
  local copies, waits for them, and re-layouts: 0.96 us -> 1.63 us
    all_to_all x1, waiting for transfers between devices: 0.34 us -> 3.02 us  [per_device(): parcels = lax.all_to_all(parcels, 'gy', 0, 0, tiled=True)]
    ppermute x4, waiting for transfers between devices: 0.18 us -> 2.49 us  [swap(): lax.ppermute(cells, axis, pairs + [(j, i) for i, j in pairs])]
    all_to_all x1, blocking collectives: 22.3 us -> 20.6 us  [per_device(): lax.all_to_all(sums, ('gx', 'gy'), 0, 0, tiled=True, axis_index_groups=sa...]
    ppermute x4, starting transfers between devices: 3.45 us -> 4.98 us  [swap(): lax.ppermute(cells, axis, pairs + [(j, i) for i, j in pairs])]
    all_to_all x1, starting transfers between devices: 5.08 us -> 4.16 us  [per_device(): parcels = lax.all_to_all(parcels, 'gy', 0, 0, tiled=True)]
    unnamed x10 -> x14, local copies, waits for them, and re-layouts: 0.96 us -> 1.63 us
  transfers between devices with their start and end apart: 6 -> 6, of which waited for: 3 -> 3; matrix products, arithmetic and copies ran while one was open for 0% -> 0% of each run, Pallas kernels for 7% -> 6%
where the time goes in v12:
time: 62 us; the launch traced here: 61.7 us
  Pallas kernels  22.7 us (37%)
  blocking collectives  20.6 us (33%)
  starting transfers between devices  9.2 us (15%)
  waiting for transfers between devices  6.75 us (11%)
  local copies, waits for them, and re-layouts  1.63 us (3%)
  between operations  0.8 us (1%)
    all_to_all x1, blocking collectives, per_device(): lax.all_to_all(sums, ('gx', 'gy'), 0, 0, tiled=True, axis_index_groups=sa...  20.6 us
    pallas_call x1, Pallas kernels, per_device(): pl.pallas_call(model_kernel, out_shape=(shape(TILE, TILE), shape(TILE, TI...  13.8 us
    ppermute x4, starting transfers between devices, swap(): lax.ppermute(cells, axis, pairs + [(j, i) for i, j in pairs])  4.98 us
    all_to_all x1, starting transfers between devices, per_device(): parcels = lax.all_to_all(parcels, 'gy', 0, 0, tiled=True)  4.16 us
    pallas_call x1, Pallas kernels, per_device(): pl.pallas_call(pack_kernel, out_shape=[shape(HALF, LANES)] * 2 + [shape(r...  3.6 us
    all_to_all x1, waiting for transfers between devices, per_device(): parcels = lax.all_to_all(parcels, 'gy', 0, 0, tiled=True)  3.02 us
    ppermute x4, waiting for transfers between devices, swap(): lax.ppermute(cells, axis, pairs + [(j, i) for i, j in pairs])  2.49 us
    pallas_call x1, Pallas kernels, per_device(): pl.pallas_call(setup_kernel, out_shape=[shape(5, ALL_ROWS, LANES), shape(...  1.82 us
  transfers between devices with their start and end apart: 6, of which 3 were waited for; matrix products, arithmetic and copies ran while one was open for 0% of the time, Pallas kernels for 6%

profile of v12, /device:TPU:0, one launch (start us, length us, event | category | flops | bytes accessed | tf_op | source)
XLA Modules:
  0.0 61.7 jit_solution(3386067882151202710)
XLA Ops:
  0.6 0.0 copy-start.1
  0.6 0.0 copy-start
  0.7 0.0 copy-start.2
  0.7 0.0 copy-start.6
  0.7 3.6 %pack.1 = (f32[128,128]{1,0:T(8,128)}, f32[128,128]{1,0:T(8,128)}, f32[8,48,128]{2,1,0:T(8,128)}) custom-call(s32[4,8]{1,0:T(4,128)} %bitcast.4, f32[4,4096]{1,0:T(4,128)} %control.1, f32[256,256]{1,0:T(8,128)} %thick.3, f32[2,256,256]{2,1,0:T(8,128)} %drive.3, f32[2,256,256]{2,1,0:T(8,128)} %obs.3), custom_call_target="tpu_custom_call" | custom-call | tf_op jit(solution)/shard_map/pack/pallas_call | solution.py:650
  4.3 3.1 %collective-permute-start = (f32[128,128]{1,0:T(8,128)}, f32[128,128]{1,0:T(8,128)S(1)}, u32[]{:S(2)}, u32[]{:S(2)}) collective-permute-start(f32[128,128]{1,0:T(8,128)} %get-tuple-element.21), channel_id=1, source_target_pairs={{0,8},{16,24},{8,0},{24,16},{1,9},{17,25},{9,1},{25,17},{2,10},{18... | collective-permute-start | bytes 196616 | tf_op jit(solution)/shard_map/ppermute | solution.py:645
  7.4 2.5 %collective-permute-done.after.first_col = f32[128,128]{1,0:T(8,128)S(1)} collective-permute-done((f32[128,128]{1,0:T(8,128)}, f32[128,128]{1,0:T(8,128)S(1)}, u32[]{:S(2)}, u32[]{:S(2)}) %collective-permute-start) | collective-permute-done | bytes 65568 | tf_op jit(solution)/shard_map/ppermute | solution.py:645
  9.9 0.0 copy-start.3
  9.9 0.9 %copy-done.3 = f32[8,48,128]{2,1,0:T(8,128)S(1)} copy-done((f32[8,48,128]{2,1,0:T(8,128)S(1)}, f32[8,48,128]{2,1,0:T(8,128)}, u32[]{:S(2)}) %copy-start.3) | copy-done | bytes 196632
  10.8 0.0 copy-start.4
  10.8 0.7 %copy-done.4 = f32[8,48,128]{2,1,0:T(8,128)} copy-done((f32[8,48,128]{2,1,0:T(8,128)}, f32[8,48,128]{2,1,0:T(8,128)S(1)}, u32[]{:S(2)}) %copy-start.4) | copy-done | bytes 196632
  11.5 4.2 %all-to-all-start = ((f32[8,48,128]{2,1,0:T(8,128)}), f32[8,48,128]{2,1,0:T(8,128)S(1)}, u32[]{:S(2)}, u32[]{:S(2)}) async-start(f32[8,48,128]{2,1,0:T(8,128)} %copy-done.4), calls=%async_computation | async-start | bytes 393216 | tf_op jit(solution)/shard_map/all_to_all | solution.py:676
  15.6 0.7 %collective-permute-start.1 = (f32[128,128]{1,0:T(8,128)}, f32[128,128]{1,0:T(8,128)S(1)}, u32[]{:S(2)}, u32[]{:S(2)}) collective-permute-start(f32[128,128]{1,0:T(8,128)} %get-tuple-element.26), channel_id=1, source_target_pairs={{8,16},{16,8},{9,17},{17,9},{10,18},{18,10},{11,19},{19,11},{12,20... | collective-permute-start | bytes 196616 | tf_op jit(solution)/shard_map/ppermute | solution.py:645
  16.3 0.0 copy-done.1
  16.3 0.0 copy-done
  16.3 0.0 copy-done.2
  16.3 1.1 %weave.1 = (f32[5,2,256,128]{3,2,1,0:T(8,128)S(1)}, f32[5,128,128]{2,1,0:T(8,128)S(1)}, f32[2,3,64,128]{3,2,1,0:T(8,128)S(1)}) custom-call(f32[256,256]{1,0:T(8,128)S(1)} %copy-done.2, f32[2,256,256]{2,1,0:T(8,128)S(1)} %copy-done, f32[2,256,256]{2,1,0:T(8,128)S(1)} %copy-done.1), custom_call_target="tpu_custom_call" | custom-call | tf_op jit(solution)/shard_map/weave/pallas_call | solution.py:677
  17.5 0.0 collective-permute-done.1.second_col
  17.5 0.1 rows.1
  17.6 0.6 collective-permute-start.2
  18.2 0.7 %collective-permute-start.3 = (f32[3,64,128]{2,1,0:T(8,128)S(1)}, f32[3,64,128]{2,1,0:T(8,128)S(1)}, u32[]{:S(2)}, u32[]{:S(2)}) collective-permute-start(f32[3,64,128]{2,1,0:T(8,128)S(1)} %get-tuple-element.31), channel_id=1, source_target_pairs={{1,2},{3,4},{5,6},{2,1},{4,3},{6,5},{9,10},{11,12},{13,14},{10,9},... | collective-permute-start | bytes 294920 | tf_op jit(solution)/shard_map/ppermute | solution.py:645
  18.8 3.0 %all-to-all-done.parcels = f32[8,48,128]{2,1,0:T(8,128)S(1)} async-done(((f32[8,48,128]{2,1,0:T(8,128)}), f32[8,48,128]{2,1,0:T(8,128)S(1)}, u32[]{:S(2)}, u32[]{:S(2)}) %all-to-all-start) | async-done | bytes 196640 | tf_op jit(solution)/shard_map/all_to_all | solution.py:676
  21.9 0.0 copy-done.6
  21.9 0.8 %friction.1 = (f32[784,128]{1,0:T(8,128)S(1)}, f32[784,128]{1,0:T(8,128)S(1)}) custom-call(s32[4,8]{1,0:T(4,128)S(1)} %bitcast.6, f32[8,48,128]{2,1,0:T(8,128)S(1)} %all-to-all-done.parcels), custom_call_target="tpu_custom_call" | custom-call | tf_op jit(solution)/shard_map/friction/pallas_call | solution.py:694
  22.7 1.8 %setup.1 = (f32[5,784,128]{2,1,0:T(8,128)S(1)}, f32[2,784,128]{2,1,0:T(8,128)S(1)}) custom-call(f32[784,128]{1,0:T(8,128)S(1)} %get-tuple-element.22.fr, f32[784,128]{1,0:T(8,128)S(1)} %get-tuple-element.23.ice, f32[5,2,256,128]{3,2,1,0:T(8,128)S(1)} %get-tuple-element.24.woven, f32[5,128,128]{2,1,0:T(8,128)S(1)} %get-tuple-element.25.own_sides, ...), custom_call_target="tpu_custom_call" | custom-call | tf_op jit(solution)/shard_map/setup/pallas_call | solution.py:703
  24.5 0.0 collective-permute-done.2.first_row
  24.5 0.0 collective-permute-done.3.second_row
  24.5 0.0 copy-start.5
  24.5 13.8 %model.1 = (f32[256,256]{1,0:T(8,128)}, f32[256,256]{1,0:T(8,128)}, f32[16,32,128]{2,1,0:T(8,128)S(1)}) custom-call(f32[784,128]{1,0:T(8,128)S(1)} %get-tuple-element.22.fr, f32[784,128]{1,0:T(8,128)S(1)} %get-tuple-element.23.ice, f32[5,784,128]{2,1,0:T(8,128)S(1)} %get-tuple-element.27.ext_in, f32[2,784,128]{2,1,0:T(8,128)S(1)} %get-tuple-element.28.vel_in, ...), custom_call_target="tpu_custom_call" | custom-call | tf_op jit(solution)/shard_map/model/pallas_call | solution.py:717
  38.4 20.6 %all_to_all.10.gathered = f32[16,32,128]{2,1,0:T(8,128)S(1)} all-to-all(f32[16,32,128]{2,1,0:T(8,128)S(1)} %get-tuple-element.34), channel_id=1, replica_groups={{0,2,4,6,8,10,12,14,16,18,20,22,24,26,28,30},{1,3,5,7,9,11,13,15,17,19,..., dimensions={0} | all-to-all | bytes 524288 | tf_op jit(solution)/shard_map/all_to_all | solution.py:738
  58.9 0.0 copy-done.5
  58.9 0.8 %pick.1 = (f32[4,32,128]{2,1,0:T(8,128)S(1)}, f32[4,32,128]{2,1,0:T(8,128)S(1)}) custom-call(s32[4,8]{1,0:T(4,128)S(1)} %bitcast.5, f32[16,32,128]{2,1,0:T(8,128)S(1)} %all_to_all.10.gathered), custom_call_target="tpu_custom_call" | custom-call | tf_op jit(solution)/shard_map/pick/pallas_call | solution.py:739
  59.7 0.1 collective-permute-start.4
  59.8 1.2 %collective-permute-done.4.received = f32[4,32,128]{2,1,0:T(8,128)S(1)} collective-permute-done((f32[4,32,128]{2,1,0:T(8,128)S(1)}, f32[4,32,128]{2,1,0:T(8,128)S(1)}, u32[]{:S(2)}, u32[]{:S(2)}) %collective-permute-start.4) | collective-permute-done | bytes 65568 | tf_op jit(solution)/shard_map/ppermute | solution.py:748
  61.0 0.7 %join.1 = f32[4,4096]{1,0:T(4,128)} custom-call(f32[4,32,128]{2,1,0:T(8,128)S(1)} %get-tuple-element.35.own, f32[4,32,128]{2,1,0:T(8,128)S(1)} %collective-permute-done.4.received), custom_call_target="tpu_custom_call" | custom-call | tf_op jit(solution)/shard_map/join/pallas_call | solution.py:749
  (1 shorter events, 0.0 us)
Async XLA Ops:
  0.6 15.7 %copy-start.1 = (f32[2,256,256]{2,1,0:T(8,128)S(1)}, f32[2,256,256]{2,1,0:T(8,128)}, u32[]{:S(2)}) copy-start(f32[2,256,256]{2,1,0:T(8,128)} %obs.3) | copy-start | bytes 1572868
  0.6 15.7 %copy-start = (f32[2,256,256]{2,1,0:T(8,128)S(1)}, f32[2,256,256]{2,1,0:T(8,128)}, u32[]{:S(2)}) copy-start(f32[2,256,256]{2,1,0:T(8,128)} %drive.3) | copy-start | bytes 1572868
  0.7 15.7 %copy-start.2 = (f32[256,256]{1,0:T(8,128)S(1)}, f32[256,256]{1,0:T(8,128)}, u32[]{:S(2)}) copy-start(f32[256,256]{1,0:T(8,128)} %thick.3) | copy-start | bytes 786436
  0.7 21.2 %copy-start.6 = (s32[8,4]{0,1:T(4,128)S(1)}, s32[8,4]{0,1:T(4,128)}, u32[]{:S(2)}) copy-start(s32[8,4]{0,1:T(4,128)} %param.10) | copy-start | bytes 388
  4.3 5.6 %collective-permute-start = (f32[128,128]{1,0:T(8,128)}, f32[128,128]{1,0:T(8,128)S(1)}, u32[]{:S(2)}, u32[]{:S(2)}) collective-permute-start(f32[128,128]{1,0:T(8,128)} %get-tuple-element.21), channel_id=1, source_target_pairs={{0,8},{16,24},{8,0},{24,16},{1,9},{17,25},{9,1},{25,17},{2,10},{18... | collective-permute-start | bytes 196616 | tf_op jit(solution)/shard_map/ppermute | solution.py:645
  9.9 0.9 %copy-start.3 = (f32[8,48,128]{2,1,0:T(8,128)S(1)}, f32[8,48,128]{2,1,0:T(8,128)}, u32[]{:S(2)}) copy-start(f32[8,48,128]{2,1,0:T(8,128)} %get-tuple-element.20.parcels) | copy-start | bytes 589828
  10.8 0.7 %copy-start.4 = (f32[8,48,128]{2,1,0:T(8,128)}, f32[8,48,128]{2,1,0:T(8,128)S(1)}, u32[]{:S(2)}) copy-start(f32[8,48,128]{2,1,0:T(8,128)S(1)} %pass.1) | copy-start | bytes 589828
  11.5 10.4 %all-to-all-start = ((f32[8,48,128]{2,1,0:T(8,128)}), f32[8,48,128]{2,1,0:T(8,128)S(1)}, u32[]{:S(2)}, u32[]{:S(2)}) async-start(f32[8,48,128]{2,1,0:T(8,128)} %copy-done.4), calls=%async_computation | async-start | bytes 393216 | tf_op jit(solution)/shard_map/all_to_all | solution.py:676
  15.6 1.9 %collective-permute-start.1 = (f32[128,128]{1,0:T(8,128)}, f32[128,128]{1,0:T(8,128)S(1)}, u32[]{:S(2)}, u32[]{:S(2)}) collective-permute-start(f32[128,128]{1,0:T(8,128)} %get-tuple-element.26), channel_id=1, source_target_pairs={{8,16},{16,8},{9,17},{17,9},{10,18},{18,10},{11,19},{19,11},{12,20... | collective-permute-start | bytes 196616 | tf_op jit(solution)/shard_map/ppermute | solution.py:645
  17.6 6.9 %collective-permute-start.2 = (f32[3,64,128]{2,1,0:T(8,128)S(1)}, f32[3,64,128]{2,1,0:T(8,128)S(1)}, u32[]{:S(2)}, u32[]{:S(2)}) collective-permute-start(f32[3,64,128]{2,1,0:T(8,128)S(1)} %get-tuple-element.30), channel_id=1, source_target_pairs={{0,1},{2,3},{4,5},{6,7},{1,0},{3,2},{5,4},{7,6},{8,9},{10,11},{12,... | collective-permute-start | bytes 294920 | tf_op jit(solution)/shard_map/ppermute | solution.py:645
  18.2 6.4 %collective-permute-start.3 = (f32[3,64,128]{2,1,0:T(8,128)S(1)}, f32[3,64,128]{2,1,0:T(8,128)S(1)}, u32[]{:S(2)}, u32[]{:S(2)}) collective-permute-start(f32[3,64,128]{2,1,0:T(8,128)S(1)} %get-tuple-element.31), channel_id=1, source_target_pairs={{1,2},{3,4},{5,6},{2,1},{4,3},{6,5},{9,10},{11,12},{13,14},{10,9},... | collective-permute-start | bytes 294920 | tf_op jit(solution)/shard_map/ppermute | solution.py:645
  24.5 34.4 %copy-start.5 = (s32[8,4,1]{0,2,1:T(1,128)S(1)}, s32[8,4,1]{0,2,1:T(1,128)}, u32[]{:S(2)}) copy-start(s32[8,4,1]{0,2,1:T(1,128)} %param.11) | copy-start | bytes 388
  59.7 1.3 %collective-permute-start.4 = (f32[4,32,128]{2,1,0:T(8,128)S(1)}, f32[4,32,128]{2,1,0:T(8,128)S(1)}, u32[]{:S(2)}, u32[]{:S(2)}) collective-permute-start(f32[4,32,128]{2,1,0:T(8,128)S(1)} %get-tuple-element.36), channel_id=1, source_target_pairs={{0,1},{1,0},{2,3},{3,2},{4,5},{5,4},{6,7},{7,6},{8,9},{9,8},{10,11... | collective-permute-start | bytes 196616 | tf_op jit(solution)/shard_map/ppermute | solution.py:748

commit v13 on v11

--- a/solution.py
+++ b/solution.py
@@ -32,16 +32,13 @@
     "tile": (TOP, 4, 64, TOP, 32, 0, 0),
 }
 FACTORS = 14
-AHEAD = 2
+AHEAD = 5
 PACK = COARSE // LANES
 VMEM_LIMIT = 24 * 1024 * 1024
-PACK_VMEM_LIMIT = 62 * 1024 * 1024
 
 STRIP = ((0, HALO), (HALO, HALO), (2 * HALO, HALO), (3 * HALO, OBS), (3 * HALO + OBS, OBS))
 
-CONTROL = ((0, 0, PACK, 0), (-1, PACK - 2, 2, PACK), (1, 0, 2, PACK + 2))
-FOLDED = 40
-PARCEL = 48
+PATCH_ROWS = ((-1, PACK - 2, 2, 0), (0, 0, PACK, 4), (1, 0, 2, CT + 4))
 PATCH = CT + 8
 
 visc_scale = 0.1
@@ -56,82 +53,20 @@
     return lax.axis_index(axis) % 2 == 0
 
 
-def side_lanes(rows, ds, group):
-    place = (lanes_of(rows) - 8 * group) % CT
-    return place < 4 if ds > 0 else place >= CT - 4
-
-
-def fill_parcels(tile_block, owned_blocks, parcels):
-    tile_cols, tile_rows = tile_block.shape
-    owned = owned_blocks.shape[0]
-    mine = lax.axis_index("gy") * owned
-    col_tile = lax.axis_index("gx")
-
-    def spread(row, carry):
-        for ds in (-1, 0, 1):
-            col = col_tile + ds
-            place = tile_block[jnp.clip(col, 0, tile_cols - 1), row] - mine
-
-            @pl.when((col >= 0) & (col < tile_cols) & (place >= 0) & (place < owned))
-            def _():
-                for dr, first, count, at in CONTROL:
-                    target = row - dr
-
-                    @pl.when((target >= 0) & (target < tile_rows))
-                    def _():
-                        if ds == 0:
-                            parcels[target, at : at + count, :] = owned_blocks[place, first : first + count, :]
-                            return
-                        start = FOLDED + at % 8
-                        rows = min(count, 8)
-                        folded = parcels[target, start : start + rows, :]
-                        for i in range(count // rows):
-                            group = at // 8 + i
-                            cells = owned_blocks[place, first + 8 * i : first + 8 * i + rows, :]
-                            folded = jnp.where(side_lanes(rows, ds, group), turn(cells, 0, 8 * group), folded)
-                        parcels[target, start : start + rows, :] = folded
-
-        return carry
-
-    lax.fori_loop(0, tile_rows, spread, 0)
-
-
-def pack_kernel(
-    tile_block, control, thick, drive, obs, first_col, second_col, parcels,
-    held, held_control, owned_blocks, packed_parcels, packed_cols, sems,
-):
-    copies = [pltpu.make_async_copy(control, held_control, sems.at[5])]
-    for f, field in enumerate((thick, drive.at[0], drive.at[1], obs.at[0], obs.at[1])):
-        copies.append(pltpu.make_async_copy(field, held.at[f], sems.at[f]))
-    for copy in copies:
-        copy.start()
-    packed_parcels[...] = jnp.zeros_like(packed_parcels)
-    copies[0].wait()
-    for j in range(PACK):
-        owned_blocks[:, j, :] = held_control[:, j * LANES : (j + 1) * LANES]
-    fill_parcels(tile_block, owned_blocks, packed_parcels)
-    results = [pltpu.make_async_copy(packed_parcels, parcels, sems.at[6])]
-    results[0].start()
-
+def columns_kernel(thick, drive, obs, first_col, second_col):
     lane = lanes_of(HALF)
     left = jnp.zeros((HALF, LANES), jnp.float32)
     right = jnp.zeros((HALF, LANES), jnp.float32)
-    for f, (first, count) in enumerate(STRIP):
-        copies[1 + f].wait()
+    for field, (first, count) in zip((thick, drive.at[0], drive.at[1], obs.at[0], obs.at[1]), STRIP):
         for part in range(2):
             rows = slice(part * HALF, (part + 1) * HALF)
             start = part * BAND + first
             inside = (lane >= start) & (lane < start + count)
-            left = jnp.where(inside, turn(held[f, rows, :LANES], 0, start), left)
-            right = jnp.where(inside, turn(held[f, rows, LANES:], LANES - count, start), right)
+            left = jnp.where(inside, turn(field[rows, :LANES], 0, start), left)
+            right = jnp.where(inside, turn(field[rows, LANES:], LANES - count, start), right)
     even = is_even("gx")
-    packed_cols[0] = jnp.where(even, right, left)
-    packed_cols[1] = jnp.where(even, left, right)
-    for i, out in enumerate((first_col, second_col)):
-        results.append(pltpu.make_async_copy(packed_cols.at[i], out, sems.at[7 + i]))
-        results[-1].start()
-    for copy in results:
-        copy.wait()
+    first_col[...] = jnp.where(even, right, left)
+    second_col[...] = jnp.where(even, left, right)
 
 
 def sides(axis, first_pair, second_pair):
@@ -173,9 +108,8 @@
         own_sides[f] = jnp.where(half_lane < BAND, bands[0][:HALF], bands[1][HALF:])
         for c in range(2):
             woven[f, c] = tiles[c]
-        for c, tile in enumerate(tiles + [bands[1]]):
+        for c, tile in enumerate(tiles + [bands[0]]):
             edges[0, c, first : first + count, :] = tile[:count]
-        for c, tile in enumerate(tiles + [bands[0]]):
             edges[1, c, first : first + count, :] = tile[TILE - count :]
 
 
@@ -184,21 +118,27 @@
     even = is_even("gy")
     for c in range(2):
         top, bottom = edges[0, c], edges[1, c]
-        first_pair[c] = jnp.where(even, bottom, top)
-        second_pair[c] = jnp.where(even, top, bottom)
-    for f, (first, count) in enumerate(STRIP):
-        strips = []
-        for i, packed, source, target in (
-            (0, slice(0, count), first, BAND),
-            (1, slice(HALF - count, HALF), BAND + first, 0),
-        ):
-            own = edges[i, 2, first : first + count, :]
+        first_pair[64 * c : 64 * c + 64, :] = jnp.where(even, bottom, top)
+        second_pair[64 * c : 64 * c + 64, :] = jnp.where(even, top, bottom)
+    strips = []
+    for i in range(2):
+        fields = []
+        for f, (first, count) in enumerate(STRIP):
+            packed = slice(HALF - count, HALF) if i else slice(0, count)
+            source = BAND * i + first
+            target = BAND if f >= 2 else 0
+            own = turn(edges[i, 2, first : first + count, :], 0, target)
             from_east = scale_of(f) * turn(east[packed], source, target + HALO)
             from_west = scale_of(f) * turn(west[packed], source, target + 3 * HALO - count)
-            strips.append(choose_side(lanes_of(count), own, from_east, from_west, own))
-        top, bottom = strips
-        first_pair[2, first : first + count, :] = jnp.where(even, bottom, top)
-        second_pair[2, first : first + count, :] = jnp.where(even, top, bottom)
+            fields.append(choose_side(lanes_of(count), own, from_east, from_west, own))
+        lane = lanes_of(HALO)
+        lower = jnp.concatenate(fields[3:], axis=0)
+        strips.append((jnp.where(lane < BAND, fields[0], fields[2]), jnp.where(lane < BAND, fields[1], lower)))
+    for k in range(2):
+        top, bottom = strips[0][k], strips[1][k]
+        rows = slice(128 + HALO * k, 128 + HALO * (k + 1))
+        first_pair[rows, :] = jnp.where(even, bottom, top)
+        second_pair[rows, :] = jnp.where(even, top, bottom)
 
 
 def shift_east(tiles):
@@ -298,23 +238,29 @@
         join(TOP + HALF, False, True, HALO)
 
 
-def friction_kernel(ice_mask, parcels, fr, ice, patch):
+def friction_kernel(tile_block, ice_mask, control, fr, ice, blocks, patch):
     tile_cols, tile_rows = ice_mask.shape
     row_tile = lax.axis_index("gy")
     col_tile = lax.axis_index("gx")
 
-    flat = sum(parcels[j] for j in range(tile_rows))
-    folded = flat[FOLDED:]
-    for dr, _, count, at in CONTROL:
-        cells = flat[at : at + count]
-        if dr == 0:
-            side = jnp.concatenate([turn(folded, 8 * g, 0) for g in range(PACK // 8)], axis=0)
-        else:
-            side = turn(folded, PACK, 0)[at % 8 : at % 8 + count]
-        inner = lanes_of(count) < CT
-        row = 4 + {-1: -4, 0: 0, 1: CT}[dr]
-        patch[pl.ds(row, count, stride=2), :] = jnp.where(inner, cells, turn(side, 0, CT))
-        patch[pl.ds(row + 1, count, stride=2), :] = jnp.where(inner, turn(cells, 0, CT), side)
+    owned = control.shape[1]
+    owner_row = lax.broadcasted_iota(jnp.int32, (owned, LANES), 0)
+    for dr, first, count, at in PATCH_ROWS:
+        for ds in (-1, 0, 1):
+            row = jnp.clip(row_tile + dr, 0, tile_rows - 1)
+            col = jnp.clip(col_tile + ds, 0, tile_cols - 1)
+            block = tile_block[col, row]
+            holder = block // owned
+            here = owner_row == block - holder * owned
+            for j in range(first, first + count):
+                held = control[holder, :, j * LANES : (j + 1) * LANES]
+                blocks[ds + 1, j : j + 1, :] = jnp.sum(jnp.where(here, held, 0.0), axis=0, keepdims=True)
+        west, mid, east = (blocks[k, first : first + count, :] for k in range(3))
+        lane = lanes_of(count)
+        even = jnp.where(lane < CT, mid, jnp.where(lane < 96, turn(east, 0, CT), turn(west, 0, CT)))
+        odd = jnp.where(lane < CT, turn(mid, 0, CT), jnp.where(lane < 96, east, west))
+        patch[pl.ds(at, count, stride=2), :] = even
+        patch[pl.ds(at + 1, count, stride=2), :] = odd
 
     cells = 0.5 * jnp.exp(patch[...])
     lane = lanes_of(PATCH)
@@ -496,21 +442,20 @@
 ):
     ext[...] = ext_in[...]
     vel_b[...] = vel_in[...]
-    even = is_even("gy")
+    north, south = sides("gy", first_row[...], second_row[...])
     here = SIDE + TOP
     for f, (first, count) in enumerate(STRIP):
-        frames = []
-        for c in range(3):
-            one, two = first_row[c, first : first + count, :], second_row[c, first : first + count, :]
-            frames.append((jnp.where(even, two, one), jnp.where(even, one, two)))
         for c in range(2):
-            ext[f, MAIN[c] + TOP - count : MAIN[c] + TOP, :] = frames[c][0]
-            ext[f, MAIN[c] + TOP + TILE : MAIN[c] + TOP + TILE + count, :] = frames[c][1]
+            rows = slice(64 * c + first, 64 * c + first + count)
+            ext[f, MAIN[c] + TOP - count : MAIN[c] + TOP, :] = north[rows]
+            ext[f, MAIN[c] + TOP + TILE : MAIN[c] + TOP + TILE + count, :] = south[rows]
+        rows = slice(128 + first % 32, 128 + first % 32 + count)
+        source = BAND if f >= 2 else 0
         upper = lanes_of(count) < BAND
         above = turn(ext_in[f, here + HALF - count : here + HALF, :], 0, BAND)
         below = turn(ext_in[f, here : here + count, :], 0, BAND)
-        ext[f, here - count : here, :] = jnp.where(upper, frames[2][0], above)
-        ext[f, here + HALF : here + HALF + count, :] = jnp.where(upper, below, frames[2][1])
+        ext[f, here - count : here, :] = jnp.where(upper, turn(north[rows], source, 0), above)
+        ext[f, here + HALF : here + HALF + count, :] = jnp.where(upper, below, turn(south[rows], source, BAND))
 
     step = make_stages(ext, fr, ice, visc, vel_a, vel_b, coef)
     over_ends(32, step.read_thickness, step.first_viscosity)
@@ -643,23 +588,15 @@
 
     fields = thickness, driving, observed
     owned = control.shape[0]
-    *edges, parcels = pl.pallas_call(
-        pack_kernel,
-        out_shape=[shape(HALF, LANES)] * 2 + [shape(rows, PARCEL, LANES)],
-        in_specs=in_smem(1) + [pl.BlockSpec(memory_space=pltpu.HBM)] * 4,
-        out_specs=[pl.BlockSpec(memory_space=pltpu.HBM)] * 3,
-        scratch_shapes=[
-            pltpu.VMEM((5, TILE, TILE), f32),
-            pltpu.VMEM(control.shape, f32),
-            pltpu.VMEM((owned, PACK, LANES), f32),
-            pltpu.VMEM((rows, PARCEL, LANES), f32),
-            pltpu.VMEM((2, HALF, LANES), f32),
-            pltpu.SemaphoreType.DMA((9,)),
-        ],
-        compiler_params=pltpu.CompilerParams(vmem_limit_bytes=PACK_VMEM_LIMIT),
-        name="pack",
-    )(tile_block, control, *fields)
-    parcels = lax.all_to_all(parcels, "gy", 0, 0, tiled=True)
+    gathered = lax.all_to_all(jnp.broadcast_to(control, (rows, *control.shape)), "gy", 0, 0, tiled=True)
+    edges = pl.pallas_call(
+        columns_kernel,
+        out_shape=[shape(HALF, LANES)] * 2,
+        in_specs=in_vmem(3),
+        out_specs=in_vmem(2),
+        compiler_params=params,
+        name="columns",
+    )(*fields)
     columns_in = swap("gx", *edges)
     woven, own_sides, strips = pl.pallas_call(
         weave_kernel,
@@ -671,7 +608,7 @@
     )(*fields)
     strips = pl.pallas_call(
         rows_kernel,
-        out_shape=[shape(3, 64, LANES)] * 2,
+        out_shape=[shape(160, LANES)] * 2,
         in_specs=in_vmem(3),
         out_specs=in_vmem(2),
         compiler_params=params,
@@ -681,12 +618,12 @@
     friction = pl.pallas_call(
         friction_kernel,
         out_shape=[shape(ALL_ROWS, LANES)] * 2,
-        in_specs=in_smem(1) + in_vmem(1),
+        in_specs=in_smem(2) + in_vmem(1),
         out_specs=in_vmem(2),
-        scratch_shapes=[pltpu.VMEM((PATCH, LANES), f32)],
+        scratch_shapes=[pltpu.VMEM((3, PACK, LANES), f32), pltpu.VMEM((PATCH, LANES), f32)],
         compiler_params=params,
         name="friction",
-    )(ice_mask, parcels)
+    )(tile_block, ice_mask, gathered)
     prepared = pl.pallas_call(
         setup_kernel,
         out_shape=[shape(5, ALL_ROWS, LANES), shape(2, ALL_ROWS, LANES)],

time: 57.4 us -> 58.7 us (1.023)
  local copies, waits for them, and re-layouts: 0.96 us -> 4.75 us
  Pallas kernels: 22.7 us -> 19.5 us
  waiting for transfers between devices: 1.76 us -> 3.26 us
  blocking collectives: 22.3 us -> 21.5 us
    pallas_call x2, Pallas kernels: 3.71 us -> 0.48 us  [the longest x1 0.37 us: per_device(): pl.pallas_call(columns_kernel, out_shape=[shape(HALF, LANES)] * 2, in_spe...]
    unnamed x10, local copies, waits for them, and re-layouts: 0.96 us -> 3.04 us
    broadcast_in_dim x0 -> x1, local copies, waits for them, and re-layouts: none -> 1.71 us  [per_device(): jnp.broadcast_to(control, (rows, *control.shape))]
    ppermute x4, waiting for transfers between devices: 0.18 us -> 1.13 us  [swap(): lax.ppermute(cells, axis, pairs + [(j, i) for i, j in pairs])]
    all_to_all x1, blocking collectives: 22.3 us -> 21.5 us  [per_device(): lax.all_to_all(sums, ('gx', 'gy'), 0, 0, tiled=True, axis_index_groups=sa...]
where the time goes in v13:
time: 58.7 us; the launch traced here: 58.2 us
  blocking collectives  21.5 us (37%)
  Pallas kernels  19.5 us (33%)
  starting transfers between devices  8.4 us (14%)
  local copies, waits for them, and re-layouts  4.75 us (8%)
  waiting for transfers between devices  3.26 us (6%)
  between operations  0.74 us (1%)
    all_to_all x1, blocking collectives, per_device(): lax.all_to_all(sums, ('gx', 'gy'), 0, 0, tiled=True, axis_index_groups=sa...  21.5 us
    pallas_call x1, Pallas kernels, per_device(): pl.pallas_call(model_kernel, out_shape=(shape(TILE, TILE), shape(TILE, TI...  13.8 us
    all_to_all x1, starting transfers between devices, per_device(): lax.all_to_all(jnp.broadcast_to(control, (rows, *control.shape)), 'gy', 0...  5.3 us
    unnamed x10, local copies, waits for them, and re-layouts  3.04 us
    ppermute x4, starting transfers between devices, swap(): lax.ppermute(cells, axis, pairs + [(j, i) for i, j in pairs])  3.03 us
    pallas_call x1, Pallas kernels, per_device(): pl.pallas_call(setup_kernel, out_shape=[shape(5, ALL_ROWS, LANES), shape(...  1.78 us
    broadcast_in_dim x1, local copies, waits for them, and re-layouts, per_device(): jnp.broadcast_to(control, (rows, *control.shape))  1.71 us
    ppermute x1, waiting for transfers between devices, per_device(): received = lax.ppermute(other, 'gy', [(j, j ^ 1) for j in range(rows)])  1.24 us
  transfers between devices with their start and end apart: 6, of which 3 were waited for; matrix products, arithmetic and copies ran while one was open for 0% of the time, Pallas kernels for 7%

profile of v13, /device:TPU:0, one launch (start us, length us, event | category | flops | bytes accessed | tf_op | source)
XLA Modules:
  0.0 58.2 jit_solution(11986468830437739595)
XLA Ops:
  0.6 1.7 %broadcast_in_dim.3 = f32[8,4,4096]{2,1,0:T(4,128)} broadcast(f32[4,4096]{1,0:T(4,128)} %param.9), dimensions={1,2} | broadcast | bytes 589824 | tf_op jit(solution)/shard_map/broadcast_in_dim | solution.py:591
  2.3 0.0 copy-start.3
  2.3 0.0 copy-start.4
  2.3 5.3 %all-to-all-start = ((f32[8,4,4096]{2,1,0:T(4,128)}), f32[8,4,4096]{2,1,0:T(4,128)S(1)}, u32[]{:S(2)}, u32[]{:S(2)}) async-start(f32[8,4,4096]{2,1,0:T(4,128)} %broadcast_in_dim.3), calls=%async_computation | async-start | bytes 1048576 | tf_op jit(solution)/shard_map/all_to_all | solution.py:591
  7.7 0.0 copy-start
  7.7 1.0 %copy-done = f32[2,256,256]{2,1,0:T(8,128)S(1)} copy-done((f32[2,256,256]{2,1,0:T(8,128)S(1)}, f32[2,256,256]{2,1,0:T(8,128)}, u32[]{:S(2)}) %copy-start) | copy-done | bytes 524312
  8.7 0.0 copy-start.1
  8.7 1.0 %copy-done.1 = f32[2,256,256]{2,1,0:T(8,128)S(1)} copy-done((f32[2,256,256]{2,1,0:T(8,128)S(1)}, f32[2,256,256]{2,1,0:T(8,128)}, u32[]{:S(2)}) %copy-start.1) | copy-done | bytes 524312
  9.7 0.0 copy-start.2
  9.7 0.9 %copy-done.2 = f32[256,256]{1,0:T(8,128)S(1)} copy-done((f32[256,256]{1,0:T(8,128)S(1)}, f32[256,256]{1,0:T(8,128)}, u32[]{:S(2)}) %copy-start.2) | copy-done | bytes 262168
  10.7 0.4 columns.1
  11.1 1.6 %collective-permute-start = (f32[128,128]{1,0:T(8,128)S(1)}, f32[128,128]{1,0:T(8,128)S(1)}, u32[]{:S(2)}, u32[]{:S(2)}) collective-permute-start(f32[128,128]{1,0:T(8,128)S(1)} %get-tuple-element.23), channel_id=1, source_target_pairs={{0,8},{16,24},{8,0},{24,16},{1,9},{17,25},{9,1},{25,17},{2,10},{18... | collective-permute-start | bytes 196616 | tf_op jit(solution)/shard_map/ppermute | solution.py:586
  12.7 0.7 %collective-permute-start.1 = (f32[128,128]{1,0:T(8,128)S(1)}, f32[128,128]{1,0:T(8,128)S(1)}, u32[]{:S(2)}, u32[]{:S(2)}) collective-permute-start(f32[128,128]{1,0:T(8,128)S(1)} %get-tuple-element.24), channel_id=1, source_target_pairs={{8,16},{16,8},{9,17},{17,9},{10,18},{18,10},{11,19},{19,11},{12,20... | collective-permute-start | bytes 196616 | tf_op jit(solution)/shard_map/ppermute | solution.py:586
  13.4 1.1 %weave.1 = (f32[5,2,256,128]{3,2,1,0:T(8,128)S(1)}, f32[5,128,128]{2,1,0:T(8,128)S(1)}, f32[2,3,64,128]{3,2,1,0:T(8,128)S(1)}) custom-call(f32[256,256]{1,0:T(8,128)S(1)} %copy-done.2, f32[2,256,256]{2,1,0:T(8,128)S(1)} %copy-done, f32[2,256,256]{2,1,0:T(8,128)S(1)} %copy-done.1), custom_call_target="tpu_custom_call" | custom-call | tf_op jit(solution)/shard_map/weave/pallas_call | solution.py:601
  14.5 1.1 %collective-permute-done.first_col = f32[128,128]{1,0:T(8,128)S(1)} collective-permute-done((f32[128,128]{1,0:T(8,128)S(1)}, f32[128,128]{1,0:T(8,128)S(1)}, u32[]{:S(2)}, u32[]{:S(2)}) %collective-permute-start) | collective-permute-done | bytes 65568 | tf_op jit(solution)/shard_map/ppermute | solution.py:586
  15.6 0.0 collective-permute-done.1.second_col
  15.6 0.1 rows.1
  15.8 0.1 collective-permute-start.2
  15.8 0.7 %collective-permute-start.3 = (f32[160,128]{1,0:T(8,128)S(1)}, f32[160,128]{1,0:T(8,128)S(1)}, u32[]{:S(2)}, u32[]{:S(2)}) collective-permute-start(f32[160,128]{1,0:T(8,128)S(1)} %get-tuple-element.29), channel_id=1, source_target_pairs={{1,2},{3,4},{5,6},{2,1},{4,3},{6,5},{9,10},{11,12},{13,14},{10,9},... | collective-permute-start | bytes 245768 | tf_op jit(solution)/shard_map/ppermute | solution.py:586
  16.5 0.9 %all-to-all-done.control = f32[8,4,4096]{2,1,0:T(4,128)S(1)} async-done(((f32[8,4,4096]{2,1,0:T(4,128)}), f32[8,4,4096]{2,1,0:T(4,128)S(1)}, u32[]{:S(2)}, u32[]{:S(2)}) %all-to-all-start) | async-done | bytes 524320 | tf_op jit(solution)/shard_map/all_to_all | solution.py:591
  17.4 0.0 copy-done.3
  17.4 0.0 copy-done.4
  17.4 0.9 %friction.1 = (f32[784,128]{1,0:T(8,128)S(1)}, f32[784,128]{1,0:T(8,128)S(1)}) custom-call(s32[4,8]{1,0:T(4,128)S(1)} %bitcast.4, s32[4,8]{1,0:T(4,128)S(1)} %bitcast.6, f32[8,4,4096]{2,1,0:T(4,128)S(1)} %all-to-all-done.control), custom_call_target="tpu_custom_call" | custom-call | tf_op jit(solution)/shard_map/friction/pallas_call | solution.py:618
  18.3 1.8 %setup.1 = (f32[5,784,128]{2,1,0:T(8,128)S(1)}, f32[2,784,128]{2,1,0:T(8,128)S(1)}) custom-call(f32[784,128]{1,0:T(8,128)S(1)} %get-tuple-element.19.fr, f32[784,128]{1,0:T(8,128)S(1)} %get-tuple-element.20.ice, f32[5,2,256,128]{3,2,1,0:T(8,128)S(1)} %get-tuple-element.21.woven, f32[5,128,128]{2,1,0:T(8,128)S(1)} %get-tuple-element.22.own_sides, ...), custom_call_target="tpu_custom_call" | custom-call | tf_op jit(solution)/shard_map/setup/pallas_call | solution.py:627
  20.1 0.0 collective-permute-done.2.first_row
  20.1 0.0 collective-permute-done.3.second_row
  20.1 13.8 %model.1 = (f32[256,256]{1,0:T(8,128)}, f32[256,256]{1,0:T(8,128)}, f32[16,32,128]{2,1,0:T(8,128)S(1)}) custom-call(f32[784,128]{1,0:T(8,128)S(1)} %get-tuple-element.19.fr, f32[784,128]{1,0:T(8,128)S(1)} %get-tuple-element.20.ice, f32[5,784,128]{2,1,0:T(8,128)S(1)} %get-tuple-element.25.ext_in, f32[2,784,128]{2,1,0:T(8,128)S(1)} %get-tuple-element.26.vel_in, ...), custom_call_target="tpu_custom_call" | custom-call | tf_op jit(solution)/shard_map/model/pallas_call | solution.py:641
  33.9 21.5 %all_to_all.10.gathered = f32[16,32,128]{2,1,0:T(8,128)S(1)} all-to-all(f32[16,32,128]{2,1,0:T(8,128)S(1)} %get-tuple-element.32), channel_id=1, replica_groups={{0,2,4,6,8,10,12,14,16,18,20,22,24,26,28,30},{1,3,5,7,9,11,13,15,17,19,..., dimensions={0} | all-to-all | bytes 524288 | tf_op jit(solution)/shard_map/all_to_all | solution.py:662
  55.5 0.8 %pick.1 = (f32[4,32,128]{2,1,0:T(8,128)S(1)}, f32[4,32,128]{2,1,0:T(8,128)S(1)}) custom-call(s32[4,8]{1,0:T(4,128)S(1)} %bitcast.5, f32[16,32,128]{2,1,0:T(8,128)S(1)} %all_to_all.10.gathered), custom_call_target="tpu_custom_call" | custom-call | tf_op jit(solution)/shard_map/pick/pallas_call | solution.py:663
  56.2 0.1 collective-permute-start.4
  56.3 1.2 %collective-permute-done.4.received = f32[4,32,128]{2,1,0:T(8,128)S(1)} collective-permute-done((f32[4,32,128]{2,1,0:T(8,128)S(1)}, f32[4,32,128]{2,1,0:T(8,128)S(1)}, u32[]{:S(2)}, u32[]{:S(2)}) %collective-permute-start.4) | collective-permute-done | bytes 65568 | tf_op jit(solution)/shard_map/ppermute | solution.py:672
  57.6 0.7 %join.1 = f32[4,4096]{1,0:T(4,128)} custom-call(f32[4,32,128]{2,1,0:T(8,128)S(1)} %get-tuple-element.33.own, f32[4,32,128]{2,1,0:T(8,128)S(1)} %collective-permute-done.4.received), custom_call_target="tpu_custom_call" | custom-call | tf_op jit(solution)/shard_map/join/pallas_call | solution.py:673
Async XLA Ops:
  2.3 15.1 %copy-start.3 = (s32[8,4,1]{0,2,1:T(1,128)S(1)}, s32[8,4,1]{0,2,1:T(1,128)}, u32[]{:S(2)}) copy-start(s32[8,4,1]{0,2,1:T(1,128)} %param.11) | copy-start | bytes 388
  2.3 15.1 %copy-start.4 = (s32[8,4]{0,1:T(4,128)S(1)}, s32[8,4]{0,1:T(4,128)}, u32[]{:S(2)}) copy-start(s32[8,4]{0,1:T(4,128)} %param.10) | copy-start | bytes 388
  2.3 15.0 %all-to-all-start = ((f32[8,4,4096]{2,1,0:T(4,128)}), f32[8,4,4096]{2,1,0:T(4,128)S(1)}, u32[]{:S(2)}, u32[]{:S(2)}) async-start(f32[8,4,4096]{2,1,0:T(4,128)} %broadcast_in_dim.3), calls=%async_computation | async-start | bytes 1048576 | tf_op jit(solution)/shard_map/all_to_all | solution.py:591
  7.7 1.0 %copy-start = (f32[2,256,256]{2,1,0:T(8,128)S(1)}, f32[2,256,256]{2,1,0:T(8,128)}, u32[]{:S(2)}) copy-start(f32[2,256,256]{2,1,0:T(8,128)} %drive.3) | copy-start | bytes 1572868
  8.7 1.0 %copy-start.1 = (f32[2,256,256]{2,1,0:T(8,128)S(1)}, f32[2,256,256]{2,1,0:T(8,128)}, u32[]{:S(2)}) copy-start(f32[2,256,256]{2,1,0:T(8,128)} %obs.3) | copy-start | bytes 1572868
  9.7 0.9 %copy-start.2 = (f32[256,256]{1,0:T(8,128)S(1)}, f32[256,256]{1,0:T(8,128)}, u32[]{:S(2)}) copy-start(f32[256,256]{1,0:T(8,128)} %thick.3) | copy-start | bytes 786436
  11.1 4.6 %collective-permute-start = (f32[128,128]{1,0:T(8,128)S(1)}, f32[128,128]{1,0:T(8,128)S(1)}, u32[]{:S(2)}, u32[]{:S(2)}) collective-permute-start(f32[128,128]{1,0:T(8,128)S(1)} %get-tuple-element.23), channel_id=1, source_target_pairs={{0,8},{16,24},{8,0},{24,16},{1,9},{17,25},{9,1},{25,17},{2,10},{18... | collective-permute-start | bytes 196616 | tf_op jit(solution)/shard_map/ppermute | solution.py:586
  12.7 2.9 %collective-permute-start.1 = (f32[128,128]{1,0:T(8,128)S(1)}, f32[128,128]{1,0:T(8,128)S(1)}, u32[]{:S(2)}, u32[]{:S(2)}) collective-permute-start(f32[128,128]{1,0:T(8,128)S(1)} %get-tuple-element.24), channel_id=1, source_target_pairs={{8,16},{16,8},{9,17},{17,9},{10,18},{18,10},{11,19},{19,11},{12,20... | collective-permute-start | bytes 196616 | tf_op jit(solution)/shard_map/ppermute | solution.py:586
  15.8 4.4 %collective-permute-start.2 = (f32[160,128]{1,0:T(8,128)S(1)}, f32[160,128]{1,0:T(8,128)S(1)}, u32[]{:S(2)}, u32[]{:S(2)}) collective-permute-start(f32[160,128]{1,0:T(8,128)S(1)} %get-tuple-element.28), channel_id=1, source_target_pairs={{0,1},{2,3},{4,5},{6,7},{1,0},{3,2},{5,4},{7,6},{8,9},{10,11},{12,... | collective-permute-start | bytes 245768 | tf_op jit(solution)/shard_map/ppermute | solution.py:586
  15.8 4.3 %collective-permute-start.3 = (f32[160,128]{1,0:T(8,128)S(1)}, f32[160,128]{1,0:T(8,128)S(1)}, u32[]{:S(2)}, u32[]{:S(2)}) collective-permute-start(f32[160,128]{1,0:T(8,128)S(1)} %get-tuple-element.29), channel_id=1, source_target_pairs={{1,2},{3,4},{5,6},{2,1},{4,3},{6,5},{9,10},{11,12},{13,14},{10,9},... | collective-permute-start | bytes 245768 | tf_op jit(solution)/shard_map/ppermute | solution.py:586
  56.2 1.3 %collective-permute-start.4 = (f32[4,32,128]{2,1,0:T(8,128)S(1)}, f32[4,32,128]{2,1,0:T(8,128)S(1)}, u32[]{:S(2)}, u32[]{:S(2)}) collective-permute-start(f32[4,32,128]{2,1,0:T(8,128)S(1)} %get-tuple-element.34), channel_id=1, source_target_pairs={{0,1},{1,0},{2,3},{3,2},{4,5},{5,4},{6,7},{7,6},{8,9},{9,8},{10,11... | collective-permute-start | bytes 196616 | tf_op jit(solution)/shard_map/ppermute | solution.py:672

commit v14 on v13

--- a/solution.py
+++ b/solution.py
@@ -35,6 +35,7 @@
 AHEAD = 5
 PACK = COARSE // LANES
 VMEM_LIMIT = 24 * 1024 * 1024
+PACK_VMEM_LIMIT = 62 * 1024 * 1024
 
 STRIP = ((0, HALO), (HALO, HALO), (2 * HALO, HALO), (3 * HALO, OBS), (3 * HALO + OBS, OBS))
 
@@ -53,20 +54,31 @@
     return lax.axis_index(axis) % 2 == 0
 
 
-def columns_kernel(thick, drive, obs, first_col, second_col):
+def pack_kernel(control, thick, drive, obs, first_col, second_col, spread, held, packed, field_sems, sems):
+    results = [pltpu.make_async_copy(control, spread.at[j], sems.at[2 + j]) for j in range(spread.shape[0])]
+    fields = (thick, drive.at[0], drive.at[1], obs.at[0], obs.at[1])
+    copies = [pltpu.make_async_copy(field, held.at[f], field_sems.at[f]) for f, field in enumerate(fields)]
+    for copy in copies + results:
+        copy.start()
     lane = lanes_of(HALF)
     left = jnp.zeros((HALF, LANES), jnp.float32)
     right = jnp.zeros((HALF, LANES), jnp.float32)
-    for field, (first, count) in zip((thick, drive.at[0], drive.at[1], obs.at[0], obs.at[1]), STRIP):
+    for f, (first, count) in enumerate(STRIP):
+        copies[f].wait()
         for part in range(2):
             rows = slice(part * HALF, (part + 1) * HALF)
             start = part * BAND + first
             inside = (lane >= start) & (lane < start + count)
-            left = jnp.where(inside, turn(field[rows, :LANES], 0, start), left)
-            right = jnp.where(inside, turn(field[rows, LANES:], LANES - count, start), right)
+            left = jnp.where(inside, turn(held[f, rows, :LANES], 0, start), left)
+            right = jnp.where(inside, turn(held[f, rows, LANES:], LANES - count, start), right)
     even = is_even("gx")
-    first_col[...] = jnp.where(even, right, left)
-    second_col[...] = jnp.where(even, left, right)
+    packed[0] = jnp.where(even, right, left)
+    packed[1] = jnp.where(even, left, right)
+    for i, out in enumerate((first_col, second_col)):
+        results.append(pltpu.make_async_copy(packed.at[i], out, sems.at[i]))
+        results[-1].start()
+    for copy in results:
+        copy.wait()
 
 
 def sides(axis, first_pair, second_pair):
@@ -588,15 +600,21 @@
 
     fields = thickness, driving, observed
     owned = control.shape[0]
-    gathered = lax.all_to_all(jnp.broadcast_to(control, (rows, *control.shape)), "gy", 0, 0, tiled=True)
-    edges = pl.pallas_call(
-        columns_kernel,
-        out_shape=[shape(HALF, LANES)] * 2,
-        in_specs=in_vmem(3),
-        out_specs=in_vmem(2),
-        compiler_params=params,
-        name="columns",
-    )(*fields)
+    *edges, spread = pl.pallas_call(
+        pack_kernel,
+        out_shape=[shape(HALF, LANES)] * 2 + [shape(rows, *control.shape)],
+        in_specs=[pl.BlockSpec(memory_space=pltpu.HBM)] * 4,
+        out_specs=[pl.BlockSpec(memory_space=pltpu.HBM)] * 3,
+        scratch_shapes=[
+            pltpu.VMEM((5, TILE, TILE), f32),
+            pltpu.VMEM((2, HALF, LANES), f32),
+            pltpu.SemaphoreType.DMA((5,)),
+            pltpu.SemaphoreType.DMA((2 + rows,)),
+        ],
+        compiler_params=pltpu.CompilerParams(vmem_limit_bytes=PACK_VMEM_LIMIT),
+        name="pack",
+    )(control, *fields)
+    gathered = lax.all_to_all(spread, "gy", 0, 0, tiled=True)
     columns_in = swap("gx", *edges)
     woven, own_sides, strips = pl.pallas_call(
         weave_kernel,

time: 58.7 us -> 70.9 us (1.21)
  Pallas kernels: 19.5 us -> 36.3 us
  blocking collectives: 21.5 us -> 17.2 us
  waiting for transfers between devices: 3.26 us -> 5.62 us
  local copies, waits for them, and re-layouts: 4.75 us -> 2.41 us
    pallas_call x1, Pallas kernels: 0.37 us -> 17.1 us  [per_device(): pl.pallas_call(pack_kernel, out_shape=[shape(HALF, LANES)] * 2 + [shape(r...]
    all_to_all x1, blocking collectives: 21.5 us -> 17.2 us  [per_device(): lax.all_to_all(sums, ('gx', 'gy'), 0, 0, tiled=True, axis_index_groups=sa...]
    all_to_all x1, waiting for transfers between devices: 0.89 us -> 4.15 us  [per_device(): gathered = lax.all_to_all(spread, 'gy', 0, 0, tiled=True)]
    broadcast_in_dim x1 -> x0, local copies, waits for them, and re-layouts: 1.71 us -> none  [per_device(): jnp.broadcast_to(control, (rows, *control.shape))]
    ppermute x4, waiting for transfers between devices: 1.13 us -> 0.22 us  [swap(): lax.ppermute(cells, axis, pairs + [(j, i) for i, j in pairs])]
    unnamed x10 -> x14, local copies, waits for them, and re-layouts: 3.04 us -> 2.41 us
  transfers between devices with their start and end apart: 6 -> 6, of which waited for: 3 -> 3; matrix products, arithmetic and copies ran while one was open for 0% -> 0% of each run, Pallas kernels for 7% -> 6%
where the time goes in v14:
time: 70.9 us; the launch traced here: 70.6 us
  Pallas kernels  36.3 us (51%)
  blocking collectives  17.2 us (24%)
  starting transfers between devices  8.23 us (12%)
  waiting for transfers between devices  5.62 us (8%)
  local copies, waits for them, and re-layouts  2.41 us (3%)
  between operations  0.81 us (1%)
    all_to_all x1, blocking collectives, per_device(): lax.all_to_all(sums, ('gx', 'gy'), 0, 0, tiled=True, axis_index_groups=sa...  17.2 us
    pallas_call x1, Pallas kernels, per_device(): pl.pallas_call(pack_kernel, out_shape=[shape(HALF, LANES)] * 2 + [shape(r...  17.1 us
    pallas_call x1, Pallas kernels, per_device(): pl.pallas_call(model_kernel, out_shape=(shape(TILE, TILE), shape(TILE, TI...  13.8 us
    all_to_all x1, starting transfers between devices, per_device(): gathered = lax.all_to_all(spread, 'gy', 0, 0, tiled=True)  5.18 us
    all_to_all x1, waiting for transfers between devices, per_device(): gathered = lax.all_to_all(spread, 'gy', 0, 0, tiled=True)  4.15 us
    ppermute x4, starting transfers between devices, swap(): lax.ppermute(cells, axis, pairs + [(j, i) for i, j in pairs])  2.97 us
    unnamed x14, local copies, waits for them, and re-layouts  2.41 us
    pallas_call x1, Pallas kernels, per_device(): pl.pallas_call(setup_kernel, out_shape=[shape(5, ALL_ROWS, LANES), shape(...  1.8 us
  transfers between devices with their start and end apart: 6, of which 3 were waited for; matrix products, arithmetic and copies ran while one was open for 0% of the time, Pallas kernels for 6%

profile of v14, /device:TPU:0, one launch (start us, length us, event | category | flops | bytes accessed | tf_op | source)
XLA Modules:
  0.0 70.6 jit_solution(8705711028270362632)
XLA Ops:
  0.6 0.0 copy-start.1
  0.6 0.0 copy-start
  0.7 0.0 copy-start.4
  0.7 0.0 copy-start.5
  0.7 0.0 copy-start.6
  0.7 17.1 %pack.1 = (f32[128,128]{1,0:T(8,128)}, f32[128,128]{1,0:T(8,128)}, f32[8,4,4096]{2,1,0:T(4,128)}) custom-call(f32[4,4096]{1,0:T(4,128)} %control.1, f32[256,256]{1,0:T(8,128)} %thick.3, f32[2,256,256]{2,1,0:T(8,128)} %drive.3, f32[2,256,256]{2,1,0:T(8,128)} %obs.3), custom_call_target="tpu_custom_call" | custom-call | tf_op jit(solution)/shard_map/pack/pallas_call | solution.py:603
  17.8 5.2 %all-to-all-start = ((f32[8,4,4096]{2,1,0:T(4,128)}), f32[8,4,4096]{2,1,0:T(4,128)S(1)}, u32[]{:S(2)}, u32[]{:S(2)}) async-start(f32[8,4,4096]{2,1,0:T(4,128)} %get-tuple-element.20), calls=%async_computation | async-start | bytes 1048576 | tf_op jit(solution)/shard_map/all_to_all | solution.py:617
  23.0 1.6 %collective-permute-start = (f32[128,128]{1,0:T(8,128)}, f32[128,128]{1,0:T(8,128)S(1)}, u32[]{:S(2)}, u32[]{:S(2)}) collective-permute-start(f32[128,128]{1,0:T(8,128)} %get-tuple-element.25), channel_id=1, source_target_pairs={{0,8},{16,24},{8,0},{24,16},{1,9},{17,25},{9,1},{25,17},{2,10},{18... | collective-permute-start | bytes 196616 | tf_op jit(solution)/shard_map/ppermute | solution.py:598
  24.6 0.7 collective-permute-start.1
  25.2 0.0 copy-done.1
  25.2 0.0 copy-done
  25.3 0.0 copy-done.4
  25.3 1.1 %weave.1 = (f32[5,2,256,128]{3,2,1,0:T(8,128)S(1)}, f32[5,128,128]{2,1,0:T(8,128)S(1)}, f32[2,3,64,128]{3,2,1,0:T(8,128)S(1)}) custom-call(f32[256,256]{1,0:T(8,128)S(1)} %copy-done.4, f32[2,256,256]{2,1,0:T(8,128)S(1)} %copy-done, f32[2,256,256]{2,1,0:T(8,128)S(1)} %copy-done.1), custom_call_target="tpu_custom_call" | custom-call | tf_op jit(solution)/shard_map/weave/pallas_call | solution.py:619
  26.4 0.0 copy-start.2
  26.4 1.1 %copy-done.2 = f32[5,2,256,128]{3,2,1,0:T(8,128)} copy-done((f32[5,2,256,128]{3,2,1,0:T(8,128)}, f32[5,2,256,128]{3,2,1,0:T(8,128)S(1)}, u32[]{:S(2)}) %copy-start.2) | copy-done | bytes 1310744
  27.5 0.2 collective-permute-done.first_col
  27.7 0.0 collective-permute-done.1.second_col
  27.7 0.1 rows.1
  27.8 0.1 collective-permute-start.2
  27.9 0.7 collective-permute-start.3
  28.6 4.2 %all-to-all-done.control = f32[8,4,4096]{2,1,0:T(4,128)S(1)} async-done(((f32[8,4,4096]{2,1,0:T(4,128)}), f32[8,4,4096]{2,1,0:T(4,128)S(1)}, u32[]{:S(2)}, u32[]{:S(2)}) %all-to-all-start) | async-done | bytes 524320 | tf_op jit(solution)/shard_map/all_to_all | solution.py:617
  32.7 0.0 copy-done.5
  32.7 0.0 copy-done.6
  32.7 0.9 %friction.1 = (f32[784,128]{1,0:T(8,128)S(1)}, f32[784,128]{1,0:T(8,128)S(1)}) custom-call(s32[4,8]{1,0:T(4,128)S(1)} %bitcast.4, s32[4,8]{1,0:T(4,128)S(1)} %bitcast.6, f32[8,4,4096]{2,1,0:T(4,128)S(1)} %all-to-all-done.control), custom_call_target="tpu_custom_call" | custom-call | tf_op jit(solution)/shard_map/friction/pallas_call | solution.py:636
  33.7 0.0 copy-start.3
  33.7 1.3 %copy-done.3 = f32[5,2,256,128]{3,2,1,0:T(8,128)S(1)} copy-done((f32[5,2,256,128]{3,2,1,0:T(8,128)S(1)}, f32[5,2,256,128]{3,2,1,0:T(8,128)}, u32[]{:S(2)}) %copy-start.3) | copy-done | bytes 1310744
  35.0 1.8 %setup.1 = (f32[5,784,128]{2,1,0:T(8,128)S(1)}, f32[2,784,128]{2,1,0:T(8,128)S(1)}) custom-call(f32[784,128]{1,0:T(8,128)S(1)} %get-tuple-element.21.fr, f32[784,128]{1,0:T(8,128)S(1)} %get-tuple-element.22.ice, f32[5,2,256,128]{3,2,1,0:T(8,128)S(1)} %copy-done.3, f32[5,128,128]{2,1,0:T(8,128)S(1)} %get-tuple-element.24.own_sides, ...), custom_call_target="tpu_custom_call" | custom-call | tf_op jit(solution)/shard_map/setup/pallas_call | solution.py:645
  36.8 0.0 collective-permute-done.2.first_row
  36.8 0.0 collective-permute-done.3.second_row
  36.8 13.8 %model.1 = (f32[256,256]{1,0:T(8,128)}, f32[256,256]{1,0:T(8,128)}, f32[16,32,128]{2,1,0:T(8,128)S(1)}) custom-call(f32[784,128]{1,0:T(8,128)S(1)} %get-tuple-element.21.fr, f32[784,128]{1,0:T(8,128)S(1)} %get-tuple-element.22.ice, f32[5,784,128]{2,1,0:T(8,128)S(1)} %get-tuple-element.27.ext_in, f32[2,784,128]{2,1,0:T(8,128)S(1)} %get-tuple-element.28.vel_in, ...), custom_call_target="tpu_custom_call" | custom-call | tf_op jit(solution)/shard_map/model/pallas_call | solution.py:659
  50.7 17.2 %all_to_all.10.gathered = f32[16,32,128]{2,1,0:T(8,128)S(1)} all-to-all(f32[16,32,128]{2,1,0:T(8,128)S(1)} %get-tuple-element.34), channel_id=1, replica_groups={{0,2,4,6,8,10,12,14,16,18,20,22,24,26,28,30},{1,3,5,7,9,11,13,15,17,19,..., dimensions={0} | all-to-all | bytes 524288 | tf_op jit(solution)/shard_map/all_to_all | solution.py:680
  67.8 0.8 %pick.1 = (f32[4,32,128]{2,1,0:T(8,128)S(1)}, f32[4,32,128]{2,1,0:T(8,128)S(1)}) custom-call(s32[4,8]{1,0:T(4,128)S(1)} %bitcast.5, f32[16,32,128]{2,1,0:T(8,128)S(1)} %all_to_all.10.gathered), custom_call_target="tpu_custom_call" | custom-call | tf_op jit(solution)/shard_map/pick/pallas_call | solution.py:681
  68.6 0.1 collective-permute-start.4
  68.7 1.2 %collective-permute-done.4.received = f32[4,32,128]{2,1,0:T(8,128)S(1)} collective-permute-done((f32[4,32,128]{2,1,0:T(8,128)S(1)}, f32[4,32,128]{2,1,0:T(8,128)S(1)}, u32[]{:S(2)}, u32[]{:S(2)}) %collective-permute-start.4) | collective-permute-done | bytes 65568 | tf_op jit(solution)/shard_map/ppermute | solution.py:690
  69.9 0.7 join.1
Async XLA Ops:
  0.6 24.6 %copy-start.1 = (f32[2,256,256]{2,1,0:T(8,128)S(1)}, f32[2,256,256]{2,1,0:T(8,128)}, u32[]{:S(2)}) copy-start(f32[2,256,256]{2,1,0:T(8,128)} %obs.3) | copy-start | bytes 1572868
  0.6 24.6 %copy-start = (f32[2,256,256]{2,1,0:T(8,128)S(1)}, f32[2,256,256]{2,1,0:T(8,128)}, u32[]{:S(2)}) copy-start(f32[2,256,256]{2,1,0:T(8,128)} %drive.3) | copy-start | bytes 1572868
  0.7 24.6 %copy-start.4 = (f32[256,256]{1,0:T(8,128)S(1)}, f32[256,256]{1,0:T(8,128)}, u32[]{:S(2)}) copy-start(f32[256,256]{1,0:T(8,128)} %thick.3) | copy-start | bytes 786436
  0.7 32.1 %copy-start.5 = (s32[8,4,1]{0,2,1:T(1,128)S(1)}, s32[8,4,1]{0,2,1:T(1,128)}, u32[]{:S(2)}) copy-start(s32[8,4,1]{0,2,1:T(1,128)} %param.11) | copy-start | bytes 388
  0.7 32.1 %copy-start.6 = (s32[8,4]{0,1:T(4,128)S(1)}, s32[8,4]{0,1:T(4,128)}, u32[]{:S(2)}) copy-start(s32[8,4]{0,1:T(4,128)} %param.10) | copy-start | bytes 388
  17.8 14.9 %all-to-all-start = ((f32[8,4,4096]{2,1,0:T(4,128)}), f32[8,4,4096]{2,1,0:T(4,128)S(1)}, u32[]{:S(2)}, u32[]{:S(2)}) async-start(f32[8,4,4096]{2,1,0:T(4,128)} %get-tuple-element.20), calls=%async_computation | async-start | bytes 1048576 | tf_op jit(solution)/shard_map/all_to_all | solution.py:617
  23.0 4.7 %collective-permute-start = (f32[128,128]{1,0:T(8,128)}, f32[128,128]{1,0:T(8,128)S(1)}, u32[]{:S(2)}, u32[]{:S(2)}) collective-permute-start(f32[128,128]{1,0:T(8,128)} %get-tuple-element.25), channel_id=1, source_target_pairs={{0,8},{16,24},{8,0},{24,16},{1,9},{17,25},{9,1},{25,17},{2,10},{18... | collective-permute-start | bytes 196616 | tf_op jit(solution)/shard_map/ppermute | solution.py:598
  24.6 3.1 %collective-permute-start.1 = (f32[128,128]{1,0:T(8,128)}, f32[128,128]{1,0:T(8,128)S(1)}, u32[]{:S(2)}, u32[]{:S(2)}) collective-permute-start(f32[128,128]{1,0:T(8,128)} %get-tuple-element.26), channel_id=1, source_target_pairs={{8,16},{16,8},{9,17},{17,9},{10,18},{18,10},{11,19},{19,11},{12,20... | collective-permute-start | bytes 196616 | tf_op jit(solution)/shard_map/ppermute | solution.py:598
  26.4 1.1 %copy-start.2 = (f32[5,2,256,128]{3,2,1,0:T(8,128)}, f32[5,2,256,128]{3,2,1,0:T(8,128)S(1)}, u32[]{:S(2)}) copy-start(f32[5,2,256,128]{3,2,1,0:T(8,128)S(1)} %get-tuple-element.23.woven) | copy-start | bytes 3932164
  27.8 9.0 %collective-permute-start.2 = (f32[160,128]{1,0:T(8,128)S(1)}, f32[160,128]{1,0:T(8,128)S(1)}, u32[]{:S(2)}, u32[]{:S(2)}) collective-permute-start(f32[160,128]{1,0:T(8,128)S(1)} %get-tuple-element.30), channel_id=1, source_target_pairs={{0,1},{2,3},{4,5},{6,7},{1,0},{3,2},{5,4},{7,6},{8,9},{10,11},{12,... | collective-permute-start | bytes 245768 | tf_op jit(solution)/shard_map/ppermute | solution.py:598
  27.9 8.9 %collective-permute-start.3 = (f32[160,128]{1,0:T(8,128)S(1)}, f32[160,128]{1,0:T(8,128)S(1)}, u32[]{:S(2)}, u32[]{:S(2)}) collective-permute-start(f32[160,128]{1,0:T(8,128)S(1)} %get-tuple-element.31), channel_id=1, source_target_pairs={{1,2},{3,4},{5,6},{2,1},{4,3},{6,5},{9,10},{11,12},{13,14},{10,9},... | collective-permute-start | bytes 245768 | tf_op jit(solution)/shard_map/ppermute | solution.py:598
  33.7 1.3 %copy-start.3 = (f32[5,2,256,128]{3,2,1,0:T(8,128)S(1)}, f32[5,2,256,128]{3,2,1,0:T(8,128)}, u32[]{:S(2)}) copy-start(f32[5,2,256,128]{3,2,1,0:T(8,128)} %copy-done.2) | copy-start | bytes 3932164
  68.6 1.3 %collective-permute-start.4 = (f32[4,32,128]{2,1,0:T(8,128)S(1)}, f32[4,32,128]{2,1,0:T(8,128)S(1)}, u32[]{:S(2)}, u32[]{:S(2)}) collective-permute-start(f32[4,32,128]{2,1,0:T(8,128)S(1)} %get-tuple-element.36), channel_id=1, source_target_pairs={{0,1},{1,0},{2,3},{3,2},{4,5},{5,4},{6,7},{7,6},{8,9},{9,8},{10,11... | collective-permute-start | bytes 196616 | tf_op jit(solution)/shard_map/ppermute | solution.py:690

commit v15 on v11

--- a/solution.py
+++ b/solution.py
@@ -32,7 +32,7 @@
     "tile": (TOP, 4, 64, TOP, 32, 0, 0),
 }
 FACTORS = 14
-AHEAD = 2
+AHEAD = 5
 PACK = COARSE // LANES
 VMEM_LIMIT = 24 * 1024 * 1024
 PACK_VMEM_LIMIT = 62 * 1024 * 1024
@@ -97,9 +97,11 @@
 
 
 def pack_kernel(
-    tile_block, control, thick, drive, obs, first_col, second_col, parcels,
-    held, held_control, owned_blocks, packed_parcels, packed_cols, sems,
+    table, control, thick, drive, obs, first_col, second_col, parcels,
+    tile_block, held, held_control, owned_blocks, packed_parcels, packed_cols, sems,
 ):
+    table_copy = pltpu.make_async_copy(table, tile_block, sems.at[9])
+    table_copy.start()
     copies = [pltpu.make_async_copy(control, held_control, sems.at[5])]
     for f, field in enumerate((thick, drive.at[0], drive.at[1], obs.at[0], obs.at[1])):
         copies.append(pltpu.make_async_copy(field, held.at[f], sems.at[f]))
@@ -109,6 +111,7 @@
     copies[0].wait()
     for j in range(PACK):
         owned_blocks[:, j, :] = held_control[:, j * LANES : (j + 1) * LANES]
+    table_copy.wait()
     fill_parcels(tile_block, owned_blocks, packed_parcels)
     results = [pltpu.make_async_copy(packed_parcels, parcels, sems.at[6])]
     results[0].start()
@@ -173,9 +176,8 @@
         own_sides[f] = jnp.where(half_lane < BAND, bands[0][:HALF], bands[1][HALF:])
         for c in range(2):
             woven[f, c] = tiles[c]
-        for c, tile in enumerate(tiles + [bands[1]]):
+        for c, tile in enumerate(tiles + [bands[0]]):
             edges[0, c, first : first + count, :] = tile[:count]
-        for c, tile in enumerate(tiles + [bands[0]]):
             edges[1, c, first : first + count, :] = tile[TILE - count :]
 
 
@@ -184,21 +186,27 @@
     even = is_even("gy")
     for c in range(2):
         top, bottom = edges[0, c], edges[1, c]
-        first_pair[c] = jnp.where(even, bottom, top)
-        second_pair[c] = jnp.where(even, top, bottom)
-    for f, (first, count) in enumerate(STRIP):
-        strips = []
-        for i, packed, source, target in (
-            (0, slice(0, count), first, BAND),
-            (1, slice(HALF - count, HALF), BAND + first, 0),
-        ):
-            own = edges[i, 2, first : first + count, :]
+        first_pair[64 * c : 64 * c + 64, :] = jnp.where(even, bottom, top)
+        second_pair[64 * c : 64 * c + 64, :] = jnp.where(even, top, bottom)
+    strips = []
+    for i in range(2):
+        fields = []
+        for f, (first, count) in enumerate(STRIP):
+            packed = slice(HALF - count, HALF) if i else slice(0, count)
+            source = BAND * i + first
+            target = BAND if f >= 2 else 0
+            own = turn(edges[i, 2, first : first + count, :], 0, target)
             from_east = scale_of(f) * turn(east[packed], source, target + HALO)
             from_west = scale_of(f) * turn(west[packed], source, target + 3 * HALO - count)
-            strips.append(choose_side(lanes_of(count), own, from_east, from_west, own))
-        top, bottom = strips
-        first_pair[2, first : first + count, :] = jnp.where(even, bottom, top)
-        second_pair[2, first : first + count, :] = jnp.where(even, top, bottom)
+            fields.append(choose_side(lanes_of(count), own, from_east, from_west, own))
+        lane = lanes_of(HALO)
+        lower = jnp.concatenate(fields[3:], axis=0)
+        strips.append((jnp.where(lane < BAND, fields[0], fields[2]), jnp.where(lane < BAND, fields[1], lower)))
+    for k in range(2):
+        top, bottom = strips[0][k], strips[1][k]
+        rows = slice(128 + HALO * k, 128 + HALO * (k + 1))
+        first_pair[rows, :] = jnp.where(even, bottom, top)
+        second_pair[rows, :] = jnp.where(even, top, bottom)
 
 
 def shift_east(tiles):
@@ -298,10 +306,15 @@
         join(TOP + HALF, False, True, HALO)
 
 
-def friction_kernel(ice_mask, parcels, fr, ice, patch):
+def friction_kernel(tile_block, ice_mask, parcels, fr, ice, owners, patch):
     tile_cols, tile_rows = ice_mask.shape
     row_tile = lax.axis_index("gy")
     col_tile = lax.axis_index("gx")
+    core = row_tile % 2
+    place = lax.broadcasted_iota(jnp.int32, owners.shape[1:], 0)
+    for t in range(owners.shape[0]):
+        block = tile_block[t // (tile_rows // 2), t % (tile_rows // 2) * 2 + core]
+        owners[t] = (place == block - (row_tile - core) * (owners.shape[1] // 2)).astype(jnp.int32)
 
     flat = sum(parcels[j] for j in range(tile_rows))
     folded = flat[FOLDED:]
@@ -496,21 +509,20 @@
 ):
     ext[...] = ext_in[...]
     vel_b[...] = vel_in[...]
-    even = is_even("gy")
+    north, south = sides("gy", first_row[...], second_row[...])
     here = SIDE + TOP
     for f, (first, count) in enumerate(STRIP):
-        frames = []
-        for c in range(3):
-            one, two = first_row[c, first : first + count, :], second_row[c, first : first + count, :]
-            frames.append((jnp.where(even, two, one), jnp.where(even, one, two)))
         for c in range(2):
-            ext[f, MAIN[c] + TOP - count : MAIN[c] + TOP, :] = frames[c][0]
-            ext[f, MAIN[c] + TOP + TILE : MAIN[c] + TOP + TILE + count, :] = frames[c][1]
+            rows = slice(64 * c + first, 64 * c + first + count)
+            ext[f, MAIN[c] + TOP - count : MAIN[c] + TOP, :] = north[rows]
+            ext[f, MAIN[c] + TOP + TILE : MAIN[c] + TOP + TILE + count, :] = south[rows]
+        rows = slice(128 + first % 32, 128 + first % 32 + count)
+        source = BAND if f >= 2 else 0
         upper = lanes_of(count) < BAND
         above = turn(ext_in[f, here + HALF - count : here + HALF, :], 0, BAND)
         below = turn(ext_in[f, here : here + count, :], 0, BAND)
-        ext[f, here - count : here, :] = jnp.where(upper, frames[2][0], above)
-        ext[f, here + HALF : here + HALF + count, :] = jnp.where(upper, below, frames[2][1])
+        ext[f, here - count : here, :] = jnp.where(upper, turn(north[rows], source, 0), above)
+        ext[f, here + HALF : here + HALF + count, :] = jnp.where(upper, below, turn(south[rows], source, BAND))
 
     step = make_stages(ext, fr, ice, visc, vel_a, vel_b, coef)
     over_ends(32, step.read_thickness, step.first_viscosity)
@@ -592,28 +604,20 @@
         copy.wait()
 
 
-def pick_kernel(tile_block, gathered, own, other, total):
+def pick_kernel(owners, gathered, own, other):
     owned = own.shape[0]
-    row_tile = lax.axis_index("gy")
-    core = row_tile % 2
-    first = (row_tile - core) * owned
-    tile_cols, tile_rows = tile_block.shape
-    total[...] = jnp.zeros_like(total)
-    for t in range(tile_cols * tile_rows // 2):
-        place = tile_block[t // (tile_rows // 2), t % (tile_rows // 2) * 2 + core] - first
-
-        @pl.when((place >= 0) & (place < 2 * owned))
-        def _():
-            total[place] += gathered[t]
-
-    own[...] = total[pl.ds(core * owned, owned)]
-    other[...] = total[pl.ds((1 - core) * owned, owned)]
-
-
-def join_kernel(own, received, out):
-    total = own[...] + received[...]
-    for j in range(PACK):
-        out[:, j * LANES : (j + 1) * LANES] = total[:, j, :]
+    first = lax.axis_index("gy") % 2 == 0
+    total = []
+    for block in range(2 * owned):
+        parts = [jnp.where(owners[t, block : block + 1, :] > 0, gathered[t], 0.0) for t in range(owners.shape[0])]
+        while len(parts) > 1:
+            parts = [sum(parts[i : i + 2]) for i in range(0, len(parts), 2)]
+        total.append(parts[0])
+    for block in range(owned):
+        low, high = total[block], total[block + owned]
+        for out, cells in ((own, jnp.where(first, low, high)), (other, jnp.where(first, high, low))):
+            for j in range(PACK):
+                out[block : block + 1, j * LANES : (j + 1) * LANES] = cells[j : j + 1]
 
 
 def in_vmem(count):
@@ -646,15 +650,16 @@
     *edges, parcels = pl.pallas_call(
         pack_kernel,
         out_shape=[shape(HALF, LANES)] * 2 + [shape(rows, PARCEL, LANES)],
-        in_specs=in_smem(1) + [pl.BlockSpec(memory_space=pltpu.HBM)] * 4,
+        in_specs=[pl.BlockSpec(memory_space=pltpu.HBM)] * 5,
         out_specs=[pl.BlockSpec(memory_space=pltpu.HBM)] * 3,
         scratch_shapes=[
+            pltpu.SMEM(tile_block.shape, jnp.int32),
             pltpu.VMEM((5, TILE, TILE), f32),
             pltpu.VMEM(control.shape, f32),
             pltpu.VMEM((owned, PACK, LANES), f32),
             pltpu.VMEM((rows, PARCEL, LANES), f32),
             pltpu.VMEM((2, HALF, LANES), f32),
-            pltpu.SemaphoreType.DMA((9,)),
+            pltpu.SemaphoreType.DMA((10,)),
         ],
         compiler_params=pltpu.CompilerParams(vmem_limit_bytes=PACK_VMEM_LIMIT),
         name="pack",
@@ -671,22 +676,23 @@
     )(*fields)
     strips = pl.pallas_call(
         rows_kernel,
-        out_shape=[shape(3, 64, LANES)] * 2,
+        out_shape=[shape(160, LANES)] * 2,
         in_specs=in_vmem(3),
         out_specs=in_vmem(2),
         compiler_params=params,
         name="rows",
     )(strips, *columns_in)
     rows_in = swap("gy", *strips)
-    friction = pl.pallas_call(
+    *friction, owners = pl.pallas_call(
         friction_kernel,
-        out_shape=[shape(ALL_ROWS, LANES)] * 2,
-        in_specs=in_smem(1) + in_vmem(1),
-        out_specs=in_vmem(2),
+        out_shape=[shape(ALL_ROWS, LANES)] * 2
+        + [jax.ShapeDtypeStruct((cols * rows // 2, 2 * owned, LANES), jnp.int32)],
+        in_specs=in_smem(2) + in_vmem(1),
+        out_specs=in_vmem(3),
         scratch_shapes=[pltpu.VMEM((PATCH, LANES), f32)],
         compiler_params=params,
         name="friction",
-    )(ice_mask, parcels)
+    )(tile_block, ice_mask, parcels)
     prepared = pl.pallas_call(
         setup_kernel,
         out_shape=[shape(5, ALL_ROWS, LANES), shape(2, ALL_ROWS, LANES)],
@@ -725,22 +731,13 @@
     sums = lax.all_to_all(sums, ("gx", "gy"), 0, 0, tiled=True, axis_index_groups=same_core)
     own, other = pl.pallas_call(
         pick_kernel,
-        out_shape=[shape(owned, PACK, LANES)] * 2,
-        in_specs=in_smem(1) + in_vmem(1),
+        out_shape=[shape(*control.shape)] * 2,
+        in_specs=in_vmem(2),
         out_specs=in_vmem(2),
-        scratch_shapes=[pltpu.VMEM((2 * owned, PACK, LANES), f32)],
         compiler_params=params,
         name="pick",
-    )(tile_block, sums)
-    received = lax.ppermute(other, "gy", [(j, j ^ 1) for j in range(rows)])
-    gradient = pl.pallas_call(
-        join_kernel,
-        out_shape=shape(*control.shape),
-        in_specs=in_vmem(2),
-        out_specs=pl.BlockSpec(memory_space=pltpu.VMEM),
-        compiler_params=params,
-        name="join",
-    )(own, received)
+    )(owners, sums)
+    gradient = own + lax.ppermute(other, "gy", [(j, j ^ 1) for j in range(rows)])
     return vel_u, vel_v, gradient
 
 

time: 57.4 us -> 56 us (0.976)
  Pallas kernels: 22.7 us -> 21 us
  other arithmetic: 0 us -> 0.65 us
    pallas_call x4 -> x3, Pallas kernels: 2.36 us -> 1.3 us  [the longest x1 0.85 us: per_device(): pl.pallas_call(friction_kernel, out_shape=[shape(ALL_ROWS, LANES)] * 2 +...]
    pallas_call x1, Pallas kernels: 3.6 us -> 2.92 us  [per_device(): pl.pallas_call(pack_kernel, out_shape=[shape(HALF, LANES)] * 2 + [shape(r...]
    add x0 -> x1, other arithmetic: none -> 0.65 us  [per_device(): own + lax.ppermute(other, 'gy', [(j, j ^ 1) for j in range(rows)])]
where the time goes in v15:
time: 56 us; the launch traced here: 55.8 us
  blocking collectives  21.9 us (39%)
  Pallas kernels  21 us (38%)
  starting transfers between devices  8.35 us (15%)
  waiting for transfers between devices  2.13 us (4%)
  local copies, waits for them, and re-layouts  0.96 us (2%)
  between operations  0.79 us (1%)
  other arithmetic  0.65 us (1%)
    all_to_all x1, blocking collectives, per_device(): lax.all_to_all(sums, ('gx', 'gy'), 0, 0, tiled=True, axis_index_groups=sa...  21.9 us
    pallas_call x1, Pallas kernels, per_device(): pl.pallas_call(model_kernel, out_shape=(shape(TILE, TILE), shape(TILE, TI...  13.8 us
    all_to_all x1, starting transfers between devices, per_device(): parcels = lax.all_to_all(parcels, 'gy', 0, 0, tiled=True)  5.19 us
    ppermute x4, starting transfers between devices, swap(): lax.ppermute(cells, axis, pairs + [(j, i) for i, j in pairs])  3.09 us
    pallas_call x1, Pallas kernels, per_device(): pl.pallas_call(pack_kernel, out_shape=[shape(HALF, LANES)] * 2 + [shape(r...  2.92 us
    pallas_call x1, Pallas kernels, per_device(): pl.pallas_call(setup_kernel, out_shape=[shape(5, ALL_ROWS, LANES), shape(...  1.82 us
    ppermute x1, waiting for transfers between devices, per_device(): lax.ppermute(other, 'gy', [(j, j ^ 1) for j in range(rows)])  1.24 us
    pallas_call x1, Pallas kernels, per_device(): pl.pallas_call(weave_kernel, out_shape=[shape(5, 2, TILE, LANES), shape(5...  1.14 us
  transfers between devices with their start and end apart: 6, of which 3 were waited for; matrix products, arithmetic and copies ran while one was open for 0% of the time, Pallas kernels for 7%

profile of v15, /device:TPU:0, one launch (start us, length us, event | category | flops | bytes accessed | tf_op | source)
XLA Modules:
  0.0 55.8 jit_solution(10329393355502596863)
XLA Ops:
  0.6 0.0 copy-start.1
  0.6 0.0 copy-start
  0.7 0.0 copy-start.3
  0.7 0.0 copy-start.4
  0.7 2.9 %pack.1 = (f32[128,128]{1,0:T(8,128)}, f32[128,128]{1,0:T(8,128)}, f32[8,48,128]{2,1,0:T(8,128)}) custom-call(s32[4,8]{1,0:T(4,128)} %bitcast.4, f32[4,4096]{1,0:T(4,128)} %control.1, f32[256,256]{1,0:T(8,128)} %thick.3, f32[2,256,256]{2,1,0:T(8,128)} %drive.3, f32[2,256,256]{2,1,0:T(8,128)} %obs.3), custom_call_target="tpu_custom_call" | custom-call | tf_op jit(solution)/shard_map/pack/pallas_call | solution.py:650
  3.6 5.2 %all-to-all-start = ((f32[8,48,128]{2,1,0:T(8,128)}), f32[8,48,128]{2,1,0:T(8,128)S(1)}, u32[]{:S(2)}, u32[]{:S(2)}) async-start(f32[8,48,128]{2,1,0:T(8,128)} %get-tuple-element.21), calls=%async_computation | async-start | bytes 393216 | tf_op jit(solution)/shard_map/all_to_all | solution.py:667
  8.8 1.7 %collective-permute-start = (f32[128,128]{1,0:T(8,128)}, f32[128,128]{1,0:T(8,128)S(1)}, u32[]{:S(2)}, u32[]{:S(2)}) collective-permute-start(f32[128,128]{1,0:T(8,128)} %get-tuple-element.26), channel_id=1, source_target_pairs={{0,8},{16,24},{8,0},{24,16},{1,9},{17,25},{9,1},{25,17},{2,10},{18... | collective-permute-start | bytes 196616 | tf_op jit(solution)/shard_map/ppermute | solution.py:645
  10.5 0.7 %collective-permute-start.1 = (f32[128,128]{1,0:T(8,128)}, f32[128,128]{1,0:T(8,128)S(1)}, u32[]{:S(2)}, u32[]{:S(2)}) collective-permute-start(f32[128,128]{1,0:T(8,128)} %get-tuple-element.27), channel_id=1, source_target_pairs={{8,16},{16,8},{9,17},{17,9},{10,18},{18,10},{11,19},{19,11},{12,20... | collective-permute-start | bytes 196616 | tf_op jit(solution)/shard_map/ppermute | solution.py:645
  11.1 0.0 copy-done.1
  11.2 0.0 copy-done
  11.2 0.0 copy-start.2
  11.2 0.9 %copy-done.2 = f32[256,256]{1,0:T(8,128)S(1)} copy-done((f32[256,256]{1,0:T(8,128)S(1)}, f32[256,256]{1,0:T(8,128)}, u32[]{:S(2)}) %copy-start.2) | copy-done | bytes 262168
  12.1 1.1 %weave.1 = (f32[5,2,256,128]{3,2,1,0:T(8,128)S(1)}, f32[5,128,128]{2,1,0:T(8,128)S(1)}, f32[2,3,64,128]{3,2,1,0:T(8,128)S(1)}) custom-call(f32[256,256]{1,0:T(8,128)S(1)} %copy-done.2, f32[2,256,256]{2,1,0:T(8,128)S(1)} %copy-done, f32[2,256,256]{2,1,0:T(8,128)S(1)} %copy-done.1), custom_call_target="tpu_custom_call" | custom-call | tf_op jit(solution)/shard_map/weave/pallas_call | solution.py:669
  13.3 0.2 collective-permute-done.first_col
  13.5 0.0 collective-permute-done.1.second_col
  13.5 0.1 rows.1
  13.6 0.1 collective-permute-start.2
  13.7 0.7 %collective-permute-start.3 = (f32[160,128]{1,0:T(8,128)S(1)}, f32[160,128]{1,0:T(8,128)S(1)}, u32[]{:S(2)}, u32[]{:S(2)}) collective-permute-start(f32[160,128]{1,0:T(8,128)S(1)} %get-tuple-element.32), channel_id=1, source_target_pairs={{1,2},{3,4},{5,6},{2,1},{4,3},{6,5},{9,10},{11,12},{13,14},{10,9},... | collective-permute-start | bytes 245768 | tf_op jit(solution)/shard_map/ppermute | solution.py:645
  14.4 0.6 %all-to-all-done.parcels = f32[8,48,128]{2,1,0:T(8,128)S(1)} async-done(((f32[8,48,128]{2,1,0:T(8,128)}), f32[8,48,128]{2,1,0:T(8,128)S(1)}, u32[]{:S(2)}, u32[]{:S(2)}) %all-to-all-start) | async-done | bytes 196640 | tf_op jit(solution)/shard_map/all_to_all | solution.py:667
  15.0 0.0 copy-done.3
  15.0 0.0 copy-done.4
  15.0 0.9 %friction.1 = (f32[784,128]{1,0:T(8,128)S(1)}, f32[784,128]{1,0:T(8,128)S(1)}, s32[16,8,128]{2,1,0:T(8,128)S(1)}) custom-call(s32[4,8]{1,0:T(4,128)S(1)} %bitcast.5, s32[4,8]{1,0:T(4,128)S(1)} %bitcast.6, f32[8,48,128]{2,1,0:T(8,128)S(1)} %all-to-all-done.parcels), custom_call_target="tpu_custom_call" | custom-call | tf_op jit(solution)/shard_map/friction/pallas_call | solution.py:686
  15.9 1.8 %setup.1 = (f32[5,784,128]{2,1,0:T(8,128)S(1)}, f32[2,784,128]{2,1,0:T(8,128)S(1)}) custom-call(f32[784,128]{1,0:T(8,128)S(1)} %get-tuple-element.22.fr, f32[784,128]{1,0:T(8,128)S(1)} %get-tuple-element.23.ice, f32[5,2,256,128]{3,2,1,0:T(8,128)S(1)} %get-tuple-element.24.woven, f32[5,128,128]{2,1,0:T(8,128)S(1)} %get-tuple-element.25.own_sides, ...), custom_call_target="tpu_custom_call" | custom-call | tf_op jit(solution)/shard_map/setup/pallas_call | solution.py:696
  17.7 0.0 collective-permute-done.2.first_row
  17.7 0.0 collective-permute-done.3.second_row
  17.7 13.8 %model.1 = (f32[256,256]{1,0:T(8,128)}, f32[256,256]{1,0:T(8,128)}, f32[16,32,128]{2,1,0:T(8,128)S(1)}) custom-call(f32[784,128]{1,0:T(8,128)S(1)} %get-tuple-element.22.fr, f32[784,128]{1,0:T(8,128)S(1)} %get-tuple-element.23.ice, f32[5,784,128]{2,1,0:T(8,128)S(1)} %get-tuple-element.28.ext_in, f32[2,784,128]{2,1,0:T(8,128)S(1)} %get-tuple-element.29.vel_in, ...), custom_call_target="tpu_custom_call" | custom-call | tf_op jit(solution)/shard_map/model/pallas_call | solution.py:710
  31.6 21.9 %all_to_all.10.gathered = f32[16,32,128]{2,1,0:T(8,128)S(1)} all-to-all(f32[16,32,128]{2,1,0:T(8,128)S(1)} %get-tuple-element.36), channel_id=1, replica_groups={{0,2,4,6,8,10,12,14,16,18,20,22,24,26,28,30},{1,3,5,7,9,11,13,15,17,19,..., dimensions={0} | all-to-all | bytes 524288 | tf_op jit(solution)/shard_map/all_to_all | solution.py:731
  53.5 0.3 pick.1
  53.8 0.1 collective-permute-start.4
  53.9 1.2 %collective-permute-done.4 = f32[4,4096]{1,0:T(4,128)S(1)} collective-permute-done((f32[4,4096]{1,0:T(4,128)S(1)}, f32[4,4096]{1,0:T(4,128)S(1)}, u32[]{:S(2)}, u32[]{:S(2)}) %collective-permute-start.4) | collective-permute-done | bytes 65568 | tf_op jit(solution)/shard_map/ppermute | solution.py:740
  55.1 0.6 %add.3 = f32[4,4096]{1,0:T(4,128)} add(f32[4,4096]{1,0:T(4,128)S(1)} %get-tuple-element.37, f32[4,4096]{1,0:T(4,128)S(1)} %collective-permute-done.4) | non-fusion elementwise | flops 16384 | bytes 196608 | tf_op jit(solution)/shard_map/add | solution.py:740
Async XLA Ops:
  0.6 10.5 %copy-start.1 = (f32[2,256,256]{2,1,0:T(8,128)S(1)}, f32[2,256,256]{2,1,0:T(8,128)}, u32[]{:S(2)}) copy-start(f32[2,256,256]{2,1,0:T(8,128)} %obs.3) | copy-start | bytes 1572868
  0.6 10.5 %copy-start = (f32[2,256,256]{2,1,0:T(8,128)S(1)}, f32[2,256,256]{2,1,0:T(8,128)}, u32[]{:S(2)}) copy-start(f32[2,256,256]{2,1,0:T(8,128)} %drive.3) | copy-start | bytes 1572868
  0.7 14.4 %copy-start.3 = (s32[8,4,1]{0,2,1:T(1,128)S(1)}, s32[8,4,1]{0,2,1:T(1,128)}, u32[]{:S(2)}) copy-start(s32[8,4,1]{0,2,1:T(1,128)} %param.11) | copy-start | bytes 388
  0.7 14.4 %copy-start.4 = (s32[8,4]{0,1:T(4,128)S(1)}, s32[8,4]{0,1:T(4,128)}, u32[]{:S(2)}) copy-start(s32[8,4]{0,1:T(4,128)} %param.10) | copy-start | bytes 388
  3.6 11.4 %all-to-all-start = ((f32[8,48,128]{2,1,0:T(8,128)}), f32[8,48,128]{2,1,0:T(8,128)S(1)}, u32[]{:S(2)}, u32[]{:S(2)}) async-start(f32[8,48,128]{2,1,0:T(8,128)} %get-tuple-element.21), calls=%async_computation | async-start | bytes 393216 | tf_op jit(solution)/shard_map/all_to_all | solution.py:667
  8.8 4.7 %collective-permute-start = (f32[128,128]{1,0:T(8,128)}, f32[128,128]{1,0:T(8,128)S(1)}, u32[]{:S(2)}, u32[]{:S(2)}) collective-permute-start(f32[128,128]{1,0:T(8,128)} %get-tuple-element.26), channel_id=1, source_target_pairs={{0,8},{16,24},{8,0},{24,16},{1,9},{17,25},{9,1},{25,17},{2,10},{18... | collective-permute-start | bytes 196616 | tf_op jit(solution)/shard_map/ppermute | solution.py:645
  10.5 3.0 %collective-permute-start.1 = (f32[128,128]{1,0:T(8,128)}, f32[128,128]{1,0:T(8,128)S(1)}, u32[]{:S(2)}, u32[]{:S(2)}) collective-permute-start(f32[128,128]{1,0:T(8,128)} %get-tuple-element.27), channel_id=1, source_target_pairs={{8,16},{16,8},{9,17},{17,9},{10,18},{18,10},{11,19},{19,11},{12,20... | collective-permute-start | bytes 196616 | tf_op jit(solution)/shard_map/ppermute | solution.py:645
  11.2 1.0 %copy-start.2 = (f32[256,256]{1,0:T(8,128)S(1)}, f32[256,256]{1,0:T(8,128)}, u32[]{:S(2)}) copy-start(f32[256,256]{1,0:T(8,128)} %thick.3) | copy-start | bytes 786436
  13.6 4.1 %collective-permute-start.2 = (f32[160,128]{1,0:T(8,128)S(1)}, f32[160,128]{1,0:T(8,128)S(1)}, u32[]{:S(2)}, u32[]{:S(2)}) collective-permute-start(f32[160,128]{1,0:T(8,128)S(1)} %get-tuple-element.31), channel_id=1, source_target_pairs={{0,1},{2,3},{4,5},{6,7},{1,0},{3,2},{5,4},{7,6},{8,9},{10,11},{12,... | collective-permute-start | bytes 245768 | tf_op jit(solution)/shard_map/ppermute | solution.py:645
  13.7 4.0 %collective-permute-start.3 = (f32[160,128]{1,0:T(8,128)S(1)}, f32[160,128]{1,0:T(8,128)S(1)}, u32[]{:S(2)}, u32[]{:S(2)}) collective-permute-start(f32[160,128]{1,0:T(8,128)S(1)} %get-tuple-element.32), channel_id=1, source_target_pairs={{1,2},{3,4},{5,6},{2,1},{4,3},{6,5},{9,10},{11,12},{13,14},{10,9},... | collective-permute-start | bytes 245768 | tf_op jit(solution)/shard_map/ppermute | solution.py:645
  53.8 1.3 %collective-permute-start.4 = (f32[4,4096]{1,0:T(4,128)S(1)}, f32[4,4096]{1,0:T(4,128)S(1)}, u32[]{:S(2)}, u32[]{:S(2)}) collective-permute-start(f32[4,4096]{1,0:T(4,128)S(1)} %get-tuple-element.38), channel_id=1, source_target_pairs={{0,1},{1,0},{2,3},{3,2},{4,5},{5,4},{6,7},{7,6},{8,9},{9,8},{10,11... | collective-permute-start | bytes 196616 | tf_op jit(solution)/shard_map/ppermute | solution.py:740

commit v16 on v15

--- a/solution.py
+++ b/solution.py
@@ -159,7 +159,7 @@
 
 
 def scale_of(f):
-    return 0.5 if f in (1, 2) else 1.0
+    return (0.25 * visc_scale * 4.0 ** (1.0 / 3.0), 0.5, 0.5, 1.0, 1.0)[f]
 
 
 def weave_kernel(thick, drive, obs, woven, own_sides, edges):
@@ -382,7 +382,7 @@
         return [(visc, (0,), q), (visc, (1,), shift_west(q)), (visc, (2,), shift_east(q))]
 
     def first_viscosity(part, thickness):
-        factor = 0.25 * visc_scale * strain_floor ** (-1.0 / 3.0)
+        factor = (4.0 * strain_floor) ** (-1.0 / 3.0)
         return keep_viscosity([factor * t for t in thickness])
 
     def read_viscosity(part, row, count):
@@ -397,8 +397,8 @@
             ux, vx = u_e[c] - u_w[c], v_e[c] - v_w[c]
             uy, vy = u_s[c] - u_n[c], v_s[c] - v_n[c]
             shear = uy + vx
-            strain = 0.25 * (ux * (ux + vy) + vy * vy) + (0.0625 * (shear * shear) + strain_floor)
-            result.append((0.25 * visc_scale) * thickness[c] * jnp.exp(jnp.log(strain) * (-1.0 / 3.0)))
+            strain = (ux * (ux + vy) + vy * vy) + (0.25 * (shear * shear) + 4.0 * strain_floor)
+            result.append(thickness[c] * jnp.exp(jnp.log(strain) * (-1.0 / 3.0)))
         return keep_viscosity(result)
 
     def inverse(x):
@@ -504,8 +504,8 @@
 
 def model_kernel(
     fr, ice, ext_in, vel_in, first_row, second_row,
-    vel_u, vel_v, sums,
-    ext, visc, vel_a, vel_b, vel_c, coef, plain, small, sems,
+    vel_b, sums,
+    ext, visc, vel_a, vel_c, coef, small,
 ):
     ext[...] = ext_in[...]
     vel_b[...] = vel_in[...]
@@ -529,45 +529,30 @@
     over_ends(32, step.read_first, step.first_start)
     over_ends(24, step.read_sweep(vel_a), step.sweep(vel_b))
 
-    def iterate(span):
-        over_rows(span, step.read_viscosity, step.viscosity)
-        over_rows(span, step.read_start, step.start)
-        over_rows(span, step.read_sweep(vel_a), step.sweep(vel_b))
-
     def iteration(i, carry):
-        iterate("frame")
+        over_rows("frame", step.read_viscosity, step.viscosity)
+        over_rows("frame", step.read_start, step.start)
+        over_rows("frame", step.read_sweep(vel_a), step.sweep(vel_b))
         return carry
 
     lax.fori_loop(1, PIC - 1, iteration, 0)
     join_parts(vel_b, ((0,), (1,)), True)
-    iterate("inner")
-    join_parts(vel_b, ((0,), (1,)), False)
-    lane = lanes_of(TILE)
-    copies = []
-    for i, out in enumerate((vel_u, vel_v)):
-        even, odd = (vel_b[i, tile + TOP : tile + TOP + TILE, :] for tile in MAIN)
-        for c in range(2):
-            source = BAND * c + lane // 2
-            plain[i, c] = jnp.where(lane % 2 == 0, gather(even, source), gather(odd, source))
-            copies.append(
-                pltpu.make_async_copy(plain.at[i, c], out.at[:, c * LANES : (c + 1) * LANES], sems.at[2 * i + c])
-            )
-            copies[-1].start()
+    over_rows("inner", step.read_viscosity, step.viscosity)
+    over_rows("inner", step.read_start, step.start)
 
     load = step.load
 
-    def read_misfit(part, row, count):
-        return [
-            [load(vel_b, part, row, count, i), load(ext, part, row, count, 3 + i), load(coef, part, row, count, 4 + i)]
-            for i in range(2)
-        ]
-
-    def first_adjoint(part, read):
-        misfit = [[0.5 * (a - b) for a, b in zip(u, seen)] for u, seen, _ in read]
-        first = [[a * b for a, b in zip(read[i][2], misfit[i])] for i in range(2)]
-        return step.put(vel_c, first) + [(ext, (1 + i,), misfit[i]) for i in range(2)]
-
-    over_rows("inner", read_misfit, first_adjoint)
+    def read_last(part, row, count):
+        return (*step.read_sweep(vel_a)(part, row, count), [load(ext, part, row, count, 3 + i) for i in range(2)])
+
+    def last_sweep(part, read):
+        k, around, right, seen = read
+        new = step.relax(part, k, around, right)
+        misfit = [[0.5 * (a - b) for a, b in zip(new[i], seen[i])] for i in range(2)]
+        first = [[a * b for a, b in zip(k[4 + i], misfit[i])] for i in range(2)]
+        return step.put(vel_b, new) + step.put(vel_c, first) + [(ext, (1 + i,), misfit[i]) for i in range(2)]
+
+    over_rows("inner", read_last, last_sweep)
 
     def two_sweeps(i, carry):
         over_rows("inner", step.read_sweep(vel_c), step.sweep(vel_a))
@@ -575,13 +560,14 @@
         return carry
 
     lax.fori_loop(0, (ADJ - 2) // 2, two_sweeps, 0)
-    over_rows("tile", step.read_sweep(vel_c), step.sweep(vel_a))
 
     def read_gradient(part, row, count):
-        return [load(ref, part, row, count, i) for ref in (vel_b, vel_a) for i in range(2)] + [load(fr, part, row, count)]
+        others = [load(vel_b, part, row, count, i) for i in range(2)] + [load(fr, part, row, count)]
+        return (*step.read_sweep(vel_c)(part, row, count), others)
 
     def gradient(part, read):
-        u, v, lu, lv, friction = read
+        k, around, right, (u, v, friction) = read
+        lu, lv = step.relax(part, k, around, right)
         return [(visc, (0,), [-2.0 * friction[c] * (u[c] * lu[c] + v[c] * lv[c]) for c in range(len(part))])]
 
     over_rows("tile", read_gradient, gradient)
@@ -600,8 +586,24 @@
     )
     for j in range(sums.shape[0]):
         sums[j] = packed
-    for copy in copies:
-        copy.wait()
+
+
+def unweave_kernel(vel, vel_u, vel_v):
+    lane, half_lane = lanes_of(TILE), lanes_of(HALF)
+    edge = HALO // 2
+    for i, out in enumerate((vel_u, vel_v)):
+        even, odd = (vel[i, tile + TOP : tile + TOP + TILE, :] for tile in MAIN)
+        mixed = vel[i, SIDE + TOP : SIDE + TOP + HALF, :]
+        for c in range(2):
+            source = BAND * c + lane // 2
+            cells = jnp.where(lane % 2 == 0, gather(even, source), gather(odd, source))
+            for band in range(2):
+                rows = slice(HALF * band, HALF * (band + 1))
+                if c == 0:
+                    outer, side = half_lane < edge, turn(mixed, BAND * band + 3 * HALO, 0)
+                else:
+                    outer, side = half_lane >= LANES - edge, turn(mixed, BAND * band + edge, LANES - edge)
+                out[rows, c * LANES : (c + 1) * LANES] = jnp.where(outer, side, cells[rows])
 
 
 def pick_kernel(owners, gathered, own, other):
@@ -707,25 +709,30 @@
         name="setup",
     )(*friction, woven, own_sides, *columns_in)
 
-    vel_u, vel_v, sums = pl.pallas_call(
+    vel, sums = pl.pallas_call(
         model_kernel,
-        out_shape=(shape(TILE, TILE), shape(TILE, TILE), shape(cols * rows // 2, PACK, LANES)),
+        out_shape=(shape(2, ALL_ROWS, LANES), shape(cols * rows // 2, PACK, LANES)),
         in_specs=in_vmem(6),
-        out_specs=[pl.BlockSpec(memory_space=pltpu.HBM)] * 2 + in_vmem(1),
+        out_specs=in_vmem(2),
         scratch_shapes=[
             pltpu.VMEM((5, ALL_ROWS, LANES), f32),
             pltpu.VMEM((3, ALL_ROWS, LANES), f32),
             pltpu.VMEM((2, ALL_ROWS, LANES), f32),
             pltpu.VMEM((2, ALL_ROWS, LANES), f32),
-            pltpu.VMEM((2, ALL_ROWS, LANES), f32),
             pltpu.VMEM((FACTORS, ALL_ROWS, LANES), f32),
-            pltpu.VMEM((2, 2, TILE, LANES), f32),
             pltpu.VMEM((CT, LANES), f32),
-            pltpu.SemaphoreType.DMA((4,)),
         ],
         compiler_params=params,
         name="model",
     )(*friction, *prepared, *rows_in)
+    vel_u, vel_v = pl.pallas_call(
+        unweave_kernel,
+        out_shape=[shape(TILE, TILE)] * 2,
+        in_specs=in_vmem(1),
+        out_specs=in_vmem(2),
+        compiler_params=params,
+        name="unweave",
+    )(vel)
 
     same_core = [[i * rows + j for i in range(cols) for j in range(core, rows, 2)] for core in range(2)]
     sums = lax.all_to_all(sums, ("gx", "gy"), 0, 0, tiled=True, axis_index_groups=same_core)

time: 56 us -> 55.2 us (0.986)
  waiting for transfers between devices: 2.13 us -> 1.01 us
    ppermute x1, waiting for transfers between devices: 1.24 us -> 0.05 us  [per_device(): lax.ppermute(other, 'gy', [(j, j ^ 1) for j in range(rows)])]
    pallas_call x1 -> x2, Pallas kernels: 13.8 us -> 14.2 us  [the longest x1 13 us: per_device(): pl.pallas_call(model_kernel, out_shape=(shape(2, ALL_ROWS, LANES), shape(...]
  transfers between devices with their start and end apart: 6 -> 6, of which waited for: 3 -> 2; matrix products, arithmetic and copies ran while one was open for 0% -> 0% of each run, Pallas kernels for 7% -> 9%
where the time goes in v16:
time: 55.2 us; the launch traced here: 54.8 us
  blocking collectives  21.8 us (39%)
  Pallas kernels  21.2 us (38%)
  starting transfers between devices  8.37 us (15%)
  waiting for transfers between devices  1.01 us (2%)
  local copies, waits for them, and re-layouts  0.96 us (2%)
  between operations  0.79 us (1%)
  other arithmetic  0.65 us (1%)
    all_to_all x1, blocking collectives, per_device(): lax.all_to_all(sums, ('gx', 'gy'), 0, 0, tiled=True, axis_index_groups=sa...  21.8 us
    pallas_call x1, Pallas kernels, per_device(): pl.pallas_call(model_kernel, out_shape=(shape(2, ALL_ROWS, LANES), shape(...  13 us
    all_to_all x1, starting transfers between devices, per_device(): parcels = lax.all_to_all(parcels, 'gy', 0, 0, tiled=True)  5.29 us
    ppermute x4, starting transfers between devices, swap(): lax.ppermute(cells, axis, pairs + [(j, i) for i, j in pairs])  3.01 us
    pallas_call x1, Pallas kernels, per_device(): pl.pallas_call(pack_kernel, out_shape=[shape(HALF, LANES)] * 2 + [shape(r...  2.79 us
    pallas_call x1, Pallas kernels, per_device(): pl.pallas_call(setup_kernel, out_shape=[shape(5, ALL_ROWS, LANES), shape(...  1.82 us
    pallas_call x1, Pallas kernels, per_device(): pl.pallas_call(unweave_kernel, out_shape=[shape(TILE, TILE)] * 2, in_spec...  1.19 us
    pallas_call x1, Pallas kernels, per_device(): pl.pallas_call(weave_kernel, out_shape=[shape(5, 2, TILE, LANES), shape(5...  1.14 us
  transfers between devices with their start and end apart: 6, of which 2 were waited for; matrix products, arithmetic and copies ran while one was open for 0% of the time, Pallas kernels for 9%

profile of v16, /device:TPU:0, one launch (start us, length us, event | category | flops | bytes accessed | tf_op | source)
XLA Modules:
  0.0 54.8 jit_solution(15534057998735241030)
XLA Ops:
  0.6 0.0 copy-start.1
  0.6 0.0 copy-start
  0.7 0.0 copy-start.3
  0.7 0.0 copy-start.4
  0.7 2.8 %pack.1 = (f32[128,128]{1,0:T(8,128)}, f32[128,128]{1,0:T(8,128)}, f32[8,48,128]{2,1,0:T(8,128)}) custom-call(s32[4,8]{1,0:T(4,128)} %bitcast.4, f32[4,4096]{1,0:T(4,128)} %control.1, f32[256,256]{1,0:T(8,128)} %thick.3, f32[2,256,256]{2,1,0:T(8,128)} %drive.3, f32[2,256,256]{2,1,0:T(8,128)} %obs.3), custom_call_target="tpu_custom_call" | custom-call | tf_op jit(solution)/shard_map/pack/pallas_call | solution.py:652
  3.5 5.3 %all-to-all-start = ((f32[8,48,128]{2,1,0:T(8,128)}), f32[8,48,128]{2,1,0:T(8,128)S(1)}, u32[]{:S(2)}, u32[]{:S(2)}) async-start(f32[8,48,128]{2,1,0:T(8,128)} %get-tuple-element.22), calls=%async_computation | async-start | bytes 393216 | tf_op jit(solution)/shard_map/all_to_all | solution.py:669
  8.8 1.6 %collective-permute-start = (f32[128,128]{1,0:T(8,128)}, f32[128,128]{1,0:T(8,128)S(1)}, u32[]{:S(2)}, u32[]{:S(2)}) collective-permute-start(f32[128,128]{1,0:T(8,128)} %get-tuple-element.27), channel_id=1, source_target_pairs={{0,8},{16,24},{8,0},{24,16},{1,9},{17,25},{9,1},{25,17},{2,10},{18... | collective-permute-start | bytes 196616 | tf_op jit(solution)/shard_map/ppermute | solution.py:647
  10.4 0.7 %collective-permute-start.1 = (f32[128,128]{1,0:T(8,128)}, f32[128,128]{1,0:T(8,128)S(1)}, u32[]{:S(2)}, u32[]{:S(2)}) collective-permute-start(f32[128,128]{1,0:T(8,128)} %get-tuple-element.28), channel_id=1, source_target_pairs={{8,16},{16,8},{9,17},{17,9},{10,18},{18,10},{11,19},{19,11},{12,20... | collective-permute-start | bytes 196616 | tf_op jit(solution)/shard_map/ppermute | solution.py:647
  11.0 0.0 copy-done.1
  11.0 0.0 copy-done
  11.1 0.0 copy-start.2
  11.1 0.9 %copy-done.2 = f32[256,256]{1,0:T(8,128)S(1)} copy-done((f32[256,256]{1,0:T(8,128)S(1)}, f32[256,256]{1,0:T(8,128)}, u32[]{:S(2)}) %copy-start.2) | copy-done | bytes 262168
  12.0 1.1 %weave.1 = (f32[5,2,256,128]{3,2,1,0:T(8,128)S(1)}, f32[5,128,128]{2,1,0:T(8,128)S(1)}, f32[2,3,64,128]{3,2,1,0:T(8,128)S(1)}) custom-call(f32[256,256]{1,0:T(8,128)S(1)} %copy-done.2, f32[2,256,256]{2,1,0:T(8,128)S(1)} %copy-done, f32[2,256,256]{2,1,0:T(8,128)S(1)} %copy-done.1), custom_call_target="tpu_custom_call" | custom-call | tf_op jit(solution)/shard_map/weave/pallas_call | solution.py:671
  13.2 0.3 collective-permute-done.first_col
  13.5 0.0 collective-permute-done.1.second_col
  13.5 0.1 rows.1
  13.6 0.1 collective-permute-start.2
  13.7 0.7 %collective-permute-start.3 = (f32[160,128]{1,0:T(8,128)S(1)}, f32[160,128]{1,0:T(8,128)S(1)}, u32[]{:S(2)}, u32[]{:S(2)}) collective-permute-start(f32[160,128]{1,0:T(8,128)S(1)} %get-tuple-element.33), channel_id=1, source_target_pairs={{1,2},{3,4},{5,6},{2,1},{4,3},{6,5},{9,10},{11,12},{13,14},{10,9},... | collective-permute-start | bytes 245768 | tf_op jit(solution)/shard_map/ppermute | solution.py:647
  14.4 0.6 %all-to-all-done.parcels = f32[8,48,128]{2,1,0:T(8,128)S(1)} async-done(((f32[8,48,128]{2,1,0:T(8,128)}), f32[8,48,128]{2,1,0:T(8,128)S(1)}, u32[]{:S(2)}, u32[]{:S(2)}) %all-to-all-start) | async-done | bytes 196640 | tf_op jit(solution)/shard_map/all_to_all | solution.py:669
  15.0 0.0 copy-done.3
  15.0 0.0 copy-done.4
  15.0 0.9 %friction.1 = (f32[784,128]{1,0:T(8,128)S(1)}, f32[784,128]{1,0:T(8,128)S(1)}, s32[16,8,128]{2,1,0:T(8,128)S(1)}) custom-call(s32[4,8]{1,0:T(4,128)S(1)} %bitcast.5, s32[4,8]{1,0:T(4,128)S(1)} %bitcast.6, f32[8,48,128]{2,1,0:T(8,128)S(1)} %all-to-all-done.parcels), custom_call_target="tpu_custom_call" | custom-call | tf_op jit(solution)/shard_map/friction/pallas_call | solution.py:688
  15.9 1.8 %setup.1 = (f32[5,784,128]{2,1,0:T(8,128)S(1)}, f32[2,784,128]{2,1,0:T(8,128)S(1)}) custom-call(f32[784,128]{1,0:T(8,128)S(1)} %get-tuple-element.23.fr, f32[784,128]{1,0:T(8,128)S(1)} %get-tuple-element.24.ice, f32[5,2,256,128]{3,2,1,0:T(8,128)S(1)} %get-tuple-element.25.woven, f32[5,128,128]{2,1,0:T(8,128)S(1)} %get-tuple-element.26.own_sides, ...), custom_call_target="tpu_custom_call" | custom-call | tf_op jit(solution)/shard_map/setup/pallas_call | solution.py:698
  17.7 0.0 collective-permute-done.2.first_row
  17.7 0.0 collective-permute-done.3.second_row
  17.7 13.0 %model.1 = (f32[2,784,128]{2,1,0:T(8,128)S(1)}, f32[16,32,128]{2,1,0:T(8,128)S(1)}) custom-call(f32[784,128]{1,0:T(8,128)S(1)} %get-tuple-element.23.fr, f32[784,128]{1,0:T(8,128)S(1)} %get-tuple-element.24.ice, f32[5,784,128]{2,1,0:T(8,128)S(1)} %get-tuple-element.29.ext_in, f32[2,784,128]{2,1,0:T(8,128)S(1)} %get-tuple-element.30.vel_in, ...), custom_call_target="tpu_custom_call" | custom-call | tf_op jit(solution)/shard_map/model/pallas_call | solution.py:712
  30.7 21.8 %all_to_all.10.gathered = f32[16,32,128]{2,1,0:T(8,128)S(1)} all-to-all(f32[16,32,128]{2,1,0:T(8,128)S(1)} %get-tuple-element.38), channel_id=1, replica_groups={{0,2,4,6,8,10,12,14,16,18,20,22,24,26,28,30},{1,3,5,7,9,11,13,15,17,19,..., dimensions={0} | all-to-all | bytes 524288 | tf_op jit(solution)/shard_map/all_to_all | solution.py:738
  52.5 0.3 pick.1
  52.8 0.1 collective-permute-start.4
  52.9 1.2 %unweave.1 = (f32[256,256]{1,0:T(8,128)}, f32[256,256]{1,0:T(8,128)}) custom-call(f32[2,784,128]{2,1,0:T(8,128)S(1)} %get-tuple-element.34.vel), custom_call_target="tpu_custom_call" | custom-call | tf_op jit(solution)/shard_map/unweave/pallas_call | solution.py:728
  54.1 0.0 collective-permute-done.4
  54.1 0.6 %add.3 = f32[4,4096]{1,0:T(4,128)} add(f32[4,4096]{1,0:T(4,128)S(1)} %get-tuple-element.39, f32[4,4096]{1,0:T(4,128)S(1)} %collective-permute-done.4) | non-fusion elementwise | flops 16384 | bytes 196608 | tf_op jit(solution)/shard_map/add | solution.py:747
Async XLA Ops:
  0.6 10.4 %copy-start.1 = (f32[2,256,256]{2,1,0:T(8,128)S(1)}, f32[2,256,256]{2,1,0:T(8,128)}, u32[]{:S(2)}) copy-start(f32[2,256,256]{2,1,0:T(8,128)} %obs.3) | copy-start | bytes 1572868
  0.6 10.4 %copy-start = (f32[2,256,256]{2,1,0:T(8,128)S(1)}, f32[2,256,256]{2,1,0:T(8,128)}, u32[]{:S(2)}) copy-start(f32[2,256,256]{2,1,0:T(8,128)} %drive.3) | copy-start | bytes 1572868
  0.7 14.3 %copy-start.3 = (s32[8,4,1]{0,2,1:T(1,128)S(1)}, s32[8,4,1]{0,2,1:T(1,128)}, u32[]{:S(2)}) copy-start(s32[8,4,1]{0,2,1:T(1,128)} %param.11) | copy-start | bytes 388
  0.7 14.3 %copy-start.4 = (s32[8,4]{0,1:T(4,128)S(1)}, s32[8,4]{0,1:T(4,128)}, u32[]{:S(2)}) copy-start(s32[8,4]{0,1:T(4,128)} %param.10) | copy-start | bytes 388
  3.5 11.5 %all-to-all-start = ((f32[8,48,128]{2,1,0:T(8,128)}), f32[8,48,128]{2,1,0:T(8,128)S(1)}, u32[]{:S(2)}, u32[]{:S(2)}) async-start(f32[8,48,128]{2,1,0:T(8,128)} %get-tuple-element.22), calls=%async_computation | async-start | bytes 393216 | tf_op jit(solution)/shard_map/all_to_all | solution.py:669
  8.8 4.7 %collective-permute-start = (f32[128,128]{1,0:T(8,128)}, f32[128,128]{1,0:T(8,128)S(1)}, u32[]{:S(2)}, u32[]{:S(2)}) collective-permute-start(f32[128,128]{1,0:T(8,128)} %get-tuple-element.27), channel_id=1, source_target_pairs={{0,8},{16,24},{8,0},{24,16},{1,9},{17,25},{9,1},{25,17},{2,10},{18... | collective-permute-start | bytes 196616 | tf_op jit(solution)/shard_map/ppermute | solution.py:647
  10.4 3.1 %collective-permute-start.1 = (f32[128,128]{1,0:T(8,128)}, f32[128,128]{1,0:T(8,128)S(1)}, u32[]{:S(2)}, u32[]{:S(2)}) collective-permute-start(f32[128,128]{1,0:T(8,128)} %get-tuple-element.28), channel_id=1, source_target_pairs={{8,16},{16,8},{9,17},{17,9},{10,18},{18,10},{11,19},{19,11},{12,20... | collective-permute-start | bytes 196616 | tf_op jit(solution)/shard_map/ppermute | solution.py:647
  11.1 1.0 %copy-start.2 = (f32[256,256]{1,0:T(8,128)S(1)}, f32[256,256]{1,0:T(8,128)}, u32[]{:S(2)}) copy-start(f32[256,256]{1,0:T(8,128)} %thick.3) | copy-start | bytes 786436
  13.6 4.1 %collective-permute-start.2 = (f32[160,128]{1,0:T(8,128)S(1)}, f32[160,128]{1,0:T(8,128)S(1)}, u32[]{:S(2)}, u32[]{:S(2)}) collective-permute-start(f32[160,128]{1,0:T(8,128)S(1)} %get-tuple-element.32), channel_id=1, source_target_pairs={{0,1},{2,3},{4,5},{6,7},{1,0},{3,2},{5,4},{7,6},{8,9},{10,11},{12,... | collective-permute-start | bytes 245768 | tf_op jit(solution)/shard_map/ppermute | solution.py:647
  13.7 4.0 %collective-permute-start.3 = (f32[160,128]{1,0:T(8,128)S(1)}, f32[160,128]{1,0:T(8,128)S(1)}, u32[]{:S(2)}, u32[]{:S(2)}) collective-permute-start(f32[160,128]{1,0:T(8,128)S(1)} %get-tuple-element.33), channel_id=1, source_target_pairs={{1,2},{3,4},{5,6},{2,1},{4,3},{6,5},{9,10},{11,12},{13,14},{10,9},... | collective-permute-start | bytes 245768 | tf_op jit(solution)/shard_map/ppermute | solution.py:647
  52.8 1.3 %collective-permute-start.4 = (f32[4,4096]{1,0:T(4,128)S(1)}, f32[4,4096]{1,0:T(4,128)S(1)}, u32[]{:S(2)}, u32[]{:S(2)}) collective-permute-start(f32[4,4096]{1,0:T(4,128)S(1)} %get-tuple-element.40), channel_id=1, source_target_pairs={{0,1},{1,0},{2,3},{3,2},{4,5},{5,4},{6,7},{7,6},{8,9},{9,8},{10,11... | collective-permute-start | bytes 196616 | tf_op jit(solution)/shard_map/ppermute | solution.py:747

commit v17 on v16

--- a/solution.py
+++ b/solution.py
@@ -27,9 +27,9 @@
 MAIN = (0, ROWS)
 SIDES = (SIDE,)
 SPANS = {
-    "frame": (MARGIN, 4, 72, MARGIN, 40, 0, 0),
-    "inner": (MARGIN + 8, 3, 72, MARGIN + 8, 40, 56, 24),
-    "tile": (TOP, 4, 64, TOP, 32, 0, 0),
+    "frame": (MARGIN, 2, 144, MARGIN, 80, 0, 0),
+    "inner": (MARGIN + 8, 2, 136, MARGIN + 8, 72, 0, 0),
+    "tile": (TOP, 2, 128, TOP, 64, 0, 0),
 }
 FACTORS = 14
 AHEAD = 5
@@ -588,22 +588,27 @@
         sums[j] = packed
 
 
-def unweave_kernel(vel, vel_u, vel_v):
-    lane, half_lane = lanes_of(TILE), lanes_of(HALF)
+def unweave_kernel(vel, vel_u, vel_v, plain, sems):
+    lane = lanes_of(HALF)
     edge = HALO // 2
+    copies = []
     for i, out in enumerate((vel_u, vel_v)):
-        even, odd = (vel[i, tile + TOP : tile + TOP + TILE, :] for tile in MAIN)
         mixed = vel[i, SIDE + TOP : SIDE + TOP + HALF, :]
-        for c in range(2):
-            source = BAND * c + lane // 2
-            cells = jnp.where(lane % 2 == 0, gather(even, source), gather(odd, source))
-            for band in range(2):
-                rows = slice(HALF * band, HALF * (band + 1))
+        for band in range(2):
+            rows = slice(HALF * band, HALF * (band + 1))
+            even, odd = (vel[i, tile + TOP + HALF * band : tile + TOP + HALF * (band + 1), :] for tile in MAIN)
+            for c in range(2):
+                source = BAND * c + lane // 2
+                cells = jnp.where(lane % 2 == 0, gather(even, source), gather(odd, source))
                 if c == 0:
-                    outer, side = half_lane < edge, turn(mixed, BAND * band + 3 * HALO, 0)
+                    outer, side = lane < edge, turn(mixed, BAND * band + 3 * HALO, 0)
                 else:
-                    outer, side = half_lane >= LANES - edge, turn(mixed, BAND * band + edge, LANES - edge)
-                out[rows, c * LANES : (c + 1) * LANES] = jnp.where(outer, side, cells[rows])
+                    outer, side = lane >= LANES - edge, turn(mixed, BAND * band + edge, LANES - edge)
+                plain[i, rows, c * LANES : (c + 1) * LANES] = jnp.where(outer, side, cells)
+            copies.append(pltpu.make_async_copy(plain.at[i, rows], out.at[rows], sems.at[2 * i + band]))
+            copies[-1].start()
+    for copy in copies:
+        copy.wait()
 
 
 def pick_kernel(owners, gathered, own, other):
@@ -729,7 +734,8 @@
         unweave_kernel,
         out_shape=[shape(TILE, TILE)] * 2,
         in_specs=in_vmem(1),
-        out_specs=in_vmem(2),
+        out_specs=[pl.BlockSpec(memory_space=pltpu.HBM)] * 2,
+        scratch_shapes=[pltpu.VMEM((2, TILE, TILE), f32), pltpu.SemaphoreType.DMA((4,))],
         compiler_params=params,
         name="unweave",
     )(vel)

time: 55.2 us -> 54.5 us (0.987)
  Pallas kernels: 21.2 us -> 20.3 us
    pallas_call x1, Pallas kernels: 13 us -> 12.3 us  [per_device(): pl.pallas_call(model_kernel, out_shape=(shape(2, ALL_ROWS, LANES), shape(...]
where the time goes in v17:
time: 54.5 us; the launch traced here: 54.2 us
  blocking collectives  22 us (40%)
  Pallas kernels  20.3 us (37%)
  starting transfers between devices  8.45 us (16%)
  waiting for transfers between devices  1.08 us (2%)
  local copies, waits for them, and re-layouts  0.96 us (2%)
  between operations  0.8 us (1%)
  other arithmetic  0.65 us (1%)
    all_to_all x1, blocking collectives, per_device(): lax.all_to_all(sums, ('gx', 'gy'), 0, 0, tiled=True, axis_index_groups=sa...  22 us
    pallas_call x1, Pallas kernels, per_device(): pl.pallas_call(model_kernel, out_shape=(shape(2, ALL_ROWS, LANES), shape(...  12.3 us
    all_to_all x1, starting transfers between devices, per_device(): parcels = lax.all_to_all(parcels, 'gy', 0, 0, tiled=True)  5.45 us
    ppermute x4, starting transfers between devices, swap(): lax.ppermute(cells, axis, pairs + [(j, i) for i, j in pairs])  2.93 us
    pallas_call x1, Pallas kernels, per_device(): pl.pallas_call(pack_kernel, out_shape=[shape(HALF, LANES)] * 2 + [shape(r...  2.77 us
    pallas_call x1, Pallas kernels, per_device(): pl.pallas_call(setup_kernel, out_shape=[shape(5, ALL_ROWS, LANES), shape(...  1.51 us
    pallas_call x1, Pallas kernels, per_device(): pl.pallas_call(unweave_kernel, out_shape=[shape(TILE, TILE)] * 2, in_spec...  1.2 us
    pallas_call x1, Pallas kernels, per_device(): pl.pallas_call(weave_kernel, out_shape=[shape(5, 2, TILE, LANES), shape(5...  1.14 us
  transfers between devices with their start and end apart: 6, of which 2 were waited for; matrix products, arithmetic and copies ran while one was open for 0% of the time, Pallas kernels for 9%

profile of v17, /device:TPU:0, one launch (start us, length us, event | category | flops | bytes accessed | tf_op | source)
XLA Modules:
  0.0 54.2 jit_solution(8703787644087359331)
XLA Ops:
  0.6 0.0 copy-start.1
  0.6 0.0 copy-start
  0.7 0.0 copy-start.3
  0.7 0.0 copy-start.4
  0.7 2.8 %pack.1 = (f32[128,128]{1,0:T(8,128)}, f32[128,128]{1,0:T(8,128)}, f32[8,48,128]{2,1,0:T(8,128)}) custom-call(s32[4,8]{1,0:T(4,128)} %bitcast.4, f32[4,4096]{1,0:T(4,128)} %control.1, f32[256,256]{1,0:T(8,128)} %thick.3, f32[2,256,256]{2,1,0:T(8,128)} %drive.3, f32[2,256,256]{2,1,0:T(8,128)} %obs.3), custom_call_target="tpu_custom_call" | custom-call | tf_op jit(solution)/shard_map/pack/pallas_call | solution.py:657
  3.4 5.4 %all-to-all-start = ((f32[8,48,128]{2,1,0:T(8,128)}), f32[8,48,128]{2,1,0:T(8,128)S(1)}, u32[]{:S(2)}, u32[]{:S(2)}) async-start(f32[8,48,128]{2,1,0:T(8,128)} %get-tuple-element.22), calls=%async_computation | async-start | bytes 393216 | tf_op jit(solution)/shard_map/all_to_all | solution.py:674
  8.9 1.5 %collective-permute-start = (f32[128,128]{1,0:T(8,128)}, f32[128,128]{1,0:T(8,128)S(1)}, u32[]{:S(2)}, u32[]{:S(2)}) collective-permute-start(f32[128,128]{1,0:T(8,128)} %get-tuple-element.27), channel_id=1, source_target_pairs={{0,8},{16,24},{8,0},{24,16},{1,9},{17,25},{9,1},{25,17},{2,10},{18... | collective-permute-start | bytes 196616 | tf_op jit(solution)/shard_map/ppermute | solution.py:652
  10.4 0.7 %collective-permute-start.1 = (f32[128,128]{1,0:T(8,128)}, f32[128,128]{1,0:T(8,128)S(1)}, u32[]{:S(2)}, u32[]{:S(2)}) collective-permute-start(f32[128,128]{1,0:T(8,128)} %get-tuple-element.28), channel_id=1, source_target_pairs={{8,16},{16,8},{9,17},{17,9},{10,18},{18,10},{11,19},{19,11},{12,20... | collective-permute-start | bytes 196616 | tf_op jit(solution)/shard_map/ppermute | solution.py:652
  11.1 0.0 copy-done.1
  11.1 0.0 copy-done
  11.1 0.0 copy-start.2
  11.1 0.9 %copy-done.2 = f32[256,256]{1,0:T(8,128)S(1)} copy-done((f32[256,256]{1,0:T(8,128)S(1)}, f32[256,256]{1,0:T(8,128)}, u32[]{:S(2)}) %copy-start.2) | copy-done | bytes 262168
  12.1 1.1 %weave.1 = (f32[5,2,256,128]{3,2,1,0:T(8,128)S(1)}, f32[5,128,128]{2,1,0:T(8,128)S(1)}, f32[2,3,64,128]{3,2,1,0:T(8,128)S(1)}) custom-call(f32[256,256]{1,0:T(8,128)S(1)} %copy-done.2, f32[2,256,256]{2,1,0:T(8,128)S(1)} %copy-done, f32[2,256,256]{2,1,0:T(8,128)S(1)} %copy-done.1), custom_call_target="tpu_custom_call" | custom-call | tf_op jit(solution)/shard_map/weave/pallas_call | solution.py:676
  13.2 0.4 collective-permute-done.first_col
  13.6 0.0 collective-permute-done.1.second_col
  13.6 0.1 rows.1
  13.7 0.1 collective-permute-start.2
  13.8 0.7 %collective-permute-start.3 = (f32[160,128]{1,0:T(8,128)S(1)}, f32[160,128]{1,0:T(8,128)S(1)}, u32[]{:S(2)}, u32[]{:S(2)}) collective-permute-start(f32[160,128]{1,0:T(8,128)S(1)} %get-tuple-element.33), channel_id=1, source_target_pairs={{1,2},{3,4},{5,6},{2,1},{4,3},{6,5},{9,10},{11,12},{13,14},{10,9},... | collective-permute-start | bytes 245768 | tf_op jit(solution)/shard_map/ppermute | solution.py:652
  14.5 0.6 %all-to-all-done.parcels = f32[8,48,128]{2,1,0:T(8,128)S(1)} async-done(((f32[8,48,128]{2,1,0:T(8,128)}), f32[8,48,128]{2,1,0:T(8,128)S(1)}, u32[]{:S(2)}, u32[]{:S(2)}) %all-to-all-start) | async-done | bytes 196640 | tf_op jit(solution)/shard_map/all_to_all | solution.py:674
  15.1 0.0 copy-done.3
  15.1 0.0 copy-done.4
  15.1 0.9 %friction.1 = (f32[784,128]{1,0:T(8,128)S(1)}, f32[784,128]{1,0:T(8,128)S(1)}, s32[16,8,128]{2,1,0:T(8,128)S(1)}) custom-call(s32[4,8]{1,0:T(4,128)S(1)} %bitcast.5, s32[4,8]{1,0:T(4,128)S(1)} %bitcast.6, f32[8,48,128]{2,1,0:T(8,128)S(1)} %all-to-all-done.parcels), custom_call_target="tpu_custom_call" | custom-call | tf_op jit(solution)/shard_map/friction/pallas_call | solution.py:693
  16.0 1.5 %setup.1 = (f32[5,784,128]{2,1,0:T(8,128)S(1)}, f32[2,784,128]{2,1,0:T(8,128)S(1)}) custom-call(f32[784,128]{1,0:T(8,128)S(1)} %get-tuple-element.23.fr, f32[784,128]{1,0:T(8,128)S(1)} %get-tuple-element.24.ice, f32[5,2,256,128]{3,2,1,0:T(8,128)S(1)} %get-tuple-element.25.woven, f32[5,128,128]{2,1,0:T(8,128)S(1)} %get-tuple-element.26.own_sides, ...), custom_call_target="tpu_custom_call" | custom-call | tf_op jit(solution)/shard_map/setup/pallas_call | solution.py:703
  17.5 0.0 collective-permute-done.2.first_row
  17.5 0.0 collective-permute-done.3.second_row
  17.5 12.3 %model.1 = (f32[2,784,128]{2,1,0:T(8,128)S(1)}, f32[16,32,128]{2,1,0:T(8,128)S(1)}) custom-call(f32[784,128]{1,0:T(8,128)S(1)} %get-tuple-element.23.fr, f32[784,128]{1,0:T(8,128)S(1)} %get-tuple-element.24.ice, f32[5,784,128]{2,1,0:T(8,128)S(1)} %get-tuple-element.29.ext_in, f32[2,784,128]{2,1,0:T(8,128)S(1)} %get-tuple-element.30.vel_in, ...), custom_call_target="tpu_custom_call" | custom-call | tf_op jit(solution)/shard_map/model/pallas_call | solution.py:717
  29.9 22.0 %all_to_all.10.gathered = f32[16,32,128]{2,1,0:T(8,128)S(1)} all-to-all(f32[16,32,128]{2,1,0:T(8,128)S(1)} %get-tuple-element.38), channel_id=1, replica_groups={{0,2,4,6,8,10,12,14,16,18,20,22,24,26,28,30},{1,3,5,7,9,11,13,15,17,19,..., dimensions={0} | all-to-all | bytes 524288 | tf_op jit(solution)/shard_map/all_to_all | solution.py:744
  51.9 0.3 pick.1
  52.2 0.1 collective-permute-start.4
  52.3 1.2 %unweave.1 = (f32[256,256]{1,0:T(8,128)}, f32[256,256]{1,0:T(8,128)}) custom-call(f32[2,784,128]{2,1,0:T(8,128)S(1)} %get-tuple-element.34.vel), custom_call_target="tpu_custom_call" | custom-call | tf_op jit(solution)/shard_map/unweave/pallas_call | solution.py:733
  53.5 0.0 collective-permute-done.4
  53.5 0.6 %add.3 = f32[4,4096]{1,0:T(4,128)} add(f32[4,4096]{1,0:T(4,128)S(1)} %get-tuple-element.39, f32[4,4096]{1,0:T(4,128)S(1)} %collective-permute-done.4) | non-fusion elementwise | flops 16384 | bytes 196608 | tf_op jit(solution)/shard_map/add | solution.py:753
Async XLA Ops:
  0.6 10.5 %copy-start.1 = (f32[2,256,256]{2,1,0:T(8,128)S(1)}, f32[2,256,256]{2,1,0:T(8,128)}, u32[]{:S(2)}) copy-start(f32[2,256,256]{2,1,0:T(8,128)} %obs.3) | copy-start | bytes 1572868
  0.6 10.5 %copy-start = (f32[2,256,256]{2,1,0:T(8,128)S(1)}, f32[2,256,256]{2,1,0:T(8,128)}, u32[]{:S(2)}) copy-start(f32[2,256,256]{2,1,0:T(8,128)} %drive.3) | copy-start | bytes 1572868
  0.7 14.5 %copy-start.3 = (s32[8,4,1]{0,2,1:T(1,128)S(1)}, s32[8,4,1]{0,2,1:T(1,128)}, u32[]{:S(2)}) copy-start(s32[8,4,1]{0,2,1:T(1,128)} %param.11) | copy-start | bytes 388
  0.7 14.5 %copy-start.4 = (s32[8,4]{0,1:T(4,128)S(1)}, s32[8,4]{0,1:T(4,128)}, u32[]{:S(2)}) copy-start(s32[8,4]{0,1:T(4,128)} %param.10) | copy-start | bytes 388
  3.4 11.7 %all-to-all-start = ((f32[8,48,128]{2,1,0:T(8,128)}), f32[8,48,128]{2,1,0:T(8,128)S(1)}, u32[]{:S(2)}, u32[]{:S(2)}) async-start(f32[8,48,128]{2,1,0:T(8,128)} %get-tuple-element.22), calls=%async_computation | async-start | bytes 393216 | tf_op jit(solution)/shard_map/all_to_all | solution.py:674
  8.9 4.7 %collective-permute-start = (f32[128,128]{1,0:T(8,128)}, f32[128,128]{1,0:T(8,128)S(1)}, u32[]{:S(2)}, u32[]{:S(2)}) collective-permute-start(f32[128,128]{1,0:T(8,128)} %get-tuple-element.27), channel_id=1, source_target_pairs={{0,8},{16,24},{8,0},{24,16},{1,9},{17,25},{9,1},{25,17},{2,10},{18... | collective-permute-start | bytes 196616 | tf_op jit(solution)/shard_map/ppermute | solution.py:652
  10.4 3.2 %collective-permute-start.1 = (f32[128,128]{1,0:T(8,128)}, f32[128,128]{1,0:T(8,128)S(1)}, u32[]{:S(2)}, u32[]{:S(2)}) collective-permute-start(f32[128,128]{1,0:T(8,128)} %get-tuple-element.28), channel_id=1, source_target_pairs={{8,16},{16,8},{9,17},{17,9},{10,18},{18,10},{11,19},{19,11},{12,20... | collective-permute-start | bytes 196616 | tf_op jit(solution)/shard_map/ppermute | solution.py:652
  11.1 1.0 %copy-start.2 = (f32[256,256]{1,0:T(8,128)S(1)}, f32[256,256]{1,0:T(8,128)}, u32[]{:S(2)}) copy-start(f32[256,256]{1,0:T(8,128)} %thick.3) | copy-start | bytes 786436
  13.7 3.8 %collective-permute-start.2 = (f32[160,128]{1,0:T(8,128)S(1)}, f32[160,128]{1,0:T(8,128)S(1)}, u32[]{:S(2)}, u32[]{:S(2)}) collective-permute-start(f32[160,128]{1,0:T(8,128)S(1)} %get-tuple-element.32), channel_id=1, source_target_pairs={{0,1},{2,3},{4,5},{6,7},{1,0},{3,2},{5,4},{7,6},{8,9},{10,11},{12,... | collective-permute-start | bytes 245768 | tf_op jit(solution)/shard_map/ppermute | solution.py:652
  13.8 3.7 %collective-permute-start.3 = (f32[160,128]{1,0:T(8,128)S(1)}, f32[160,128]{1,0:T(8,128)S(1)}, u32[]{:S(2)}, u32[]{:S(2)}) collective-permute-start(f32[160,128]{1,0:T(8,128)S(1)} %get-tuple-element.33), channel_id=1, source_target_pairs={{1,2},{3,4},{5,6},{2,1},{4,3},{6,5},{9,10},{11,12},{13,14},{10,9},... | collective-permute-start | bytes 245768 | tf_op jit(solution)/shard_map/ppermute | solution.py:652
  52.2 1.3 %collective-permute-start.4 = (f32[4,4096]{1,0:T(4,128)S(1)}, f32[4,4096]{1,0:T(4,128)S(1)}, u32[]{:S(2)}, u32[]{:S(2)}) collective-permute-start(f32[4,4096]{1,0:T(4,128)S(1)} %get-tuple-element.40), channel_id=1, source_target_pairs={{0,1},{1,0},{2,3},{3,2},{4,5},{5,4},{6,7},{7,6},{8,9},{9,8},{10,11... | collective-permute-start | bytes 196616 | tf_op jit(solution)/shard_map/ppermute | solution.py:753

commit v18 on v17

--- a/solution.py
+++ b/solution.py
@@ -27,12 +27,12 @@
 MAIN = (0, ROWS)
 SIDES = (SIDE,)
 SPANS = {
-    "frame": (MARGIN, 2, 144, MARGIN, 80, 0, 0),
-    "inner": (MARGIN + 8, 2, 136, MARGIN + 8, 72, 0, 0),
-    "tile": (TOP, 2, 128, TOP, 64, 0, 0),
+    "frame": (MARGIN, 288, 160),
+    "inner": (MARGIN + 8, 272, 144),
+    "tile": (TOP, 256, 128),
 }
 FACTORS = 14
-AHEAD = 5
+AHEAD = 8
 PACK = COARSE // LANES
 VMEM_LIMIT = 24 * 1024 * 1024
 PACK_VMEM_LIMIT = 62 * 1024 * 1024
@@ -229,30 +229,16 @@
                 ref[(*lead, pl.ds(row + tile, count), slice(None))] = value
 
 
-def block_groups(row, main, side_row, side):
-    step = 32 if main % 32 == 0 else 24
-    first = side // 16 * 8 if side > 24 else side
-    groups = [(MAIN, row + g, min(step, main - g)) for g in range(0, main, step)]
-    groups[1:1] = [(SIDES, side_row, first)]
-    if first < side:
-        groups[3:3] = [(SIDES, side_row + first, side - first)]
-    return groups
-
-
 def over_rows(span, read, work):
-    start, blocks, main, side_start, side, main_rest, side_rest = SPANS[span]
-
-    def block(i, carry):
-        row, side_row = pl.multiple_of(start + i * main, 8), pl.multiple_of(side_start + i * side, 8)
-        run_groups(block_groups(row, main, side_row, side), read, work)
-        return carry
-
-    lax.fori_loop(0, blocks, block, 0)
-    if main_rest:
-        none = 8 * jnp.minimum(lax.axis_index("gx"), 0)
-        row = pl.multiple_of(none + start + blocks * main, 8)
-        side_row = pl.multiple_of(none + side_start + blocks * side, 8)
-        run_groups(block_groups(row, main_rest, side_row, side_rest), read, work)
+    start, main, side = SPANS[span]
+    row = pl.multiple_of(start + 8 * jnp.minimum(lax.axis_index("gx"), 0), 8)
+    step = 32 if main % 32 == 0 else 16
+    groups = [(MAIN, row + g, step) for g in range(0, main, step)]
+    side_step = 32 if side % 32 == 0 else 48
+    pieces = [(SIDES, row + g, side_step) for g in range(0, side, side_step)]
+    for k, piece in enumerate(pieces):
+        groups.insert((2 * k + 1) * len(groups) // (2 * len(pieces)), piece)
+    run_groups(groups, read, work)
 
 
 def over_ends(count, read, work):
@@ -588,7 +574,7 @@
         sums[j] = packed
 
 
-def unweave_kernel(vel, vel_u, vel_v, plain, sems):
+def unweave_kernel(vel, vel_u, vel_v, token, plain, sems):
     lane = lanes_of(HALF)
     edge = HALO // 2
     copies = []
@@ -607,11 +593,12 @@
                 plain[i, rows, c * LANES : (c + 1) * LANES] = jnp.where(outer, side, cells)
             copies.append(pltpu.make_async_copy(plain.at[i, rows], out.at[rows], sems.at[2 * i + band]))
             copies[-1].start()
+    token[...] = jnp.zeros_like(token)
     for copy in copies:
         copy.wait()
 
 
-def pick_kernel(owners, gathered, own, other):
+def pick_kernel(owners, gathered, token, own, other):
     owned = own.shape[0]
     first = lax.axis_index("gy") % 2 == 0
     total = []
@@ -730,11 +717,11 @@
         compiler_params=params,
         name="model",
     )(*friction, *prepared, *rows_in)
-    vel_u, vel_v = pl.pallas_call(
+    vel_u, vel_v, token = pl.pallas_call(
         unweave_kernel,
-        out_shape=[shape(TILE, TILE)] * 2,
+        out_shape=[shape(TILE, TILE)] * 2 + [shape(8, LANES)],
         in_specs=in_vmem(1),
-        out_specs=[pl.BlockSpec(memory_space=pltpu.HBM)] * 2,
+        out_specs=[pl.BlockSpec(memory_space=pltpu.HBM)] * 2 + in_vmem(1),
         scratch_shapes=[pltpu.VMEM((2, TILE, TILE), f32), pltpu.SemaphoreType.DMA((4,))],
         compiler_params=params,
         name="unweave",
@@ -745,11 +732,11 @@
     own, other = pl.pallas_call(
         pick_kernel,
         out_shape=[shape(*control.shape)] * 2,
-        in_specs=in_vmem(2),
+        in_specs=in_vmem(3),
         out_specs=in_vmem(2),
         compiler_params=params,
         name="pick",
-    )(owners, sums)
+    )(owners, sums, token)
     gradient = own + lax.ppermute(other, "gy", [(j, j ^ 1) for j in range(rows)])
     return vel_u, vel_v, gradient
 

time: 54.5 us -> 56.2 us (1.031)
  blocking collectives: 22 us -> 0 us
  starting transfers between devices: 8.45 us -> 20.2 us
  waiting for transfers between devices: 1.08 us -> 11.3 us
  Pallas kernels: 20.3 us -> 21.8 us
    all_to_all x1 -> x0, blocking collectives: 22 us -> none  [per_device(): lax.all_to_all(sums, ('gx', 'gy'), 0, 0, tiled=True, axis_index_groups=sa...]
    all_to_all x0 -> x1, starting transfers between devices: none -> 11.7 us  [per_device(): lax.all_to_all(sums, ('gx', 'gy'), 0, 0, tiled=True, axis_index_groups=sa...]
    all_to_all x0 -> x1, waiting for transfers between devices: none -> 9.27 us  [per_device(): lax.all_to_all(sums, ('gx', 'gy'), 0, 0, tiled=True, axis_index_groups=sa...]
    pallas_call x1, Pallas kernels: 12.3 us -> 13.9 us  [per_device(): pl.pallas_call(model_kernel, out_shape=(shape(2, ALL_ROWS, LANES), shape(...]
    ppermute x1, waiting for transfers between devices: 0.04 us -> 1.24 us  [per_device(): lax.ppermute(other, 'gy', [(j, j ^ 1) for j in range(rows)])]
  transfers between devices with their start and end apart: 6 -> 7, of which waited for: 2 -> 4; matrix products, arithmetic and copies ran while one was open for 0% -> 0% of each run, Pallas kernels for 9% -> 9%
where the time goes in v18:
time: 56.2 us; the launch traced here: 55.8 us
  Pallas kernels  21.8 us (39%)
  starting transfers between devices  20.2 us (36%)
  waiting for transfers between devices  11.3 us (20%)
  local copies, waits for them, and re-layouts  0.96 us (2%)
  between operations  0.79 us (1%)
  other arithmetic  0.65 us (1%)
    pallas_call x1, Pallas kernels, per_device(): pl.pallas_call(model_kernel, out_shape=(shape(2, ALL_ROWS, LANES), shape(...  13.9 us
    all_to_all x1, starting transfers between devices, per_device(): lax.all_to_all(sums, ('gx', 'gy'), 0, 0, tiled=True, axis_index_groups=sa...  11.7 us
    all_to_all x1, waiting for transfers between devices, per_device(): lax.all_to_all(sums, ('gx', 'gy'), 0, 0, tiled=True, axis_index_groups=sa...  9.27 us
    all_to_all x1, starting transfers between devices, per_device(): parcels = lax.all_to_all(parcels, 'gy', 0, 0, tiled=True)  5.26 us
    ppermute x4, starting transfers between devices, swap(): lax.ppermute(cells, axis, pairs + [(j, i) for i, j in pairs])  3.17 us
    pallas_call x1, Pallas kernels, per_device(): pl.pallas_call(pack_kernel, out_shape=[shape(HALF, LANES)] * 2 + [shape(r...  2.79 us
    pallas_call x1, Pallas kernels, per_device(): pl.pallas_call(setup_kernel, out_shape=[shape(5, ALL_ROWS, LANES), shape(...  1.52 us
    ppermute x1, waiting for transfers between devices, per_device(): lax.ppermute(other, 'gy', [(j, j ^ 1) for j in range(rows)])  1.24 us
  transfers between devices with their start and end apart: 7, of which 4 were waited for; matrix products, arithmetic and copies ran while one was open for 0% of the time, Pallas kernels for 9%

profile of v18, /device:TPU:0, one launch (start us, length us, event | category | flops | bytes accessed | tf_op | source)
XLA Modules:
  0.0 55.8 jit_solution(11525326775341081502)
XLA Ops:
  0.6 0.0 copy-start.1
  0.6 0.0 copy-start
  0.7 0.0 copy-start.3
  0.7 0.0 copy-start.4
  0.7 2.8 %pack.1 = (f32[128,128]{1,0:T(8,128)}, f32[128,128]{1,0:T(8,128)}, f32[8,48,128]{2,1,0:T(8,128)}) custom-call(s32[4,8]{1,0:T(4,128)} %bitcast.4, f32[4,4096]{1,0:T(4,128)} %control.1, f32[256,256]{1,0:T(8,128)} %thick.3, f32[2,256,256]{2,1,0:T(8,128)} %drive.3, f32[2,256,256]{2,1,0:T(8,128)} %obs.3), custom_call_target="tpu_custom_call" | custom-call | tf_op jit(solution)/shard_map/pack/pallas_call | solution.py:644
  3.5 5.3 %all-to-all-start = ((f32[8,48,128]{2,1,0:T(8,128)}), f32[8,48,128]{2,1,0:T(8,128)S(1)}, u32[]{:S(2)}, u32[]{:S(2)}) async-start(f32[8,48,128]{2,1,0:T(8,128)} %get-tuple-element.23), calls=%async_computation | async-start | bytes 393216 | tf_op jit(solution)/shard_map/all_to_all | solution.py:661
  8.7 1.7 %collective-permute-start = (f32[128,128]{1,0:T(8,128)}, f32[128,128]{1,0:T(8,128)S(1)}, u32[]{:S(2)}, u32[]{:S(2)}) collective-permute-start(f32[128,128]{1,0:T(8,128)} %get-tuple-element.28), channel_id=1, source_target_pairs={{0,8},{16,24},{8,0},{24,16},{1,9},{17,25},{9,1},{25,17},{2,10},{18... | collective-permute-start | bytes 196616 | tf_op jit(solution)/shard_map/ppermute | solution.py:639
  10.5 0.7 %collective-permute-start.1 = (f32[128,128]{1,0:T(8,128)}, f32[128,128]{1,0:T(8,128)S(1)}, u32[]{:S(2)}, u32[]{:S(2)}) collective-permute-start(f32[128,128]{1,0:T(8,128)} %get-tuple-element.29), channel_id=1, source_target_pairs={{8,16},{16,8},{9,17},{17,9},{10,18},{18,10},{11,19},{19,11},{12,20... | collective-permute-start | bytes 196616 | tf_op jit(solution)/shard_map/ppermute | solution.py:639
  11.1 0.0 copy-done.1
  11.1 0.0 copy-done
  11.2 0.0 copy-start.2
  11.2 0.9 %copy-done.2 = f32[256,256]{1,0:T(8,128)S(1)} copy-done((f32[256,256]{1,0:T(8,128)S(1)}, f32[256,256]{1,0:T(8,128)}, u32[]{:S(2)}) %copy-start.2) | copy-done | bytes 262168
  12.1 1.1 %weave.1 = (f32[5,2,256,128]{3,2,1,0:T(8,128)S(1)}, f32[5,128,128]{2,1,0:T(8,128)S(1)}, f32[2,3,64,128]{3,2,1,0:T(8,128)S(1)}) custom-call(f32[256,256]{1,0:T(8,128)S(1)} %copy-done.2, f32[2,256,256]{2,1,0:T(8,128)S(1)} %copy-done, f32[2,256,256]{2,1,0:T(8,128)S(1)} %copy-done.1), custom_call_target="tpu_custom_call" | custom-call | tf_op jit(solution)/shard_map/weave/pallas_call | solution.py:663
  13.3 0.2 collective-permute-done.first_col
  13.4 0.0 collective-permute-done.1.second_col
  13.5 0.1 rows.1
  13.6 0.1 collective-permute-start.2
  13.7 0.7 %collective-permute-start.3 = (f32[160,128]{1,0:T(8,128)S(1)}, f32[160,128]{1,0:T(8,128)S(1)}, u32[]{:S(2)}, u32[]{:S(2)}) collective-permute-start(f32[160,128]{1,0:T(8,128)S(1)} %get-tuple-element.34), channel_id=1, source_target_pairs={{1,2},{3,4},{5,6},{2,1},{4,3},{6,5},{9,10},{11,12},{13,14},{10,9},... | collective-permute-start | bytes 245768 | tf_op jit(solution)/shard_map/ppermute | solution.py:639
  14.4 0.6 %all-to-all-done.parcels = f32[8,48,128]{2,1,0:T(8,128)S(1)} async-done(((f32[8,48,128]{2,1,0:T(8,128)}), f32[8,48,128]{2,1,0:T(8,128)S(1)}, u32[]{:S(2)}, u32[]{:S(2)}) %all-to-all-start) | async-done | bytes 196640 | tf_op jit(solution)/shard_map/all_to_all | solution.py:661
  15.0 0.0 copy-done.3
  15.0 0.0 copy-done.4
  15.0 0.9 %friction.1 = (f32[784,128]{1,0:T(8,128)S(1)}, f32[784,128]{1,0:T(8,128)S(1)}, s32[16,8,128]{2,1,0:T(8,128)S(1)}) custom-call(s32[4,8]{1,0:T(4,128)S(1)} %bitcast.5, s32[4,8]{1,0:T(4,128)S(1)} %bitcast.6, f32[8,48,128]{2,1,0:T(8,128)S(1)} %all-to-all-done.parcels), custom_call_target="tpu_custom_call" | custom-call | tf_op jit(solution)/shard_map/friction/pallas_call | solution.py:680
  15.8 1.5 %setup.1 = (f32[5,784,128]{2,1,0:T(8,128)S(1)}, f32[2,784,128]{2,1,0:T(8,128)S(1)}) custom-call(f32[784,128]{1,0:T(8,128)S(1)} %get-tuple-element.24.fr, f32[784,128]{1,0:T(8,128)S(1)} %get-tuple-element.25.ice, f32[5,2,256,128]{3,2,1,0:T(8,128)S(1)} %get-tuple-element.26.woven, f32[5,128,128]{2,1,0:T(8,128)S(1)} %get-tuple-element.27.own_sides, ...), custom_call_target="tpu_custom_call" | custom-call | tf_op jit(solution)/shard_map/setup/pallas_call | solution.py:690
  17.4 0.0 collective-permute-done.2.first_row
  17.4 0.0 collective-permute-done.3.second_row
  17.4 13.9 %model.1 = (f32[2,784,128]{2,1,0:T(8,128)S(1)}, f32[16,32,128]{2,1,0:T(8,128)}) custom-call(f32[784,128]{1,0:T(8,128)S(1)} %get-tuple-element.24.fr, f32[784,128]{1,0:T(8,128)S(1)} %get-tuple-element.25.ice, f32[5,784,128]{2,1,0:T(8,128)S(1)} %get-tuple-element.30.ext_in, f32[2,784,128]{2,1,0:T(8,128)S(1)} %get-tuple-element.31.vel_in, ...), custom_call_target="tpu_custom_call" | custom-call | tf_op jit(solution)/shard_map/model/pallas_call | solution.py:704
  31.3 11.7 %all-to-all-start.1 = ((f32[16,32,128]{2,1,0:T(8,128)}), f32[16,32,128]{2,1,0:T(8,128)S(1)}, u32[]{:S(2)}, u32[]{:S(2)}) async-start(f32[16,32,128]{2,1,0:T(8,128)} %get-tuple-element.39), calls=%async_computation.1 | async-start | bytes 524288 | tf_op jit(solution)/shard_map/all_to_all | solution.py:731
  43.0 1.2 %unweave.1 = (f32[256,256]{1,0:T(8,128)}, f32[256,256]{1,0:T(8,128)}, f32[8,128]{1,0:T(8,128)S(1)}) custom-call(f32[2,784,128]{2,1,0:T(8,128)S(1)} %get-tuple-element.35.vel), custom_call_target="tpu_custom_call" | custom-call | tf_op jit(solution)/shard_map/unweave/pallas_call | solution.py:720
  44.2 9.3 %all-to-all-done.1.gathered = f32[16,32,128]{2,1,0:T(8,128)S(1)} async-done(((f32[16,32,128]{2,1,0:T(8,128)}), f32[16,32,128]{2,1,0:T(8,128)S(1)}, u32[]{:S(2)}, u32[]{:S(2)}) %all-to-all-start.1) | async-done | bytes 262176 | tf_op jit(solution)/shard_map/all_to_all | solution.py:731
  53.5 0.3 pick.1
  53.8 0.1 collective-permute-start.4
  53.9 1.2 %collective-permute-done.4 = f32[4,4096]{1,0:T(4,128)S(1)} collective-permute-done((f32[4,4096]{1,0:T(4,128)S(1)}, f32[4,4096]{1,0:T(4,128)S(1)}, u32[]{:S(2)}, u32[]{:S(2)}) %collective-permute-start.4) | collective-permute-done | bytes 65568 | tf_op jit(solution)/shard_map/ppermute | solution.py:740
  55.1 0.6 %add.3 = f32[4,4096]{1,0:T(4,128)} add(f32[4,4096]{1,0:T(4,128)S(1)} %get-tuple-element.41, f32[4,4096]{1,0:T(4,128)S(1)} %collective-permute-done.4) | non-fusion elementwise | flops 16384 | bytes 196608 | tf_op jit(solution)/shard_map/add | solution.py:740
Async XLA Ops:
  0.6 10.5 %copy-start.1 = (f32[2,256,256]{2,1,0:T(8,128)S(1)}, f32[2,256,256]{2,1,0:T(8,128)}, u32[]{:S(2)}) copy-start(f32[2,256,256]{2,1,0:T(8,128)} %obs.3) | copy-start | bytes 1572868
  0.6 10.5 %copy-start = (f32[2,256,256]{2,1,0:T(8,128)S(1)}, f32[2,256,256]{2,1,0:T(8,128)}, u32[]{:S(2)}) copy-start(f32[2,256,256]{2,1,0:T(8,128)} %drive.3) | copy-start | bytes 1572868
  0.7 14.3 %copy-start.3 = (s32[8,4,1]{0,2,1:T(1,128)S(1)}, s32[8,4,1]{0,2,1:T(1,128)}, u32[]{:S(2)}) copy-start(s32[8,4,1]{0,2,1:T(1,128)} %param.11) | copy-start | bytes 388
  0.7 14.3 %copy-start.4 = (s32[8,4]{0,1:T(4,128)S(1)}, s32[8,4]{0,1:T(4,128)}, u32[]{:S(2)}) copy-start(s32[8,4]{0,1:T(4,128)} %param.10) | copy-start | bytes 388
  3.5 11.5 %all-to-all-start = ((f32[8,48,128]{2,1,0:T(8,128)}), f32[8,48,128]{2,1,0:T(8,128)S(1)}, u32[]{:S(2)}, u32[]{:S(2)}) async-start(f32[8,48,128]{2,1,0:T(8,128)} %get-tuple-element.23), calls=%async_computation | async-start | bytes 393216 | tf_op jit(solution)/shard_map/all_to_all | solution.py:661
  8.7 4.7 %collective-permute-start = (f32[128,128]{1,0:T(8,128)}, f32[128,128]{1,0:T(8,128)S(1)}, u32[]{:S(2)}, u32[]{:S(2)}) collective-permute-start(f32[128,128]{1,0:T(8,128)} %get-tuple-element.28), channel_id=1, source_target_pairs={{0,8},{16,24},{8,0},{24,16},{1,9},{17,25},{9,1},{25,17},{2,10},{18... | collective-permute-start | bytes 196616 | tf_op jit(solution)/shard_map/ppermute | solution.py:639
  10.5 3.0 %collective-permute-start.1 = (f32[128,128]{1,0:T(8,128)}, f32[128,128]{1,0:T(8,128)S(1)}, u32[]{:S(2)}, u32[]{:S(2)}) collective-permute-start(f32[128,128]{1,0:T(8,128)} %get-tuple-element.29), channel_id=1, source_target_pairs={{8,16},{16,8},{9,17},{17,9},{10,18},{18,10},{11,19},{19,11},{12,20... | collective-permute-start | bytes 196616 | tf_op jit(solution)/shard_map/ppermute | solution.py:639
  11.2 1.0 %copy-start.2 = (f32[256,256]{1,0:T(8,128)S(1)}, f32[256,256]{1,0:T(8,128)}, u32[]{:S(2)}) copy-start(f32[256,256]{1,0:T(8,128)} %thick.3) | copy-start | bytes 786436
  13.6 3.8 %collective-permute-start.2 = (f32[160,128]{1,0:T(8,128)S(1)}, f32[160,128]{1,0:T(8,128)S(1)}, u32[]{:S(2)}, u32[]{:S(2)}) collective-permute-start(f32[160,128]{1,0:T(8,128)S(1)} %get-tuple-element.33), channel_id=1, source_target_pairs={{0,1},{2,3},{4,5},{6,7},{1,0},{3,2},{5,4},{7,6},{8,9},{10,11},{12,... | collective-permute-start | bytes 245768 | tf_op jit(solution)/shard_map/ppermute | solution.py:639
  13.7 3.7 %collective-permute-start.3 = (f32[160,128]{1,0:T(8,128)S(1)}, f32[160,128]{1,0:T(8,128)S(1)}, u32[]{:S(2)}, u32[]{:S(2)}) collective-permute-start(f32[160,128]{1,0:T(8,128)S(1)} %get-tuple-element.34), channel_id=1, source_target_pairs={{1,2},{3,4},{5,6},{2,1},{4,3},{6,5},{9,10},{11,12},{13,14},{10,9},... | collective-permute-start | bytes 245768 | tf_op jit(solution)/shard_map/ppermute | solution.py:639
  31.3 22.2 %all-to-all-start.1 = ((f32[16,32,128]{2,1,0:T(8,128)}), f32[16,32,128]{2,1,0:T(8,128)S(1)}, u32[]{:S(2)}, u32[]{:S(2)}) async-start(f32[16,32,128]{2,1,0:T(8,128)} %get-tuple-element.39), calls=%async_computation.1 | async-start | bytes 524288 | tf_op jit(solution)/shard_map/all_to_all | solution.py:731
  53.8 1.3 %collective-permute-start.4 = (f32[4,4096]{1,0:T(4,128)S(1)}, f32[4,4096]{1,0:T(4,128)S(1)}, u32[]{:S(2)}, u32[]{:S(2)}) collective-permute-start(f32[4,4096]{1,0:T(4,128)S(1)} %get-tuple-element.42), channel_id=1, source_target_pairs={{0,1},{1,0},{2,3},{3,2},{4,5},{5,4},{6,7},{7,6},{8,9},{9,8},{10,11... | collective-permute-start | bytes 196616 | tf_op jit(solution)/shard_map/ppermute | solution.py:740

commit v19 on v17

--- a/solution.py
+++ b/solution.py
@@ -32,7 +32,7 @@
     "tile": (TOP, 2, 128, TOP, 64, 0, 0),
 }
 FACTORS = 14
-AHEAD = 5
+AHEAD = 8
 PACK = COARSE // LANES
 VMEM_LIMIT = 24 * 1024 * 1024
 PACK_VMEM_LIMIT = 62 * 1024 * 1024

time: 54.5 us -> 54.4 us (level)
  no operation moved by 1% of the time
where the time goes in v19:
time: 54.4 us; the launch traced here: 54 us
  blocking collectives  22 us (40%)
  Pallas kernels  20.4 us (38%)
  starting transfers between devices  8.2 us (15%)
  waiting for transfers between devices  1.04 us (2%)
  local copies, waits for them, and re-layouts  0.96 us (2%)
  between operations  0.8 us (1%)
  other arithmetic  0.65 us (1%)
    all_to_all x1, blocking collectives, per_device(): lax.all_to_all(sums, ('gx', 'gy'), 0, 0, tiled=True, axis_index_groups=sa...  22 us
    pallas_call x1, Pallas kernels, per_device(): pl.pallas_call(model_kernel, out_shape=(shape(2, ALL_ROWS, LANES), shape(...  12.3 us
    all_to_all x1, starting transfers between devices, per_device(): parcels = lax.all_to_all(parcels, 'gy', 0, 0, tiled=True)  5.16 us
    ppermute x4, starting transfers between devices, swap(): lax.ppermute(cells, axis, pairs + [(j, i) for i, j in pairs])  2.97 us
    pallas_call x1, Pallas kernels, per_device(): pl.pallas_call(pack_kernel, out_shape=[shape(HALF, LANES)] * 2 + [shape(r...  2.93 us
    pallas_call x1, Pallas kernels, per_device(): pl.pallas_call(setup_kernel, out_shape=[shape(5, ALL_ROWS, LANES), shape(...  1.51 us
    pallas_call x1, Pallas kernels, per_device(): pl.pallas_call(unweave_kernel, out_shape=[shape(TILE, TILE)] * 2, in_spec...  1.2 us
    pallas_call x1, Pallas kernels, per_device(): pl.pallas_call(weave_kernel, out_shape=[shape(5, 2, TILE, LANES), shape(5...  1.14 us
  transfers between devices with their start and end apart: 6, of which 2 were waited for; matrix products, arithmetic and copies ran while one was open for 0% of the time, Pallas kernels for 9%

profile of v19, /device:TPU:0, one launch (start us, length us, event | category | flops | bytes accessed | tf_op | source)
XLA Modules:
  0.0 54.0 jit_solution(12635117440716008718)
XLA Ops:
  0.6 0.0 copy-start.1
  0.6 0.0 copy-start
  0.7 0.0 copy-start.3
  0.7 0.0 copy-start.4
  0.7 2.9 %pack.1 = (f32[128,128]{1,0:T(8,128)}, f32[128,128]{1,0:T(8,128)}, f32[8,48,128]{2,1,0:T(8,128)}) custom-call(s32[4,8]{1,0:T(4,128)} %bitcast.4, f32[4,4096]{1,0:T(4,128)} %control.1, f32[256,256]{1,0:T(8,128)} %thick.3, f32[2,256,256]{2,1,0:T(8,128)} %drive.3, f32[2,256,256]{2,1,0:T(8,128)} %obs.3), custom_call_target="tpu_custom_call" | custom-call | tf_op jit(solution)/shard_map/pack/pallas_call | solution.py:657
  3.6 5.2 %all-to-all-start = ((f32[8,48,128]{2,1,0:T(8,128)}), f32[8,48,128]{2,1,0:T(8,128)S(1)}, u32[]{:S(2)}, u32[]{:S(2)}) async-start(f32[8,48,128]{2,1,0:T(8,128)} %get-tuple-element.22), calls=%async_computation | async-start | bytes 393216 | tf_op jit(solution)/shard_map/all_to_all | solution.py:674
  8.8 1.6 %collective-permute-start = (f32[128,128]{1,0:T(8,128)}, f32[128,128]{1,0:T(8,128)S(1)}, u32[]{:S(2)}, u32[]{:S(2)}) collective-permute-start(f32[128,128]{1,0:T(8,128)} %get-tuple-element.27), channel_id=1, source_target_pairs={{0,8},{16,24},{8,0},{24,16},{1,9},{17,25},{9,1},{25,17},{2,10},{18... | collective-permute-start | bytes 196616 | tf_op jit(solution)/shard_map/ppermute | solution.py:652
  10.3 0.7 %collective-permute-start.1 = (f32[128,128]{1,0:T(8,128)}, f32[128,128]{1,0:T(8,128)S(1)}, u32[]{:S(2)}, u32[]{:S(2)}) collective-permute-start(f32[128,128]{1,0:T(8,128)} %get-tuple-element.28), channel_id=1, source_target_pairs={{8,16},{16,8},{9,17},{17,9},{10,18},{18,10},{11,19},{19,11},{12,20... | collective-permute-start | bytes 196616 | tf_op jit(solution)/shard_map/ppermute | solution.py:652
  11.0 0.0 copy-done.1
  11.0 0.0 copy-done
  11.0 0.0 copy-start.2
  11.0 0.9 %copy-done.2 = f32[256,256]{1,0:T(8,128)S(1)} copy-done((f32[256,256]{1,0:T(8,128)S(1)}, f32[256,256]{1,0:T(8,128)}, u32[]{:S(2)}) %copy-start.2) | copy-done | bytes 262168
  12.0 1.1 %weave.1 = (f32[5,2,256,128]{3,2,1,0:T(8,128)S(1)}, f32[5,128,128]{2,1,0:T(8,128)S(1)}, f32[2,3,64,128]{3,2,1,0:T(8,128)S(1)}) custom-call(f32[256,256]{1,0:T(8,128)S(1)} %copy-done.2, f32[2,256,256]{2,1,0:T(8,128)S(1)} %copy-done, f32[2,256,256]{2,1,0:T(8,128)S(1)} %copy-done.1), custom_call_target="tpu_custom_call" | custom-call | tf_op jit(solution)/shard_map/weave/pallas_call | solution.py:676
  13.1 0.4 collective-permute-done.first_col
  13.5 0.0 collective-permute-done.1.second_col
  13.5 0.1 rows.1
  13.6 0.1 collective-permute-start.2
  13.7 0.7 %collective-permute-start.3 = (f32[160,128]{1,0:T(8,128)S(1)}, f32[160,128]{1,0:T(8,128)S(1)}, u32[]{:S(2)}, u32[]{:S(2)}) collective-permute-start(f32[160,128]{1,0:T(8,128)S(1)} %get-tuple-element.33), channel_id=1, source_target_pairs={{1,2},{3,4},{5,6},{2,1},{4,3},{6,5},{9,10},{11,12},{13,14},{10,9},... | collective-permute-start | bytes 245768 | tf_op jit(solution)/shard_map/ppermute | solution.py:652
  14.4 0.6 %all-to-all-done.parcels = f32[8,48,128]{2,1,0:T(8,128)S(1)} async-done(((f32[8,48,128]{2,1,0:T(8,128)}), f32[8,48,128]{2,1,0:T(8,128)S(1)}, u32[]{:S(2)}, u32[]{:S(2)}) %all-to-all-start) | async-done | bytes 196640 | tf_op jit(solution)/shard_map/all_to_all | solution.py:674
  15.0 0.0 copy-done.3
  15.0 0.0 copy-done.4
  15.0 0.9 %friction.1 = (f32[784,128]{1,0:T(8,128)S(1)}, f32[784,128]{1,0:T(8,128)S(1)}, s32[16,8,128]{2,1,0:T(8,128)S(1)}) custom-call(s32[4,8]{1,0:T(4,128)S(1)} %bitcast.5, s32[4,8]{1,0:T(4,128)S(1)} %bitcast.6, f32[8,48,128]{2,1,0:T(8,128)S(1)} %all-to-all-done.parcels), custom_call_target="tpu_custom_call" | custom-call | tf_op jit(solution)/shard_map/friction/pallas_call | solution.py:693
  15.9 1.5 %setup.1 = (f32[5,784,128]{2,1,0:T(8,128)S(1)}, f32[2,784,128]{2,1,0:T(8,128)S(1)}) custom-call(f32[784,128]{1,0:T(8,128)S(1)} %get-tuple-element.23.fr, f32[784,128]{1,0:T(8,128)S(1)} %get-tuple-element.24.ice, f32[5,2,256,128]{3,2,1,0:T(8,128)S(1)} %get-tuple-element.25.woven, f32[5,128,128]{2,1,0:T(8,128)S(1)} %get-tuple-element.26.own_sides, ...), custom_call_target="tpu_custom_call" | custom-call | tf_op jit(solution)/shard_map/setup/pallas_call | solution.py:703
  17.4 0.0 collective-permute-done.2.first_row
  17.4 0.0 collective-permute-done.3.second_row
  17.4 12.3 %model.1 = (f32[2,784,128]{2,1,0:T(8,128)S(1)}, f32[16,32,128]{2,1,0:T(8,128)S(1)}) custom-call(f32[784,128]{1,0:T(8,128)S(1)} %get-tuple-element.23.fr, f32[784,128]{1,0:T(8,128)S(1)} %get-tuple-element.24.ice, f32[5,784,128]{2,1,0:T(8,128)S(1)} %get-tuple-element.29.ext_in, f32[2,784,128]{2,1,0:T(8,128)S(1)} %get-tuple-element.30.vel_in, ...), custom_call_target="tpu_custom_call" | custom-call | tf_op jit(solution)/shard_map/model/pallas_call | solution.py:717
  29.7 22.0 %all_to_all.10.gathered = f32[16,32,128]{2,1,0:T(8,128)S(1)} all-to-all(f32[16,32,128]{2,1,0:T(8,128)S(1)} %get-tuple-element.38), channel_id=1, replica_groups={{0,2,4,6,8,10,12,14,16,18,20,22,24,26,28,30},{1,3,5,7,9,11,13,15,17,19,..., dimensions={0} | all-to-all | bytes 524288 | tf_op jit(solution)/shard_map/all_to_all | solution.py:744
  51.7 0.3 pick.1
  52.1 0.1 collective-permute-start.4
  52.1 1.2 %unweave.1 = (f32[256,256]{1,0:T(8,128)}, f32[256,256]{1,0:T(8,128)}) custom-call(f32[2,784,128]{2,1,0:T(8,128)S(1)} %get-tuple-element.34.vel), custom_call_target="tpu_custom_call" | custom-call | tf_op jit(solution)/shard_map/unweave/pallas_call | solution.py:733
  53.4 0.0 collective-permute-done.4
  53.4 0.6 %add.3 = f32[4,4096]{1,0:T(4,128)} add(f32[4,4096]{1,0:T(4,128)S(1)} %get-tuple-element.39, f32[4,4096]{1,0:T(4,128)S(1)} %collective-permute-done.4) | non-fusion elementwise | flops 16384 | bytes 196608 | tf_op jit(solution)/shard_map/add | solution.py:753
Async XLA Ops:
  0.6 10.4 %copy-start.1 = (f32[2,256,256]{2,1,0:T(8,128)S(1)}, f32[2,256,256]{2,1,0:T(8,128)}, u32[]{:S(2)}) copy-start(f32[2,256,256]{2,1,0:T(8,128)} %obs.3) | copy-start | bytes 1572868
  0.6 10.4 %copy-start = (f32[2,256,256]{2,1,0:T(8,128)S(1)}, f32[2,256,256]{2,1,0:T(8,128)}, u32[]{:S(2)}) copy-start(f32[2,256,256]{2,1,0:T(8,128)} %drive.3) | copy-start | bytes 1572868
  0.7 14.4 %copy-start.3 = (s32[8,4,1]{0,2,1:T(1,128)S(1)}, s32[8,4,1]{0,2,1:T(1,128)}, u32[]{:S(2)}) copy-start(s32[8,4,1]{0,2,1:T(1,128)} %param.11) | copy-start | bytes 388
  0.7 14.3 %copy-start.4 = (s32[8,4]{0,1:T(4,128)S(1)}, s32[8,4]{0,1:T(4,128)}, u32[]{:S(2)}) copy-start(s32[8,4]{0,1:T(4,128)} %param.10) | copy-start | bytes 388
  3.6 11.4 %all-to-all-start = ((f32[8,48,128]{2,1,0:T(8,128)}), f32[8,48,128]{2,1,0:T(8,128)S(1)}, u32[]{:S(2)}, u32[]{:S(2)}) async-start(f32[8,48,128]{2,1,0:T(8,128)} %get-tuple-element.22), calls=%async_computation | async-start | bytes 393216 | tf_op jit(solution)/shard_map/all_to_all | solution.py:674
  8.8 4.7 %collective-permute-start = (f32[128,128]{1,0:T(8,128)}, f32[128,128]{1,0:T(8,128)S(1)}, u32[]{:S(2)}, u32[]{:S(2)}) collective-permute-start(f32[128,128]{1,0:T(8,128)} %get-tuple-element.27), channel_id=1, source_target_pairs={{0,8},{16,24},{8,0},{24,16},{1,9},{17,25},{9,1},{25,17},{2,10},{18... | collective-permute-start | bytes 196616 | tf_op jit(solution)/shard_map/ppermute | solution.py:652
  10.3 3.1 %collective-permute-start.1 = (f32[128,128]{1,0:T(8,128)}, f32[128,128]{1,0:T(8,128)S(1)}, u32[]{:S(2)}, u32[]{:S(2)}) collective-permute-start(f32[128,128]{1,0:T(8,128)} %get-tuple-element.28), channel_id=1, source_target_pairs={{8,16},{16,8},{9,17},{17,9},{10,18},{18,10},{11,19},{19,11},{12,20... | collective-permute-start | bytes 196616 | tf_op jit(solution)/shard_map/ppermute | solution.py:652
  11.0 1.0 %copy-start.2 = (f32[256,256]{1,0:T(8,128)S(1)}, f32[256,256]{1,0:T(8,128)}, u32[]{:S(2)}) copy-start(f32[256,256]{1,0:T(8,128)} %thick.3) | copy-start | bytes 786436
  13.6 3.8 %collective-permute-start.2 = (f32[160,128]{1,0:T(8,128)S(1)}, f32[160,128]{1,0:T(8,128)S(1)}, u32[]{:S(2)}, u32[]{:S(2)}) collective-permute-start(f32[160,128]{1,0:T(8,128)S(1)} %get-tuple-element.32), channel_id=1, source_target_pairs={{0,1},{2,3},{4,5},{6,7},{1,0},{3,2},{5,4},{7,6},{8,9},{10,11},{12,... | collective-permute-start | bytes 245768 | tf_op jit(solution)/shard_map/ppermute | solution.py:652
  13.7 3.7 %collective-permute-start.3 = (f32[160,128]{1,0:T(8,128)S(1)}, f32[160,128]{1,0:T(8,128)S(1)}, u32[]{:S(2)}, u32[]{:S(2)}) collective-permute-start(f32[160,128]{1,0:T(8,128)S(1)} %get-tuple-element.33), channel_id=1, source_target_pairs={{1,2},{3,4},{5,6},{2,1},{4,3},{6,5},{9,10},{11,12},{13,14},{10,9},... | collective-permute-start | bytes 245768 | tf_op jit(solution)/shard_map/ppermute | solution.py:652
  52.1 1.3 %collective-permute-start.4 = (f32[4,4096]{1,0:T(4,128)S(1)}, f32[4,4096]{1,0:T(4,128)S(1)}, u32[]{:S(2)}, u32[]{:S(2)}) collective-permute-start(f32[4,4096]{1,0:T(4,128)S(1)} %get-tuple-element.40), channel_id=1, source_target_pairs={{0,1},{1,0},{2,3},{3,2},{4,5},{5,4},{6,7},{7,6},{8,9},{9,8},{10,11... | collective-permute-start | bytes 196616 | tf_op jit(solution)/shard_map/ppermute | solution.py:753

commit v20 on v19

--- a/solution.py
+++ b/solution.py
@@ -256,54 +256,41 @@
 
 
 def over_ends(count, read, work):
-    def block(i, carry):
-        row = pl.multiple_of(MARGIN + i * (TILE + 2 * HALO - count), 8)
-        side_row = pl.multiple_of(MARGIN + i * (HALF + 2 * HALO - count), 8)
-        run_groups([(MAIN, row, count), (SIDES, side_row, count)], read, work)
-        return carry
-
-    lax.fori_loop(0, 2, block, 0)
+    row = pl.multiple_of(MARGIN + 8 * jnp.minimum(lax.axis_index("gx"), 0), 8)
+    far, side_far = TILE + 2 * HALO - count, HALF + 2 * HALO - count
+    run_groups(
+        [(MAIN, row, count), (SIDES, row, count), (MAIN, row + far, count), (SIDES, row + side_far, count)], read, work
+    )
 
 
 def join_parts(ref, leads, whole):
     edge = HALO // 2
-
-    def join(row, upper, lower, count):
-        lane = lanes_of(count)
-        place = lane % BAND
-        for lead in leads:
-            def at(tile_row):
-                return (*lead, pl.ds(tile_row, count), slice(None))
-
-            mixed = ref[at(SIDE + row)]
-            if whole:
-                source = jnp.where(place < edge, LANES - edge + place // 2, place // 2 - 24)
-                source = jnp.clip(source, 0, LANES - 1)
-                halves = []
-                for main_row in (row, row + HALF):
-                    even, odd = (gather(ref[at(tile + main_row)], source) for tile in MAIN)
-                    halves.append(jnp.where(lane % 2 == 0, even, odd))
-                outer = (place < edge) | (place >= BAND - edge)
-                ref[at(SIDE + row)] = jnp.where(outer, jnp.where(lane < BAND, halves[0], halves[1]), mixed)
-            for wanted, band, main_row in ((upper, 0, row), (lower, BAND, row + HALF)):
-                if wanted:
-                    few = edge // 2
-                    source = band + jnp.where(lane < few, 3 * HALO + 2 * lane, edge + 2 * (lane - LANES + few))
-                    source = jnp.clip(source, 0, LANES - 2)
-                    outer = (lane < few) | (lane >= LANES - few)
-                    for c, tile in enumerate(MAIN):
-                        ref[at(tile + main_row)] = jnp.where(outer, gather(mixed, source + c), ref[at(tile + main_row)])
-
-    step = 32
-
-    def middle(i, carry):
-        join(pl.multiple_of(TOP + i * step, 8), True, True, step)
-        return carry
-
-    lax.fori_loop(0, HALF // step, middle, 0)
-    if whole:
-        join(MARGIN, True, False, HALO)
-        join(TOP + HALF, False, True, HALO)
+    few = edge // 2
+    frame = HALO if whole else 0
+    first, count = TOP - frame, HALF + 2 * frame
+    kept = HALF + frame
+    lane = lanes_of(kept)
+    outer = (lane < few) | (lane >= LANES - few)
+    near = jnp.where(lane < few, 3 * HALO + 2 * lane, edge + 2 * (lane - LANES + few))
+    near = jnp.clip(near, 0, LANES - 2 - BAND)
+    side_lane = lanes_of(count)
+    place = side_lane % BAND
+    inner = jnp.clip(jnp.where(place < edge, LANES - edge + place // 2, place // 2 - 24), 0, LANES - 1)
+    for lead in leads:
+        def at(row, rows):
+            return (*lead, slice(row, row + rows), slice(None))
+
+        mixed = ref[at(SIDE + first, count)]
+        halves = [[ref[at(tile + first + HALF * h, count)] for tile in MAIN] for h in range(2)]
+        if whole:
+            parts = [jnp.where(side_lane % 2 == 0, gather(even, inner), gather(odd, inner)) for even, odd in halves]
+            wanted = (place < edge) | (place >= BAND - edge)
+            ref[at(SIDE + first, count)] = jnp.where(wanted, jnp.where(side_lane < BAND, *parts), mixed)
+        for h, skip in ((0, 0), (1, frame)):
+            cells = mixed[skip : skip + kept]
+            for c, tile in enumerate(MAIN):
+                new = jnp.where(outer, gather(cells, near + (BAND * h + c)), halves[h][c][skip : skip + kept])
+                ref[at(tile + first + HALF * h + skip, kept)] = new
 
 
 def friction_kernel(tile_block, ice_mask, parcels, fr, ice, owners, patch):

time: 54.4 us -> 53.6 us (0.985)
  Pallas kernels: 20.4 us -> 19.5 us
    pallas_call x1, Pallas kernels: 12.3 us -> 11.5 us  [per_device(): pl.pallas_call(model_kernel, out_shape=(shape(2, ALL_ROWS, LANES), shape(...]
where the time goes in v20:
time: 53.6 us; the launch traced here: 53.2 us
  blocking collectives  21.8 us (41%)
  Pallas kernels  19.5 us (36%)
  starting transfers between devices  8.37 us (16%)
  waiting for transfers between devices  1.05 us (2%)
  local copies, waits for them, and re-layouts  0.96 us (2%)
  between operations  0.8 us (1%)
  other arithmetic  0.65 us (1%)
    all_to_all x1, blocking collectives, per_device(): lax.all_to_all(sums, ('gx', 'gy'), 0, 0, tiled=True, axis_index_groups=sa...  21.8 us
    pallas_call x1, Pallas kernels, per_device(): pl.pallas_call(model_kernel, out_shape=(shape(2, ALL_ROWS, LANES), shape(...  11.5 us
    all_to_all x1, starting transfers between devices, per_device(): parcels = lax.all_to_all(parcels, 'gy', 0, 0, tiled=True)  5.34 us
    ppermute x4, starting transfers between devices, swap(): lax.ppermute(cells, axis, pairs + [(j, i) for i, j in pairs])  2.96 us
    pallas_call x1, Pallas kernels, per_device(): pl.pallas_call(pack_kernel, out_shape=[shape(HALF, LANES)] * 2 + [shape(r...  2.9 us
    pallas_call x1, Pallas kernels, per_device(): pl.pallas_call(setup_kernel, out_shape=[shape(5, ALL_ROWS, LANES), shape(...  1.51 us
    pallas_call x1, Pallas kernels, per_device(): pl.pallas_call(unweave_kernel, out_shape=[shape(TILE, TILE)] * 2, in_spec...  1.2 us
    pallas_call x1, Pallas kernels, per_device(): pl.pallas_call(weave_kernel, out_shape=[shape(5, 2, TILE, LANES), shape(5...  1.14 us
  transfers between devices with their start and end apart: 6, of which 2 were waited for; matrix products, arithmetic and copies ran while one was open for 0% of the time, Pallas kernels for 9%

profile of v20, /device:TPU:0, one launch (start us, length us, event | category | flops | bytes accessed | tf_op | source)
XLA Modules:
  0.0 53.2 jit_solution(16035993861662398290)
XLA Ops:
  0.6 0.0 copy-start.1
  0.6 0.0 copy-start
  0.7 0.0 copy-start.3
  0.7 0.0 copy-start.4
  0.7 2.9 %pack.1 = (f32[128,128]{1,0:T(8,128)}, f32[128,128]{1,0:T(8,128)}, f32[8,48,128]{2,1,0:T(8,128)}) custom-call(s32[4,8]{1,0:T(4,128)} %bitcast.4, f32[4,4096]{1,0:T(4,128)} %control.1, f32[256,256]{1,0:T(8,128)} %thick.3, f32[2,256,256]{2,1,0:T(8,128)} %drive.3, f32[2,256,256]{2,1,0:T(8,128)} %obs.3), custom_call_target="tpu_custom_call" | custom-call | tf_op jit(solution)/shard_map/pack/pallas_call | solution.py:644
  3.6 5.3 %all-to-all-start = ((f32[8,48,128]{2,1,0:T(8,128)}), f32[8,48,128]{2,1,0:T(8,128)S(1)}, u32[]{:S(2)}, u32[]{:S(2)}) async-start(f32[8,48,128]{2,1,0:T(8,128)} %get-tuple-element.22), calls=%async_computation | async-start | bytes 393216 | tf_op jit(solution)/shard_map/all_to_all | solution.py:661
  8.9 1.6 %collective-permute-start = (f32[128,128]{1,0:T(8,128)}, f32[128,128]{1,0:T(8,128)S(1)}, u32[]{:S(2)}, u32[]{:S(2)}) collective-permute-start(f32[128,128]{1,0:T(8,128)} %get-tuple-element.27), channel_id=1, source_target_pairs={{0,8},{16,24},{8,0},{24,16},{1,9},{17,25},{9,1},{25,17},{2,10},{18... | collective-permute-start | bytes 196616 | tf_op jit(solution)/shard_map/ppermute | solution.py:639
  10.5 0.7 %collective-permute-start.1 = (f32[128,128]{1,0:T(8,128)}, f32[128,128]{1,0:T(8,128)S(1)}, u32[]{:S(2)}, u32[]{:S(2)}) collective-permute-start(f32[128,128]{1,0:T(8,128)} %get-tuple-element.28), channel_id=1, source_target_pairs={{8,16},{16,8},{9,17},{17,9},{10,18},{18,10},{11,19},{19,11},{12,20... | collective-permute-start | bytes 196616 | tf_op jit(solution)/shard_map/ppermute | solution.py:639
  11.1 0.0 copy-done.1
  11.2 0.0 copy-done
  11.2 0.0 copy-start.2
  11.2 0.9 %copy-done.2 = f32[256,256]{1,0:T(8,128)S(1)} copy-done((f32[256,256]{1,0:T(8,128)S(1)}, f32[256,256]{1,0:T(8,128)}, u32[]{:S(2)}) %copy-start.2) | copy-done | bytes 262168
  12.1 1.1 %weave.1 = (f32[5,2,256,128]{3,2,1,0:T(8,128)S(1)}, f32[5,128,128]{2,1,0:T(8,128)S(1)}, f32[2,3,64,128]{3,2,1,0:T(8,128)S(1)}) custom-call(f32[256,256]{1,0:T(8,128)S(1)} %copy-done.2, f32[2,256,256]{2,1,0:T(8,128)S(1)} %copy-done, f32[2,256,256]{2,1,0:T(8,128)S(1)} %copy-done.1), custom_call_target="tpu_custom_call" | custom-call | tf_op jit(solution)/shard_map/weave/pallas_call | solution.py:663
  13.3 0.4 collective-permute-done.first_col
  13.6 0.0 collective-permute-done.1.second_col
  13.6 0.1 rows.1
  13.8 0.1 collective-permute-start.2
  13.8 0.7 %collective-permute-start.3 = (f32[160,128]{1,0:T(8,128)S(1)}, f32[160,128]{1,0:T(8,128)S(1)}, u32[]{:S(2)}, u32[]{:S(2)}) collective-permute-start(f32[160,128]{1,0:T(8,128)S(1)} %get-tuple-element.33), channel_id=1, source_target_pairs={{1,2},{3,4},{5,6},{2,1},{4,3},{6,5},{9,10},{11,12},{13,14},{10,9},... | collective-permute-start | bytes 245768 | tf_op jit(solution)/shard_map/ppermute | solution.py:639
  14.5 0.6 %all-to-all-done.parcels = f32[8,48,128]{2,1,0:T(8,128)S(1)} async-done(((f32[8,48,128]{2,1,0:T(8,128)}), f32[8,48,128]{2,1,0:T(8,128)S(1)}, u32[]{:S(2)}, u32[]{:S(2)}) %all-to-all-start) | async-done | bytes 196640 | tf_op jit(solution)/shard_map/all_to_all | solution.py:661
  15.2 0.0 copy-done.3
  15.2 0.0 copy-done.4
  15.2 0.9 %friction.1 = (f32[784,128]{1,0:T(8,128)S(1)}, f32[784,128]{1,0:T(8,128)S(1)}, s32[16,8,128]{2,1,0:T(8,128)S(1)}) custom-call(s32[4,8]{1,0:T(4,128)S(1)} %bitcast.5, s32[4,8]{1,0:T(4,128)S(1)} %bitcast.6, f32[8,48,128]{2,1,0:T(8,128)S(1)} %all-to-all-done.parcels), custom_call_target="tpu_custom_call" | custom-call | tf_op jit(solution)/shard_map/friction/pallas_call | solution.py:680
  16.0 1.5 %setup.1 = (f32[5,784,128]{2,1,0:T(8,128)S(1)}, f32[2,784,128]{2,1,0:T(8,128)S(1)}) custom-call(f32[784,128]{1,0:T(8,128)S(1)} %get-tuple-element.23.fr, f32[784,128]{1,0:T(8,128)S(1)} %get-tuple-element.24.ice, f32[5,2,256,128]{3,2,1,0:T(8,128)S(1)} %get-tuple-element.25.woven, f32[5,128,128]{2,1,0:T(8,128)S(1)} %get-tuple-element.26.own_sides, ...), custom_call_target="tpu_custom_call" | custom-call | tf_op jit(solution)/shard_map/setup/pallas_call | solution.py:690
  17.5 0.0 collective-permute-done.2.first_row
  17.5 0.0 collective-permute-done.3.second_row
  17.6 11.5 %model.1 = (f32[2,784,128]{2,1,0:T(8,128)S(1)}, f32[16,32,128]{2,1,0:T(8,128)S(1)}) custom-call(f32[784,128]{1,0:T(8,128)S(1)} %get-tuple-element.23.fr, f32[784,128]{1,0:T(8,128)S(1)} %get-tuple-element.24.ice, f32[5,784,128]{2,1,0:T(8,128)S(1)} %get-tuple-element.29.ext_in, f32[2,784,128]{2,1,0:T(8,128)S(1)} %get-tuple-element.30.vel_in, ...), custom_call_target="tpu_custom_call" | custom-call | tf_op jit(solution)/shard_map/model/pallas_call | solution.py:704
  29.1 21.8 %all_to_all.10.gathered = f32[16,32,128]{2,1,0:T(8,128)S(1)} all-to-all(f32[16,32,128]{2,1,0:T(8,128)S(1)} %get-tuple-element.38), channel_id=1, replica_groups={{0,2,4,6,8,10,12,14,16,18,20,22,24,26,28,30},{1,3,5,7,9,11,13,15,17,19,..., dimensions={0} | all-to-all | bytes 524288 | tf_op jit(solution)/shard_map/all_to_all | solution.py:731
  50.9 0.3 pick.1
  51.2 0.1 collective-permute-start.4
  51.3 1.2 %unweave.1 = (f32[256,256]{1,0:T(8,128)}, f32[256,256]{1,0:T(8,128)}) custom-call(f32[2,784,128]{2,1,0:T(8,128)S(1)} %get-tuple-element.34.vel), custom_call_target="tpu_custom_call" | custom-call | tf_op jit(solution)/shard_map/unweave/pallas_call | solution.py:720
  52.5 0.0 collective-permute-done.4
  52.6 0.6 %add.3 = f32[4,4096]{1,0:T(4,128)} add(f32[4,4096]{1,0:T(4,128)S(1)} %get-tuple-element.39, f32[4,4096]{1,0:T(4,128)S(1)} %collective-permute-done.4) | non-fusion elementwise | flops 16384 | bytes 196608 | tf_op jit(solution)/shard_map/add | solution.py:740
Async XLA Ops:
  0.6 10.5 %copy-start.1 = (f32[2,256,256]{2,1,0:T(8,128)S(1)}, f32[2,256,256]{2,1,0:T(8,128)}, u32[]{:S(2)}) copy-start(f32[2,256,256]{2,1,0:T(8,128)} %obs.3) | copy-start | bytes 1572868
  0.6 10.5 %copy-start = (f32[2,256,256]{2,1,0:T(8,128)S(1)}, f32[2,256,256]{2,1,0:T(8,128)}, u32[]{:S(2)}) copy-start(f32[2,256,256]{2,1,0:T(8,128)} %drive.3) | copy-start | bytes 1572868
  0.7 14.5 %copy-start.3 = (s32[8,4,1]{0,2,1:T(1,128)S(1)}, s32[8,4,1]{0,2,1:T(1,128)}, u32[]{:S(2)}) copy-start(s32[8,4,1]{0,2,1:T(1,128)} %param.11) | copy-start | bytes 388
  0.7 14.5 %copy-start.4 = (s32[8,4]{0,1:T(4,128)S(1)}, s32[8,4]{0,1:T(4,128)}, u32[]{:S(2)}) copy-start(s32[8,4]{0,1:T(4,128)} %param.10) | copy-start | bytes 388
  3.6 11.6 %all-to-all-start = ((f32[8,48,128]{2,1,0:T(8,128)}), f32[8,48,128]{2,1,0:T(8,128)S(1)}, u32[]{:S(2)}, u32[]{:S(2)}) async-start(f32[8,48,128]{2,1,0:T(8,128)} %get-tuple-element.22), calls=%async_computation | async-start | bytes 393216 | tf_op jit(solution)/shard_map/all_to_all | solution.py:661
  8.9 4.7 %collective-permute-start = (f32[128,128]{1,0:T(8,128)}, f32[128,128]{1,0:T(8,128)S(1)}, u32[]{:S(2)}, u32[]{:S(2)}) collective-permute-start(f32[128,128]{1,0:T(8,128)} %get-tuple-element.27), channel_id=1, source_target_pairs={{0,8},{16,24},{8,0},{24,16},{1,9},{17,25},{9,1},{25,17},{2,10},{18... | collective-permute-start | bytes 196616 | tf_op jit(solution)/shard_map/ppermute | solution.py:639
  10.5 3.1 %collective-permute-start.1 = (f32[128,128]{1,0:T(8,128)}, f32[128,128]{1,0:T(8,128)S(1)}, u32[]{:S(2)}, u32[]{:S(2)}) collective-permute-start(f32[128,128]{1,0:T(8,128)} %get-tuple-element.28), channel_id=1, source_target_pairs={{8,16},{16,8},{9,17},{17,9},{10,18},{18,10},{11,19},{19,11},{12,20... | collective-permute-start | bytes 196616 | tf_op jit(solution)/shard_map/ppermute | solution.py:639
  11.2 1.0 %copy-start.2 = (f32[256,256]{1,0:T(8,128)S(1)}, f32[256,256]{1,0:T(8,128)}, u32[]{:S(2)}) copy-start(f32[256,256]{1,0:T(8,128)} %thick.3) | copy-start | bytes 786436
  13.8 3.8 %collective-permute-start.2 = (f32[160,128]{1,0:T(8,128)S(1)}, f32[160,128]{1,0:T(8,128)S(1)}, u32[]{:S(2)}, u32[]{:S(2)}) collective-permute-start(f32[160,128]{1,0:T(8,128)S(1)} %get-tuple-element.32), channel_id=1, source_target_pairs={{0,1},{2,3},{4,5},{6,7},{1,0},{3,2},{5,4},{7,6},{8,9},{10,11},{12,... | collective-permute-start | bytes 245768 | tf_op jit(solution)/shard_map/ppermute | solution.py:639
  13.8 3.7 %collective-permute-start.3 = (f32[160,128]{1,0:T(8,128)S(1)}, f32[160,128]{1,0:T(8,128)S(1)}, u32[]{:S(2)}, u32[]{:S(2)}) collective-permute-start(f32[160,128]{1,0:T(8,128)S(1)} %get-tuple-element.33), channel_id=1, source_target_pairs={{1,2},{3,4},{5,6},{2,1},{4,3},{6,5},{9,10},{11,12},{13,14},{10,9},... | collective-permute-start | bytes 245768 | tf_op jit(solution)/shard_map/ppermute | solution.py:639
  51.2 1.3 %collective-permute-start.4 = (f32[4,4096]{1,0:T(4,128)S(1)}, f32[4,4096]{1,0:T(4,128)S(1)}, u32[]{:S(2)}, u32[]{:S(2)}) collective-permute-start(f32[4,4096]{1,0:T(4,128)S(1)} %get-tuple-element.40), channel_id=1, source_target_pairs={{0,1},{1,0},{2,3},{3,2},{4,5},{5,4},{6,7},{7,6},{8,9},{9,8},{10,11... | collective-permute-start | bytes 196616 | tf_op jit(solution)/shard_map/ppermute | solution.py:740

commit v21 on v20

--- a/solution.py
+++ b/solution.py
@@ -109,8 +109,9 @@
         copy.start()
     packed_parcels[...] = jnp.zeros_like(packed_parcels)
     copies[0].wait()
+    shard = [held_control[:, j * LANES : (j + 1) * LANES] for j in range(PACK)]
     for j in range(PACK):
-        owned_blocks[:, j, :] = held_control[:, j * LANES : (j + 1) * LANES]
+        owned_blocks[:, j, :] = shard[j]
     table_copy.wait()
     fill_parcels(tile_block, owned_blocks, packed_parcels)
     results = [pltpu.make_async_copy(packed_parcels, parcels, sems.at[6])]
@@ -494,22 +495,28 @@
     vel_b, sums,
     ext, visc, vel_a, vel_c, coef, small,
 ):
-    ext[...] = ext_in[...]
-    vel_b[...] = vel_in[...]
+    half = ALL_ROWS // 2
+    for target, source in ((ext, ext_in), (vel_b, vel_in)):
+        for f in range(source.shape[0]):
+            for row in (0, half):
+                target[f, row : row + half, :] = source[f, row : row + half, :]
     north, south = sides("gy", first_row[...], second_row[...])
     here = SIDE + TOP
+    ends = []
     for f, (first, count) in enumerate(STRIP):
         for c in range(2):
             rows = slice(64 * c + first, 64 * c + first + count)
-            ext[f, MAIN[c] + TOP - count : MAIN[c] + TOP, :] = north[rows]
-            ext[f, MAIN[c] + TOP + TILE : MAIN[c] + TOP + TILE + count, :] = south[rows]
+            ends.append((f, MAIN[c] + TOP - count, north[rows]))
+            ends.append((f, MAIN[c] + TOP + TILE, south[rows]))
         rows = slice(128 + first % 32, 128 + first % 32 + count)
         source = BAND if f >= 2 else 0
         upper = lanes_of(count) < BAND
         above = turn(ext_in[f, here + HALF - count : here + HALF, :], 0, BAND)
         below = turn(ext_in[f, here : here + count, :], 0, BAND)
-        ext[f, here - count : here, :] = jnp.where(upper, turn(north[rows], source, 0), above)
-        ext[f, here + HALF : here + HALF + count, :] = jnp.where(upper, below, turn(south[rows], source, BAND))
+        ends.append((f, here - count, jnp.where(upper, turn(north[rows], source, 0), above)))
+        ends.append((f, here + HALF, jnp.where(upper, below, turn(south[rows], source, BAND))))
+    for f, row, cells in ends:
+        ext[f, row : row + cells.shape[0], :] = cells
 
     step = make_stages(ext, fr, ice, visc, vel_a, vel_b, coef)
     over_ends(32, step.read_thickness, step.first_viscosity)
@@ -578,22 +585,30 @@
 def unweave_kernel(vel, vel_u, vel_v, plain, sems):
     lane = lanes_of(HALF)
     edge = HALO // 2
+    parts = [(i, band) for i in range(2) for band in range(2)]
+
+    def read(i, band):
+        row = TOP + HALF * band
+        return [vel[i, tile + row : tile + row + HALF, :] for tile in MAIN] + [vel[i, SIDE + TOP : SIDE + TOP + HALF, :]]
+
     copies = []
-    for i, out in enumerate((vel_u, vel_v)):
-        mixed = vel[i, SIDE + TOP : SIDE + TOP + HALF, :]
-        for band in range(2):
-            rows = slice(HALF * band, HALF * (band + 1))
-            even, odd = (vel[i, tile + TOP + HALF * band : tile + TOP + HALF * (band + 1), :] for tile in MAIN)
-            for c in range(2):
-                source = BAND * c + lane // 2
-                cells = jnp.where(lane % 2 == 0, gather(even, source), gather(odd, source))
-                if c == 0:
-                    outer, side = lane < edge, turn(mixed, BAND * band + 3 * HALO, 0)
-                else:
-                    outer, side = lane >= LANES - edge, turn(mixed, BAND * band + edge, LANES - edge)
-                plain[i, rows, c * LANES : (c + 1) * LANES] = jnp.where(outer, side, cells)
-            copies.append(pltpu.make_async_copy(plain.at[i, rows], out.at[rows], sems.at[2 * i + band]))
-            copies[-1].start()
+    pending = read(*parts[0])
+    for k, (i, band) in enumerate(parts):
+        even, odd, mixed = pending
+        if k + 1 < len(parts):
+            pending = read(*parts[k + 1])
+        cells = []
+        for c in range(2):
+            source = BAND * c + lane // 2
+            cells.append(jnp.where(lane % 2 == 0, gather(even, source), gather(odd, source)))
+        low = jnp.where(lane < edge, turn(mixed, BAND * band + 3 * HALO, 0), cells[0])
+        high = jnp.where(lane >= LANES - edge, turn(mixed, BAND * band + edge, LANES - edge), cells[1])
+        rows = slice(HALF * band, HALF * (band + 1))
+        plain[i, rows, :LANES] = low
+        plain[i, rows, LANES:] = high
+        out = (vel_u, vel_v)[i]
+        copies.append(pltpu.make_async_copy(plain.at[i, rows], out.at[rows], sems.at[2 * i + band]))
+        copies[-1].start()
     for copy in copies:
         copy.wait()
 

time: 53.6 us -> 53.7 us (level)
  blocking collectives: 21.8 us -> 22.4 us
    all_to_all x1, blocking collectives: 21.8 us -> 22.4 us  [per_device(): lax.all_to_all(sums, ('gx', 'gy'), 0, 0, tiled=True, axis_index_groups=sa...]
where the time goes in v21:
time: 53.7 us; the launch traced here: 53.5 us
  blocking collectives  22.4 us (42%)
  Pallas kernels  19.7 us (37%)
  starting transfers between devices  8.34 us (16%)
  local copies, waits for them, and re-layouts  0.96 us (2%)
  between operations  0.79 us (1%)
  other arithmetic  0.65 us (1%)
  waiting for transfers between devices  0.64 us (1%)
    all_to_all x1, blocking collectives, per_device(): lax.all_to_all(sums, ('gx', 'gy'), 0, 0, tiled=True, axis_index_groups=sa...  22.4 us
    pallas_call x1, Pallas kernels, per_device(): pl.pallas_call(model_kernel, out_shape=(shape(2, ALL_ROWS, LANES), shape(...  11.5 us
    all_to_all x1, starting transfers between devices, per_device(): parcels = lax.all_to_all(parcels, 'gy', 0, 0, tiled=True)  4.89 us
    ppermute x4, starting transfers between devices, swap(): lax.ppermute(cells, axis, pairs + [(j, i) for i, j in pairs])  3.38 us
    pallas_call x1, Pallas kernels, per_device(): pl.pallas_call(pack_kernel, out_shape=[shape(HALF, LANES)] * 2 + [shape(r...  3.07 us
    pallas_call x1, Pallas kernels, per_device(): pl.pallas_call(setup_kernel, out_shape=[shape(5, ALL_ROWS, LANES), shape(...  1.51 us
    pallas_call x1, Pallas kernels, per_device(): pl.pallas_call(unweave_kernel, out_shape=[shape(TILE, TILE)] * 2, in_spec...  1.19 us
    pallas_call x1, Pallas kernels, per_device(): pl.pallas_call(weave_kernel, out_shape=[shape(5, 2, TILE, LANES), shape(5...  1.14 us
  transfers between devices with their start and end apart: 6, of which 2 were waited for; matrix products, arithmetic and copies ran while one was open for 0% of the time, Pallas kernels for 9%

profile of v21, /device:TPU:0, one launch (start us, length us, event | category | flops | bytes accessed | tf_op | source)
XLA Modules:
  0.0 53.5 jit_solution(15746865516353876756)
XLA Ops:
  0.6 0.0 copy-start.1
  0.6 0.0 copy-start
  0.7 0.0 copy-start.3
  0.7 0.0 copy-start.4
  0.7 3.1 %pack.1 = (f32[128,128]{1,0:T(8,128)}, f32[128,128]{1,0:T(8,128)}, f32[8,48,128]{2,1,0:T(8,128)}) custom-call(s32[4,8]{1,0:T(4,128)} %bitcast.4, f32[4,4096]{1,0:T(4,128)} %control.1, f32[256,256]{1,0:T(8,128)} %thick.3, f32[2,256,256]{2,1,0:T(8,128)} %drive.3, f32[2,256,256]{2,1,0:T(8,128)} %obs.3), custom_call_target="tpu_custom_call" | custom-call | tf_op jit(solution)/shard_map/pack/pallas_call | solution.py:659
  3.8 4.9 %all-to-all-start = ((f32[8,48,128]{2,1,0:T(8,128)}), f32[8,48,128]{2,1,0:T(8,128)S(1)}, u32[]{:S(2)}, u32[]{:S(2)}) async-start(f32[8,48,128]{2,1,0:T(8,128)} %get-tuple-element.22), calls=%async_computation | async-start | bytes 393216 | tf_op jit(solution)/shard_map/all_to_all | solution.py:676
  8.6 1.9 %collective-permute-start = (f32[128,128]{1,0:T(8,128)}, f32[128,128]{1,0:T(8,128)S(1)}, u32[]{:S(2)}, u32[]{:S(2)}) collective-permute-start(f32[128,128]{1,0:T(8,128)} %get-tuple-element.27), channel_id=1, source_target_pairs={{0,8},{16,24},{8,0},{24,16},{1,9},{17,25},{9,1},{25,17},{2,10},{18... | collective-permute-start | bytes 196616 | tf_op jit(solution)/shard_map/ppermute | solution.py:654
  10.6 0.7 %collective-permute-start.1 = (f32[128,128]{1,0:T(8,128)}, f32[128,128]{1,0:T(8,128)S(1)}, u32[]{:S(2)}, u32[]{:S(2)}) collective-permute-start(f32[128,128]{1,0:T(8,128)} %get-tuple-element.28), channel_id=1, source_target_pairs={{8,16},{16,8},{9,17},{17,9},{10,18},{18,10},{11,19},{19,11},{12,20... | collective-permute-start | bytes 196616 | tf_op jit(solution)/shard_map/ppermute | solution.py:654
  11.2 0.0 copy-done.1
  11.3 0.0 copy-done
  11.3 0.0 copy-start.2
  11.3 0.9 %copy-done.2 = f32[256,256]{1,0:T(8,128)S(1)} copy-done((f32[256,256]{1,0:T(8,128)S(1)}, f32[256,256]{1,0:T(8,128)}, u32[]{:S(2)}) %copy-start.2) | copy-done | bytes 262168
  12.2 1.1 %weave.1 = (f32[5,2,256,128]{3,2,1,0:T(8,128)S(1)}, f32[5,128,128]{2,1,0:T(8,128)S(1)}, f32[2,3,64,128]{3,2,1,0:T(8,128)S(1)}) custom-call(f32[256,256]{1,0:T(8,128)S(1)} %copy-done.2, f32[2,256,256]{2,1,0:T(8,128)S(1)} %copy-done, f32[2,256,256]{2,1,0:T(8,128)S(1)} %copy-done.1), custom_call_target="tpu_custom_call" | custom-call | tf_op jit(solution)/shard_map/weave/pallas_call | solution.py:678
  13.4 0.2 collective-permute-done.first_col
  13.6 0.0 collective-permute-done.1.second_col
  13.6 0.1 rows.1
  13.7 0.1 collective-permute-start.2
  13.8 0.7 %collective-permute-start.3 = (f32[160,128]{1,0:T(8,128)S(1)}, f32[160,128]{1,0:T(8,128)S(1)}, u32[]{:S(2)}, u32[]{:S(2)}) collective-permute-start(f32[160,128]{1,0:T(8,128)S(1)} %get-tuple-element.33), channel_id=1, source_target_pairs={{1,2},{3,4},{5,6},{2,1},{4,3},{6,5},{9,10},{11,12},{13,14},{10,9},... | collective-permute-start | bytes 245768 | tf_op jit(solution)/shard_map/ppermute | solution.py:654
  14.5 0.4 all-to-all-done.parcels
  14.9 0.0 copy-done.3
  14.9 0.0 copy-done.4
  14.9 0.9 %friction.1 = (f32[784,128]{1,0:T(8,128)S(1)}, f32[784,128]{1,0:T(8,128)S(1)}, s32[16,8,128]{2,1,0:T(8,128)S(1)}) custom-call(s32[4,8]{1,0:T(4,128)S(1)} %bitcast.5, s32[4,8]{1,0:T(4,128)S(1)} %bitcast.6, f32[8,48,128]{2,1,0:T(8,128)S(1)} %all-to-all-done.parcels), custom_call_target="tpu_custom_call" | custom-call | tf_op jit(solution)/shard_map/friction/pallas_call | solution.py:695
  15.7 1.5 %setup.1 = (f32[5,784,128]{2,1,0:T(8,128)S(1)}, f32[2,784,128]{2,1,0:T(8,128)S(1)}) custom-call(f32[784,128]{1,0:T(8,128)S(1)} %get-tuple-element.23.fr, f32[784,128]{1,0:T(8,128)S(1)} %get-tuple-element.24.ice, f32[5,2,256,128]{3,2,1,0:T(8,128)S(1)} %get-tuple-element.25.woven, f32[5,128,128]{2,1,0:T(8,128)S(1)} %get-tuple-element.26.own_sides, ...), custom_call_target="tpu_custom_call" | custom-call | tf_op jit(solution)/shard_map/setup/pallas_call | solution.py:705
  17.3 0.0 collective-permute-done.2.first_row
  17.3 0.0 collective-permute-done.3.second_row
  17.3 11.5 %model.1 = (f32[2,784,128]{2,1,0:T(8,128)S(1)}, f32[16,32,128]{2,1,0:T(8,128)S(1)}) custom-call(f32[784,128]{1,0:T(8,128)S(1)} %get-tuple-element.23.fr, f32[784,128]{1,0:T(8,128)S(1)} %get-tuple-element.24.ice, f32[5,784,128]{2,1,0:T(8,128)S(1)} %get-tuple-element.29.ext_in, f32[2,784,128]{2,1,0:T(8,128)S(1)} %get-tuple-element.30.vel_in, ...), custom_call_target="tpu_custom_call" | custom-call | tf_op jit(solution)/shard_map/model/pallas_call | solution.py:719
  28.8 22.4 %all_to_all.10.gathered = f32[16,32,128]{2,1,0:T(8,128)S(1)} all-to-all(f32[16,32,128]{2,1,0:T(8,128)S(1)} %get-tuple-element.38), channel_id=1, replica_groups={{0,2,4,6,8,10,12,14,16,18,20,22,24,26,28,30},{1,3,5,7,9,11,13,15,17,19,..., dimensions={0} | all-to-all | bytes 524288 | tf_op jit(solution)/shard_map/all_to_all | solution.py:746
  51.2 0.3 pick.1
  51.5 0.1 collective-permute-start.4
  51.6 1.2 %unweave.1 = (f32[256,256]{1,0:T(8,128)}, f32[256,256]{1,0:T(8,128)}) custom-call(f32[2,784,128]{2,1,0:T(8,128)S(1)} %get-tuple-element.34.vel), custom_call_target="tpu_custom_call" | custom-call | tf_op jit(solution)/shard_map/unweave/pallas_call | solution.py:735
  52.8 0.0 collective-permute-done.4
  52.8 0.6 %add.3 = f32[4,4096]{1,0:T(4,128)} add(f32[4,4096]{1,0:T(4,128)S(1)} %get-tuple-element.39, f32[4,4096]{1,0:T(4,128)S(1)} %collective-permute-done.4) | non-fusion elementwise | flops 16384 | bytes 196608 | tf_op jit(solution)/shard_map/add | solution.py:755
Async XLA Ops:
  0.6 10.6 %copy-start.1 = (f32[2,256,256]{2,1,0:T(8,128)S(1)}, f32[2,256,256]{2,1,0:T(8,128)}, u32[]{:S(2)}) copy-start(f32[2,256,256]{2,1,0:T(8,128)} %obs.3) | copy-start | bytes 1572868
  0.6 10.6 %copy-start = (f32[2,256,256]{2,1,0:T(8,128)S(1)}, f32[2,256,256]{2,1,0:T(8,128)}, u32[]{:S(2)}) copy-start(f32[2,256,256]{2,1,0:T(8,128)} %drive.3) | copy-start | bytes 1572868
  0.7 14.2 %copy-start.3 = (s32[8,4,1]{0,2,1:T(1,128)S(1)}, s32[8,4,1]{0,2,1:T(1,128)}, u32[]{:S(2)}) copy-start(s32[8,4,1]{0,2,1:T(1,128)} %param.11) | copy-start | bytes 388
  0.7 14.2 %copy-start.4 = (s32[8,4]{0,1:T(4,128)S(1)}, s32[8,4]{0,1:T(4,128)}, u32[]{:S(2)}) copy-start(s32[8,4]{0,1:T(4,128)} %param.10) | copy-start | bytes 388
  3.8 11.1 %all-to-all-start = ((f32[8,48,128]{2,1,0:T(8,128)}), f32[8,48,128]{2,1,0:T(8,128)S(1)}, u32[]{:S(2)}, u32[]{:S(2)}) async-start(f32[8,48,128]{2,1,0:T(8,128)} %get-tuple-element.22), calls=%async_computation | async-start | bytes 393216 | tf_op jit(solution)/shard_map/all_to_all | solution.py:676
  8.6 4.9 %collective-permute-start = (f32[128,128]{1,0:T(8,128)}, f32[128,128]{1,0:T(8,128)S(1)}, u32[]{:S(2)}, u32[]{:S(2)}) collective-permute-start(f32[128,128]{1,0:T(8,128)} %get-tuple-element.27), channel_id=1, source_target_pairs={{0,8},{16,24},{8,0},{24,16},{1,9},{17,25},{9,1},{25,17},{2,10},{18... | collective-permute-start | bytes 196616 | tf_op jit(solution)/shard_map/ppermute | solution.py:654
  10.6 3.0 %collective-permute-start.1 = (f32[128,128]{1,0:T(8,128)}, f32[128,128]{1,0:T(8,128)S(1)}, u32[]{:S(2)}, u32[]{:S(2)}) collective-permute-start(f32[128,128]{1,0:T(8,128)} %get-tuple-element.28), channel_id=1, source_target_pairs={{8,16},{16,8},{9,17},{17,9},{10,18},{18,10},{11,19},{19,11},{12,20... | collective-permute-start | bytes 196616 | tf_op jit(solution)/shard_map/ppermute | solution.py:654
  11.3 1.0 %copy-start.2 = (f32[256,256]{1,0:T(8,128)S(1)}, f32[256,256]{1,0:T(8,128)}, u32[]{:S(2)}) copy-start(f32[256,256]{1,0:T(8,128)} %thick.3) | copy-start | bytes 786436
  13.7 3.6 %collective-permute-start.2 = (f32[160,128]{1,0:T(8,128)S(1)}, f32[160,128]{1,0:T(8,128)S(1)}, u32[]{:S(2)}, u32[]{:S(2)}) collective-permute-start(f32[160,128]{1,0:T(8,128)S(1)} %get-tuple-element.32), channel_id=1, source_target_pairs={{0,1},{2,3},{4,5},{6,7},{1,0},{3,2},{5,4},{7,6},{8,9},{10,11},{12,... | collective-permute-start | bytes 245768 | tf_op jit(solution)/shard_map/ppermute | solution.py:654
  13.8 3.5 %collective-permute-start.3 = (f32[160,128]{1,0:T(8,128)S(1)}, f32[160,128]{1,0:T(8,128)S(1)}, u32[]{:S(2)}, u32[]{:S(2)}) collective-permute-start(f32[160,128]{1,0:T(8,128)S(1)} %get-tuple-element.33), channel_id=1, source_target_pairs={{1,2},{3,4},{5,6},{2,1},{4,3},{6,5},{9,10},{11,12},{13,14},{10,9},... | collective-permute-start | bytes 245768 | tf_op jit(solution)/shard_map/ppermute | solution.py:654
  51.5 1.3 %collective-permute-start.4 = (f32[4,4096]{1,0:T(4,128)S(1)}, f32[4,4096]{1,0:T(4,128)S(1)}, u32[]{:S(2)}, u32[]{:S(2)}) collective-permute-start(f32[4,4096]{1,0:T(4,128)S(1)} %get-tuple-element.40), channel_id=1, source_target_pairs={{0,1},{1,0},{2,3},{3,2},{4,5},{5,4},{6,7},{7,6},{8,9},{9,8},{10,11... | collective-permute-start | bytes 196616 | tf_op jit(solution)/shard_map/ppermute | solution.py:755

commit v22 on v21

--- a/solution.py
+++ b/solution.py
@@ -567,13 +567,7 @@
     over_rows("tile", read_gradient, gradient)
     join_parts(visc, ((0,),), False)
     down = sum(visc[0, pl.ds(tile + TOP + j, CT, stride=4), :] for tile in MAIN for j in range(4))
-    k = lax.broadcasted_iota(jnp.int32, (LANES, LANES), 0)
-    total = jnp.dot(
-        down,
-        (k // 2 == lanes_of(LANES) % CT).astype(jnp.float32),
-        precision=lax.Precision.HIGHEST,
-        preferred_element_type=jnp.float32,
-    )
+    total = gather(down + turn(down, 1, 0), 2 * (lanes_of(CT) % CT))
     small[...] = total
     packed = jnp.where(
         lanes_of(PACK) < CT, small[pl.ds(0, PACK, stride=2), :], small[pl.ds(1, PACK, stride=2), :]
@@ -649,10 +643,10 @@
     def swap(axis, cells_first, cells_second):
         count = lax.axis_size(axis)
         received = []
-        for cells, low in ((cells_second, 1), (cells_first, 0)):
+        for cells, low in ((cells_first, 0), (cells_second, 1)):
             pairs = [(i, i + 1) for i in range(low, count - 1, 2)]
             received.append(lax.ppermute(cells, axis, pairs + [(j, i) for i, j in pairs]))
-        return received[1], received[0]
+        return received
 
     fields = thickness, driving, observed
     owned = control.shape[0]

time: 53.7 us -> 53.7 us (level)
  no operation moved by 1% of the time
where the time goes in v22:
time: 53.7 us; the launch traced here: 53.4 us
  blocking collectives  22.3 us (42%)
  Pallas kernels  19.6 us (36%)
  starting transfers between devices  8.55 us (16%)
  local copies, waits for them, and re-layouts  0.96 us (2%)
  between operations  0.79 us (1%)
  other arithmetic  0.65 us (1%)
    all_to_all x1, blocking collectives, per_device(): lax.all_to_all(sums, ('gx', 'gy'), 0, 0, tiled=True, axis_index_groups=sa...  22.3 us
    pallas_call x1, Pallas kernels, per_device(): pl.pallas_call(model_kernel, out_shape=(shape(2, ALL_ROWS, LANES), shape(...  11.5 us
    all_to_all x1, starting transfers between devices, per_device(): parcels = lax.all_to_all(parcels, 'gy', 0, 0, tiled=True)  4.99 us
    ppermute x4, starting transfers between devices, swap(): lax.ppermute(cells, axis, pairs + [(j, i) for i, j in pairs])  3.49 us
    pallas_call x1, Pallas kernels, per_device(): pl.pallas_call(pack_kernel, out_shape=[shape(HALF, LANES)] * 2 + [shape(r...  2.99 us
    pallas_call x1, Pallas kernels, per_device(): pl.pallas_call(setup_kernel, out_shape=[shape(5, ALL_ROWS, LANES), shape(...  1.51 us
    pallas_call x1, Pallas kernels, per_device(): pl.pallas_call(unweave_kernel, out_shape=[shape(TILE, TILE)] * 2, in_spec...  1.19 us
    pallas_call x1, Pallas kernels, per_device(): pl.pallas_call(weave_kernel, out_shape=[shape(5, 2, TILE, LANES), shape(5...  1.14 us
  transfers between devices with their start and end apart: 6, of which 2 were waited for; matrix products, arithmetic and copies ran while one was open for 0% of the time, Pallas kernels for 9%

profile of v22, /device:TPU:0, one launch (start us, length us, event | category | flops | bytes accessed | tf_op | source)
XLA Modules:
  0.0 53.4 jit_solution(9495653695547668649)
XLA Ops:
  0.6 0.0 copy-start.1
  0.6 0.0 copy-start
  0.7 0.0 copy-start.3
  0.7 0.0 copy-start.4
  0.7 3.0 %pack.1 = (f32[128,128]{1,0:T(8,128)}, f32[128,128]{1,0:T(8,128)}, f32[8,48,128]{2,1,0:T(8,128)}) custom-call(s32[4,8]{1,0:T(4,128)} %bitcast.4, f32[4,4096]{1,0:T(4,128)} %control.1, f32[256,256]{1,0:T(8,128)} %thick.3, f32[2,256,256]{2,1,0:T(8,128)} %drive.3, f32[2,256,256]{2,1,0:T(8,128)} %obs.3), custom_call_target="tpu_custom_call" | custom-call | tf_op jit(solution)/shard_map/pack/pallas_call | solution.py:653
  3.7 5.0 %all-to-all-start = ((f32[8,48,128]{2,1,0:T(8,128)}), f32[8,48,128]{2,1,0:T(8,128)S(1)}, u32[]{:S(2)}, u32[]{:S(2)}) async-start(f32[8,48,128]{2,1,0:T(8,128)} %get-tuple-element.22), calls=%async_computation | async-start | bytes 393216 | tf_op jit(solution)/shard_map/all_to_all | solution.py:670
  8.7 2.1 %collective-permute-start = (f32[128,128]{1,0:T(8,128)}, f32[128,128]{1,0:T(8,128)S(1)}, u32[]{:S(2)}, u32[]{:S(2)}) collective-permute-start(f32[128,128]{1,0:T(8,128)} %get-tuple-element.27), channel_id=1, source_target_pairs={{0,8},{16,24},{8,0},{24,16},{1,9},{17,25},{9,1},{25,17},{2,10},{18... | collective-permute-start | bytes 196616 | tf_op jit(solution)/shard_map/ppermute | solution.py:648
  10.7 0.7 %collective-permute-start.1 = (f32[128,128]{1,0:T(8,128)}, f32[128,128]{1,0:T(8,128)S(1)}, u32[]{:S(2)}, u32[]{:S(2)}) collective-permute-start(f32[128,128]{1,0:T(8,128)} %get-tuple-element.28), channel_id=1, source_target_pairs={{8,16},{16,8},{9,17},{17,9},{10,18},{18,10},{11,19},{19,11},{12,20... | collective-permute-start | bytes 196616 | tf_op jit(solution)/shard_map/ppermute | solution.py:648
  11.4 0.0 copy-done.1
  11.4 0.0 copy-done
  11.4 0.0 copy-start.2
  11.4 0.9 %copy-done.2 = f32[256,256]{1,0:T(8,128)S(1)} copy-done((f32[256,256]{1,0:T(8,128)S(1)}, f32[256,256]{1,0:T(8,128)}, u32[]{:S(2)}) %copy-start.2) | copy-done | bytes 262168
  12.3 1.1 %weave.1 = (f32[5,2,256,128]{3,2,1,0:T(8,128)S(1)}, f32[5,128,128]{2,1,0:T(8,128)S(1)}, f32[2,3,64,128]{3,2,1,0:T(8,128)S(1)}) custom-call(f32[256,256]{1,0:T(8,128)S(1)} %copy-done.2, f32[2,256,256]{2,1,0:T(8,128)S(1)} %copy-done, f32[2,256,256]{2,1,0:T(8,128)S(1)} %copy-done.1), custom_call_target="tpu_custom_call" | custom-call | tf_op jit(solution)/shard_map/weave/pallas_call | solution.py:672
  13.5 0.2 collective-permute-done.first_col
  13.7 0.0 collective-permute-done.1.second_col
  13.7 0.1 rows.1
  13.8 0.1 collective-permute-start.2
  13.9 0.7 %collective-permute-start.3 = (f32[160,128]{1,0:T(8,128)S(1)}, f32[160,128]{1,0:T(8,128)S(1)}, u32[]{:S(2)}, u32[]{:S(2)}) collective-permute-start(f32[160,128]{1,0:T(8,128)S(1)} %get-tuple-element.33), channel_id=1, source_target_pairs={{1,2},{3,4},{5,6},{2,1},{4,3},{6,5},{9,10},{11,12},{13,14},{10,9},... | collective-permute-start | bytes 245768 | tf_op jit(solution)/shard_map/ppermute | solution.py:648
  14.6 0.3 all-to-all-done.parcels
  14.9 0.0 copy-done.3
  14.9 0.0 copy-done.4
  14.9 0.9 %friction.1 = (f32[784,128]{1,0:T(8,128)S(1)}, f32[784,128]{1,0:T(8,128)S(1)}, s32[16,8,128]{2,1,0:T(8,128)S(1)}) custom-call(s32[4,8]{1,0:T(4,128)S(1)} %bitcast.5, s32[4,8]{1,0:T(4,128)S(1)} %bitcast.6, f32[8,48,128]{2,1,0:T(8,128)S(1)} %all-to-all-done.parcels), custom_call_target="tpu_custom_call" | custom-call | tf_op jit(solution)/shard_map/friction/pallas_call | solution.py:689
  15.8 1.5 %setup.1 = (f32[5,784,128]{2,1,0:T(8,128)S(1)}, f32[2,784,128]{2,1,0:T(8,128)S(1)}) custom-call(f32[784,128]{1,0:T(8,128)S(1)} %get-tuple-element.23.fr, f32[784,128]{1,0:T(8,128)S(1)} %get-tuple-element.24.ice, f32[5,2,256,128]{3,2,1,0:T(8,128)S(1)} %get-tuple-element.25.woven, f32[5,128,128]{2,1,0:T(8,128)S(1)} %get-tuple-element.26.own_sides, ...), custom_call_target="tpu_custom_call" | custom-call | tf_op jit(solution)/shard_map/setup/pallas_call | solution.py:699
  17.3 0.0 collective-permute-done.2.first_row
  17.3 0.0 collective-permute-done.3.second_row
  17.3 11.5 %model.1 = (f32[2,784,128]{2,1,0:T(8,128)S(1)}, f32[16,32,128]{2,1,0:T(8,128)S(1)}) custom-call(f32[784,128]{1,0:T(8,128)S(1)} %get-tuple-element.23.fr, f32[784,128]{1,0:T(8,128)S(1)} %get-tuple-element.24.ice, f32[5,784,128]{2,1,0:T(8,128)S(1)} %get-tuple-element.29.ext_in, f32[2,784,128]{2,1,0:T(8,128)S(1)} %get-tuple-element.30.vel_in, ...), custom_call_target="tpu_custom_call" | custom-call | tf_op jit(solution)/shard_map/model/pallas_call | solution.py:713
  28.8 22.3 %all_to_all.10.gathered = f32[16,32,128]{2,1,0:T(8,128)S(1)} all-to-all(f32[16,32,128]{2,1,0:T(8,128)S(1)} %get-tuple-element.38), channel_id=1, replica_groups={{0,2,4,6,8,10,12,14,16,18,20,22,24,26,28,30},{1,3,5,7,9,11,13,15,17,19,..., dimensions={0} | all-to-all | bytes 524288 | tf_op jit(solution)/shard_map/all_to_all | solution.py:740
  51.1 0.3 pick.1
  51.4 0.1 collective-permute-start.4
  51.5 1.2 %unweave.1 = (f32[256,256]{1,0:T(8,128)}, f32[256,256]{1,0:T(8,128)}) custom-call(f32[2,784,128]{2,1,0:T(8,128)S(1)} %get-tuple-element.34.vel), custom_call_target="tpu_custom_call" | custom-call | tf_op jit(solution)/shard_map/unweave/pallas_call | solution.py:729
  52.7 0.0 collective-permute-done.4
  52.8 0.6 %add.3 = f32[4,4096]{1,0:T(4,128)} add(f32[4,4096]{1,0:T(4,128)S(1)} %get-tuple-element.39, f32[4,4096]{1,0:T(4,128)S(1)} %collective-permute-done.4) | non-fusion elementwise | flops 16384 | bytes 196608 | tf_op jit(solution)/shard_map/add | solution.py:749
Async XLA Ops:
  0.6 10.7 %copy-start.1 = (f32[2,256,256]{2,1,0:T(8,128)S(1)}, f32[2,256,256]{2,1,0:T(8,128)}, u32[]{:S(2)}) copy-start(f32[2,256,256]{2,1,0:T(8,128)} %obs.3) | copy-start | bytes 1572868
  0.6 10.7 %copy-start = (f32[2,256,256]{2,1,0:T(8,128)S(1)}, f32[2,256,256]{2,1,0:T(8,128)}, u32[]{:S(2)}) copy-start(f32[2,256,256]{2,1,0:T(8,128)} %drive.3) | copy-start | bytes 1572868
  0.7 14.2 %copy-start.3 = (s32[8,4,1]{0,2,1:T(1,128)S(1)}, s32[8,4,1]{0,2,1:T(1,128)}, u32[]{:S(2)}) copy-start(s32[8,4,1]{0,2,1:T(1,128)} %param.11) | copy-start | bytes 388
  0.7 14.2 %copy-start.4 = (s32[8,4]{0,1:T(4,128)S(1)}, s32[8,4]{0,1:T(4,128)}, u32[]{:S(2)}) copy-start(s32[8,4]{0,1:T(4,128)} %param.10) | copy-start | bytes 388
  3.7 11.2 %all-to-all-start = ((f32[8,48,128]{2,1,0:T(8,128)}), f32[8,48,128]{2,1,0:T(8,128)S(1)}, u32[]{:S(2)}, u32[]{:S(2)}) async-start(f32[8,48,128]{2,1,0:T(8,128)} %get-tuple-element.22), calls=%async_computation | async-start | bytes 393216 | tf_op jit(solution)/shard_map/all_to_all | solution.py:670
  8.7 5.0 %collective-permute-start = (f32[128,128]{1,0:T(8,128)}, f32[128,128]{1,0:T(8,128)S(1)}, u32[]{:S(2)}, u32[]{:S(2)}) collective-permute-start(f32[128,128]{1,0:T(8,128)} %get-tuple-element.27), channel_id=1, source_target_pairs={{0,8},{16,24},{8,0},{24,16},{1,9},{17,25},{9,1},{25,17},{2,10},{18... | collective-permute-start | bytes 196616 | tf_op jit(solution)/shard_map/ppermute | solution.py:648
  10.7 3.0 %collective-permute-start.1 = (f32[128,128]{1,0:T(8,128)}, f32[128,128]{1,0:T(8,128)S(1)}, u32[]{:S(2)}, u32[]{:S(2)}) collective-permute-start(f32[128,128]{1,0:T(8,128)} %get-tuple-element.28), channel_id=1, source_target_pairs={{8,16},{16,8},{9,17},{17,9},{10,18},{18,10},{11,19},{19,11},{12,20... | collective-permute-start | bytes 196616 | tf_op jit(solution)/shard_map/ppermute | solution.py:648
  11.4 1.0 %copy-start.2 = (f32[256,256]{1,0:T(8,128)S(1)}, f32[256,256]{1,0:T(8,128)}, u32[]{:S(2)}) copy-start(f32[256,256]{1,0:T(8,128)} %thick.3) | copy-start | bytes 786436
  13.8 3.5 %collective-permute-start.2 = (f32[160,128]{1,0:T(8,128)S(1)}, f32[160,128]{1,0:T(8,128)S(1)}, u32[]{:S(2)}, u32[]{:S(2)}) collective-permute-start(f32[160,128]{1,0:T(8,128)S(1)} %get-tuple-element.32), channel_id=1, source_target_pairs={{0,1},{2,3},{4,5},{6,7},{1,0},{3,2},{5,4},{7,6},{8,9},{10,11},{12,... | collective-permute-start | bytes 245768 | tf_op jit(solution)/shard_map/ppermute | solution.py:648
  13.9 3.4 %collective-permute-start.3 = (f32[160,128]{1,0:T(8,128)S(1)}, f32[160,128]{1,0:T(8,128)S(1)}, u32[]{:S(2)}, u32[]{:S(2)}) collective-permute-start(f32[160,128]{1,0:T(8,128)S(1)} %get-tuple-element.33), channel_id=1, source_target_pairs={{1,2},{3,4},{5,6},{2,1},{4,3},{6,5},{9,10},{11,12},{13,14},{10,9},... | collective-permute-start | bytes 245768 | tf_op jit(solution)/shard_map/ppermute | solution.py:648
  51.4 1.3 %collective-permute-start.4 = (f32[4,4096]{1,0:T(4,128)S(1)}, f32[4,4096]{1,0:T(4,128)S(1)}, u32[]{:S(2)}, u32[]{:S(2)}) collective-permute-start(f32[4,4096]{1,0:T(4,128)S(1)} %get-tuple-element.40), channel_id=1, source_target_pairs={{0,1},{1,0},{2,3},{3,2},{4,5},{5,4},{6,7},{7,6},{8,9},{9,8},{10,11... | collective-permute-start | bytes 196616 | tf_op jit(solution)/shard_map/ppermute | solution.py:749

commit v23 on v22

--- a/solution.py
+++ b/solution.py
@@ -231,7 +231,7 @@
 
 
 def block_groups(row, main, side_row, side):
-    step = 32 if main % 32 == 0 else 24
+    step = 64 if main % 32 == 0 else 48
     first = side // 16 * 8 if side > 24 else side
     groups = [(MAIN, row + g, min(step, main - g)) for g in range(0, main, step)]
     groups[1:1] = [(SIDES, side_row, first)]

time: 53.7 us -> 53.9 us (level)
  waiting for transfers between devices: 0.53 us -> 1.22 us
  blocking collectives: 22.3 us -> 21.7 us
    ppermute x4, starting transfers between devices: 3.49 us -> 2.79 us  [swap(): lax.ppermute(cells, axis, pairs + [(j, i) for i, j in pairs])]
    all_to_all x1, blocking collectives: 22.3 us -> 21.7 us  [per_device(): lax.all_to_all(sums, ('gx', 'gy'), 0, 0, tiled=True, axis_index_groups=sa...]
where the time goes in v23:
time: 53.9 us; the launch traced here: 53.5 us
  blocking collectives  21.7 us (40%)
  Pallas kernels  19.8 us (37%)
  starting transfers between devices  8.31 us (15%)
  waiting for transfers between devices  1.22 us (2%)
  local copies, waits for them, and re-layouts  0.96 us (2%)
  between operations  0.8 us (1%)
  other arithmetic  0.65 us (1%)
    all_to_all x1, blocking collectives, per_device(): lax.all_to_all(sums, ('gx', 'gy'), 0, 0, tiled=True, axis_index_groups=sa...  21.7 us
    pallas_call x1, Pallas kernels, per_device(): pl.pallas_call(model_kernel, out_shape=(shape(2, ALL_ROWS, LANES), shape(...  11.8 us
    all_to_all x1, starting transfers between devices, per_device(): parcels = lax.all_to_all(parcels, 'gy', 0, 0, tiled=True)  5.45 us
    ppermute x4, starting transfers between devices, swap(): lax.ppermute(cells, axis, pairs + [(j, i) for i, j in pairs])  2.79 us
    pallas_call x1, Pallas kernels, per_device(): pl.pallas_call(pack_kernel, out_shape=[shape(HALF, LANES)] * 2 + [shape(r...  2.78 us
    pallas_call x1, Pallas kernels, per_device(): pl.pallas_call(setup_kernel, out_shape=[shape(5, ALL_ROWS, LANES), shape(...  1.62 us
    pallas_call x1, Pallas kernels, per_device(): pl.pallas_call(unweave_kernel, out_shape=[shape(TILE, TILE)] * 2, in_spec...  1.19 us
    pallas_call x1, Pallas kernels, per_device(): pl.pallas_call(weave_kernel, out_shape=[shape(5, 2, TILE, LANES), shape(5...  1.14 us
  transfers between devices with their start and end apart: 6, of which 2 were waited for; matrix products, arithmetic and copies ran while one was open for 0% of the time, Pallas kernels for 9%

profile of v23, /device:TPU:0, one launch (start us, length us, event | category | flops | bytes accessed | tf_op | source)
XLA Modules:
  0.0 53.5 jit_solution(18195657947351380601)
XLA Ops:
  0.6 0.0 copy-start.1
  0.6 0.0 copy-start
  0.7 0.0 copy-start.3
  0.7 0.0 copy-start.4
  0.7 2.8 %pack.1 = (f32[128,128]{1,0:T(8,128)}, f32[128,128]{1,0:T(8,128)}, f32[8,48,128]{2,1,0:T(8,128)}) custom-call(s32[4,8]{1,0:T(4,128)} %bitcast.4, f32[4,4096]{1,0:T(4,128)} %control.1, f32[256,256]{1,0:T(8,128)} %thick.3, f32[2,256,256]{2,1,0:T(8,128)} %drive.3, f32[2,256,256]{2,1,0:T(8,128)} %obs.3), custom_call_target="tpu_custom_call" | custom-call | tf_op jit(solution)/shard_map/pack/pallas_call | solution.py:653
  3.5 5.4 %all-to-all-start = ((f32[8,48,128]{2,1,0:T(8,128)}), f32[8,48,128]{2,1,0:T(8,128)S(1)}, u32[]{:S(2)}, u32[]{:S(2)}) async-start(f32[8,48,128]{2,1,0:T(8,128)} %get-tuple-element.22), calls=%async_computation | async-start | bytes 393216 | tf_op jit(solution)/shard_map/all_to_all | solution.py:670
  8.9 1.4 %collective-permute-start = (f32[128,128]{1,0:T(8,128)}, f32[128,128]{1,0:T(8,128)S(1)}, u32[]{:S(2)}, u32[]{:S(2)}) collective-permute-start(f32[128,128]{1,0:T(8,128)} %get-tuple-element.27), channel_id=1, source_target_pairs={{0,8},{16,24},{8,0},{24,16},{1,9},{17,25},{9,1},{25,17},{2,10},{18... | collective-permute-start | bytes 196616 | tf_op jit(solution)/shard_map/ppermute | solution.py:648
  10.3 0.7 %collective-permute-start.1 = (f32[128,128]{1,0:T(8,128)}, f32[128,128]{1,0:T(8,128)S(1)}, u32[]{:S(2)}, u32[]{:S(2)}) collective-permute-start(f32[128,128]{1,0:T(8,128)} %get-tuple-element.28), channel_id=1, source_target_pairs={{8,16},{16,8},{9,17},{17,9},{10,18},{18,10},{11,19},{19,11},{12,20... | collective-permute-start | bytes 196616 | tf_op jit(solution)/shard_map/ppermute | solution.py:648
  11.0 0.0 copy-done.1
  11.0 0.0 copy-done
  11.0 0.0 copy-start.2
  11.0 0.9 %copy-done.2 = f32[256,256]{1,0:T(8,128)S(1)} copy-done((f32[256,256]{1,0:T(8,128)S(1)}, f32[256,256]{1,0:T(8,128)}, u32[]{:S(2)}) %copy-start.2) | copy-done | bytes 262168
  11.9 1.1 %weave.1 = (f32[5,2,256,128]{3,2,1,0:T(8,128)S(1)}, f32[5,128,128]{2,1,0:T(8,128)S(1)}, f32[2,3,64,128]{3,2,1,0:T(8,128)S(1)}) custom-call(f32[256,256]{1,0:T(8,128)S(1)} %copy-done.2, f32[2,256,256]{2,1,0:T(8,128)S(1)} %copy-done, f32[2,256,256]{2,1,0:T(8,128)S(1)} %copy-done.1), custom_call_target="tpu_custom_call" | custom-call | tf_op jit(solution)/shard_map/weave/pallas_call | solution.py:672
  13.1 0.5 collective-permute-done.first_col
  13.6 0.0 collective-permute-done.1.second_col
  13.6 0.1 rows.1
  13.7 0.1 collective-permute-start.2
  13.8 0.7 %collective-permute-start.3 = (f32[160,128]{1,0:T(8,128)S(1)}, f32[160,128]{1,0:T(8,128)S(1)}, u32[]{:S(2)}, u32[]{:S(2)}) collective-permute-start(f32[160,128]{1,0:T(8,128)S(1)} %get-tuple-element.33), channel_id=1, source_target_pairs={{1,2},{3,4},{5,6},{2,1},{4,3},{6,5},{9,10},{11,12},{13,14},{10,9},... | collective-permute-start | bytes 245768 | tf_op jit(solution)/shard_map/ppermute | solution.py:648
  14.5 0.6 %all-to-all-done.parcels = f32[8,48,128]{2,1,0:T(8,128)S(1)} async-done(((f32[8,48,128]{2,1,0:T(8,128)}), f32[8,48,128]{2,1,0:T(8,128)S(1)}, u32[]{:S(2)}, u32[]{:S(2)}) %all-to-all-start) | async-done | bytes 196640 | tf_op jit(solution)/shard_map/all_to_all | solution.py:670
  15.1 0.0 copy-done.3
  15.1 0.0 copy-done.4
  15.1 0.9 %friction.1 = (f32[784,128]{1,0:T(8,128)S(1)}, f32[784,128]{1,0:T(8,128)S(1)}, s32[16,8,128]{2,1,0:T(8,128)S(1)}) custom-call(s32[4,8]{1,0:T(4,128)S(1)} %bitcast.5, s32[4,8]{1,0:T(4,128)S(1)} %bitcast.6, f32[8,48,128]{2,1,0:T(8,128)S(1)} %all-to-all-done.parcels), custom_call_target="tpu_custom_call" | custom-call | tf_op jit(solution)/shard_map/friction/pallas_call | solution.py:689
  16.0 1.6 %setup.1 = (f32[5,784,128]{2,1,0:T(8,128)S(1)}, f32[2,784,128]{2,1,0:T(8,128)S(1)}) custom-call(f32[784,128]{1,0:T(8,128)S(1)} %get-tuple-element.23.fr, f32[784,128]{1,0:T(8,128)S(1)} %get-tuple-element.24.ice, f32[5,2,256,128]{3,2,1,0:T(8,128)S(1)} %get-tuple-element.25.woven, f32[5,128,128]{2,1,0:T(8,128)S(1)} %get-tuple-element.26.own_sides, ...), custom_call_target="tpu_custom_call" | custom-call | tf_op jit(solution)/shard_map/setup/pallas_call | solution.py:699
  17.6 0.0 collective-permute-done.2.first_row
  17.6 0.0 collective-permute-done.3.second_row
  17.7 11.8 %model.1 = (f32[2,784,128]{2,1,0:T(8,128)S(1)}, f32[16,32,128]{2,1,0:T(8,128)S(1)}) custom-call(f32[784,128]{1,0:T(8,128)S(1)} %get-tuple-element.23.fr, f32[784,128]{1,0:T(8,128)S(1)} %get-tuple-element.24.ice, f32[5,784,128]{2,1,0:T(8,128)S(1)} %get-tuple-element.29.ext_in, f32[2,784,128]{2,1,0:T(8,128)S(1)} %get-tuple-element.30.vel_in, ...), custom_call_target="tpu_custom_call" | custom-call | tf_op jit(solution)/shard_map/model/pallas_call | solution.py:713
  29.4 21.7 %all_to_all.10.gathered = f32[16,32,128]{2,1,0:T(8,128)S(1)} all-to-all(f32[16,32,128]{2,1,0:T(8,128)S(1)} %get-tuple-element.38), channel_id=1, replica_groups={{0,2,4,6,8,10,12,14,16,18,20,22,24,26,28,30},{1,3,5,7,9,11,13,15,17,19,..., dimensions={0} | all-to-all | bytes 524288 | tf_op jit(solution)/shard_map/all_to_all | solution.py:740
  51.2 0.3 pick.1
  51.5 0.1 collective-permute-start.4
  51.6 1.2 %unweave.1 = (f32[256,256]{1,0:T(8,128)}, f32[256,256]{1,0:T(8,128)}) custom-call(f32[2,784,128]{2,1,0:T(8,128)S(1)} %get-tuple-element.34.vel), custom_call_target="tpu_custom_call" | custom-call | tf_op jit(solution)/shard_map/unweave/pallas_call | solution.py:729
  52.8 0.0 collective-permute-done.4
  52.8 0.6 %add.3 = f32[4,4096]{1,0:T(4,128)} add(f32[4,4096]{1,0:T(4,128)S(1)} %get-tuple-element.39, f32[4,4096]{1,0:T(4,128)S(1)} %collective-permute-done.4) | non-fusion elementwise | flops 16384 | bytes 196608 | tf_op jit(solution)/shard_map/add | solution.py:749
Async XLA Ops:
  0.6 10.3 %copy-start.1 = (f32[2,256,256]{2,1,0:T(8,128)S(1)}, f32[2,256,256]{2,1,0:T(8,128)}, u32[]{:S(2)}) copy-start(f32[2,256,256]{2,1,0:T(8,128)} %obs.3) | copy-start | bytes 1572868
  0.6 10.3 %copy-start = (f32[2,256,256]{2,1,0:T(8,128)S(1)}, f32[2,256,256]{2,1,0:T(8,128)}, u32[]{:S(2)}) copy-start(f32[2,256,256]{2,1,0:T(8,128)} %drive.3) | copy-start | bytes 1572868
  0.7 14.5 %copy-start.3 = (s32[8,4,1]{0,2,1:T(1,128)S(1)}, s32[8,4,1]{0,2,1:T(1,128)}, u32[]{:S(2)}) copy-start(s32[8,4,1]{0,2,1:T(1,128)} %param.11) | copy-start | bytes 388
  0.7 14.5 %copy-start.4 = (s32[8,4]{0,1:T(4,128)S(1)}, s32[8,4]{0,1:T(4,128)}, u32[]{:S(2)}) copy-start(s32[8,4]{0,1:T(4,128)} %param.10) | copy-start | bytes 388
  3.5 11.7 %all-to-all-start = ((f32[8,48,128]{2,1,0:T(8,128)}), f32[8,48,128]{2,1,0:T(8,128)S(1)}, u32[]{:S(2)}, u32[]{:S(2)}) async-start(f32[8,48,128]{2,1,0:T(8,128)} %get-tuple-element.22), calls=%async_computation | async-start | bytes 393216 | tf_op jit(solution)/shard_map/all_to_all | solution.py:670
  8.9 4.7 %collective-permute-start = (f32[128,128]{1,0:T(8,128)}, f32[128,128]{1,0:T(8,128)S(1)}, u32[]{:S(2)}, u32[]{:S(2)}) collective-permute-start(f32[128,128]{1,0:T(8,128)} %get-tuple-element.27), channel_id=1, source_target_pairs={{0,8},{16,24},{8,0},{24,16},{1,9},{17,25},{9,1},{25,17},{2,10},{18... | collective-permute-start | bytes 196616 | tf_op jit(solution)/shard_map/ppermute | solution.py:648
  10.3 3.3 %collective-permute-start.1 = (f32[128,128]{1,0:T(8,128)}, f32[128,128]{1,0:T(8,128)S(1)}, u32[]{:S(2)}, u32[]{:S(2)}) collective-permute-start(f32[128,128]{1,0:T(8,128)} %get-tuple-element.28), channel_id=1, source_target_pairs={{8,16},{16,8},{9,17},{17,9},{10,18},{18,10},{11,19},{19,11},{12,20... | collective-permute-start | bytes 196616 | tf_op jit(solution)/shard_map/ppermute | solution.py:648
  11.0 1.0 %copy-start.2 = (f32[256,256]{1,0:T(8,128)S(1)}, f32[256,256]{1,0:T(8,128)}, u32[]{:S(2)}) copy-start(f32[256,256]{1,0:T(8,128)} %thick.3) | copy-start | bytes 786436
  13.7 3.9 %collective-permute-start.2 = (f32[160,128]{1,0:T(8,128)S(1)}, f32[160,128]{1,0:T(8,128)S(1)}, u32[]{:S(2)}, u32[]{:S(2)}) collective-permute-start(f32[160,128]{1,0:T(8,128)S(1)} %get-tuple-element.32), channel_id=1, source_target_pairs={{0,1},{2,3},{4,5},{6,7},{1,0},{3,2},{5,4},{7,6},{8,9},{10,11},{12,... | collective-permute-start | bytes 245768 | tf_op jit(solution)/shard_map/ppermute | solution.py:648
  13.8 3.8 %collective-permute-start.3 = (f32[160,128]{1,0:T(8,128)S(1)}, f32[160,128]{1,0:T(8,128)S(1)}, u32[]{:S(2)}, u32[]{:S(2)}) collective-permute-start(f32[160,128]{1,0:T(8,128)S(1)} %get-tuple-element.33), channel_id=1, source_target_pairs={{1,2},{3,4},{5,6},{2,1},{4,3},{6,5},{9,10},{11,12},{13,14},{10,9},... | collective-permute-start | bytes 245768 | tf_op jit(solution)/shard_map/ppermute | solution.py:648
  51.5 1.3 %collective-permute-start.4 = (f32[4,4096]{1,0:T(4,128)S(1)}, f32[4,4096]{1,0:T(4,128)S(1)}, u32[]{:S(2)}, u32[]{:S(2)}) collective-permute-start(f32[4,4096]{1,0:T(4,128)S(1)} %get-tuple-element.40), channel_id=1, source_target_pairs={{0,1},{1,0},{2,3},{3,2},{4,5},{5,4},{6,7},{7,6},{8,9},{9,8},{10,11... | collective-permute-start | bytes 196616 | tf_op jit(solution)/shard_map/ppermute | solution.py:749

commit v24 on v23

--- a/solution.py
+++ b/solution.py
@@ -32,7 +32,7 @@
     "tile": (TOP, 2, 128, TOP, 64, 0, 0),
 }
 FACTORS = 14
-AHEAD = 8
+AHEAD = 16
 PACK = COARSE // LANES
 VMEM_LIMIT = 24 * 1024 * 1024
 PACK_VMEM_LIMIT = 62 * 1024 * 1024
@@ -231,13 +231,10 @@
 
 
 def block_groups(row, main, side_row, side):
-    step = 64 if main % 32 == 0 else 48
-    first = side // 16 * 8 if side > 24 else side
-    groups = [(MAIN, row + g, min(step, main - g)) for g in range(0, main, step)]
-    groups[1:1] = [(SIDES, side_row, first)]
-    if first < side:
-        groups[3:3] = [(SIDES, side_row + first, side - first)]
-    return groups
+    step = 16
+    groups = [(g / main, MAIN, row + g, min(step, main - g)) for g in range(0, main, step)]
+    groups += [((g + 1) / side, SIDES, side_row + g, min(step, side - g)) for g in range(0, side, step)]
+    return [group[1:] for group in sorted(groups, key=lambda group: group[0])]
 
 
 def over_rows(span, read, work):

time: 53.9 us -> 53.3 us (0.989)
  blocking collectives: 21.7 us -> 22.4 us
  Pallas kernels: 19.8 us -> 19.2 us
  waiting for transfers between devices: 1.22 us -> 0.65 us
    all_to_all x1, blocking collectives: 21.7 us -> 22.4 us  [per_device(): lax.all_to_all(sums, ('gx', 'gy'), 0, 0, tiled=True, axis_index_groups=sa...]
    pallas_call x1, Pallas kernels: 11.8 us -> 11.2 us  [per_device(): pl.pallas_call(model_kernel, out_shape=(shape(2, ALL_ROWS, LANES), shape(...]
    ppermute x4, starting transfers between devices: 2.79 us -> 3.37 us  [swap(): lax.ppermute(cells, axis, pairs + [(j, i) for i, j in pairs])]
where the time goes in v24:
time: 53.3 us; the launch traced here: 53.1 us
  blocking collectives  22.4 us (42%)
  Pallas kernels  19.2 us (36%)
  starting transfers between devices  8.43 us (16%)
  local copies, waits for them, and re-layouts  0.96 us (2%)
  between operations  0.79 us (1%)
  waiting for transfers between devices  0.65 us (1%)
  other arithmetic  0.65 us (1%)
    all_to_all x1, blocking collectives, per_device(): lax.all_to_all(sums, ('gx', 'gy'), 0, 0, tiled=True, axis_index_groups=sa...  22.4 us
    pallas_call x1, Pallas kernels, per_device(): pl.pallas_call(model_kernel, out_shape=(shape(2, ALL_ROWS, LANES), shape(...  11.2 us
    all_to_all x1, starting transfers between devices, per_device(): parcels = lax.all_to_all(parcels, 'gy', 0, 0, tiled=True)  4.99 us
    ppermute x4, starting transfers between devices, swap(): lax.ppermute(cells, axis, pairs + [(j, i) for i, j in pairs])  3.37 us
    pallas_call x1, Pallas kernels, per_device(): pl.pallas_call(pack_kernel, out_shape=[shape(HALF, LANES)] * 2 + [shape(r...  2.98 us
    pallas_call x1, Pallas kernels, per_device(): pl.pallas_call(setup_kernel, out_shape=[shape(5, ALL_ROWS, LANES), shape(...  1.46 us
    pallas_call x1, Pallas kernels, per_device(): pl.pallas_call(unweave_kernel, out_shape=[shape(TILE, TILE)] * 2, in_spec...  1.19 us
    pallas_call x1, Pallas kernels, per_device(): pl.pallas_call(weave_kernel, out_shape=[shape(5, 2, TILE, LANES), shape(5...  1.14 us
  transfers between devices with their start and end apart: 6, of which 2 were waited for; matrix products, arithmetic and copies ran while one was open for 0% of the time, Pallas kernels for 9%

profile of v24, /device:TPU:0, one launch (start us, length us, event | category | flops | bytes accessed | tf_op | source)
XLA Modules:
  0.0 53.1 jit_solution(6764673087657198205)
XLA Ops:
  0.6 0.0 copy-start.1
  0.6 0.0 copy-start
  0.7 0.0 copy-start.3
  0.7 0.0 copy-start.4
  0.7 3.0 %pack.1 = (f32[128,128]{1,0:T(8,128)}, f32[128,128]{1,0:T(8,128)}, f32[8,48,128]{2,1,0:T(8,128)}) custom-call(s32[4,8]{1,0:T(4,128)} %bitcast.4, f32[4,4096]{1,0:T(4,128)} %control.1, f32[256,256]{1,0:T(8,128)} %thick.3, f32[2,256,256]{2,1,0:T(8,128)} %drive.3, f32[2,256,256]{2,1,0:T(8,128)} %obs.3), custom_call_target="tpu_custom_call" | custom-call | tf_op jit(solution)/shard_map/pack/pallas_call | solution.py:650
  3.7 5.0 %all-to-all-start = ((f32[8,48,128]{2,1,0:T(8,128)}), f32[8,48,128]{2,1,0:T(8,128)S(1)}, u32[]{:S(2)}, u32[]{:S(2)}) async-start(f32[8,48,128]{2,1,0:T(8,128)} %get-tuple-element.22), calls=%async_computation | async-start | bytes 393216 | tf_op jit(solution)/shard_map/all_to_all | solution.py:667
  8.6 1.9 %collective-permute-start = (f32[128,128]{1,0:T(8,128)}, f32[128,128]{1,0:T(8,128)S(1)}, u32[]{:S(2)}, u32[]{:S(2)}) collective-permute-start(f32[128,128]{1,0:T(8,128)} %get-tuple-element.27), channel_id=1, source_target_pairs={{0,8},{16,24},{8,0},{24,16},{1,9},{17,25},{9,1},{25,17},{2,10},{18... | collective-permute-start | bytes 196616 | tf_op jit(solution)/shard_map/ppermute | solution.py:645
  10.6 0.7 %collective-permute-start.1 = (f32[128,128]{1,0:T(8,128)}, f32[128,128]{1,0:T(8,128)S(1)}, u32[]{:S(2)}, u32[]{:S(2)}) collective-permute-start(f32[128,128]{1,0:T(8,128)} %get-tuple-element.28), channel_id=1, source_target_pairs={{8,16},{16,8},{9,17},{17,9},{10,18},{18,10},{11,19},{19,11},{12,20... | collective-permute-start | bytes 196616 | tf_op jit(solution)/shard_map/ppermute | solution.py:645
  11.2 0.0 copy-done.1
  11.3 0.0 copy-done
  11.3 0.0 copy-start.2
  11.3 0.9 %copy-done.2 = f32[256,256]{1,0:T(8,128)S(1)} copy-done((f32[256,256]{1,0:T(8,128)S(1)}, f32[256,256]{1,0:T(8,128)}, u32[]{:S(2)}) %copy-start.2) | copy-done | bytes 262168
  12.2 1.1 %weave.1 = (f32[5,2,256,128]{3,2,1,0:T(8,128)S(1)}, f32[5,128,128]{2,1,0:T(8,128)S(1)}, f32[2,3,64,128]{3,2,1,0:T(8,128)S(1)}) custom-call(f32[256,256]{1,0:T(8,128)S(1)} %copy-done.2, f32[2,256,256]{2,1,0:T(8,128)S(1)} %copy-done, f32[2,256,256]{2,1,0:T(8,128)S(1)} %copy-done.1), custom_call_target="tpu_custom_call" | custom-call | tf_op jit(solution)/shard_map/weave/pallas_call | solution.py:669
  13.4 0.2 collective-permute-done.first_col
  13.6 0.0 collective-permute-done.1.second_col
  13.6 0.1 rows.1
  13.7 0.1 collective-permute-start.2
  13.8 0.7 %collective-permute-start.3 = (f32[160,128]{1,0:T(8,128)S(1)}, f32[160,128]{1,0:T(8,128)S(1)}, u32[]{:S(2)}, u32[]{:S(2)}) collective-permute-start(f32[160,128]{1,0:T(8,128)S(1)} %get-tuple-element.33), channel_id=1, source_target_pairs={{1,2},{3,4},{5,6},{2,1},{4,3},{6,5},{9,10},{11,12},{13,14},{10,9},... | collective-permute-start | bytes 245768 | tf_op jit(solution)/shard_map/ppermute | solution.py:645
  14.5 0.4 all-to-all-done.parcels
  14.9 0.0 copy-done.3
  14.9 0.0 copy-done.4
  14.9 0.9 %friction.1 = (f32[784,128]{1,0:T(8,128)S(1)}, f32[784,128]{1,0:T(8,128)S(1)}, s32[16,8,128]{2,1,0:T(8,128)S(1)}) custom-call(s32[4,8]{1,0:T(4,128)S(1)} %bitcast.5, s32[4,8]{1,0:T(4,128)S(1)} %bitcast.6, f32[8,48,128]{2,1,0:T(8,128)S(1)} %all-to-all-done.parcels), custom_call_target="tpu_custom_call" | custom-call | tf_op jit(solution)/shard_map/friction/pallas_call | solution.py:686
  15.7 1.5 %setup.1 = (f32[5,784,128]{2,1,0:T(8,128)S(1)}, f32[2,784,128]{2,1,0:T(8,128)S(1)}) custom-call(f32[784,128]{1,0:T(8,128)S(1)} %get-tuple-element.23.fr, f32[784,128]{1,0:T(8,128)S(1)} %get-tuple-element.24.ice, f32[5,2,256,128]{3,2,1,0:T(8,128)S(1)} %get-tuple-element.25.woven, f32[5,128,128]{2,1,0:T(8,128)S(1)} %get-tuple-element.26.own_sides, ...), custom_call_target="tpu_custom_call" | custom-call | tf_op jit(solution)/shard_map/setup/pallas_call | solution.py:696
  17.2 0.0 collective-permute-done.2.first_row
  17.2 0.0 collective-permute-done.3.second_row
  17.2 11.2 %model.1 = (f32[2,784,128]{2,1,0:T(8,128)S(1)}, f32[16,32,128]{2,1,0:T(8,128)S(1)}) custom-call(f32[784,128]{1,0:T(8,128)S(1)} %get-tuple-element.23.fr, f32[784,128]{1,0:T(8,128)S(1)} %get-tuple-element.24.ice, f32[5,784,128]{2,1,0:T(8,128)S(1)} %get-tuple-element.29.ext_in, f32[2,784,128]{2,1,0:T(8,128)S(1)} %get-tuple-element.30.vel_in, ...), custom_call_target="tpu_custom_call" | custom-call | tf_op jit(solution)/shard_map/model/pallas_call | solution.py:710
  28.4 22.4 %all_to_all.10.gathered = f32[16,32,128]{2,1,0:T(8,128)S(1)} all-to-all(f32[16,32,128]{2,1,0:T(8,128)S(1)} %get-tuple-element.38), channel_id=1, replica_groups={{0,2,4,6,8,10,12,14,16,18,20,22,24,26,28,30},{1,3,5,7,9,11,13,15,17,19,..., dimensions={0} | all-to-all | bytes 524288 | tf_op jit(solution)/shard_map/all_to_all | solution.py:737
  50.8 0.3 pick.1
  51.1 0.1 collective-permute-start.4
  51.2 1.2 %unweave.1 = (f32[256,256]{1,0:T(8,128)}, f32[256,256]{1,0:T(8,128)}) custom-call(f32[2,784,128]{2,1,0:T(8,128)S(1)} %get-tuple-element.34.vel), custom_call_target="tpu_custom_call" | custom-call | tf_op jit(solution)/shard_map/unweave/pallas_call | solution.py:726
  52.4 0.0 collective-permute-done.4
  52.4 0.6 %add.3 = f32[4,4096]{1,0:T(4,128)} add(f32[4,4096]{1,0:T(4,128)S(1)} %get-tuple-element.39, f32[4,4096]{1,0:T(4,128)S(1)} %collective-permute-done.4) | non-fusion elementwise | flops 16384 | bytes 196608 | tf_op jit(solution)/shard_map/add | solution.py:746
Async XLA Ops:
  0.6 10.6 %copy-start.1 = (f32[2,256,256]{2,1,0:T(8,128)S(1)}, f32[2,256,256]{2,1,0:T(8,128)}, u32[]{:S(2)}) copy-start(f32[2,256,256]{2,1,0:T(8,128)} %obs.3) | copy-start | bytes 1572868
  0.6 10.6 %copy-start = (f32[2,256,256]{2,1,0:T(8,128)S(1)}, f32[2,256,256]{2,1,0:T(8,128)}, u32[]{:S(2)}) copy-start(f32[2,256,256]{2,1,0:T(8,128)} %drive.3) | copy-start | bytes 1572868
  0.7 14.2 %copy-start.3 = (s32[8,4,1]{0,2,1:T(1,128)S(1)}, s32[8,4,1]{0,2,1:T(1,128)}, u32[]{:S(2)}) copy-start(s32[8,4,1]{0,2,1:T(1,128)} %param.11) | copy-start | bytes 388
  0.7 14.2 %copy-start.4 = (s32[8,4]{0,1:T(4,128)S(1)}, s32[8,4]{0,1:T(4,128)}, u32[]{:S(2)}) copy-start(s32[8,4]{0,1:T(4,128)} %param.10) | copy-start | bytes 388
  3.7 11.2 %all-to-all-start = ((f32[8,48,128]{2,1,0:T(8,128)}), f32[8,48,128]{2,1,0:T(8,128)S(1)}, u32[]{:S(2)}, u32[]{:S(2)}) async-start(f32[8,48,128]{2,1,0:T(8,128)} %get-tuple-element.22), calls=%async_computation | async-start | bytes 393216 | tf_op jit(solution)/shard_map/all_to_all | solution.py:667
  8.6 4.9 %collective-permute-start = (f32[128,128]{1,0:T(8,128)}, f32[128,128]{1,0:T(8,128)S(1)}, u32[]{:S(2)}, u32[]{:S(2)}) collective-permute-start(f32[128,128]{1,0:T(8,128)} %get-tuple-element.27), channel_id=1, source_target_pairs={{0,8},{16,24},{8,0},{24,16},{1,9},{17,25},{9,1},{25,17},{2,10},{18... | collective-permute-start | bytes 196616 | tf_op jit(solution)/shard_map/ppermute | solution.py:645
  10.6 3.0 %collective-permute-start.1 = (f32[128,128]{1,0:T(8,128)}, f32[128,128]{1,0:T(8,128)S(1)}, u32[]{:S(2)}, u32[]{:S(2)}) collective-permute-start(f32[128,128]{1,0:T(8,128)} %get-tuple-element.28), channel_id=1, source_target_pairs={{8,16},{16,8},{9,17},{17,9},{10,18},{18,10},{11,19},{19,11},{12,20... | collective-permute-start | bytes 196616 | tf_op jit(solution)/shard_map/ppermute | solution.py:645
  11.3 1.0 %copy-start.2 = (f32[256,256]{1,0:T(8,128)S(1)}, f32[256,256]{1,0:T(8,128)}, u32[]{:S(2)}) copy-start(f32[256,256]{1,0:T(8,128)} %thick.3) | copy-start | bytes 786436
  13.7 3.5 %collective-permute-start.2 = (f32[160,128]{1,0:T(8,128)S(1)}, f32[160,128]{1,0:T(8,128)S(1)}, u32[]{:S(2)}, u32[]{:S(2)}) collective-permute-start(f32[160,128]{1,0:T(8,128)S(1)} %get-tuple-element.32), channel_id=1, source_target_pairs={{0,1},{2,3},{4,5},{6,7},{1,0},{3,2},{5,4},{7,6},{8,9},{10,11},{12,... | collective-permute-start | bytes 245768 | tf_op jit(solution)/shard_map/ppermute | solution.py:645
  13.8 3.4 %collective-permute-start.3 = (f32[160,128]{1,0:T(8,128)S(1)}, f32[160,128]{1,0:T(8,128)S(1)}, u32[]{:S(2)}, u32[]{:S(2)}) collective-permute-start(f32[160,128]{1,0:T(8,128)S(1)} %get-tuple-element.33), channel_id=1, source_target_pairs={{1,2},{3,4},{5,6},{2,1},{4,3},{6,5},{9,10},{11,12},{13,14},{10,9},... | collective-permute-start | bytes 245768 | tf_op jit(solution)/shard_map/ppermute | solution.py:645
  51.1 1.3 %collective-permute-start.4 = (f32[4,4096]{1,0:T(4,128)S(1)}, f32[4,4096]{1,0:T(4,128)S(1)}, u32[]{:S(2)}, u32[]{:S(2)}) collective-permute-start(f32[4,4096]{1,0:T(4,128)S(1)} %get-tuple-element.40), channel_id=1, source_target_pairs={{0,1},{1,0},{2,3},{3,2},{4,5},{5,4},{6,7},{7,6},{8,9},{9,8},{10,11... | collective-permute-start | bytes 196616 | tf_op jit(solution)/shard_map/ppermute | solution.py:746
